TPU v7x, 32 devices: a whole 2x2x4 slice. The times are simulated.
32 devices in a mesh: sp: 4 (over z), fsdp: 8 (over y, x, core).
Axes of the slice: x: 2, y: 2, z: 4, core: 2. Of those that a mesh axis runs over, the one named last changes fastest.
Arguments:
- tokens: bfloat16 [8, 512, 2048], P('fsdp', 'sp'), may hold values from -6 to 6
- expert_ids: int32 [8, 512, 8], P('fsdp', 'sp'), may hold values from 0 to 15, all different within a row; in each aligned block of 128 rows (0 to 127, 128 to 255, ..., all dimensions but the last counted through in order) at most 80 rows name the same one
- attn_gain: float32 [2048], P('fsdp'), may hold values from 0.25 to 1.75
- query_weight: float32 [2048, 4096], P('fsdp'), may hold values from -0.125 to 0.125
- key_weight: float32 [2048, 512], P('fsdp'), may hold values from -0.125 to 0.125
- value_weight: float32 [2048, 512], P('fsdp'), may hold values from -0.125 to 0.125
- q_gain: float32 [128], P('fsdp'), may hold values from 0.25 to 1.75
- k_gain: float32 [128], P('fsdp'), may hold values from 0.25 to 1.75
- output_weight: float32 [4096, 2048], P('fsdp'), may hold values from -0.375 to 0.375
- ffn_gain: float32 [2048], P('fsdp'), may hold values from 0.25 to 1.75
- router_weight: float32 [2048, 16], P('fsdp'), may hold values from -0.0625 to 0.0625
- w_gate: float32 [16, 2048, 768], P(None, 'fsdp'), may hold values from -0.125 to 0.125
- w_up: float32 [16, 2048, 768], P(None, 'fsdp'), may hold values from -0.125 to 0.125
- w_down: float32 [16, 768, 2048], P(None, 'fsdp'), may hold values from -0.625 to 0.625
- cotangent: bfloat16 [8, 512, 2048], P('fsdp', 'sp'), may hold values from -6 to 6
Outputs:
- mixed: bfloat16 [8, 512, 2048], P('fsdp', 'sp')
- grad_tokens: float32 [8, 512, 2048], P('fsdp', 'sp')
- grad_attn_gain: float32 [2048], P('fsdp')
- grad_w_query: float32 [2048, 4096], P('fsdp')
- grad_w_key: float32 [2048, 512], P('fsdp')
- grad_w_value: float32 [2048, 512], P('fsdp')
- grad_q_gain: float32 [128], P('fsdp')
- grad_k_gain: float32 [128], P('fsdp')
- grad_w_out: float32 [4096, 2048], P('fsdp')
- grad_ffn_gain: float32 [2048], P('fsdp')
- grad_w_router: float32 [2048, 16], P('fsdp')
- grad_w_gate: float32 [16, 2048, 768], P(None, 'fsdp')
- grad_w_up: float32 [16, 2048, 768], P(None, 'fsdp')
- grad_w_down: float32 [16, 768, 2048], P(None, 'fsdp')
Inputs may be any that keep to these rules, and one draw needn't show every extreme that they name: `expert_ids`: each token names 8 different experts. In the rows of one device, no expert is named more than 80 times, and in every draw some expert of some device is named exactly 80 times.
All inputs are finite; a program needn't handle non-finite values.
Results may differ from a plain program's by a relative error of at most 0.023.
Values may be sent and summed in bfloat16 or wider, within the bound.
A program may use at most 320 MiB of HBM per device.

v0:
```python
import math

import jax
import jax.numpy as jnp
from jax import lax
from jax.sharding import PartitionSpec as P

QUERY_HEADS = 32
KEY_VALUE_HEADS = 4
HEAD_SIZE = 128
CAP = 80


EPS = 1e-06
THETA = 1000000.0
HIGH_PRECISION = lax.Precision.HIGHEST
BF16 = jnp.bfloat16
FLOAT = jnp.float32


def rms_norm(values_in, gain_vec):
    return (
        values_in
        * lax.rsqrt(jnp.mean(values_in * values_in, axis=-1, keepdims=True) + EPS)
        * gain_vec
    )


def rotate(values_in, angles):
    half_dim = values_in.shape[-1] // 2
    cosine = jnp.cos(angles)[:, None, :]
    sine_part = jnp.sin(angles)[:, None, :]
    first_half = values_in[..., :half_dim]
    second = values_in[..., half_dim:]
    return jnp.concatenate(
        [first_half * cosine - second * sine_part, second * cosine + first_half * sine_part],
        axis=-1,
    )


def block_scores(query_blk, key_part, row_start, score_scale):
    scores = (
        jnp.einsum("qhd,kd->hqk", query_blk, key_part, preferred_element_type=FLOAT) * score_scale
    )
    row_idx = row_start + jnp.arange(query_blk.shape[0], dtype=jnp.int32)[:, None]
    col_idx = jnp.arange(key_part.shape[0], dtype=jnp.int32)[None, :]
    return jnp.where((col_idx <= row_idx)[None], scores, -1e30)


def contract_rows(left_mat, right_mat):
    return lax.dot_general(
        left_mat, right_mat, (((0,), (0,)), ((), ())), preferred_element_type=FLOAT
    )


def contract_cols(left_mat, right_mat):
    return lax.dot_general(
        left_mat, right_mat, (((1,), (1,)), ((), ())), preferred_element_type=FLOAT
    )


def fetch_all(gate_shard, up_shard, down_shard):
    return (
        lax.all_gather(gate_shard, "fsdp", axis=0, tiled=True),
        lax.all_gather(up_shard, "fsdp", axis=0, tiled=True),
        lax.all_gather(down_shard, "fsdp", axis=0, tiled=True),
    )


def reduce_all(grad_first, grad_second, grad_third):
    return (
        lax.psum_scatter(
            grad_first.astype(jnp.bfloat16), "fsdp", scatter_dimension=0, tiled=True
        ).astype(jnp.float32),
        lax.psum_scatter(
            grad_second.astype(jnp.bfloat16), "fsdp", scatter_dimension=0, tiled=True
        ).astype(jnp.float32),
        lax.psum_scatter(
            grad_third.astype(jnp.bfloat16), "fsdp", scatter_dimension=0, tiled=True
        ).astype(jnp.float32),
    )


def expert_forward_pass(fetch, gate_sh, up_sh, down_sh, rows_all):

    def step(carry_in, pieces):
        gate_shard, up_shard, down_shard, expert_rows = pieces
        wg_b, wu_b, wd_b = fetch(gate_shard, up_shard, down_shard)
        gate_pre = jnp.dot(expert_rows, wg_b, preferred_element_type=FLOAT)
        up_pre = jnp.dot(expert_rows, wu_b, preferred_element_type=FLOAT)
        hidden = (jax.nn.silu(gate_pre) * up_pre).astype(BF16)
        result = jnp.dot(hidden, wd_b, preferred_element_type=FLOAT)
        return (carry_in, (gate_pre, up_pre, result))

    unused, kept = lax.scan(step, jnp.zeros((), FLOAT), (gate_sh, up_sh, down_sh, rows_all))
    return kept


def expert_backward_pass(
    fetch, reduce_fn, gate_sh, up_sh, down_sh, gate_pres, up_pres, rows_all, d_res_all
):

    def step(carry_in, pieces):
        gate_shard, up_shard, down_shard, gate_pre, up_pre, expert_rows, d_res = pieces
        wg_b, wu_b, wd_b = fetch(gate_shard, up_shard, down_shard)
        sigma = jax.nn.sigmoid(gate_pre)
        act_f = gate_pre * sigma
        hidden = (act_f * up_pre).astype(BF16)
        d_hidden = contract_cols(d_res, wd_b)
        d_down = contract_rows(hidden, d_res)
        d_gate_pre = (d_hidden * up_pre * sigma * (1.0 + gate_pre * (1.0 - sigma))).astype(BF16)
        d_up_pre = (d_hidden * act_f).astype(BF16)
        d_wg = contract_rows(expert_rows, d_gate_pre)
        d_wu = contract_rows(expert_rows, d_up_pre)
        d_rows = contract_cols(d_gate_pre, wg_b) + contract_cols(d_up_pre, wu_b)
        shard_g, shard_u, shard_d = reduce_fn(d_wg, d_wu, d_down)
        return (carry_in, (shard_g, shard_u, shard_d, d_rows))

    unused, outputs = lax.scan(
        step,
        jnp.zeros((), FLOAT),
        (gate_sh, up_sh, down_sh, gate_pres, up_pres, rows_all, d_res_all),
    )
    return outputs


def body(
    tokens,
    expert_ids,
    attn_gain,
    query_weight,
    key_weight,
    value_weight,
    q_gain,
    k_gain,
    output_weight,
    ffn_gain,
    router_weight,
    w_gate,
    w_up,
    w_down,
    cotangent,
):
    sp_count = lax.axis_size("sp")
    tok_rows = tokens.shape[1]
    model_width = tokens.shape[2]
    n_heads = QUERY_HEADS
    kv_heads = KEY_VALUE_HEADS
    head_dim = HEAD_SIZE
    repeat = sp_count // kv_heads
    sequence_length = tok_rows * sp_count
    score_scale = 1.0 / math.sqrt(head_dim)
    n_experts = w_gate.shape[0]
    top_k = expert_ids.shape[2]
    capacity = CAP
    full = (
        lax.all_gather(attn_gain.astype(BF16), "fsdp", axis=0, tiled=True),
        lax.all_gather(query_weight.astype(BF16), "fsdp", axis=0, tiled=True),
        lax.all_gather(key_weight.astype(BF16), "fsdp", axis=0, tiled=True),
        lax.all_gather(value_weight.astype(BF16), "fsdp", axis=0, tiled=True),
        lax.all_gather(q_gain.astype(BF16), "fsdp", axis=0, tiled=True),
        lax.all_gather(k_gain.astype(BF16), "fsdp", axis=0, tiled=True),
        lax.all_gather(output_weight.astype(BF16), "fsdp", axis=0, tiled=True),
        lax.all_gather(ffn_gain.astype(BF16), "fsdp", axis=0, tiled=True),
        lax.all_gather(router_weight.astype(BF16), "fsdp", axis=0, tiled=True),
    )
    g_attn, wq_b, wk_b, wv_b, g_query, g_key, wo_b, g_ffn, wr_b = full
    x_rows = tokens[0].astype(FLOAT)
    xn_b = rms_norm(x_rows, g_attn.astype(FLOAT)).astype(BF16)
    query_linear = jnp.dot(xn_b, wq_b, preferred_element_type=FLOAT).reshape(
        tok_rows, n_heads, head_dim
    )
    key_linear = jnp.dot(xn_b, wk_b, preferred_element_type=FLOAT).reshape(
        tok_rows, kv_heads, head_dim
    )
    v_b = (
        jnp.dot(xn_b, wv_b, preferred_element_type=FLOAT)
        .astype(BF16)
        .reshape(tok_rows, kv_heads, head_dim)
    )
    half_dim = head_dim // 2
    inverse_freq = THETA ** (-(jnp.arange(half_dim, dtype=FLOAT) * 2.0 / head_dim))
    positions = (lax.axis_index("sp") * tok_rows + jnp.arange(tok_rows, dtype=jnp.int32)).astype(
        FLOAT
    )
    angles = positions[:, None] * inverse_freq[None, :]

    def prep_heads(linear, gain_vec):
        return rotate(rms_norm(linear, gain_vec), angles)

    q_b = prep_heads(query_linear, g_query.astype(FLOAT)).astype(BF16)
    k_b = prep_heads(key_linear, g_key.astype(FLOAT)).astype(BF16)
    k_rep = jnp.repeat(k_b, repeat, axis=1)
    v_rep = jnp.repeat(v_b, repeat, axis=1)
    q_heads, k_heads, v_heads = (
        lax.all_to_all(q_b, "sp", split_axis=1, concat_axis=0, tiled=True),
        lax.all_to_all(k_rep, "sp", split_axis=1, concat_axis=0, tiled=True),
        lax.all_to_all(v_rep, "sp", split_axis=1, concat_axis=0, tiled=True),
    )
    key_mat = k_heads[:, 0, :]
    val_mat = v_heads[:, 0, :]
    block_rows = min(512, sequence_length)
    n_blocks = sequence_length // block_rows
    out_list = []
    lse_list = []
    for blk_idx in range(n_blocks):
        row_start = blk_idx * block_rows
        row_stop = row_start + block_rows
        scores = block_scores(
            q_heads[row_start:row_stop], key_mat[:row_stop], row_start, score_scale
        )
        row_top = jnp.max(scores, axis=2, keepdims=True)
        expo = jnp.exp(scores - row_top)
        row_total = jnp.sum(expo, axis=2, keepdims=True)
        prob_rows = (expo / row_total).astype(BF16)
        lse_list.append((row_top + jnp.log(row_total))[:, :, 0])
        out_list.append(
            jnp.einsum(
                "hqk,kd->qhd", prob_rows, val_mat[:row_stop], preferred_element_type=FLOAT
            ).astype(BF16)
        )
    o_heads = jnp.concatenate(out_list, axis=0)
    lse_all = jnp.concatenate(lse_list, axis=1)
    o_tok = lax.all_to_all(o_heads, "sp", split_axis=0, concat_axis=1, tiled=True).reshape(
        tok_rows, n_heads * head_dim
    )
    mid_rows = x_rows + jnp.dot(o_tok, wo_b, preferred_element_type=FLOAT)
    hn_b = rms_norm(mid_rows, g_ffn.astype(FLOAT)).astype(BF16)
    router_logits = jnp.dot(hn_b, wr_b, preferred_element_type=FLOAT)
    routes = expert_ids[0]
    chosen = jnp.take_along_axis(router_logits, routes, axis=1)
    gate_probs = jax.nn.softmax(chosen, axis=-1)
    flat_routes = routes.reshape(-1)
    expert_iota = jnp.arange(n_experts, dtype=jnp.int32)
    onehot = (flat_routes[:, None] == expert_iota[None, :]).astype(jnp.int32)
    before = jnp.cumsum(onehot, axis=0) - onehot
    slot_rank = jnp.sum(before * onehot, axis=1)
    slot_ids = flat_routes * capacity + slot_rank
    owner_rows = jnp.repeat(jnp.arange(tok_rows, dtype=jnp.int32), top_k)
    slot_token = jnp.zeros((n_experts * capacity,), jnp.int32).at[slot_ids].set(owner_rows)
    slot_gate = jnp.zeros((n_experts * capacity,), FLOAT).at[slot_ids].set(gate_probs.reshape(-1))
    rows_in = hn_b[slot_token].reshape(n_experts, capacity, model_width)
    low_gate = w_gate.astype(BF16)
    low_up = w_up.astype(BF16)
    low_down = w_down.astype(BF16)
    gate_pres, up_pres, results = expert_forward_pass(
        fetch_all, low_gate, low_up, low_down, rows_in
    )
    picked = results.reshape(n_experts * capacity, model_width)[slot_ids].reshape(
        tok_rows, top_k, model_width
    )
    moe_sum = jnp.sum(gate_probs[:, :, None] * picked, axis=1)
    mixed = (mid_rows + moe_sum).astype(BF16)[None]
    grad_out = cotangent[0].astype(FLOAT)
    d_gates = jnp.sum(grad_out[:, None, :] * picked, axis=2)
    d_chosen = gate_probs * (d_gates - jnp.sum(gate_probs * d_gates, axis=1, keepdims=True))
    route_hot = (routes[:, :, None] == expert_iota[None, None, :]).astype(FLOAT)
    d_logits = jnp.sum(d_chosen[:, :, None] * route_hot, axis=1)
    d_router = jnp.dot(hn_b.astype(FLOAT).T, d_logits, precision=HIGH_PRECISION)
    d_hn = jnp.dot(d_logits, wr_b.astype(FLOAT).T, precision=HIGH_PRECISION)
    d_result = (
        (slot_gate[:, None] * grad_out[slot_token])
        .astype(BF16)
        .reshape(n_experts, capacity, model_width)
    )
    grad_gate_sh, grad_up_sh, grad_down_sh, d_rows_all = expert_backward_pass(
        fetch_all, reduce_all, low_gate, low_up, low_down, gate_pres, up_pres, rows_in, d_result
    )
    d_hn = d_hn + jnp.sum(
        d_rows_all.reshape(n_experts * capacity, model_width)[slot_ids].reshape(
            tok_rows, top_k, model_width
        ),
        axis=1,
    )
    unused3, ffn_pull = jax.vjp(rms_norm, mid_rows, g_ffn.astype(FLOAT))
    d_mid_norm, d_ffn_gain = ffn_pull(d_hn)
    d_mid = grad_out + d_mid_norm
    d_attn_b = d_mid.astype(BF16)
    d_wo = contract_rows(o_tok, d_attn_b)
    d_o = contract_cols(d_attn_b, wo_b).astype(BF16).reshape(tok_rows, n_heads, head_dim)
    d_o_heads = lax.all_to_all(d_o, "sp", split_axis=1, concat_axis=0, tiled=True)
    dq_list = []
    d_key = jnp.zeros((sequence_length, head_dim), FLOAT)
    d_val = jnp.zeros((sequence_length, head_dim), FLOAT)
    for blk_idx in range(n_blocks):
        row_start = blk_idx * block_rows
        row_stop = row_start + block_rows
        query_blk = q_heads[row_start:row_stop]
        scores = block_scores(query_blk, key_mat[:row_stop], row_start, score_scale)
        prob_rows = jnp.exp(scores - lse_all[:, row_start:row_stop, None])
        d_out_blk = d_o_heads[row_start:row_stop]
        d_val = d_val.at[:row_stop].add(
            jnp.einsum(
                "hqk,qhd->kd", prob_rows.astype(BF16), d_out_blk, preferred_element_type=FLOAT
            )
        )
        d_probs = jnp.einsum(
            "qhd,kd->hqk", d_out_blk, val_mat[:row_stop], preferred_element_type=FLOAT
        )
        d_scores = (
            prob_rows * (d_probs - jnp.sum(prob_rows * d_probs, axis=2, keepdims=True))
        ).astype(BF16)
        dq_list.append(
            (
                jnp.einsum(
                    "hqk,kd->qhd", d_scores, key_mat[:row_stop], preferred_element_type=FLOAT
                )
                * score_scale
            ).astype(BF16)
        )
        d_key = d_key.at[:row_stop].add(
            jnp.einsum("hqk,qhd->kd", d_scores, query_blk, preferred_element_type=FLOAT)
            * score_scale
        )
    dq_heads = jnp.concatenate(dq_list, axis=0)
    dq_tok, dk_tok, dv_tok = (
        lax.all_to_all(dq_heads, "sp", split_axis=0, concat_axis=1, tiled=True),
        lax.all_to_all(
            d_key.astype(BF16)[:, None, :], "sp", split_axis=0, concat_axis=1, tiled=True
        ),
        lax.all_to_all(
            d_val.astype(BF16)[:, None, :], "sp", split_axis=0, concat_axis=1, tiled=True
        ),
    )
    dk_sum = jnp.sum(dk_tok.astype(FLOAT).reshape(tok_rows, kv_heads, repeat, head_dim), axis=2)
    dv_sum = jnp.sum(dv_tok.astype(FLOAT).reshape(tok_rows, kv_heads, repeat, head_dim), axis=2)
    unused4, q_pull = jax.vjp(prep_heads, query_linear, g_query.astype(FLOAT))
    d_q_lin, d_q_gain = q_pull(dq_tok.astype(FLOAT))
    unused5, k_pull = jax.vjp(prep_heads, key_linear, g_key.astype(FLOAT))
    d_k_lin, d_k_gain = k_pull(dk_sum)
    dq_b = d_q_lin.astype(BF16).reshape(tok_rows, n_heads * head_dim)
    dk_b = d_k_lin.astype(BF16).reshape(tok_rows, kv_heads * head_dim)
    dv_b = dv_sum.astype(BF16).reshape(tok_rows, kv_heads * head_dim)
    d_xn = contract_cols(dq_b, wq_b) + contract_cols(dk_b, wk_b) + contract_cols(dv_b, wv_b)
    d_wq = contract_rows(xn_b, dq_b)
    d_wk = contract_rows(xn_b, dk_b)
    d_wv = contract_rows(xn_b, dv_b)
    unused6, attn_pull = jax.vjp(rms_norm, x_rows, g_attn.astype(FLOAT))
    d_x_norm, d_attn_gain = attn_pull(d_xn)
    grad_tokens = (d_mid + d_x_norm)[None]
    attn_shards = (
        lax.psum_scatter(
            d_attn_gain.astype(jnp.bfloat16), "fsdp", scatter_dimension=0, tiled=True
        ).astype(jnp.float32),
        lax.psum_scatter(d_wq.astype(jnp.bfloat16), "fsdp", scatter_dimension=0, tiled=True).astype(
            jnp.float32
        ),
        lax.psum_scatter(d_wk.astype(jnp.bfloat16), "fsdp", scatter_dimension=0, tiled=True).astype(
            jnp.float32
        ),
        lax.psum_scatter(d_wv.astype(jnp.bfloat16), "fsdp", scatter_dimension=0, tiled=True).astype(
            jnp.float32
        ),
        lax.psum_scatter(
            d_q_gain.astype(jnp.bfloat16), "fsdp", scatter_dimension=0, tiled=True
        ).astype(jnp.float32),
        lax.psum_scatter(
            d_k_gain.astype(jnp.bfloat16), "fsdp", scatter_dimension=0, tiled=True
        ).astype(jnp.float32),
        lax.psum_scatter(d_wo.astype(jnp.bfloat16), "fsdp", scatter_dimension=0, tiled=True).astype(
            jnp.float32
        ),
        lax.psum_scatter(
            d_ffn_gain.astype(jnp.bfloat16), "fsdp", scatter_dimension=0, tiled=True
        ).astype(jnp.float32),
        lax.psum_scatter(
            d_router.astype(jnp.bfloat16), "fsdp", scatter_dimension=0, tiled=True
        ).astype(jnp.float32),
    )
    summed = (
        lax.psum(attn_shards[0].astype(jnp.bfloat16), "sp").astype(jnp.float32),
        lax.psum(attn_shards[1].astype(jnp.bfloat16), "sp").astype(jnp.float32),
        lax.psum(attn_shards[2].astype(jnp.bfloat16), "sp").astype(jnp.float32),
        lax.psum(attn_shards[3].astype(jnp.bfloat16), "sp").astype(jnp.float32),
        lax.psum(attn_shards[4].astype(jnp.bfloat16), "sp").astype(jnp.float32),
        lax.psum(attn_shards[5].astype(jnp.bfloat16), "sp").astype(jnp.float32),
        lax.psum(attn_shards[6].astype(jnp.bfloat16), "sp").astype(jnp.float32),
        lax.psum(attn_shards[7].astype(jnp.bfloat16), "sp").astype(jnp.float32),
        lax.psum(attn_shards[8].astype(jnp.bfloat16), "sp").astype(jnp.float32),
        lax.psum(grad_gate_sh.astype(jnp.bfloat16), "sp").astype(jnp.float32),
        lax.psum(grad_up_sh.astype(jnp.bfloat16), "sp").astype(jnp.float32),
        lax.psum(grad_down_sh.astype(jnp.bfloat16), "sp").astype(jnp.float32),
    )
    return (
        mixed,
        grad_tokens,
        summed[0],
        summed[1],
        summed[2],
        summed[3],
        summed[4],
        summed[5],
        summed[6],
        summed[7],
        summed[8],
        summed[9],
        summed[10],
        summed[11],
    )


def solution(mesh):
    in_specs = (
        P("fsdp", "sp", None),
        P("fsdp", "sp", None),
        P("fsdp"),
        P("fsdp", None),
        P("fsdp", None),
        P("fsdp", None),
        P("fsdp"),
        P("fsdp"),
        P("fsdp", None),
        P("fsdp"),
        P("fsdp", None),
        P(None, "fsdp", None),
        P(None, "fsdp", None),
        P(None, "fsdp", None),
        P("fsdp", "sp", None),
    )
    out_specs = (
        P("fsdp", "sp", None),
        P("fsdp", "sp", None),
        P("fsdp"),
        P("fsdp", None),
        P("fsdp", None),
        P("fsdp", None),
        P("fsdp"),
        P("fsdp"),
        P("fsdp", None),
        P("fsdp"),
        P("fsdp", None),
        P(None, "fsdp", None),
        P(None, "fsdp", None),
        P(None, "fsdp", None),
    )
    return jax.shard_map(body, mesh=mesh, in_specs=in_specs, out_specs=out_specs, check_vma=False)
```

profile of v0, /device:TPU:0, one launch (start us, length us, event | category | flops | bytes accessed | tf_op | source)
XLA Modules:
  0.0 7420.1 jit_solution(11706762338554560625)
XLA Ops:
  56.6 77.0 %all-gather.35.cloned.1.call-done = bf16[2048,4096]{1,0:T(8,128)(2,1)} async-done(((bf16[256,4096]{1,0:T(8,128)(2,1)}), bf16[2048,4096]{1,0:T(8,128)(2,1)}) %all-gather.35.cloned.1.call-update) | async-done | bytes 16777232 | tf_op jit(solution)/shard_map/all_gather | solution.py:158
  296.6 1721.7 %while.34 = (s32[]{:T(128)}, f32[16,80,768]{2,1,0:T(8,128)}, f32[16,80,768]{2,1,0:T(8,128)}, f32[16,80,2048]{2,1,0:T(8,128)}, bf16[16,80,2048]{2,1,0:T(8,128)(2,...) while((s32[]{:T(128)}, f32[16,80,768]{2,1,0:T(8,128)}, ...), condition=%wide.region_13.14_spmd, body=%wide.region_12.13_spmd.sunk | while | flops 755343360 | bytes 46434540 | solution.py:95
  2054.3 4098.9 %while.35 = (s32[]{:T(128)}, bf16[16,256,768]{2,1,0:T(8,128)(2,1)}, bf16[16,256,768]{2,1,0:T(8,128)(2,1)}, bf16[16,96,2048]{2,1,0:T(8,128)(2,1)}, f32[16,80,2048...) while((s32[]{:T(128)}, bf16[16,256,768]{2,1,0:T(8,128)(2,1)}, ...), condition=%wide.region_23.24_spmd, body=%wide.region_19.23_spmd.sunk | while | flops 1516589056 | bytes 93473184 | solution.py:119
  2100.1 39.1 reduce-scatter.23.cloned.1.call-done
  2212.4 46.3 reduce-scatter.21.cloned.1.call-done
  2260.4 48.3 reduce-scatter.19.cloned.1.call-done
  2356.3 39.1 reduce-scatter.23.cloned.1.call-done
  2468.6 46.1 reduce-scatter.21.cloned.1.call-done
  2516.5 48.3 reduce-scatter.19.cloned.1.call-done
  2724.6 46.3 reduce-scatter.21.cloned.1.call-done
  2772.7 48.3 reduce-scatter.19.cloned.1.call-done
  2980.7 46.3 reduce-scatter.21.cloned.1.call-done
  3028.7 48.3 reduce-scatter.19.cloned.1.call-done
  3125.0 39.1 reduce-scatter.23.cloned.1.call-done
  3237.2 46.3 reduce-scatter.21.cloned.1.call-done
  3285.2 48.3 reduce-scatter.19.cloned.1.call-done
  3493.4 46.1 reduce-scatter.21.cloned.1.call-done
  3541.3 48.3 reduce-scatter.19.cloned.1.call-done
  3637.5 39.1 reduce-scatter.23.cloned.1.call-done
  3749.6 46.1 reduce-scatter.21.cloned.1.call-done
  3797.5 48.5 reduce-scatter.19.cloned.1.call-done
  3893.9 39.1 reduce-scatter.23.cloned.1.call-done
  4005.8 46.1 reduce-scatter.21.cloned.1.call-done
  4053.7 48.3 reduce-scatter.19.cloned.1.call-done
  4150.0 39.1 reduce-scatter.23.cloned.1.call-done
  4261.9 46.1 reduce-scatter.21.cloned.1.call-done
  4309.8 48.4 reduce-scatter.19.cloned.1.call-done
  4405.9 39.1 reduce-scatter.23.cloned.1.call-done
  4518.0 46.3 reduce-scatter.21.cloned.1.call-done
  4566.0 48.5 reduce-scatter.19.cloned.1.call-done
  4662.4 39.1 reduce-scatter.23.cloned.1.call-done
  4774.5 46.1 reduce-scatter.21.cloned.1.call-done
  4822.4 48.3 reduce-scatter.19.cloned.1.call-done
  4918.3 39.1 reduce-scatter.23.cloned.1.call-done
  5030.4 46.3 reduce-scatter.21.cloned.1.call-done
  5078.4 48.3 reduce-scatter.19.cloned.1.call-done
  5286.5 46.3 reduce-scatter.21.cloned.1.call-done
  5334.5 48.3 reduce-scatter.19.cloned.1.call-done
  5542.7 46.1 reduce-scatter.21.cloned.1.call-done
  5590.6 48.3 reduce-scatter.19.cloned.1.call-done
  5686.9 39.1 reduce-scatter.23.cloned.1.call-done
  5799.0 46.1 reduce-scatter.21.cloned.1.call-done
  5846.8 48.3 reduce-scatter.19.cloned.1.call-done
  6055.0 46.1 reduce-scatter.21.cloned.1.call-done
  6102.9 48.5 reduce-scatter.19.cloned.1.call-done
  6320.4 118.6 %reduce-scatter.15.cloned.1.call-done = bf16[512,2048]{1,0:T(8,128)(2,1)} async-done(((bf16[4096,2048]{1,0:T(8,128)(2,1)}), bf16[512,2048]{1,0:T(8,128)(2,1)}) %reduce-scatter.15.cloned.1.call-update) | async-done | bytes 2097168 | tf_op jit(solution)/shard_map/reduce_scatter | solution.py:360
  6439.0 119.4 %reduce-scatter.9.cloned.1.call-done = bf16[256,4096]{1,0:T(8,128)(2,1)} async-done(((bf16[2048,4096]{1,0:T(8,128)(2,1)}), bf16[256,4096]{1,0:T(8,128)(2,1)}) %reduce-scatter.9.cloned.1.call-update) | async-done | bytes 2097168 | tf_op jit(solution)/shard_map/reduce_scatter | solution.py:345
  6616.4 768.1 %all-reduce.16.cloned.1.call-done = (bf16[256,4096]{1,0:T(8,128)(2,1)}, bf16[256,512]{1,0:T(8,128)(2,1)}, bf16[256,512]{1,0:T(8,128)(2,1)}, bf16[512,2048]{1,0:T...) async-done(((bf16[256,4096]{1,0:T(8,128)(2,1)}, bf16[256,512]{1,0:T(8,128)(2,1)}, ...) | async-done | bytes 23592976 | tf_op jit(solution)/shard_map/psum | solution.py:372
  (1047 shorter events, 4413.3 us)
Async XLA Ops:
  13.0 199.0 %all-gather.31.cloned.1.call-start = ((), (), s32[]{:S(2)}) async-start(), calls=%async_computation.16 | async-start | bytes 2359296 | tf_op jit(solution)/shard_map/all_gather | solution.py:160
  13.8 253.7 %all-gather.37.cloned.1.call-start = ((), (), s32[]{:S(2)}) async-start(), calls=%async_computation.19 | async-start | bytes 18874368 | tf_op jit(solution)/shard_map/all_gather | solution.py:163
  2061.9 146.7 %all-gather.49.cloned.1.call-start = ((), (), s32[]{:S(2)}) async-start(), calls=%async_computation.34 | async-start | bytes 3538944 | tf_op jit(solution)/shard_map/while/body/eval_jaxpr/all_gather | solution.py:64
  2063.8 194.9 %reduce-scatter.21.cloned.1.call-start = ((), (), s32[]{:S(2)}) async-start(), calls=%async_computation.31 | async-start | bytes 3538944 | tf_op jit(solution)/shard_map/while/body/eval_jaxpr/reduce_scatter | solution.py:75
  2096.4 212.3 %reduce-scatter.19.cloned.1.call-start = ((), (), s32[]{:S(2)}) async-start(), calls=%async_computation.30 | async-start | bytes 3538944 | tf_op jit(solution)/shard_map/while/body/eval_jaxpr/reduce_scatter | solution.py:72
  2320.0 194.7 %reduce-scatter.21.cloned.1.call-start = ((), (), s32[]{:S(2)}) async-start(), calls=%async_computation.31 | async-start | bytes 3538944 | tf_op jit(solution)/shard_map/while/body/eval_jaxpr/reduce_scatter | solution.py:75
  2352.6 212.2 %reduce-scatter.19.cloned.1.call-start = ((), (), s32[]{:S(2)}) async-start(), calls=%async_computation.30 | async-start | bytes 3538944 | tf_op jit(solution)/shard_map/while/body/eval_jaxpr/reduce_scatter | solution.py:72
  2576.0 194.9 %reduce-scatter.21.cloned.1.call-start = ((), (), s32[]{:S(2)}) async-start(), calls=%async_computation.31 | async-start | bytes 3538944 | tf_op jit(solution)/shard_map/while/body/eval_jaxpr/reduce_scatter | solution.py:75
  2609.0 212.0 %reduce-scatter.19.cloned.1.call-start = ((), (), s32[]{:S(2)}) async-start(), calls=%async_computation.30 | async-start | bytes 3538944 | tf_op jit(solution)/shard_map/while/body/eval_jaxpr/reduce_scatter | solution.py:72
  2832.2 194.7 %reduce-scatter.21.cloned.1.call-start = ((), (), s32[]{:S(2)}) async-start(), calls=%async_computation.31 | async-start | bytes 3538944 | tf_op jit(solution)/shard_map/while/body/eval_jaxpr/reduce_scatter | solution.py:75
  2865.2 211.8 %reduce-scatter.19.cloned.1.call-start = ((), (), s32[]{:S(2)}) async-start(), calls=%async_computation.30 | async-start | bytes 3538944 | tf_op jit(solution)/shard_map/while/body/eval_jaxpr/reduce_scatter | solution.py:72
  3086.4 147.0 %all-gather.49.cloned.1.call-start = ((), (), s32[]{:S(2)}) async-start(), calls=%async_computation.34 | async-start | bytes 3538944 | tf_op jit(solution)/shard_map/while/body/eval_jaxpr/all_gather | solution.py:64
  3088.3 195.2 %reduce-scatter.21.cloned.1.call-start = ((), (), s32[]{:S(2)}) async-start(), calls=%async_computation.31 | async-start | bytes 3538944 | tf_op jit(solution)/shard_map/while/body/eval_jaxpr/reduce_scatter | solution.py:75
  3121.2 212.3 %reduce-scatter.19.cloned.1.call-start = ((), (), s32[]{:S(2)}) async-start(), calls=%async_computation.30 | async-start | bytes 3538944 | tf_op jit(solution)/shard_map/while/body/eval_jaxpr/reduce_scatter | solution.py:72
  3342.9 146.7 %all-gather.49.cloned.1.call-start = ((), (), s32[]{:S(2)}) async-start(), calls=%async_computation.34 | async-start | bytes 3538944 | tf_op jit(solution)/shard_map/while/body/eval_jaxpr/all_gather | solution.py:64
  3344.8 194.7 %reduce-scatter.21.cloned.1.call-start = ((), (), s32[]{:S(2)}) async-start(), calls=%async_computation.31 | async-start | bytes 3538944 | tf_op jit(solution)/shard_map/while/body/eval_jaxpr/reduce_scatter | solution.py:75
  3377.7 211.8 %reduce-scatter.19.cloned.1.call-start = ((), (), s32[]{:S(2)}) async-start(), calls=%async_computation.30 | async-start | bytes 3538944 | tf_op jit(solution)/shard_map/while/body/eval_jaxpr/reduce_scatter | solution.py:72
  3599.0 146.8 %all-gather.49.cloned.1.call-start = ((), (), s32[]{:S(2)}) async-start(), calls=%async_computation.34 | async-start | bytes 3538944 | tf_op jit(solution)/shard_map/while/body/eval_jaxpr/all_gather | solution.py:64
  3600.9 194.9 %reduce-scatter.21.cloned.1.call-start = ((), (), s32[]{:S(2)}) async-start(), calls=%async_computation.31 | async-start | bytes 3538944 | tf_op jit(solution)/shard_map/while/body/eval_jaxpr/reduce_scatter | solution.py:75
  3633.8 212.2 %reduce-scatter.19.cloned.1.call-start = ((), (), s32[]{:S(2)}) async-start(), calls=%async_computation.30 | async-start | bytes 3538944 | tf_op jit(solution)/shard_map/while/body/eval_jaxpr/reduce_scatter | solution.py:72
  3855.4 146.7 %all-gather.49.cloned.1.call-start = ((), (), s32[]{:S(2)}) async-start(), calls=%async_computation.34 | async-start | bytes 3538944 | tf_op jit(solution)/shard_map/while/body/eval_jaxpr/all_gather | solution.py:64
  3857.2 194.7 %reduce-scatter.21.cloned.1.call-start = ((), (), s32[]{:S(2)}) async-start(), calls=%async_computation.31 | async-start | bytes 3538944 | tf_op jit(solution)/shard_map/while/body/eval_jaxpr/reduce_scatter | solution.py:75
  3890.2 211.9 %reduce-scatter.19.cloned.1.call-start = ((), (), s32[]{:S(2)}) async-start(), calls=%async_computation.30 | async-start | bytes 3538944 | tf_op jit(solution)/shard_map/while/body/eval_jaxpr/reduce_scatter | solution.py:72
  4111.5 146.7 %all-gather.49.cloned.1.call-start = ((), (), s32[]{:S(2)}) async-start(), calls=%async_computation.34 | async-start | bytes 3538944 | tf_op jit(solution)/shard_map/while/body/eval_jaxpr/all_gather | solution.py:64
  4113.3 194.7 %reduce-scatter.21.cloned.1.call-start = ((), (), s32[]{:S(2)}) async-start(), calls=%async_computation.31 | async-start | bytes 3538944 | tf_op jit(solution)/shard_map/while/body/eval_jaxpr/reduce_scatter | solution.py:75
  4146.2 212.0 %reduce-scatter.19.cloned.1.call-start = ((), (), s32[]{:S(2)}) async-start(), calls=%async_computation.30 | async-start | bytes 3538944 | tf_op jit(solution)/shard_map/while/body/eval_jaxpr/reduce_scatter | solution.py:72
  4369.5 194.7 %reduce-scatter.21.cloned.1.call-start = ((), (), s32[]{:S(2)}) async-start(), calls=%async_computation.31 | async-start | bytes 3538944 | tf_op jit(solution)/shard_map/while/body/eval_jaxpr/reduce_scatter | solution.py:75
  4402.1 212.3 %reduce-scatter.19.cloned.1.call-start = ((), (), s32[]{:S(2)}) async-start(), calls=%async_computation.30 | async-start | bytes 3538944 | tf_op jit(solution)/shard_map/while/body/eval_jaxpr/reduce_scatter | solution.py:72
  4623.9 146.8 %all-gather.49.cloned.1.call-start = ((), (), s32[]{:S(2)}) async-start(), calls=%async_computation.34 | async-start | bytes 3538944 | tf_op jit(solution)/shard_map/while/body/eval_jaxpr/all_gather | solution.py:64
  4625.7 194.9 %reduce-scatter.21.cloned.1.call-start = ((), (), s32[]{:S(2)}) async-start(), calls=%async_computation.31 | async-start | bytes 3538944 | tf_op jit(solution)/shard_map/while/body/eval_jaxpr/reduce_scatter | solution.py:75
  4658.7 212.0 %reduce-scatter.19.cloned.1.call-start = ((), (), s32[]{:S(2)}) async-start(), calls=%async_computation.30 | async-start | bytes 3538944 | tf_op jit(solution)/shard_map/while/body/eval_jaxpr/reduce_scatter | solution.py:72
  4882.0 194.7 %reduce-scatter.21.cloned.1.call-start = ((), (), s32[]{:S(2)}) async-start(), calls=%async_computation.31 | async-start | bytes 3538944 | tf_op jit(solution)/shard_map/while/body/eval_jaxpr/reduce_scatter | solution.py:75
  4914.6 212.1 %reduce-scatter.19.cloned.1.call-start = ((), (), s32[]{:S(2)}) async-start(), calls=%async_computation.30 | async-start | bytes 3538944 | tf_op jit(solution)/shard_map/while/body/eval_jaxpr/reduce_scatter | solution.py:72
  5138.0 194.7 %reduce-scatter.21.cloned.1.call-start = ((), (), s32[]{:S(2)}) async-start(), calls=%async_computation.31 | async-start | bytes 3538944 | tf_op jit(solution)/shard_map/while/body/eval_jaxpr/reduce_scatter | solution.py:75
  5170.7 212.1 %reduce-scatter.19.cloned.1.call-start = ((), (), s32[]{:S(2)}) async-start(), calls=%async_computation.30 | async-start | bytes 3538944 | tf_op jit(solution)/shard_map/while/body/eval_jaxpr/reduce_scatter | solution.py:72
  5392.3 146.7 %all-gather.49.cloned.1.call-start = ((), (), s32[]{:S(2)}) async-start(), calls=%async_computation.34 | async-start | bytes 3538944 | tf_op jit(solution)/shard_map/while/body/eval_jaxpr/all_gather | solution.py:64
  5394.1 194.7 %reduce-scatter.21.cloned.1.call-start = ((), (), s32[]{:S(2)}) async-start(), calls=%async_computation.31 | async-start | bytes 3538944 | tf_op jit(solution)/shard_map/while/body/eval_jaxpr/reduce_scatter | solution.py:75
  5427.1 211.8 %reduce-scatter.19.cloned.1.call-start = ((), (), s32[]{:S(2)}) async-start(), calls=%async_computation.30 | async-start | bytes 3538944 | tf_op jit(solution)/shard_map/while/body/eval_jaxpr/reduce_scatter | solution.py:72
  5648.4 146.8 %all-gather.49.cloned.1.call-start = ((), (), s32[]{:S(2)}) async-start(), calls=%async_computation.34 | async-start | bytes 3538944 | tf_op jit(solution)/shard_map/while/body/eval_jaxpr/all_gather | solution.py:64
  5650.2 194.9 %reduce-scatter.21.cloned.1.call-start = ((), (), s32[]{:S(2)}) async-start(), calls=%async_computation.31 | async-start | bytes 3538944 | tf_op jit(solution)/shard_map/while/body/eval_jaxpr/reduce_scatter | solution.py:75
  5683.1 212.0 %reduce-scatter.19.cloned.1.call-start = ((), (), s32[]{:S(2)}) async-start(), calls=%async_computation.30 | async-start | bytes 3538944 | tf_op jit(solution)/shard_map/while/body/eval_jaxpr/reduce_scatter | solution.py:72
  5904.6 146.7 %all-gather.49.cloned.1.call-start = ((), (), s32[]{:S(2)}) async-start(), calls=%async_computation.34 | async-start | bytes 3538944 | tf_op jit(solution)/shard_map/while/body/eval_jaxpr/all_gather | solution.py:64
  5906.4 194.7 %reduce-scatter.21.cloned.1.call-start = ((), (), s32[]{:S(2)}) async-start(), calls=%async_computation.31 | async-start | bytes 3538944 | tf_op jit(solution)/shard_map/while/body/eval_jaxpr/reduce_scatter | solution.py:75
  5939.4 212.0 %reduce-scatter.19.cloned.1.call-start = ((), (), s32[]{:S(2)}) async-start(), calls=%async_computation.30 | async-start | bytes 3538944 | tf_op jit(solution)/shard_map/while/body/eval_jaxpr/reduce_scatter | solution.py:72
  6260.3 178.6 %reduce-scatter.15.cloned.1.call-start = ((), (), s32[]{:S(2)}) async-start(), calls=%async_computation.23 | async-start | bytes 18874368 | tf_op jit(solution)/shard_map/reduce_scatter | solution.py:360
  6268.8 289.6 %reduce-scatter.9.cloned.1.call-start = ((), (), s32[]{:S(2)}) async-start(), calls=%async_computation.20 | async-start | bytes 18874368 | tf_op jit(solution)/shard_map/reduce_scatter | solution.py:345
  6318.0 275.2 %reduce-scatter.17.cloned.1.call-start = ((), (), s32[]{:S(2)}) async-start(), calls=%async_computation.24 | async-start | bytes 73728 | tf_op jit(solution)/shard_map/reduce_scatter | solution.py:366
  6320.0 1064.5 %all-reduce.16.cloned.1.call-start = ((), (), s32[]{:S(2)}) async-start(), calls=%async_computation.25 | async-start | bytes 47185920 | tf_op jit(solution)/shard_map/psum | solution.py:372
  (188 other events, 10206.5 us)
Sparse Core Ops, SparseCore 0:
  43.7 89.8 all-gather.34
  166.4 89.8 all-gather.36
  2093.0 46.2 reduce-scatter.22
  2212.3 46.2 reduce-scatter.20
  2262.4 46.2 reduce-scatter.18
  2349.2 46.2 reduce-scatter.22
  2468.4 46.2 reduce-scatter.20
  2518.5 46.2 reduce-scatter.18
  2605.4 46.2 reduce-scatter.22
  2724.6 46.2 reduce-scatter.20
  2774.7 46.2 reduce-scatter.18
  2861.6 46.2 reduce-scatter.22
  2980.6 46.2 reduce-scatter.20
  3030.7 46.2 reduce-scatter.18
  3117.8 46.2 reduce-scatter.22
  3237.2 46.2 reduce-scatter.20
  3287.3 46.2 reduce-scatter.18
  3374.1 46.2 reduce-scatter.22
  3493.2 46.2 reduce-scatter.20
  3543.3 46.2 reduce-scatter.18
  3630.4 46.2 reduce-scatter.22
  3749.4 46.2 reduce-scatter.20
  3799.7 46.2 reduce-scatter.18
  3886.7 46.2 reduce-scatter.22
  4005.7 46.2 reduce-scatter.20
  4142.8 46.2 reduce-scatter.22
  4261.7 46.2 reduce-scatter.20
  4312.0 46.2 reduce-scatter.18
  4398.7 46.2 reduce-scatter.22
  4517.9 46.2 reduce-scatter.20
  4655.2 46.2 reduce-scatter.22
  4774.3 46.2 reduce-scatter.20
  5030.4 46.2 reduce-scatter.20
  5167.2 46.2 reduce-scatter.22
  5286.4 46.2 reduce-scatter.20
  5336.5 46.2 reduce-scatter.18
  5423.5 46.2 reduce-scatter.22
  5542.5 46.2 reduce-scatter.20
  5592.6 46.2 reduce-scatter.18
  5679.7 46.2 reduce-scatter.22
  5798.8 46.2 reduce-scatter.20
  5848.9 46.2 reduce-scatter.18
  5935.8 46.2 reduce-scatter.22
  6054.8 46.2 reduce-scatter.20
  6105.1 46.2 reduce-scatter.18
  6323.0 115.9 reduce-scatter.14
  6442.4 115.9 reduce-scatter.8
  6596.9 787.5 all-reduce.15
  (106 shorter events, 3494.5 us)
where the time goes:
time: 7440 us; the launch traced here: 7420 us
  waiting for transfers between devices  6180 us (83%)
  matrix products  593 us (8%)
  local copies, waits for them, and re-layouts  288 us (4%)
  other arithmetic  193 us (3%)
  blocking collectives  117 us (2%)
    all_gather x32, waiting for transfers between devices, fetch_all(): lax.all_gather(up_shard, 'fsdp', axis=0, tiled=True)  1010 us
    all_gather x32, waiting for transfers between devices, fetch_all(): lax.all_gather(gate_shard, 'fsdp', axis=0, tiled=True)  1000 us
    all_gather x32, waiting for transfers between devices, fetch_all(): lax.all_gather(down_shard, 'fsdp', axis=0, tiled=True)  909 us
    reduce_scatter x16, waiting for transfers between devices, reduce_all(): lax.psum_scatter(grad_first.astype(jnp.bfloat16), 'fsdp', scatter_dimensi...  773 us
    psum x1, waiting for transfers between devices, body(): lax.psum(attn_shards[1].astype(jnp.bfloat16), 'sp').astype(jnp.float32)  768 us
    reduce_scatter x16, waiting for transfers between devices, reduce_all(): lax.psum_scatter(grad_second.astype(jnp.bfloat16), 'fsdp', scatter_dimens...  739 us
    reduce_scatter x16, waiting for transfers between devices, reduce_all(): lax.psum_scatter(grad_third.astype(jnp.bfloat16), 'fsdp', scatter_dimensi...  625 us
    dot_general x52, matrix products, contract_rows(): lax.dot_general(left_mat, right_mat, (((0,), (0,)), ((), ())), preferred_...  202 us
  transfers between devices with their start and end apart: 159, of which 151 were waited for; matrix products, arithmetic and copies ran while one was open for 11% of the time, Pallas kernels for 0%

commit v1 on v0

v1 whole, which is shorter than its diff:
```python
import math
from typing import Callable, NamedTuple

import jax
import jax.numpy as jnp
from jax import lax
from jax.experimental import pallas as pl
from jax.experimental.pallas import tpu as pltpu
from jax.sharding import PartitionSpec as P

QUERY_HEADS = 32
KEY_VALUE_HEADS = 4
HEAD_SIZE = 128
CAP = 80
LANES = 128

EPS = 1e-06
THETA = 1000000.0
HIGH_PRECISION = lax.Precision.HIGHEST
BF16 = jnp.bfloat16
FLOAT = jnp.float32
MESH = pl.DeviceIdType.MESH


def rms_norm(values_in, gain_vec):
    return (
        values_in
        * lax.rsqrt(jnp.mean(values_in * values_in, axis=-1, keepdims=True) + EPS)
        * gain_vec
    )


def rotate(values_in, cosine, sine_part):
    half_dim = values_in.shape[-1] // 2
    first_half = values_in[..., :half_dim]
    second = values_in[..., half_dim:]
    return jnp.concatenate(
        [first_half * cosine - second * sine_part, second * cosine + first_half * sine_part],
        axis=-1,
    )


def contract_rows(left_mat, right_mat):
    return lax.dot_general(
        left_mat, right_mat, (((0,), (0,)), ((), ())), preferred_element_type=FLOAT
    )


def contract_cols(left_mat, right_mat):
    return lax.dot_general(
        left_mat, right_mat, (((1,), (1,)), ((), ())), preferred_element_type=FLOAT
    )


def matmul(left_mat, right_mat):
    return jnp.dot(left_mat, right_mat, preferred_element_type=FLOAT)


def flip(index, mask):
    bit = 1
    while bit <= mask:
        if mask & bit:
            index = index + bit * (1 - 2 * lax.rem(lax.div(index, bit), 2))
        bit *= 2
    return index


class Send(NamedTuple):
    src: Callable
    dst: Callable
    dz: int
    df: int
    after: int | None = None


def exchange(name, cid, arrays, out_shapes, sends):
    n_in, n_out = len(arrays), len(out_shapes)
    peers = sorted({(s.dz, s.df) for s in sends} - {(0, 0)})

    def kernel(*refs):
        ins, outs = refs[:n_in], refs[n_in : n_in + n_out]
        send_sems, recv_sems = refs[n_in + n_out :]
        z = lax.axis_index("sp")
        f = lax.axis_index("fsdp")
        barrier = pltpu.get_barrier_semaphore()
        for dz, df in peers:
            pl.semaphore_signal(
                barrier, inc=1, device_id=(flip(z, dz), flip(f, df)), device_id_type=MESH
            )
        pl.semaphore_wait(barrier, len(peers))
        copies = []
        for k, s in enumerate(sends):
            src = s.src(ins, outs, z, f)
            dst = s.dst(ins, outs, z, f)
            if (s.dz, s.df) == (0, 0):
                copies.append(pltpu.make_async_copy(src, dst, recv_sems.at[k]))
            else:
                copies.append(
                    pltpu.make_async_remote_copy(
                        src_ref=src,
                        dst_ref=dst,
                        send_sem=send_sems.at[k],
                        recv_sem=recv_sems.at[k],
                        device_id=(flip(z, s.dz), flip(f, s.df)),
                        device_id_type=MESH,
                    )
                )
        arrived = set()

        def arrive(k):
            if k not in arrived:
                arrived.add(k)
                s = sends[k]
                if (s.dz, s.df) == (0, 0):
                    copies[k].wait()
                else:
                    copies[k].wait_recv()

        for k, s in enumerate(sends):
            if s.after is None:
                copies[k].start()
        for k, s in enumerate(sends):
            if s.after is not None:
                arrive(s.after)
                copies[k].start()
        for k, s in enumerate(sends):
            if (s.dz, s.df) != (0, 0):
                copies[k].wait_send()
            arrive(k)

    result = pl.pallas_call(
        kernel,
        out_shape=[jax.ShapeDtypeStruct(shape, BF16) for shape in out_shapes],
        in_specs=[pl.BlockSpec(memory_space=pl.ANY)] * n_in,
        out_specs=[pl.BlockSpec(memory_space=pl.ANY)] * n_out,
        scratch_shapes=[
            pltpu.SemaphoreType.DMA((len(sends),)),
            pltpu.SemaphoreType.DMA((len(sends),)),
        ],
        compiler_params=pltpu.CompilerParams(collective_id=cid, has_side_effects=True),
        name=name,
    )(*arrays)
    return result


def body(
    tokens,
    expert_ids,
    attn_gain,
    query_weight,
    key_weight,
    value_weight,
    q_gain,
    k_gain,
    output_weight,
    ffn_gain,
    router_weight,
    w_gate,
    w_up,
    w_down,
    cotangent,
):
    nsp = lax.axis_size("sp")
    nf = lax.axis_size("fsdp")
    z = lax.axis_index("sp")
    f = lax.axis_index("fsdp")
    rows = tokens.shape[1]
    width = tokens.shape[2]
    shard = width // nf
    n_heads, kv_heads, head_dim = QUERY_HEADS, KEY_VALUE_HEADS, HEAD_SIZE
    my_heads = n_heads // nf
    rep = nf // kv_heads
    q_cols = my_heads * head_dim
    qkv_cols = q_cols + 2 * head_dim
    score_scale = 1.0 / math.sqrt(head_dim)
    n_experts = w_gate.shape[0]
    hidden_size = w_gate.shape[2]
    hid_shard = w_down.shape[1]
    plane_experts = n_experts // nsp
    parts = nf // plane_experts
    cap = CAP
    seqs = nf
    part = lax.rem(f, parts)
    place = lax.div(f, parts)
    expert = z * plane_experts + place

    small = jnp.concatenate(
        [
            attn_gain.astype(BF16),
            ffn_gain.astype(BF16),
            q_gain.astype(BF16),
            k_gain.astype(BF16),
            router_weight.astype(BF16).reshape(-1),
        ]
    )
    small_rows = 16
    small = jnp.pad(small, (0, small_rows * width - small.shape[0])).reshape(small_rows, width)
    x_pay = jnp.concatenate([tokens[0], small], axis=0)
    pay_rows = rows + small_rows
    by_head = query_weight.astype(BF16).reshape(shard, nf, q_cols)
    key_b = jnp.repeat(key_weight.astype(BF16).reshape(shard, kv_heads, head_dim), rep, axis=1)
    value_b = jnp.repeat(value_weight.astype(BF16).reshape(shard, kv_heads, head_dim), rep, axis=1)
    qkv_pay = jnp.concatenate([by_head, key_b, value_b], axis=2).transpose(1, 0, 2)
    routes = expert_ids[0]
    expert_iota = jnp.arange(n_experts, dtype=jnp.int32)
    routed = jnp.any(routes[:, :, None] == expert_iota[None, None, :], axis=1)
    dy_pay = jnp.concatenate(
        [
            cotangent[0],
            routed.astype(BF16),
            jnp.zeros((rows, LANES - n_experts), BF16),
        ],
        axis=1,
    )
    wide = width + LANES

    def plane_cast(weight):
        return lax.dynamic_slice_in_dim(weight, z * plane_experts, plane_experts, 0).astype(BF16)

    gate_pay, up_pay, down_pay = plane_cast(w_gate), plane_cast(w_up), plane_cast(w_down)

    sends = []
    for m in range(0, nf, 2):
        sends.append(
            Send(
                lambda i, o, z, f, m=m: i[0],
                lambda i, o, z, f: o[0].at[f],
                0,
                m,
            )
        )
    for m in range(nf):
        sends.append(
            Send(
                lambda i, o, z, f, m=m: i[1].at[flip(f, m)],
                lambda i, o, z, f, m=m: o[1].at[f],
                0,
                m,
            )
        )
    for m in range(nsp):
        sends.append(
            Send(lambda i, o, z, f: i[2], lambda i, o, z, f, m=m: o[2].at[m], m, 0)
        )
    for m in range(0, nf, 2):
        if m == 0:
            sends.append(
                Send(lambda i, o, z, f: i[0], lambda i, o, z, f: o[0].at[f], 0, 1)
            )
        else:
            sends.append(
                Send(
                    lambda i, o, z, f, m=m: o[0].at[flip(f, m)],
                    lambda i, o, z, f, m=m: o[0].at[flip(f, m)],
                    0,
                    1,
                    m // 2,
                )
            )
    x_all, w_qkv, dy_z = exchange(
        "gather_inputs",
        0,
        (x_pay, qkv_pay, dy_pay),
        ((nf, pay_rows, width), (nf, shard, qkv_cols), (nsp, rows, wide)),
        sends,
    )

    sends = []
    for which in range(3):
        for s in range(plane_experts):
            first = len(sends)
            sends.append(
                Send(
                    lambda i, o, z, f, s=s, w=which: i[w].at[flip(lax.div(f, parts), s)],
                    lambda i, o, z, f, w=which: o[w].at[f],
                    0,
                    s * parts,
                )
            )
    first_stage = len(sends)
    for which in range(3):
        for s in range(plane_experts):
            for p in range(1, parts):
                index = which * plane_experts + s
                if s == 0:
                    sends.append(
                        Send(
                            lambda i, o, z, f, w=which: i[w].at[lax.div(f, parts)],
                            lambda i, o, z, f, w=which: o[w].at[f],
                            0,
                            p,
                        )
                    )
                else:
                    sends.append(
                        Send(
                            lambda i, o, z, f, s=s, w=which: o[w].at[flip(f, s * parts)],
                            lambda i, o, z, f, s=s, w=which: o[w].at[flip(f, s * parts)],
                            0,
                            p,
                            index,
                        )
                    )
    gate_all, up_all, down_all = exchange(
        "gather_experts",
        1,
        (gate_pay, up_pay, down_pay),
        ((nf, shard, hidden_size), (nf, shard, hidden_size), (nf, hid_shard, width)),
        sends,
    )
    wg_b = gate_all.reshape(width, hidden_size)
    wu_b = up_all.reshape(width, hidden_size)
    wd_b = down_all.reshape(hidden_size, width)

    small_all = x_all[:, rows:, :].reshape(nf, small_rows * width)
    at = 0
    pieces = []
    for size in (shard, shard, head_dim // nf, head_dim // nf, shard * n_experts):
        pieces.append(small_all[:, at : at + size])
        at += size
    g_attn = pieces[0].reshape(width).astype(FLOAT)
    g_ffn = pieces[1].reshape(width).astype(FLOAT)
    g_query = pieces[2].reshape(head_dim).astype(FLOAT)
    g_key = pieces[3].reshape(head_dim).astype(FLOAT)
    wr_b = pieces[4].reshape(width, n_experts)

    xn_b = (
        rms_norm(x_all[:, :rows, :].astype(FLOAT), g_attn).astype(BF16).reshape(seqs * rows, width)
    )
    w_qkv = w_qkv.reshape(width, qkv_cols)
    qkv_lin = matmul(xn_b, w_qkv)
    q_lin = qkv_lin[:, :q_cols].reshape(seqs, rows, my_heads, head_dim)
    k_lin = qkv_lin[:, q_cols : q_cols + head_dim].reshape(seqs, rows, 1, head_dim)
    v_b = qkv_lin[:, q_cols + head_dim :].astype(BF16)
    half_dim = head_dim // 2
    inverse_freq = THETA ** (-(jnp.arange(half_dim, dtype=FLOAT) * 2.0 / head_dim))
    positions = (z * rows + jnp.arange(rows, dtype=jnp.int32)).astype(FLOAT)
    angles = positions[:, None] * inverse_freq[None, :]
    cosine = jnp.cos(angles)[None, :, None, :]
    sine_part = jnp.sin(angles)[None, :, None, :]

    def prep_heads(linear, gain_vec):
        return rotate(rms_norm(linear, gain_vec), cosine, sine_part)

    q_b = prep_heads(q_lin, g_query).astype(BF16)
    k_b = prep_heads(k_lin, g_key).astype(BF16).reshape(seqs * rows, head_dim)

    kv_pay = jnp.concatenate([k_b, v_b], axis=1)
    piece = seqs * rows // rep
    sends = []
    for d in range(nsp):
        sends.append(
            Send(
                lambda i, o, z, f: i[0].at[pl.ds(lax.rem(f, rep) * piece, piece)],
                lambda i, o, z, f, d=d: o[0].at[d, pl.ds(lax.rem(f, rep) * piece, piece)],
                d,
                0,
            )
        )
    for d in range(nsp):
        for p in range(1, rep):
            sends.append(
                Send(
                    lambda i, o, z, f, d=d: o[0].at[d, pl.ds(lax.rem(f, rep) * piece, piece)],
                    lambda i, o, z, f, d=d: o[0].at[d, pl.ds(lax.rem(f, rep) * piece, piece)],
                    0,
                    p,
                    d,
                )
            )
    (kv_z,) = exchange(
        "gather_keys", 2, (kv_pay,), ((nsp, seqs * rows, 2 * head_dim),), sends
    )
    kv_seq = kv_z.reshape(nsp, seqs, rows, 2 * head_dim).transpose(1, 0, 2, 3)
    kv_seq = kv_seq.reshape(seqs, nsp * rows, 2 * head_dim)
    keys = kv_seq[:, :, :head_dim]
    values = kv_seq[:, :, head_dim:]

    q_rows = q_b.transpose(0, 2, 1, 3)
    plane_of = jnp.bitwise_xor(jnp.arange(nsp, dtype=jnp.int32), z)
    key_pos = (plane_of[:, None] * rows + jnp.arange(rows, dtype=jnp.int32)[None, :]).reshape(-1)
    query_pos = z * rows + jnp.arange(rows, dtype=jnp.int32)
    causal = key_pos[None, :] <= query_pos[:, None]
    scores = (
        jnp.einsum("nhqd,nkd->nhqk", q_rows, keys, preferred_element_type=FLOAT) * score_scale
    )
    scores = jnp.where(causal[None, None], scores, -1e30)
    row_top = jnp.max(scores, axis=3, keepdims=True)
    expo = jnp.exp(scores - row_top)
    probs = (expo / jnp.sum(expo, axis=3, keepdims=True)).astype(BF16)
    o_rows = jnp.einsum("nhqk,nkd->nqhd", probs, values, preferred_element_type=FLOAT)
    o_mat = o_rows.astype(BF16).reshape(seqs * rows, q_cols)
    wo_b = output_weight.astype(BF16)

    def pair_then_plane(partial, name, cid):
        split = partial.astype(BF16).reshape(nf // 2, 2, rows, width)
        (other,) = exchange(
            name + "_pair",
            cid,
            (split,),
            ((nf // 2, rows, width),),
            [Send(lambda i, o, z, f: i[0].at[:, 1 - lax.rem(f, 2)], lambda i, o, z, f: o[0], 0, 1)],
        )
        own = lax.dynamic_index_in_dim(split, lax.rem(f, 2), 1, keepdims=False)
        summed = (own.astype(FLOAT) + other.astype(FLOAT)).astype(BF16)
        sends = [
            Send(
                lambda i, o, z, f, j=j: i[0].at[flip(lax.div(f, 2), j)],
                lambda i, o, z, f, j=j: o[0].at[j],
                0,
                2 * j,
            )
            for j in range(nf // 2)
        ]
        (blocks,) = exchange(
            name + "_plane", cid + 1, (summed,), ((nf // 2, rows, width),), sends
        )
        return jnp.sum(blocks.astype(FLOAT), axis=0)

    x_rows = tokens[0].astype(FLOAT)
    mid_rows = x_rows + pair_then_plane(matmul(o_mat, wo_b), "out_sum", 3)
    hn_b = rms_norm(mid_rows, g_ffn).astype(BF16)
    logits = matmul(hn_b, wr_b)
    logits = jnp.where(routed, logits, -1e30)
    expo = jnp.where(routed, jnp.exp(logits - jnp.max(logits, axis=1, keepdims=True)), 0.0)
    gates = expo / jnp.sum(expo, axis=1, keepdims=True)

    def two_parts(exact):
        high = exact.astype(BF16)
        return high, (exact - high.astype(FLOAT)).astype(BF16)

    gate_high, gate_low = two_parts(gates)
    hn_pay = jnp.concatenate(
        [hn_b, gate_high, gate_low, jnp.zeros((rows, LANES - 2 * n_experts), BF16)], axis=1
    )
    (hn_z,) = exchange(
        "hidden_planes",
        5,
        (hn_pay,),
        ((nsp, rows, wide),),
        [
            Send(lambda i, o, z, f: i[0], lambda i, o, z, f, d=d: o[0].at[d], d, 0)
            for d in range(nsp)
        ],
    )

    own_experts = z * plane_experts + jnp.bitwise_xor(
        place, jnp.arange(plane_experts, dtype=jnp.int32)
    )
    own_hot = (expert_iota[:, None] == own_experts[None, :]).astype(FLOAT)
    routed_z = lax.dot_general(
        own_hot,
        dy_z[:, :, width : width + n_experts].astype(FLOAT),
        (((0,), (2,)), ((), ())),
        preferred_element_type=FLOAT,
    ).transpose(1, 0, 2)
    earlier = jnp.triu(jnp.ones((rows, rows), FLOAT), 1)
    rank = jnp.dot(
        routed_z.reshape(nsp * plane_experts, rows), earlier, preferred_element_type=FLOAT
    ).reshape(nsp, plane_experts, rows)
    rank = rank * routed_z + (routed_z - 1.0)
    pick = (
        rank[:, :, None, :] == jnp.arange(cap, dtype=FLOAT)[None, None, :, None]
    ).astype(BF16)
    pick = pick.reshape(nsp, plane_experts * cap, rows)

    def select(source):
        picked = jnp.einsum("drt,dtc->drc", pick, source, preferred_element_type=FLOAT)
        return picked.astype(BF16).reshape(nsp, plane_experts, cap, source.shape[2])

    hn_pick = select(hn_z)
    dy_pick = select(dy_z[:, :, :width])
    sends = []
    for which in range(2):
        for s in range(plane_experts):
            sends.append(
                Send(
                    lambda i, o, z, f, s=s, w=which: i[w].at[:, s],
                    lambda i, o, z, f, s=s, w=which: o[w].at[s],
                    0,
                    s * parts,
                )
            )
    hn_rows, dy_rows = exchange(
        "rows_to_experts",
        6,
        (hn_pick, dy_pick),
        ((plane_experts, nsp, cap, wide), (plane_experts, nsp, cap, width)),
        sends,
    )

    n_rows = plane_experts * nsp * cap
    hn_wide = hn_rows.reshape(n_rows, wide)
    hn_in = hn_wide[:, :width]
    dy_in = dy_rows.reshape(n_rows, width)
    hot = (jnp.arange(n_experts, dtype=jnp.int32) == expert).astype(FLOAT)
    tail = hn_wide[:, width : width + 2 * n_experts].astype(FLOAT)
    row_gate = jnp.sum(
        (tail[:, :n_experts] + tail[:, n_experts:]) * hot[None, :], axis=1, keepdims=True
    )
    gate_pre = matmul(hn_in, wg_b)
    up_pre = matmul(hn_in, wu_b)
    sigma = jax.nn.sigmoid(gate_pre)
    act_f = gate_pre * sigma
    hidden = (act_f * up_pre).astype(BF16)
    result = matmul(hidden, wd_b)
    dy_f = dy_in.astype(FLOAT)
    row_dgate = jnp.sum(result * dy_f, axis=1, keepdims=True)
    weighted = (row_gate * result).astype(BF16)
    d_result = (row_gate * dy_f).astype(BF16)
    d_hidden = contract_cols(d_result, wd_b)
    d_gate_pre = (d_hidden * up_pre * sigma * (1.0 + gate_pre * (1.0 - sigma))).astype(BF16)
    d_up_pre = (d_hidden * act_f).astype(BF16)
    d_in = (contract_cols(d_gate_pre, wg_b) + contract_cols(d_up_pre, wu_b)).astype(BF16)
    dgate_high, dgate_low = two_parts(row_dgate * hot[None, :])
    d_in_wide = jnp.concatenate(
        [d_in, dgate_high, dgate_low, jnp.zeros((n_rows, LANES - 2 * n_experts), BF16)], axis=1
    )

    (d_back,) = exchange(
        "rows_from_experts",
        7,
        (d_in_wide.reshape(plane_experts, nsp, cap, wide),),
        ((nsp, plane_experts, cap, wide),),
        [
            Send(
                lambda i, o, z, f, s=s: i[0].at[s],
                lambda i, o, z, f, s=s: o[0].at[:, s],
                0,
                s * parts,
            )
            for s in range(plane_experts)
        ],
    )

    def combine(returned):
        flat = returned.reshape(nsp, plane_experts * cap, returned.shape[3])
        return jnp.einsum("drt,drc->dtc", pick, flat, preferred_element_type=FLOAT).astype(BF16)

    (d_home,) = exchange(
        "hidden_grads_home",
        8,
        (combine(d_back),),
        ((nsp, rows, wide),),
        [
            Send(lambda i, o, z, f, d=d: i[0].at[d], lambda i, o, z, f, d=d: o[0].at[d], d, 0)
            for d in range(nsp)
        ],
    )
    d_home = jnp.sum(d_home.astype(FLOAT), axis=0)
    tail = d_home[:, width:]
    d_gates = tail[:, :n_experts] + tail[:, n_experts : 2 * n_experts]
    d_logits = gates * (d_gates - jnp.sum(gates * d_gates, axis=1, keepdims=True))
    d_router = jnp.dot(hn_b.astype(FLOAT).T, d_logits, precision=HIGH_PRECISION)
    d_hn = d_home[:, :width] + jnp.dot(d_logits, wr_b.astype(FLOAT).T, precision=HIGH_PRECISION)
    grad_out = cotangent[0].astype(FLOAT)
    unused, ffn_pull = jax.vjp(rms_norm, mid_rows, g_ffn)
    d_mid_norm, d_ffn_gain = ffn_pull(d_hn)
    d_mid = grad_out + d_mid_norm

    back = weighted.reshape(plane_experts, nsp, cap, width)
    back = [
        lax.ppermute(back[s], "fsdp", [(i, i ^ (s * parts)) for i in range(nf)])
        if s
        else back[0]
        for s in range(plane_experts)
    ]
    out_blocks = combine(jnp.stack(back, axis=1))
    moe_sum = out_blocks[0].astype(FLOAT)
    for d in range(1, nsp):
        moe_sum = moe_sum + lax.ppermute(
            out_blocks[d], "sp", [(i, i ^ d) for i in range(nsp)]
        ).astype(FLOAT)
    mixed = (mid_rows + moe_sum).astype(BF16)[None]

    def to_shards(full):
        tail_shape = full.shape[1:]
        full = full.astype(BF16).reshape((plane_experts, parts) + tail_shape)

        def of_part(p):
            return lax.dynamic_index_in_dim(full, flip(part, p), 1, keepdims=False)

        total = of_part(0).astype(FLOAT)
        for p in range(1, parts):
            total = total + lax.ppermute(
                of_part(p), "fsdp", [(i, i ^ p) for i in range(nf)]
            ).astype(FLOAT)
        total = total.astype(BF16)
        got = []
        for s in range(plane_experts):
            block = lax.dynamic_index_in_dim(total, flip(place, s), 0, keepdims=False)
            if s:
                block = lax.ppermute(
                    block, "fsdp", [(i, i ^ (s * parts)) for i in range(nf)]
                )
            got.append(block)
        return jnp.stack(got)

    def all_planes(block):
        block = jnp.take(
            block, jnp.bitwise_xor(jnp.arange(plane_experts, dtype=jnp.int32), place), axis=0
        )
        right, left = [block], [block]
        for step in range(1, nsp):
            right.append(
                lax.ppermute(right[-1], "sp", [(i, i + 1) for i in range(step - 1, nsp - 1)])
            )
            left.append(
                lax.ppermute(left[-1], "sp", [(i + 1, i) for i in range(0, nsp - step)])
            )
        full = jnp.zeros((n_experts,) + block.shape[1:], FLOAT)
        for d in range(nsp):
            value = block.astype(FLOAT)
            if d:
                value = right[d].astype(FLOAT) + left[nsp - d].astype(FLOAT)
            full = lax.dynamic_update_slice_in_dim(
                full, value, lax.rem(z - d + nsp, nsp) * plane_experts, 0
            )
        return full

    d_down = contract_rows(hidden, d_result).reshape(nf, hid_shard, width)
    d_gate_w = contract_rows(hn_in, d_gate_pre).reshape(nf, shard, hidden_size)
    d_up_w = contract_rows(hn_in, d_up_pre).reshape(nf, shard, hidden_size)
    grad_down = all_planes(to_shards(d_down))
    grad_gate = all_planes(to_shards(d_gate_w))
    grad_up = all_planes(to_shards(d_up_w))

    d_attn_b = d_mid.astype(BF16)
    sends = [
        Send(lambda i, o, z, f: i[0], lambda i, o, z, f: o[0].at[f], 0, m)
        for m in range(0, nf, 2)
    ]
    for m in range(0, nf, 2):
        if m == 0:
            sends.append(Send(lambda i, o, z, f: i[0], lambda i, o, z, f: o[0].at[f], 0, 1))
        else:
            sends.append(
                Send(
                    lambda i, o, z, f, m=m: o[0].at[flip(f, m)],
                    lambda i, o, z, f, m=m: o[0].at[flip(f, m)],
                    0,
                    1,
                    m // 2,
                )
            )
    (da_all,) = exchange("gather_grads", 9, (d_attn_b,), ((nf, rows, width),), sends)
    da_all = da_all.reshape(seqs * rows, width)
    d_wo = contract_rows(o_mat, da_all)
    d_o = contract_cols(da_all, wo_b).astype(BF16).reshape(seqs, rows, my_heads, head_dim)
    d_o = d_o.transpose(0, 2, 1, 3)
    d_val = jnp.einsum("nhqk,nhqd->nkd", probs, d_o, preferred_element_type=FLOAT)
    d_probs = jnp.einsum("nhqd,nkd->nhqk", d_o, values, preferred_element_type=FLOAT)
    probs_f = probs.astype(FLOAT)
    d_scores = (
        probs_f * (d_probs - jnp.sum(probs_f * d_probs, axis=3, keepdims=True))
    ).astype(BF16)
    dq = (
        jnp.einsum("nhqk,nkd->nqhd", d_scores, keys, preferred_element_type=FLOAT) * score_scale
    ).astype(BF16)
    d_key = (
        jnp.einsum("nhqk,nhqd->nkd", d_scores, q_rows, preferred_element_type=FLOAT) * score_scale
    )
    d_kv = jnp.concatenate([d_key, d_val], axis=2).astype(BF16)
    d_kv = d_kv.reshape(seqs, nsp, rows, 2 * head_dim).transpose(1, 0, 2, 3)
    d_kv = d_kv.reshape(nsp, seqs * rows, 2 * head_dim)
    (d_kv,) = exchange(
        "key_grads_planes",
        10,
        (d_kv,),
        ((nsp, seqs * rows, 2 * head_dim),),
        [
            Send(lambda i, o, z, f, d=d: i[0].at[d], lambda i, o, z, f, d=d: o[0].at[d], d, 0)
            for d in range(nsp)
        ],
    )
    d_kv = jnp.sum(d_kv.astype(FLOAT), axis=0).astype(BF16)
    (d_kv,) = exchange(
        "key_grads_group",
        11,
        (d_kv,),
        ((rep, seqs * rows, 2 * head_dim),),
        [
            Send(lambda i, o, z, f: i[0], lambda i, o, z, f, p=p: o[0].at[p], 0, p)
            for p in range(rep)
        ],
    )
    d_kv = jnp.sum(d_kv.astype(FLOAT), axis=0)
    unused, q_pull = jax.vjp(prep_heads, q_lin, g_query)
    d_q_lin, d_q_gain = q_pull(dq.astype(FLOAT))
    unused, k_pull = jax.vjp(prep_heads, k_lin, g_key)
    d_k_lin, d_k_gain = k_pull(d_kv[:, :head_dim].reshape(seqs, rows, 1, head_dim))
    dq_b = d_q_lin.astype(BF16).reshape(seqs * rows, q_cols)
    dk_b = d_k_lin.astype(BF16).reshape(seqs * rows, head_dim)
    dv_b = d_kv[:, head_dim:].astype(BF16)
    d_qkv = jnp.concatenate([dq_b, dk_b, dv_b], axis=1)
    share = 1.0 / rep
    d_qkv_shared = jnp.concatenate([dq_b, dk_b * BF16(share), dv_b * BF16(share)], axis=1)
    d_w_qkv = contract_rows(xn_b, d_qkv).astype(BF16).reshape(nf, shard, qkv_cols)
    (d_w_shard,) = exchange(
        "head_grads_to_shards",
        12,
        (d_w_qkv,),
        ((nf, shard, qkv_cols),),
        [
            Send(
                lambda i, o, z, f, m=m: i[0].at[flip(f, m)],
                lambda i, o, z, f, m=m: o[0].at[f],
                0,
                m,
            )
            for m in range(nf)
        ],
    )
    d_wq = d_w_shard[:, :, :q_cols].transpose(1, 0, 2).reshape(shard, n_heads * head_dim)
    d_wkv = d_w_shard[::rep, :, q_cols:].reshape(kv_heads, shard, 2, head_dim)
    d_wkv = d_wkv.transpose(2, 1, 0, 3).reshape(2 * shard, kv_heads * head_dim)
    d_xn = pair_then_plane(contract_cols(d_qkv_shared, w_qkv), "input_sum", 13)
    unused, attn_pull = jax.vjp(rms_norm, x_rows, g_attn)
    d_x_norm, d_attn_gain = attn_pull(d_xn)
    grad_tokens = (d_mid + d_x_norm)[None]

    sum_out = lax.psum(d_wo.astype(BF16), "sp").astype(FLOAT)
    sum_q, sum_kv = lax.psum((d_wq, d_wkv), "sp")
    sum_q = sum_q.astype(FLOAT)
    sum_kv = sum_kv.astype(FLOAT)
    gain_sums = lax.psum(
        jnp.concatenate(
            [
                d_attn_gain,
                d_ffn_gain,
                d_q_gain,
                d_k_gain * share,
                d_router.reshape(-1),
            ]
        ),
        ("sp", "fsdp"),
    )
    at = 0
    pieces = []
    for size in (width, width, head_dim, head_dim, width * n_experts):
        whole = gain_sums[at : at + size]
        pieces.append(lax.dynamic_slice_in_dim(whole, f * (size // nf), size // nf, 0))
        at += size
    return (
        mixed,
        grad_tokens,
        pieces[0],
        sum_q,
        sum_kv[:shard],
        sum_kv[shard:],
        pieces[2],
        pieces[3],
        sum_out,
        pieces[1],
        pieces[4].reshape(shard, n_experts),
        grad_gate,
        grad_up,
        grad_down,
    )


def solution(mesh):
    by_token = P("fsdp", "sp", None)
    by_row = P("fsdp", None)
    by_inner = P(None, "fsdp", None)
    in_specs = (
        by_token,
        by_token,
        P("fsdp"),
        by_row,
        by_row,
        by_row,
        P("fsdp"),
        P("fsdp"),
        by_row,
        P("fsdp"),
        by_row,
        by_inner,
        by_inner,
        by_inner,
        by_token,
    )
    out_specs = (
        by_token,
        by_token,
        P("fsdp"),
        by_row,
        by_row,
        by_row,
        P("fsdp"),
        P("fsdp"),
        by_row,
        P("fsdp"),
        by_row,
        by_inner,
        by_inner,
        by_inner,
    )
    return jax.shard_map(body, mesh=mesh, in_specs=in_specs, out_specs=out_specs, check_vma=False)
```

time: 7440 us -> 1590 us (0.21)
  waiting for transfers between devices: 6180 us -> 376 us
  Pallas kernels: 0 us -> 689 us
  matrix products: 593 us -> 148 us
  local copies, waits for them, and re-layouts: 288 us -> 138 us
  blocking collectives: 117 us -> 0 us
    all_gather x100 -> x0, waiting for transfers between devices: 3000 us -> none  [the longest x32 1010 us: fetch_all(): lax.all_gather(up_shard, 'fsdp', axis=0, tiled=True)]
    reduce_scatter x53 -> x0, waiting for transfers between devices: 2380 us -> none  [the longest x16 773 us: reduce_all(): lax.psum_scatter(grad_first.astype(jnp.bfloat16), 'fsdp', scatter_dimensi...]
    psum x1 -> x2, waiting for transfers between devices: 768 us -> 0.02 us  [the longest x1 0.02 us: body(): lax.psum(jnp.concatenate([d_attn_gain, d_ffn_gain, d_q_gain, d_k_gain * s...]
    pallas_call x0 -> x15, Pallas kernels: none -> 689 us  [exchange(): pl.pallas_call(kernel, out_shape=[jax.ShapeDtypeStruct(shape, BF16) for s...]
    ppermute x0 -> x36, waiting for transfers between devices: none -> 376 us  [the longest x9 154 us: all_planes(): lax.ppermute(left[-1], 'sp', [(i + 1, i) for i in range(0, nsp - step)])]
    dot_general x52 -> x5, matrix products: 202 us -> 32 us  [contract_rows(): lax.dot_general(left_mat, right_mat, (((0,), (0,)), ((), ())), preferred_...]
    dynamic_slice x96 -> x8, local copies, waits for them, and re-layouts: 170 us -> 4.79 us  [the longest x5 2.45 us: body(): lax.dynamic_slice_in_dim(whole, f * (size // nf), size // nf, 0)]
    dot_general x52 -> x5, matrix products: 185 us -> 43.5 us  [contract_cols(): lax.dot_general(left_mat, right_mat, (((1,), (1,)), ((), ())), preferred_...]
  transfers between devices with their start and end apart: 159 -> 38, of which waited for: 151 -> 13; matrix products, arithmetic and copies ran while one was open for 11% -> 17% of each run, Pallas kernels for 0% -> 22%
where the time goes in v1:
time: 1590 us
  Pallas kernels  689 us (43%)
  waiting for transfers between devices  376 us (24%)
  matrix products  148 us (9%)
  local copies, waits for them, and re-layouts  138 us (9%)
  other arithmetic  131 us (8%)
  starting transfers between devices  89.6 us (6%)
  between operations  16 us (1%)
    pallas_call x15, Pallas kernels, exchange(): pl.pallas_call(kernel, out_shape=[jax.ShapeDtypeStruct(shape, BF16) for s...  689 us
    ppermute x9, waiting for transfers between devices, all_planes(): lax.ppermute(left[-1], 'sp', [(i + 1, i) for i in range(0, nsp - step)])  154 us
    ppermute x3, waiting for transfers between devices, body(): lax.ppermute(out_blocks[d], 'sp', [(i, i ^ d) for i in range(nsp)])  154 us
    dot_general x5, matrix products, contract_cols(): lax.dot_general(left_mat, right_mat, (((1,), (1,)), ((), ())), preferred_...  43.5 us
    dynamic_update_slice x12, other arithmetic, all_planes(): lax.dynamic_update_slice_in_dim(full, value, lax.rem(z - d + nsp, nsp) *...  42.4 us
    ppermute x9, waiting for transfers between devices, all_planes(): lax.ppermute(right[-1], 'sp', [(i, i + 1) for i in range(step - 1, nsp -...  41.2 us
    ppermute x3, starting transfers between devices, body(): lax.ppermute(out_blocks[d], 'sp', [(i, i ^ d) for i in range(nsp)])  39.7 us
    dot_general x6, matrix products, matmul(): return jnp.dot(left_mat, right_mat, preferred_element_type=FLOAT)  36.6 us
  transfers between devices with their start and end apart: 38, of which 13 were waited for; matrix products, arithmetic and copies ran while one was open for 17% of the time, Pallas kernels for 22%

profile of v1, /device:TPU:0, one launch (start us, length us, event | category | flops | bytes accessed | tf_op | source)
XLA Modules:
  0.0 1587.0 jit_solution(3011739290089281595)
XLA Ops:
  27.9 66.5 %gather_inputs.1 = (bf16[8,144,2048]{2,1,0:T(8,128)(2,1)}, bf16[8,256,768]{2,1,0:T(8,128)(2,1)}, bf16[4,128,2176]{2,1,0:T(8,128)(2,1)}) custom-call(bf16[144,2048]{1,0:T(8,128)(2,1)} %pad_maximum_fusion.7.refs_0_, bf16[8,256,768]{2,1,0:T(8,128)(2,1)} %maximum_bitcast_fusion.refs_1_, bf16[128,2176]{1,0:T(8,128)(2,1)} %concatenate.56.refs_2_), custom_call_target="tpu_custom_call" | custom-call | tf_op jit(solution)/shard_map/gather_inputs/pallas_call | solution.py:131
  112.0 5.5 convolution_convert_fusion.2
  120.4 24.3 %gather_keys.1 = bf16[4,1024,256]{2,1,0:T(8,128)(2,1)} custom-call(bf16[1024,256]{1,0:T(8,128)(2,1)} %pad_maximum_fusion.8.refs_0_), custom_call_target="tpu_custom_call" | custom-call | tf_op jit(solution)/shard_map/gather_keys/pallas_call | solution.py:131
  147.8 12.2 reshape.565
  190.3 26.7 %out_sum_plane.1 = bf16[4,128,2048]{2,1,0:T(8,128)(2,1)} custom-call(bf16[4,128,2048]{2,1,0:T(8,128)(2,1)} %fusion.9.refs_0_), custom_call_target="tpu_custom_call" | custom-call | tf_op jit(solution)/shard_map/out_sum_plane/pallas_call | solution.py:131
  222.1 44.6 %hidden_planes.1 = bf16[4,128,2176]{2,1,0:T(8,128)(2,1)} custom-call(bf16[128,2176]{1,0:T(8,128)(2,1)} %concatenate.61.refs_0_), custom_call_target="tpu_custom_call" | custom-call | tf_op jit(solution)/shard_map/hidden_planes/pallas_call | solution.py:131
  266.7 5.7 convolution_convert_fusion
  272.4 117.9 %rows_to_experts.1 = (bf16[4,4,80,2176]{3,2,1,0:T(8,128)(2,1)}, bf16[4,4,80,2048]{3,2,1,0:T(8,128)(2,1)}) custom-call(bf16[4,4,80,2176]{3,2,1,0:T(8,128)(2,1)} %bitcast.328, bf16[4,4,80,2048]{3,2,1,0:T(8,128)(2,1)} %bitcast.330), custom_call_target="tpu_custom_call" | custom-call | tf_op jit(solution)/shard_map/rows_to_experts/pallas_call | solution.py:131
  399.9 55.6 %gather_experts.1 = (bf16[8,256,768]{2,1,0:T(8,128)(2,1)}, bf16[8,256,768]{2,1,0:T(8,128)(2,1)}, bf16[8,96,2048]{2,1,0:T(8,128)(2,1)}) custom-call(bf16[4,256,768]{2,1,0:T(8,128)(2,1)} %get-tuple-element.187.refs_0_, bf16[4,256,768]{2,1,0:T(8,128)(2,1)} %get-tuple-element.186.refs_1_, bf16[4,96,2048]{2,1,0:T(8,128)(2,1)} %dynamic-slice_convert_fusion.refs_2_), custom_call_target="tpu_custom_call" | custom-call | tf_op jit(solution)/shard_map/gather_experts/pallas_call | solution.py:131
  455.5 9.7 fusion.22
  469.8 9.9 fusion.13
  487.7 9.3 multiply_convert_fusion.2
  503.5 8.8 fusion.1
  518.6 7.1 fusion.118
  526.2 12.2 add_convert_fusion
  538.5 9.1 concatenate.62
  547.6 87.5 %rows_from_experts.1 = bf16[4,4,80,2176]{3,2,1,0:T(8,128)(2,1)} custom-call(bf16[4,4,80,2176]{3,2,1,0:T(8,128)(2,1)} %bitcast.329), custom_call_target="tpu_custom_call" | custom-call | tf_op jit(solution)/shard_map/rows_from_experts/pallas_call | solution.py:131
  635.0 5.4 convolution_convert_fusion.1.refs_0_
  640.4 55.1 %hidden_grads_home.1 = bf16[4,128,2176]{2,1,0:T(8,128)(2,1)} custom-call(bf16[4,128,2176]{2,1,0:T(8,128)(2,1)} %convolution_convert_fusion.1.refs_0_), custom_call_target="tpu_custom_call" | custom-call | tf_op jit(solution)/shard_map/hidden_grads_home/pallas_call | solution.py:131
  702.8 43.5 %gather_grads.1 = bf16[8,128,2048]{2,1,0:T(8,128)(2,1)} custom-call(bf16[128,2048]{1,0:T(8,128)(2,1)} %fusion.107.refs_0_), custom_call_target="tpu_custom_call" | custom-call | tf_op jit(solution)/shard_map/gather_grads/pallas_call | solution.py:131
  746.3 6.9 convolution_convert_fusion.12
  770.1 45.2 %key_grads_planes.1 = bf16[4,1024,256]{2,1,0:T(8,128)(2,1)} custom-call(bf16[4,1024,256]{2,1,0:T(8,128)(2,1)} %bitcast.343), custom_call_target="tpu_custom_call" | custom-call | tf_op jit(solution)/shard_map/key_grads_planes/pallas_call | solution.py:131
  818.2 31.3 %key_grads_group.1 = bf16[2,1024,256]{2,1,0:T(8,128)(2,1)} custom-call(bf16[1024,256]{1,0:T(8,128)(2,1)} %reduce_sum.280.refs_0_), custom_call_target="tpu_custom_call" | custom-call | tf_op jit(solution)/shard_map/key_grads_group/pallas_call | solution.py:131
  871.3 7.9 convolution_convert_fusion.4
  879.2 10.0 input_sum_pair.1
  893.7 32.6 %input_sum_plane.1 = bf16[4,128,2048]{2,1,0:T(8,128)(2,1)} custom-call(bf16[4,128,2048]{2,1,0:T(8,128)(2,1)} %fusion.8.refs_0_), custom_call_target="tpu_custom_call" | custom-call | tf_op jit(solution)/shard_map/input_sum_plane/pallas_call | solution.py:131
  930.4 6.0 convolution_convert_fusion.9
  936.7 7.7 convolution_convert_fusion.5
  944.4 43.7 %head_grads_to_shards.1 = bf16[8,256,768]{2,1,0:T(8,128)(2,1)} custom-call(bf16[8,256,768]{2,1,0:T(8,128)(2,1)} %bitcast.362), custom_call_target="tpu_custom_call" | custom-call | tf_op jit(solution)/shard_map/head_grads_to_shards/pallas_call | solution.py:131
  997.7 9.2 convolution_convert_fusion.7
  1029.1 12.2 collective-permute-done.9
  1043.7 6.4 collective-permute-done.8
  1057.5 6.1 broadcast.363.clone
  1078.7 6.1 broadcast.363.clone.1
  1087.4 5.7 collective-permute-start.20
  1094.5 8.1 collective-permute-done.27
  1109.7 112.5 %collective-permute-done.5 = bf16[128,2048]{1,0:T(8,128)(2,1)} collective-permute-done((bf16[128,2048]{1,0:T(8,128)(2,1)}, bf16[128,2048]{1,0:T(8,128)(2,1)}, u32[]{:S(2)}, u32[]{:S(2)}) %collective-permute-start.5) | collective-permute-done | bytes 524320 | tf_op jit(solution)/shard_map/ppermute | solution.py:571
  1222.2 38.1 %collective-permute-start.4 = (bf16[128,2048]{1,0:T(8,128)(2,1)}, bf16[128,2048]{1,0:T(8,128)(2,1)}, u32[]{:S(2)}, u32[]{:S(2)}) collective-permute-start(bf16[128,2048]{1,0:T(8,128)(2,1)} %get-tuple-element.141), channel_id=1, source_target_pairs={{0,16},{8,24},{16,0},{24,8},{1,17},{9,25},{17,1},{25,9},{2,18},{10... | collective-permute-start | bytes 1572872 | tf_op jit(solution)/shard_map/ppermute | solution.py:571
  1260.3 6.4 broadcast_in_dim.138
  1269.6 41.1 %collective-permute-done.4 = bf16[128,2048]{1,0:T(8,128)(2,1)} collective-permute-done((bf16[128,2048]{1,0:T(8,128)(2,1)}, bf16[128,2048]{1,0:T(8,128)(2,1)}, u32[]{:S(2)}, u32[]{:S(2)}) %collective-permute-start.4) | collective-permute-done | bytes 524320 | tf_op jit(solution)/shard_map/ppermute | solution.py:571
  1318.9 41.2 %collective-permute-done.30 = bf16[4,96,2048]{2,1,0:T(8,128)(2,1)} collective-permute-done((bf16[4,96,2048]{2,1,0:T(8,128)(2,1)}, bf16[4,96,2048]{2,1,0:T(8,128)(2,1)}, u32[]{:S(2)}, u32[]{:S(2)}) %collective-permute-start.30) | collective-permute-done | bytes 1572896 | tf_op jit(solution)/shard_map/ppermute | solution.py:606
  1361.8 5.4 collective-permute-done.31
  1370.4 30.6 %collective-permute-done.12 = bf16[4,256,768]{2,1,0:T(8,128)(2,1)} collective-permute-done((bf16[4,256,768]{2,1,0:T(8,128)(2,1)}, bf16[4,256,768]{2,1,0:T(8,128)(2,1)}, u32[]{:S(2)}, u32[]{:S(2)}) %collective-permute-start.12) | collective-permute-done | bytes 1572896 | tf_op jit(solution)/shard_map/ppermute | solution.py:609
  1408.0 26.7 %collective-permute-done.22 = bf16[4,256,768]{2,1,0:T(8,128)(2,1)} collective-permute-done((bf16[4,256,768]{2,1,0:T(8,128)(2,1)}, bf16[4,256,768]{2,1,0:T(8,128)(2,1)}, u32[]{:S(2)}, u32[]{:S(2)}) %collective-permute-start.22) | collective-permute-done | bytes 1572896 | tf_op jit(solution)/shard_map/ppermute | solution.py:609
  1452.1 16.3 %collective-permute-done.32 = bf16[4,96,2048]{2,1,0:T(8,128)(2,1)} collective-permute-done((bf16[4,96,2048]{2,1,0:T(8,128)(2,1)}, bf16[4,96,2048]{2,1,0:T(8,128)(2,1)}, u32[]{:S(2)}, u32[]{:S(2)}) %collective-permute-start.32) | collective-permute-done | bytes 1572896 | tf_op jit(solution)/shard_map/ppermute | solution.py:609
  1469.1 32.9 %collective-permute-done.13 = bf16[4,256,768]{2,1,0:T(8,128)(2,1)} collective-permute-done((bf16[4,256,768]{2,1,0:T(8,128)(2,1)}, bf16[4,256,768]{2,1,0:T(8,128)(2,1)}, u32[]{:S(2)}, u32[]{:S(2)}) %collective-permute-start.13) | collective-permute-done | bytes 1572896 | tf_op jit(solution)/shard_map/ppermute | solution.py:609
  1511.2 24.6 %collective-permute-done.23 = bf16[4,256,768]{2,1,0:T(8,128)(2,1)} collective-permute-done((bf16[4,256,768]{2,1,0:T(8,128)(2,1)}, bf16[4,256,768]{2,1,0:T(8,128)(2,1)}, u32[]{:S(2)}, u32[]{:S(2)}) %collective-permute-start.23) | collective-permute-done | bytes 1572896 | tf_op jit(solution)/shard_map/ppermute | solution.py:609
  1550.9 17.6 %collective-permute-done.33 = bf16[4,96,2048]{2,1,0:T(8,128)(2,1)S(1)} collective-permute-done((bf16[4,96,2048]{2,1,0:T(8,128)(2,1)}, bf16[4,96,2048]{2,1,0:T(8,128)(2,1)S(1)}, u32[]{:S(2)}, u32[]{:S(2)}) %collective-permute-start.33) | collective-permute-done | bytes 1572896 | tf_op jit(solution)/shard_map/ppermute | solution.py:609
  (450 shorter events, 315.7 us)
Async XLA Ops:
  7.2 1395.1 %all-reduce.9.cloned.1.call-start = ((), (), s32[]{:S(2)}) async-start(), calls=%async_computation | async-start | bytes 303104 | tf_op jit(solution)/shard_map/psum | solution.py:726
  110.5 51.6 %copy-start.64 = (f32[128]{0:T(128)}, f32[128]{0:T(128)S(1)}, u32[]{:S(2)}) copy-start(f32[128]{0:T(128)S(1)} %reshape.594) | copy-start | bytes 1540
  220.0 480.6 %copy-start.60 = (f32[128]{0:T(128)}, f32[128]{0:T(128)S(1)}, u32[]{:S(2)}) copy-start(f32[128]{0:T(128)S(1)} %fusion.95) | copy-start | bytes 1540
  272.4 119.1 %copy-start.73 = (f32[16]{0:T(128)S(1)}, f32[16]{0:T(128)}, u32[]{:S(2)}) copy-start(f32[16]{0:T(128)} %compare_convert_fusion) | copy-start | bytes 196
  487.0 529.7 %collective-permute-start.26 = (bf16[4,96,2048]{2,1,0:T(8,128)(2,1)}, bf16[4,96,2048]{2,1,0:T(8,128)(2,1)}, u32[]{:S(2)}, u32[]{:S(2)}) collective-permute-start(bf16[4,96,2048]{2,1,0:T(8,128)(2,1)} %dynamic-slice_bitcast_fusion), channel_id=1, source_target_pairs={{0,1},{1,0},{2,3},{3,2},{4,5},{5,4},{6,7},{7,6},{8,9},{9,8},{10,11... | collective-permute-start | bytes 4718600 | tf_op jit(solution)/shard_map/ppermute | solution.py:585
  503.1 518.9 %collective-permute-start.6 = (bf16[4,256,768]{2,1,0:T(8,128)(2,1)}, bf16[4,256,768]{2,1,0:T(8,128)(2,1)}, u32[]{:S(2)}, u32[]{:S(2)}) collective-permute-start(bf16[4,256,768]{2,1,0:T(8,128)(2,1)} %dynamic-slice_bitcast_fusion.2), channel_id=1, source_target_pairs={{0,1},{1,0},{2,3},{3,2},{4,5},{5,4},{6,7},{7,6},{8,9},{9,8},{10,11... | collective-permute-start | bytes 4718600 | tf_op jit(solution)/shard_map/ppermute | solution.py:585
  515.1 493.8 %collective-permute-start.2 = (bf16[4,80,2048]{2,1,0:T(8,128)(2,1)}, bf16[4,80,2048]{2,1,0:T(8,128)(2,1)}, u32[]{:S(2)}, u32[]{:S(2)}) collective-permute-start(bf16[4,80,2048]{2,1,0:T(8,128)(2,1)} %bitcast.41), channel_id=1, source_target_pairs={{0,6},{1,7},{2,4},{3,5},{4,2},{5,3},{6,0},{7,1},{8,14},{9,15},{10,... | collective-permute-start | bytes 3932168 | tf_op jit(solution)/shard_map/ppermute | solution.py:563
  516.9 492.5 %collective-permute-start.1 = (bf16[4,80,2048]{2,1,0:T(8,128)(2,1)}, bf16[4,80,2048]{2,1,0:T(8,128)(2,1)}, u32[]{:S(2)}, u32[]{:S(2)}) collective-permute-start(bf16[4,80,2048]{2,1,0:T(8,128)(2,1)} %bitcast.39), channel_id=1, source_target_pairs={{0,4},{1,5},{2,6},{3,7},{4,0},{5,1},{6,2},{7,3},{8,12},{9,13},{10,... | collective-permute-start | bytes 3932168 | tf_op jit(solution)/shard_map/ppermute | solution.py:563
  517.4 492.0 %collective-permute-start = (bf16[4,80,2048]{2,1,0:T(8,128)(2,1)}, bf16[4,80,2048]{2,1,0:T(8,128)(2,1)}, u32[]{:S(2)}, u32[]{:S(2)}) collective-permute-start(bf16[4,80,2048]{2,1,0:T(8,128)(2,1)} %bitcast.37), channel_id=1, source_target_pairs={{0,2},{1,3},{2,0},{3,1},{4,6},{5,7},{6,4},{7,5},{8,10},{9,11},{10,... | collective-permute-start | bytes 3932168 | tf_op jit(solution)/shard_map/ppermute | solution.py:563
  700.6 45.7 %copy-start.69 = (f32[128]{0:T(128)}, f32[128]{0:T(128)S(1)}, u32[]{:S(2)}) copy-start(f32[128]{0:T(128)S(1)} %multiply_multiply_fusion.3) | copy-start | bytes 1540
  852.7 75.9 %copy-start.71 = (f32[128]{0:T(128)}, f32[128]{0:T(128)S(1)}, u32[]{:S(2)}) copy-start(f32[128]{0:T(128)S(1)} %fusion.96) | copy-start | bytes 1540
  930.3 511.9 %all-reduce.11.cloned.1.call-start = ((), (), s32[]{:S(2)}) async-start(), calls=%async_computation.1 | async-start | bytes 9437184 | tf_op jit(solution)/shard_map/psum | solution.py:723
  1008.9 17.2 %collective-permute-start.16 = (bf16[4,256,768]{2,1,0:T(8,128)(2,1)S(1)}, bf16[4,256,768]{2,1,0:T(8,128)(2,1)S(1)}, u32[]{:S(2)}, u32[]{:S(2)}) collective-permute-start(bf16[4,256,768]{2,1,0:T(8,128)(2,1)S(1)} %dynamic-slice_bitcast_fusion.1), channel_id=1, source_target_pairs={{0,1},{1,0},{2,3},{3,2},{4,5},{5,4},{6,7},{7,6},{8,9},{9,8},{10,11... | collective-permute-start | bytes 4718600 | tf_op jit(solution)/shard_map/ppermute | solution.py:585
  1015.2 72.2 %collective-permute-start.3 = (bf16[128,2048]{1,0:T(8,128)(2,1)}, bf16[128,2048]{1,0:T(8,128)(2,1)}, u32[]{:S(2)}, u32[]{:S(2)}) collective-permute-start(bf16[128,2048]{1,0:T(8,128)(2,1)} %get-tuple-element.139), channel_id=1, source_target_pairs={{0,8},{8,0},{16,24},{24,16},{1,9},{9,1},{17,25},{25,17},{2,10},{10... | collective-permute-start | bytes 1572872 | tf_op jit(solution)/shard_map/ppermute | solution.py:571
  1019.7 73.4 %collective-permute-start.29 = (bf16[96,2048]{1,0:T(8,128)(2,1)}, bf16[96,2048]{1,0:T(8,128)(2,1)}, u32[]{:S(2)}, u32[]{:S(2)}) collective-permute-start(bf16[96,2048]{1,0:T(8,128)(2,1)} %get-tuple-element.143), channel_id=1, source_target_pairs={{0,6},{1,7},{2,4},{3,5},{4,2},{5,3},{6,0},{7,1},{8,14},{9,15},{10,... | collective-permute-start | bytes 1179656 | tf_op jit(solution)/shard_map/ppermute | solution.py:593
  1024.0 17.4 %collective-permute-start.9 = (bf16[256,768]{1,0:T(8,128)(2,1)S(1)}, bf16[256,768]{1,0:T(8,128)(2,1)S(1)}, u32[]{:S(2)}, u32[]{:S(2)}) collective-permute-start(bf16[256,768]{1,0:T(8,128)(2,1)S(1)} %get-tuple-element.151), channel_id=1, source_target_pairs={{0,6},{1,7},{2,4},{3,5},{4,2},{5,3},{6,0},{7,1},{8,14},{9,15},{10,... | collective-permute-start | bytes 1179656 | tf_op jit(solution)/shard_map/ppermute | solution.py:593
  1025.0 25.1 %collective-permute-start.8 = (bf16[256,768]{1,0:T(8,128)(2,1)S(1)}, bf16[256,768]{1,0:T(8,128)(2,1)S(1)}, u32[]{:S(2)}, u32[]{:S(2)}) collective-permute-start(bf16[256,768]{1,0:T(8,128)(2,1)S(1)} %get-tuple-element.152), channel_id=1, source_target_pairs={{0,4},{1,5},{2,6},{3,7},{4,0},{5,1},{6,2},{7,3},{8,12},{9,13},{10,... | collective-permute-start | bytes 1179656 | tf_op jit(solution)/shard_map/ppermute | solution.py:593
  1026.1 25.3 %collective-permute-start.7 = (bf16[256,768]{1,0:T(8,128)(2,1)S(1)}, bf16[256,768]{1,0:T(8,128)(2,1)S(1)}, u32[]{:S(2)}, u32[]{:S(2)}) collective-permute-start(bf16[256,768]{1,0:T(8,128)(2,1)S(1)} %get-tuple-element.153), channel_id=1, source_target_pairs={{0,2},{1,3},{2,0},{3,1},{4,6},{5,7},{6,4},{7,5},{8,10},{9,11},{10,... | collective-permute-start | bytes 1179656 | tf_op jit(solution)/shard_map/ppermute | solution.py:593
  1041.4 24.9 %collective-permute-start.19 = (bf16[256,768]{1,0:T(8,128)(2,1)}, bf16[256,768]{1,0:T(8,128)(2,1)}, u32[]{:S(2)}, u32[]{:S(2)}) collective-permute-start(bf16[256,768]{1,0:T(8,128)(2,1)} %get-tuple-element.147), channel_id=1, source_target_pairs={{0,6},{1,7},{2,4},{3,5},{4,2},{5,3},{6,0},{7,1},{8,14},{9,15},{10,... | collective-permute-start | bytes 1179656 | tf_op jit(solution)/shard_map/ppermute | solution.py:593
  1050.1 16.9 %collective-permute-start.18 = (bf16[256,768]{1,0:T(8,128)(2,1)}, bf16[256,768]{1,0:T(8,128)(2,1)}, u32[]{:S(2)}, u32[]{:S(2)}) collective-permute-start(bf16[256,768]{1,0:T(8,128)(2,1)} %get-tuple-element.148), channel_id=1, source_target_pairs={{0,4},{1,5},{2,6},{3,7},{4,0},{5,1},{6,2},{7,3},{8,12},{9,13},{10,... | collective-permute-start | bytes 1179656 | tf_op jit(solution)/shard_map/ppermute | solution.py:593
  1051.3 20.1 %collective-permute-start.17 = (bf16[256,768]{1,0:T(8,128)(2,1)}, bf16[256,768]{1,0:T(8,128)(2,1)}, u32[]{:S(2)}, u32[]{:S(2)}) collective-permute-start(bf16[256,768]{1,0:T(8,128)(2,1)} %get-tuple-element.149), channel_id=1, source_target_pairs={{0,2},{1,3},{2,0},{3,1},{4,6},{5,7},{6,4},{7,5},{8,10},{9,11},{10,... | collective-permute-start | bytes 1179656 | tf_op jit(solution)/shard_map/ppermute | solution.py:593
  1066.2 27.5 %collective-permute-start.28 = (bf16[96,2048]{1,0:T(8,128)(2,1)}, bf16[96,2048]{1,0:T(8,128)(2,1)}, u32[]{:S(2)}, u32[]{:S(2)}) collective-permute-start(bf16[96,2048]{1,0:T(8,128)(2,1)} %get-tuple-element.144), channel_id=1, source_target_pairs={{0,4},{1,5},{2,6},{3,7},{4,0},{5,1},{6,2},{7,3},{8,12},{9,13},{10,... | collective-permute-start | bytes 1179656 | tf_op jit(solution)/shard_map/ppermute | solution.py:593
  1066.9 246.2 %collective-permute-start.10 = (bf16[4,256,768]{2,1,0:T(8,128)(2,1)}, bf16[4,256,768]{2,1,0:T(8,128)(2,1)}, u32[]{:S(2)}, u32[]{:S(2)}) collective-permute-start(bf16[4,256,768]{2,1,0:T(8,128)(2,1)} %get-tuple-element.117), channel_id=1, source_target_pairs={{0,8},{8,16},{16,24},{1,9},{9,17},{17,25},{2,10},{10,18},{18,26},{... | collective-permute-start | bytes 4718600 | tf_op jit(solution)/shard_map/ppermute | solution.py:606
  1071.4 243.0 %collective-permute-start.11 = (bf16[4,256,768]{2,1,0:T(8,128)(2,1)}, bf16[4,256,768]{2,1,0:T(8,128)(2,1)}, u32[]{:S(2)}, u32[]{:S(2)}) collective-permute-start(bf16[4,256,768]{2,1,0:T(8,128)(2,1)} %get-tuple-element.117), channel_id=1, source_target_pairs={{8,0},{16,8},{24,16},{9,1},{17,9},{25,17},{10,2},{18,10},{26,18},{... | collective-permute-start | bytes 4718600 | tf_op jit(solution)/shard_map/ppermute | solution.py:609
  1087.4 228.9 %collective-permute-start.20 = (bf16[4,256,768]{2,1,0:T(8,128)(2,1)}, bf16[4,256,768]{2,1,0:T(8,128)(2,1)}, u32[]{:S(2)}, u32[]{:S(2)}) collective-permute-start(bf16[4,256,768]{2,1,0:T(8,128)(2,1)} %get-tuple-element.115), channel_id=1, source_target_pairs={{0,8},{8,16},{16,24},{1,9},{9,17},{17,25},{2,10},{10,18},{18,26},{... | collective-permute-start | bytes 4718600 | tf_op jit(solution)/shard_map/ppermute | solution.py:606
  1093.1 9.5 collective-permute-start.27
  1093.8 128.5 %collective-permute-start.5 = (bf16[128,2048]{1,0:T(8,128)(2,1)}, bf16[128,2048]{1,0:T(8,128)(2,1)}, u32[]{:S(2)}, u32[]{:S(2)}) collective-permute-start(bf16[128,2048]{1,0:T(8,128)(2,1)} %get-tuple-element.140), channel_id=1, source_target_pairs={{0,24},{8,16},{16,8},{24,0},{1,25},{9,17},{17,9},{25,1},{2,26},{10... | collective-permute-start | bytes 1572872 | tf_op jit(solution)/shard_map/ppermute | solution.py:571
  1102.6 215.0 %collective-permute-start.21 = (bf16[4,256,768]{2,1,0:T(8,128)(2,1)}, bf16[4,256,768]{2,1,0:T(8,128)(2,1)}, u32[]{:S(2)}, u32[]{:S(2)}) collective-permute-start(bf16[4,256,768]{2,1,0:T(8,128)(2,1)} %get-tuple-element.115), channel_id=1, source_target_pairs={{8,0},{16,8},{24,16},{9,1},{17,9},{25,17},{10,2},{18,10},{26,18},{... | collective-permute-start | bytes 4718600 | tf_op jit(solution)/shard_map/ppermute | solution.py:609
  1222.2 88.5 %collective-permute-start.4 = (bf16[128,2048]{1,0:T(8,128)(2,1)}, bf16[128,2048]{1,0:T(8,128)(2,1)}, u32[]{:S(2)}, u32[]{:S(2)}) collective-permute-start(bf16[128,2048]{1,0:T(8,128)(2,1)} %get-tuple-element.141), channel_id=1, source_target_pairs={{0,16},{8,24},{16,0},{24,8},{1,17},{9,25},{17,1},{25,9},{2,18},{10... | collective-permute-start | bytes 1572872 | tf_op jit(solution)/shard_map/ppermute | solution.py:571
  1266.7 135.6 %copy-start.75 = (f32[128]{0:T(128)S(1)}, f32[128]{0:T(128)}, u32[]{:S(2)}) copy-start(f32[128]{0:T(128)} %get-tuple-element.162) | copy-start | bytes 1540
  1266.7 135.6 %copy-start.76 = (f32[128]{0:T(128)S(1)}, f32[128]{0:T(128)}, u32[]{:S(2)}) copy-start(f32[128]{0:T(128)} %get-tuple-element.106) | copy-start | bytes 1540
  1266.7 169.3 %copy-start.61 = (f32[128]{0:T(128)S(1)}, f32[128]{0:T(128)}, u32[]{:S(2)}) copy-start(f32[128]{0:T(128)} %copy-done.60) | copy-start | bytes 1540
  1266.7 169.3 %copy-start.70 = (f32[128]{0:T(128)S(1)}, f32[128]{0:T(128)}, u32[]{:S(2)}) copy-start(f32[128]{0:T(128)} %copy-done.69) | copy-start | bytes 1540
  1266.7 169.3 %copy-start.72 = (f32[128]{0:T(128)S(1)}, f32[128]{0:T(128)}, u32[]{:S(2)}) copy-start(f32[128]{0:T(128)} %copy-done.71) | copy-start | bytes 1540
  1310.7 49.3 %collective-permute-start.30 = (bf16[4,96,2048]{2,1,0:T(8,128)(2,1)}, bf16[4,96,2048]{2,1,0:T(8,128)(2,1)}, u32[]{:S(2)}, u32[]{:S(2)}) collective-permute-start(bf16[4,96,2048]{2,1,0:T(8,128)(2,1)} %get-tuple-element.113), channel_id=1, source_target_pairs={{0,8},{8,16},{16,24},{1,9},{9,17},{17,25},{2,10},{10,18},{18,26},{... | collective-permute-start | bytes 4718600 | tf_op jit(solution)/shard_map/ppermute | solution.py:606
  1313.1 54.1 %collective-permute-start.31 = (bf16[4,96,2048]{2,1,0:T(8,128)(2,1)}, bf16[4,96,2048]{2,1,0:T(8,128)(2,1)}, u32[]{:S(2)}, u32[]{:S(2)}) collective-permute-start(bf16[4,96,2048]{2,1,0:T(8,128)(2,1)} %get-tuple-element.113), channel_id=1, source_target_pairs={{8,0},{16,8},{24,16},{9,1},{17,9},{25,17},{10,2},{18,10},{26,18},{... | collective-permute-start | bytes 4718600 | tf_op jit(solution)/shard_map/ppermute | solution.py:609
  1314.4 54.6 %collective-permute-start.14 = (bf16[4,256,768]{2,1,0:T(8,128)(2,1)}, bf16[4,256,768]{2,1,0:T(8,128)(2,1)}, u32[]{:S(2)}, u32[]{:S(2)}) collective-permute-start(bf16[4,256,768]{2,1,0:T(8,128)(2,1)} %collective-permute-done.10), channel_id=1, source_target_pairs={{8,16},{16,24},{9,17},{17,25},{10,18},{18,26},{11,19},{19,27},{12,... | collective-permute-start | bytes 4718600 | tf_op jit(solution)/shard_map/ppermute | solution.py:606
  1316.3 84.7 %collective-permute-start.12 = (bf16[4,256,768]{2,1,0:T(8,128)(2,1)}, bf16[4,256,768]{2,1,0:T(8,128)(2,1)}, u32[]{:S(2)}, u32[]{:S(2)}) collective-permute-start(bf16[4,256,768]{2,1,0:T(8,128)(2,1)} %collective-permute-done.11), channel_id=1, source_target_pairs={{8,0},{16,8},{9,1},{17,9},{10,2},{18,10},{11,3},{19,11},{12,4},{20... | collective-permute-start | bytes 4718600 | tf_op jit(solution)/shard_map/ppermute | solution.py:609
  1317.6 117.1 %collective-permute-start.22 = (bf16[4,256,768]{2,1,0:T(8,128)(2,1)}, bf16[4,256,768]{2,1,0:T(8,128)(2,1)}, u32[]{:S(2)}, u32[]{:S(2)}) collective-permute-start(bf16[4,256,768]{2,1,0:T(8,128)(2,1)} %collective-permute-done.21), channel_id=1, source_target_pairs={{8,0},{16,8},{9,1},{17,9},{10,2},{18,10},{11,3},{19,11},{12,4},{20... | collective-permute-start | bytes 4718600 | tf_op jit(solution)/shard_map/ppermute | solution.py:609
  1360.0 80.3 %collective-permute-start.24 = (bf16[4,256,768]{2,1,0:T(8,128)(2,1)}, bf16[4,256,768]{2,1,0:T(8,128)(2,1)}, u32[]{:S(2)}, u32[]{:S(2)}) collective-permute-start(bf16[4,256,768]{2,1,0:T(8,128)(2,1)} %collective-permute-done.20), channel_id=1, source_target_pairs={{8,16},{16,24},{9,17},{17,25},{10,18},{18,26},{11,19},{19,27},{12,... | collective-permute-start | bytes 4718600 | tf_op jit(solution)/shard_map/ppermute | solution.py:606
  1367.3 84.0 %collective-permute-start.34 = (bf16[4,96,2048]{2,1,0:T(8,128)(2,1)}, bf16[4,96,2048]{2,1,0:T(8,128)(2,1)}, u32[]{:S(2)}, u32[]{:S(2)}) collective-permute-start(bf16[4,96,2048]{2,1,0:T(8,128)(2,1)} %collective-permute-done.30), channel_id=1, source_target_pairs={{8,16},{16,24},{9,17},{17,25},{10,18},{18,26},{11,19},{19,27},{12,... | collective-permute-start | bytes 4718600 | tf_op jit(solution)/shard_map/ppermute | solution.py:606
  1369.1 99.3 %collective-permute-start.32 = (bf16[4,96,2048]{2,1,0:T(8,128)(2,1)}, bf16[4,96,2048]{2,1,0:T(8,128)(2,1)}, u32[]{:S(2)}, u32[]{:S(2)}) collective-permute-start(bf16[4,96,2048]{2,1,0:T(8,128)(2,1)} %collective-permute-done.31), channel_id=1, source_target_pairs={{8,0},{16,8},{9,1},{17,9},{10,2},{18,10},{11,3},{19,11},{12,4},{20... | collective-permute-start | bytes 4718600 | tf_op jit(solution)/shard_map/ppermute | solution.py:609
  1401.0 101.1 %collective-permute-start.13 = (bf16[4,256,768]{2,1,0:T(8,128)(2,1)}, bf16[4,256,768]{2,1,0:T(8,128)(2,1)}, u32[]{:S(2)}, u32[]{:S(2)}) collective-permute-start(bf16[4,256,768]{2,1,0:T(8,128)(2,1)} %collective-permute-done.12), channel_id=1, source_target_pairs={{8,0},{9,1},{10,2},{11,3},{12,4},{13,5},{14,6},{15,7}} | collective-permute-start | bytes 4718600 | tf_op jit(solution)/shard_map/ppermute | solution.py:609
  1434.7 101.1 %collective-permute-start.23 = (bf16[4,256,768]{2,1,0:T(8,128)(2,1)}, bf16[4,256,768]{2,1,0:T(8,128)(2,1)}, u32[]{:S(2)}, u32[]{:S(2)}) collective-permute-start(bf16[4,256,768]{2,1,0:T(8,128)(2,1)} %collective-permute-done.22), channel_id=1, source_target_pairs={{8,0},{9,1},{10,2},{11,3},{12,4},{13,5},{14,6},{15,7}} | collective-permute-start | bytes 4718600 | tf_op jit(solution)/shard_map/ppermute | solution.py:609
  1440.4 103.2 %collective-permute-start.15 = (bf16[4,256,768]{2,1,0:T(8,128)(2,1)}, bf16[4,256,768]{2,1,0:T(8,128)(2,1)}, u32[]{:S(2)}, u32[]{:S(2)}) collective-permute-start(bf16[4,256,768]{2,1,0:T(8,128)(2,1)} %collective-permute-done.14), channel_id=1, source_target_pairs={{16,24},{17,25},{18,26},{19,27},{20,28},{21,29},{22,30},{23,31}} | collective-permute-start | bytes 4718600 | tf_op jit(solution)/shard_map/ppermute | solution.py:606
  1451.3 96.2 %collective-permute-start.25 = (bf16[4,256,768]{2,1,0:T(8,128)(2,1)}, bf16[4,256,768]{2,1,0:T(8,128)(2,1)S(1)}, u32[]{:S(2)}, u32[]{:S(2)}) collective-permute-start(bf16[4,256,768]{2,1,0:T(8,128)(2,1)} %collective-permute-done.24), channel_id=1, source_target_pairs={{16,24},{17,25},{18,26},{19,27},{20,28},{21,29},{22,30},{23,31}} | collective-permute-start | bytes 4718600 | tf_op jit(solution)/shard_map/ppermute | solution.py:606
  1468.4 107.9 %collective-permute-start.35 = (bf16[4,96,2048]{2,1,0:T(8,128)(2,1)}, bf16[4,96,2048]{2,1,0:T(8,128)(2,1)S(1)}, u32[]{:S(2)}, u32[]{:S(2)}) collective-permute-start(bf16[4,96,2048]{2,1,0:T(8,128)(2,1)} %collective-permute-done.34), channel_id=1, source_target_pairs={{16,24},{17,25},{18,26},{19,27},{20,28},{21,29},{22,30},{23,31}} | collective-permute-start | bytes 4718600 | tf_op jit(solution)/shard_map/ppermute | solution.py:606
  1502.1 66.4 %collective-permute-start.33 = (bf16[4,96,2048]{2,1,0:T(8,128)(2,1)}, bf16[4,96,2048]{2,1,0:T(8,128)(2,1)S(1)}, u32[]{:S(2)}, u32[]{:S(2)}) collective-permute-start(bf16[4,96,2048]{2,1,0:T(8,128)(2,1)} %collective-permute-done.32), channel_id=1, source_target_pairs={{8,0},{9,1},{10,2},{11,3},{12,4},{13,5},{14,6},{15,7}} | collective-permute-start | bytes 4718600 | tf_op jit(solution)/shard_map/ppermute | solution.py:609
  (83 other events, 693.1 us)
Sparse Core Ops, SparseCore 0:
  930.4 126.5 all-reduce.8
  1060.2 291.3 all-reduce.10

commit v2 on v1

--- a/solution.py
+++ b/solution.py
@@ -73,7 +73,7 @@
     after: int | None = None
 
 
-def exchange(name, cid, arrays, out_shapes, sends):
+def exchange(name, cid, arrays, out_shapes, sends, micros):
     n_in, n_out = len(arrays), len(out_shapes)
     peers = sorted({(s.dz, s.df) for s in sends} - {(0, 0)})
 
@@ -138,6 +138,9 @@
             pltpu.SemaphoreType.DMA((len(sends),)),
         ],
         compiler_params=pltpu.CompilerParams(collective_id=cid, has_side_effects=True),
+        cost_estimate=pl.CostEstimate(
+            flops=0, bytes_accessed=int(micros * 3.0e6), transcendentals=0
+        ),
         name=name,
     )(*arrays)
     return result
@@ -263,54 +266,8 @@
         (x_pay, qkv_pay, dy_pay),
         ((nf, pay_rows, width), (nf, shard, qkv_cols), (nsp, rows, wide)),
         sends,
-    )
-
-    sends = []
-    for which in range(3):
-        for s in range(plane_experts):
-            first = len(sends)
-            sends.append(
-                Send(
-                    lambda i, o, z, f, s=s, w=which: i[w].at[flip(lax.div(f, parts), s)],
-                    lambda i, o, z, f, w=which: o[w].at[f],
-                    0,
-                    s * parts,
-                )
-            )
-    first_stage = len(sends)
-    for which in range(3):
-        for s in range(plane_experts):
-            for p in range(1, parts):
-                index = which * plane_experts + s
-                if s == 0:
-                    sends.append(
-                        Send(
-                            lambda i, o, z, f, w=which: i[w].at[lax.div(f, parts)],
-                            lambda i, o, z, f, w=which: o[w].at[f],
-                            0,
-                            p,
-                        )
-                    )
-                else:
-                    sends.append(
-                        Send(
-                            lambda i, o, z, f, s=s, w=which: o[w].at[flip(f, s * parts)],
-                            lambda i, o, z, f, s=s, w=which: o[w].at[flip(f, s * parts)],
-                            0,
-                            p,
-                            index,
-                        )
-                    )
-    gate_all, up_all, down_all = exchange(
-        "gather_experts",
-        1,
-        (gate_pay, up_pay, down_pay),
-        ((nf, shard, hidden_size), (nf, shard, hidden_size), (nf, hid_shard, width)),
-        sends,
-    )
-    wg_b = gate_all.reshape(width, hidden_size)
-    wu_b = up_all.reshape(width, hidden_size)
-    wd_b = down_all.reshape(hidden_size, width)
+        65,
+    )
 
     small_all = x_all[:, rows:, :].reshape(nf, small_rows * width)
     at = 0
@@ -368,9 +325,50 @@
                     d,
                 )
             )
-    (kv_z,) = exchange(
-        "gather_keys", 2, (kv_pay,), ((nsp, seqs * rows, 2 * head_dim),), sends
-    )
+    for which in range(3):
+        for s in range(plane_experts):
+            stage = len(sends)
+            sends.append(
+                Send(
+                    lambda i, o, z, f, s=s, w=which: i[1 + w].at[flip(lax.div(f, parts), s)],
+                    lambda i, o, z, f, w=which: o[1 + w].at[f],
+                    0,
+                    s * parts,
+                )
+            )
+            for p in range(1, parts):
+                if s == 0:
+                    forward = Send(
+                        lambda i, o, z, f, w=which: i[1 + w].at[lax.div(f, parts)],
+                        lambda i, o, z, f, w=which: o[1 + w].at[f],
+                        0,
+                        p,
+                    )
+                else:
+                    forward = Send(
+                        lambda i, o, z, f, s=s, w=which: o[1 + w].at[flip(f, s * parts)],
+                        lambda i, o, z, f, s=s, w=which: o[1 + w].at[flip(f, s * parts)],
+                        0,
+                        p,
+                        stage,
+                    )
+                sends.append(forward)
+    kv_z, gate_all, up_all, down_all = exchange(
+        "keys_and_experts",
+        1,
+        (kv_pay, gate_pay, up_pay, down_pay),
+        (
+            (nsp, seqs * rows, 2 * head_dim),
+            (nf, shard, hidden_size),
+            (nf, shard, hidden_size),
+            (nf, hid_shard, width),
+        ),
+        sends,
+        55,
+    )
+    wg_b = gate_all.reshape(width, hidden_size)
+    wu_b = up_all.reshape(width, hidden_size)
+    wd_b = down_all.reshape(hidden_size, width)
     kv_seq = kv_z.reshape(nsp, seqs, rows, 2 * head_dim).transpose(1, 0, 2, 3)
     kv_seq = kv_seq.reshape(seqs, nsp * rows, 2 * head_dim)
     keys = kv_seq[:, :, :head_dim]
@@ -400,6 +398,7 @@
             (split,),
             ((nf // 2, rows, width),),
             [Send(lambda i, o, z, f: i[0].at[:, 1 - lax.rem(f, 2)], lambda i, o, z, f: o[0], 0, 1)],
+            8,
         )
         own = lax.dynamic_index_in_dim(split, lax.rem(f, 2), 1, keepdims=False)
         summed = (own.astype(FLOAT) + other.astype(FLOAT)).astype(BF16)
@@ -413,7 +412,7 @@
             for j in range(nf // 2)
         ]
         (blocks,) = exchange(
-            name + "_plane", cid + 1, (summed,), ((nf // 2, rows, width),), sends
+            name + "_plane", cid + 1, (summed,), ((nf // 2, rows, width),), sends, 27
         )
         return jnp.sum(blocks.astype(FLOAT), axis=0)
 
@@ -428,21 +427,6 @@
     def two_parts(exact):
         high = exact.astype(BF16)
         return high, (exact - high.astype(FLOAT)).astype(BF16)
-
-    gate_high, gate_low = two_parts(gates)
-    hn_pay = jnp.concatenate(
-        [hn_b, gate_high, gate_low, jnp.zeros((rows, LANES - 2 * n_experts), BF16)], axis=1
-    )
-    (hn_z,) = exchange(
-        "hidden_planes",
-        5,
-        (hn_pay,),
-        ((nsp, rows, wide),),
-        [
-            Send(lambda i, o, z, f: i[0], lambda i, o, z, f, d=d: o[0].at[d], d, 0)
-            for d in range(nsp)
-        ],
-    )
 
     own_experts = z * plane_experts + jnp.bitwise_xor(
         place, jnp.arange(plane_experts, dtype=jnp.int32)
@@ -468,33 +452,48 @@
         picked = jnp.einsum("drt,dtc->drc", pick, source, preferred_element_type=FLOAT)
         return picked.astype(BF16).reshape(nsp, plane_experts, cap, source.shape[2])
 
-    hn_pick = select(hn_z)
-    dy_pick = select(dy_z[:, :, :width])
-    sends = []
-    for which in range(2):
-        for s in range(plane_experts):
-            sends.append(
-                Send(
-                    lambda i, o, z, f, s=s, w=which: i[w].at[:, s],
-                    lambda i, o, z, f, s=s, w=which: o[w].at[s],
-                    0,
-                    s * parts,
-                )
-            )
-    hn_rows, dy_rows = exchange(
+    def to_experts(which):
+        return [
+            Send(
+                lambda i, o, z, f, s=s: i[which].at[:, s],
+                lambda i, o, z, f, s=s: o[which].at[s],
+                0,
+                s * parts,
+            )
+            for s in range(plane_experts)
+        ]
+
+    gate_high, gate_low = two_parts(gates)
+    gate_lanes = jnp.concatenate(
+        [gate_high, gate_low, jnp.zeros((rows, LANES - 2 * n_experts), BF16)], axis=1
+    )
+    hn_z, gate_z, dy_rows = exchange(
+        "hidden_planes",
+        5,
+        (hn_b, gate_lanes, select(dy_z[:, :, :width])),
+        ((nsp, rows, width), (nsp, rows, LANES), (plane_experts, nsp, cap, width)),
+        [
+            Send(lambda i, o, z, f, w=w: i[w], lambda i, o, z, f, d=d, w=w: o[w].at[d], d, 0)
+            for w in range(2)
+            for d in range(nsp)
+        ]
+        + to_experts(2),
+        58,
+    )
+    hn_rows, gate_rows = exchange(
         "rows_to_experts",
         6,
-        (hn_pick, dy_pick),
-        ((plane_experts, nsp, cap, wide), (plane_experts, nsp, cap, width)),
-        sends,
+        (select(hn_z), select(gate_z)),
+        ((plane_experts, nsp, cap, width), (plane_experts, nsp, cap, LANES)),
+        to_experts(0) + to_experts(1),
+        60,
     )
 
     n_rows = plane_experts * nsp * cap
-    hn_wide = hn_rows.reshape(n_rows, wide)
-    hn_in = hn_wide[:, :width]
+    hn_in = hn_rows.reshape(n_rows, width)
     dy_in = dy_rows.reshape(n_rows, width)
     hot = (jnp.arange(n_experts, dtype=jnp.int32) == expert).astype(FLOAT)
-    tail = hn_wide[:, width : width + 2 * n_experts].astype(FLOAT)
+    tail = gate_rows.reshape(n_rows, LANES)[:, : 2 * n_experts].astype(FLOAT)
     row_gate = jnp.sum(
         (tail[:, :n_experts] + tail[:, n_experts:]) * hot[None, :], axis=1, keepdims=True
     )
@@ -513,117 +512,100 @@
     d_up_pre = (d_hidden * act_f).astype(BF16)
     d_in = (contract_cols(d_gate_pre, wg_b) + contract_cols(d_up_pre, wu_b)).astype(BF16)
     dgate_high, dgate_low = two_parts(row_dgate * hot[None, :])
-    d_in_wide = jnp.concatenate(
-        [d_in, dgate_high, dgate_low, jnp.zeros((n_rows, LANES - 2 * n_experts), BF16)], axis=1
-    )
-
-    (d_back,) = exchange(
+    dgate_lanes = jnp.concatenate(
+        [dgate_high, dgate_low, jnp.zeros((n_rows, LANES - 2 * n_experts), BF16)], axis=1
+    )
+
+    def by_shard(full, inner):
+        return full.astype(BF16).reshape((plane_experts, parts) + inner)
+
+    d_weights = (
+        by_shard(contract_rows(hidden, d_result), (hid_shard, width)),
+        by_shard(contract_rows(hn_in, d_gate_pre), (shard, hidden_size)),
+        by_shard(contract_rows(hn_in, d_up_pre), (shard, hidden_size)),
+    )
+    shard_shapes = [w.shape[2:] for w in d_weights]
+
+    sends = []
+    for w in range(2):
+        for s in range(plane_experts):
+            sends.append(
+                Send(
+                    lambda i, o, z, f, s=s, w=w: i[w].at[s],
+                    lambda i, o, z, f, s=s, w=w: o[w].at[:, s],
+                    0,
+                    s * parts,
+                )
+            )
+    for w in range(3):
+        for p in range(1, parts):
+            sends.append(
+                Send(
+                    lambda i, o, z, f, p=p, w=w: i[2 + w].at[:, flip(lax.rem(f, parts), p)],
+                    lambda i, o, z, f, p=p, w=w: o[2 + w].at[p - 1],
+                    0,
+                    p,
+                )
+            )
+    d_back, dgate_back, *d_others = exchange(
         "rows_from_experts",
         7,
-        (d_in_wide.reshape(plane_experts, nsp, cap, wide),),
-        ((nsp, plane_experts, cap, wide),),
-        [
-            Send(
-                lambda i, o, z, f, s=s: i[0].at[s],
-                lambda i, o, z, f, s=s: o[0].at[:, s],
-                0,
-                s * parts,
-            )
-            for s in range(plane_experts)
-        ],
+        (
+            d_in.reshape(plane_experts, nsp, cap, width),
+            dgate_lanes.reshape(plane_experts, nsp, cap, LANES),
+        )
+        + d_weights,
+        [(nsp, plane_experts, cap, width), (nsp, plane_experts, cap, LANES)]
+        + [(parts - 1, plane_experts) + tuple(shape) for shape in shard_shapes],
+        sends,
+        70,
     )
 
     def combine(returned):
         flat = returned.reshape(nsp, plane_experts * cap, returned.shape[3])
         return jnp.einsum("drt,drc->dtc", pick, flat, preferred_element_type=FLOAT).astype(BF16)
 
-    (d_home,) = exchange(
+    summed = []
+    for own, others in zip(d_weights, d_others):
+        total = lax.dynamic_index_in_dim(own, part, 1, keepdims=False).astype(FLOAT)
+        summed.append((total + jnp.sum(others.astype(FLOAT), axis=0)).astype(BF16))
+    sends = [
+        Send(lambda i, o, z, f, d=d, w=w: i[w].at[d], lambda i, o, z, f, d=d, w=w: o[w].at[d], d, 0)
+        for w in range(2)
+        for d in range(nsp)
+    ]
+    for w in range(2, 5):
+        for s in range(plane_experts):
+            sends.append(
+                Send(
+                    lambda i, o, z, f, s=s, w=w: i[w].at[flip(lax.div(f, parts), s)],
+                    lambda i, o, z, f, s=s, w=w: o[w].at[lax.div(f, parts)],
+                    0,
+                    s * parts,
+                )
+            )
+    d_home, dgate_home, *shards = exchange(
         "hidden_grads_home",
         8,
-        (combine(d_back),),
-        ((nsp, rows, wide),),
-        [
-            Send(lambda i, o, z, f, d=d: i[0].at[d], lambda i, o, z, f, d=d: o[0].at[d], d, 0)
-            for d in range(nsp)
-        ],
-    )
+        (combine(d_back), combine(dgate_back), *summed),
+        [(nsp, rows, width), (nsp, rows, LANES)]
+        + [(plane_experts,) + tuple(shape) for shape in shard_shapes],
+        sends,
+        58,
+    )
+    all_down, all_gate, all_up = [
+        lax.all_gather(block, "sp", axis=0, tiled=True) for block in shards
+    ]
     d_home = jnp.sum(d_home.astype(FLOAT), axis=0)
-    tail = d_home[:, width:]
+    tail = jnp.sum(dgate_home.astype(FLOAT), axis=0)
     d_gates = tail[:, :n_experts] + tail[:, n_experts : 2 * n_experts]
     d_logits = gates * (d_gates - jnp.sum(gates * d_gates, axis=1, keepdims=True))
     d_router = jnp.dot(hn_b.astype(FLOAT).T, d_logits, precision=HIGH_PRECISION)
-    d_hn = d_home[:, :width] + jnp.dot(d_logits, wr_b.astype(FLOAT).T, precision=HIGH_PRECISION)
+    d_hn = d_home + jnp.dot(d_logits, wr_b.astype(FLOAT).T, precision=HIGH_PRECISION)
     grad_out = cotangent[0].astype(FLOAT)
     unused, ffn_pull = jax.vjp(rms_norm, mid_rows, g_ffn)
     d_mid_norm, d_ffn_gain = ffn_pull(d_hn)
     d_mid = grad_out + d_mid_norm
-
-    back = weighted.reshape(plane_experts, nsp, cap, width)
-    back = [
-        lax.ppermute(back[s], "fsdp", [(i, i ^ (s * parts)) for i in range(nf)])
-        if s
-        else back[0]
-        for s in range(plane_experts)
-    ]
-    out_blocks = combine(jnp.stack(back, axis=1))
-    moe_sum = out_blocks[0].astype(FLOAT)
-    for d in range(1, nsp):
-        moe_sum = moe_sum + lax.ppermute(
-            out_blocks[d], "sp", [(i, i ^ d) for i in range(nsp)]
-        ).astype(FLOAT)
-    mixed = (mid_rows + moe_sum).astype(BF16)[None]
-
-    def to_shards(full):
-        tail_shape = full.shape[1:]
-        full = full.astype(BF16).reshape((plane_experts, parts) + tail_shape)
-
-        def of_part(p):
-            return lax.dynamic_index_in_dim(full, flip(part, p), 1, keepdims=False)
-
-        total = of_part(0).astype(FLOAT)
-        for p in range(1, parts):
-            total = total + lax.ppermute(
-                of_part(p), "fsdp", [(i, i ^ p) for i in range(nf)]
-            ).astype(FLOAT)
-        total = total.astype(BF16)
-        got = []
-        for s in range(plane_experts):
-            block = lax.dynamic_index_in_dim(total, flip(place, s), 0, keepdims=False)
-            if s:
-                block = lax.ppermute(
-                    block, "fsdp", [(i, i ^ (s * parts)) for i in range(nf)]
-                )
-            got.append(block)
-        return jnp.stack(got)
-
-    def all_planes(block):
-        block = jnp.take(
-            block, jnp.bitwise_xor(jnp.arange(plane_experts, dtype=jnp.int32), place), axis=0
-        )
-        right, left = [block], [block]
-        for step in range(1, nsp):
-            right.append(
-                lax.ppermute(right[-1], "sp", [(i, i + 1) for i in range(step - 1, nsp - 1)])
-            )
-            left.append(
-                lax.ppermute(left[-1], "sp", [(i + 1, i) for i in range(0, nsp - step)])
-            )
-        full = jnp.zeros((n_experts,) + block.shape[1:], FLOAT)
-        for d in range(nsp):
-            value = block.astype(FLOAT)
-            if d:
-                value = right[d].astype(FLOAT) + left[nsp - d].astype(FLOAT)
-            full = lax.dynamic_update_slice_in_dim(
-                full, value, lax.rem(z - d + nsp, nsp) * plane_experts, 0
-            )
-        return full
-
-    d_down = contract_rows(hidden, d_result).reshape(nf, hid_shard, width)
-    d_gate_w = contract_rows(hn_in, d_gate_pre).reshape(nf, shard, hidden_size)
-    d_up_w = contract_rows(hn_in, d_up_pre).reshape(nf, shard, hidden_size)
-    grad_down = all_planes(to_shards(d_down))
-    grad_gate = all_planes(to_shards(d_gate_w))
-    grad_up = all_planes(to_shards(d_up_w))
 
     d_attn_b = d_mid.astype(BF16)
     sends = [
@@ -643,7 +625,7 @@
                     m // 2,
                 )
             )
-    (da_all,) = exchange("gather_grads", 9, (d_attn_b,), ((nf, rows, width),), sends)
+    (da_all,) = exchange("gather_grads", 9, (d_attn_b,), ((nf, rows, width),), sends, 30)
     da_all = da_all.reshape(seqs * rows, width)
     d_wo = contract_rows(o_mat, da_all)
     d_o = contract_cols(da_all, wo_b).astype(BF16).reshape(seqs, rows, my_heads, head_dim)
@@ -663,17 +645,36 @@
     d_kv = jnp.concatenate([d_key, d_val], axis=2).astype(BF16)
     d_kv = d_kv.reshape(seqs, nsp, rows, 2 * head_dim).transpose(1, 0, 2, 3)
     d_kv = d_kv.reshape(nsp, seqs * rows, 2 * head_dim)
-    (d_kv,) = exchange(
+    sends = [
+        Send(lambda i, o, z, f, d=d: i[0].at[d], lambda i, o, z, f, d=d: o[0].at[d], d, 0)
+        for d in range(nsp)
+    ]
+    for s in range(plane_experts):
+        sends.append(
+            Send(
+                lambda i, o, z, f, s=s: i[1].at[s],
+                lambda i, o, z, f, s=s: o[1].at[:, s],
+                0,
+                s * parts,
+            )
+        )
+    d_kv, out_back = exchange(
         "key_grads_planes",
         10,
-        (d_kv,),
-        ((nsp, seqs * rows, 2 * head_dim),),
-        [
-            Send(lambda i, o, z, f, d=d: i[0].at[d], lambda i, o, z, f, d=d: o[0].at[d], d, 0)
-            for d in range(nsp)
-        ],
-    )
+        (d_kv, weighted.reshape(plane_experts, nsp, cap, width)),
+        ((nsp, seqs * rows, 2 * head_dim), (nsp, plane_experts, cap, width)),
+        sends,
+        60,
+    )
+    out_blocks = combine(out_back)
+    moe_sum = out_blocks[0].astype(FLOAT)
+    for d in range(1, nsp):
+        moe_sum = moe_sum + lax.ppermute(
+            out_blocks[d], "sp", [(i, i ^ d) for i in range(nsp)]
+        ).astype(FLOAT)
+    mixed = (mid_rows + moe_sum).astype(BF16)[None]
     d_kv = jnp.sum(d_kv.astype(FLOAT), axis=0).astype(BF16)
+    d_kv, all_down = lax.optimization_barrier((d_kv, all_down))
     (d_kv,) = exchange(
         "key_grads_group",
         11,
@@ -683,6 +684,7 @@
             Send(lambda i, o, z, f: i[0], lambda i, o, z, f, p=p: o[0].at[p], 0, p)
             for p in range(rep)
         ],
+        8,
     )
     d_kv = jnp.sum(d_kv.astype(FLOAT), axis=0)
     unused, q_pull = jax.vjp(prep_heads, q_lin, g_query)
@@ -696,50 +698,57 @@
     share = 1.0 / rep
     d_qkv_shared = jnp.concatenate([dq_b, dk_b * BF16(share), dv_b * BF16(share)], axis=1)
     d_w_qkv = contract_rows(xn_b, d_qkv).astype(BF16).reshape(nf, shard, qkv_cols)
-    (d_w_shard,) = exchange(
-        "head_grads_to_shards",
-        12,
-        (d_w_qkv,),
-        ((nf, shard, qkv_cols),),
-        [
-            Send(
-                lambda i, o, z, f, m=m: i[0].at[flip(f, m)],
-                lambda i, o, z, f, m=m: o[0].at[f],
-                0,
-                m,
-            )
-            for m in range(nf)
-        ],
-    )
-    d_wq = d_w_shard[:, :, :q_cols].transpose(1, 0, 2).reshape(shard, n_heads * head_dim)
-    d_wkv = d_w_shard[::rep, :, q_cols:].reshape(kv_heads, shard, 2, head_dim)
-    d_wkv = d_wkv.transpose(2, 1, 0, 3).reshape(2 * shard, kv_heads * head_dim)
     d_xn = pair_then_plane(contract_cols(d_qkv_shared, w_qkv), "input_sum", 13)
     unused, attn_pull = jax.vjp(rms_norm, x_rows, g_attn)
     d_x_norm, d_attn_gain = attn_pull(d_xn)
     grad_tokens = (d_mid + d_x_norm)[None]
 
+    smalls = jnp.concatenate(
+        [
+            d_attn_gain.reshape(nf, shard),
+            d_ffn_gain.reshape(nf, shard),
+            d_q_gain.reshape(nf, head_dim // nf),
+            (d_k_gain * share).reshape(nf, head_dim // nf),
+            d_router.reshape(nf, shard * n_experts),
+        ],
+        axis=1,
+    ).astype(BF16)
+    small_size = smalls.shape[1]
+    small_cols = pl.cdiv(small_size, kv_heads * head_dim) * kv_heads * head_dim // small_rows
+    small_cols = pl.cdiv(small_cols, LANES) * LANES
+    smalls = jnp.pad(smalls, ((0, 0), (0, small_rows * small_cols - small_size)))
+    d_w_shard, small_shard = exchange(
+        "head_grads_to_shards",
+        12,
+        (d_w_qkv, smalls.reshape(nf, small_rows, small_cols)),
+        ((nf, shard, qkv_cols), (nf, small_rows, small_cols)),
+        [
+            Send(
+                lambda i, o, z, f, m=m, w=w: i[w].at[flip(f, m)],
+                lambda i, o, z, f, m=m, w=w: o[w].at[f],
+                0,
+                m,
+            )
+            for w in range(2)
+            for m in range(nf)
+        ],
+        36,
+    )
+    d_wq = d_w_shard[:, :, :q_cols].transpose(1, 0, 2).reshape(shard, n_heads * head_dim)
+    d_wkv = d_w_shard[::rep, :, q_cols:].reshape(kv_heads, shard, 2, head_dim)
+    d_wkv = d_wkv.transpose(2, 1, 0, 3).reshape(2 * shard, kv_heads * head_dim)
+    small_sum = jnp.sum(small_shard.astype(FLOAT), axis=0).astype(BF16)
     sum_out = lax.psum(d_wo.astype(BF16), "sp").astype(FLOAT)
+    kv_cols = kv_heads * head_dim
+    d_wkv = jnp.concatenate([d_wkv, small_sum.reshape(-1, kv_cols)], axis=0)
     sum_q, sum_kv = lax.psum((d_wq, d_wkv), "sp")
     sum_q = sum_q.astype(FLOAT)
     sum_kv = sum_kv.astype(FLOAT)
-    gain_sums = lax.psum(
-        jnp.concatenate(
-            [
-                d_attn_gain,
-                d_ffn_gain,
-                d_q_gain,
-                d_k_gain * share,
-                d_router.reshape(-1),
-            ]
-        ),
-        ("sp", "fsdp"),
-    )
+    small_sum = sum_kv[2 * shard :].reshape(-1)
     at = 0
     pieces = []
-    for size in (width, width, head_dim, head_dim, width * n_experts):
-        whole = gain_sums[at : at + size]
-        pieces.append(lax.dynamic_slice_in_dim(whole, f * (size // nf), size // nf, 0))
+    for size in (shard, shard, head_dim // nf, head_dim // nf, shard * n_experts):
+        pieces.append(small_sum[at : at + size])
         at += size
     return (
         mixed,
@@ -747,15 +756,15 @@
         pieces[0],
         sum_q,
         sum_kv[:shard],
-        sum_kv[shard:],
+        sum_kv[shard : 2 * shard],
         pieces[2],
         pieces[3],
         sum_out,
         pieces[1],
         pieces[4].reshape(shard, n_experts),
-        grad_gate,
-        grad_up,
-        grad_down,
+        all_gate.astype(FLOAT),
+        all_up.astype(FLOAT),
+        all_down.astype(FLOAT),
     )
 
 

time: 1590 us -> 1230 us (0.77)
  waiting for transfers between devices: 376 us -> 264 us
  Pallas kernels: 689 us -> 586 us
  local copies, waits for them, and re-layouts: 138 us -> 69.4 us
  starting transfers between devices: 89.6 us -> 22.1 us
    ppermute x33 -> x0, waiting for transfers between devices: 222 us -> none  [the longest x9 154 us: all_planes(): lax.ppermute(left[-1], 'sp', [(i + 1, i) for i in range(0, nsp - step)])]
    psum x1, waiting for transfers between devices: 0.01 us -> 162 us  [body(): sum_q, sum_kv = lax.psum((d_wq, d_wkv), 'sp')]
    ppermute x3, waiting for transfers between devices: 154 us -> 0.01 us  [body(): lax.ppermute(out_blocks[d], 'sp', [(i, i ^ d) for i in range(nsp)])]
    pallas_call x15 -> x14, Pallas kernels: 689 us -> 586 us  [exchange(): pl.pallas_call(kernel, out_shape=[jax.ShapeDtypeStruct(shape, BF16) for s...]
    all_gather x0 -> x3, waiting for transfers between devices: none -> 101 us  [body(): lax.all_gather(block, 'sp', axis=0, tiled=True)]
    ppermute x33 -> x0, starting transfers between devices: 49.9 us -> none  [the longest x9 21.4 us: all_planes(): lax.ppermute(right[-1], 'sp', [(i, i + 1) for i in range(step - 1, nsp -...]
    dynamic_update_slice x12 -> x0, other arithmetic: 42.4 us -> none  [all_planes(): lax.dynamic_update_slice_in_dim(full, value, lax.rem(z - d + nsp, nsp) *...]
    convert_element_type x4 -> x8, other arithmetic: 4.3 us -> 35.7 us  [the longest x3 9.86 us: body(): summed.append((total + jnp.sum(others.astype(FLOAT), axis=0)).astype(BF16))]
  transfers between devices with their start and end apart: 38 -> 7, of which waited for: 13 -> 2; matrix products, arithmetic and copies ran while one was open for 17% -> 11% of each run, Pallas kernels for 22% -> 15%
where the time goes in v2:
time: 1230 us; the launch traced here: 1220 us
  Pallas kernels  586 us (48%)
  waiting for transfers between devices  264 us (21%)
  matrix products  144 us (12%)
  other arithmetic  116 us (9%)
  local copies, waits for them, and re-layouts  69.4 us (6%)
  starting transfers between devices  22.1 us (2%)
  between operations  15.5 us (1%)
    pallas_call x14, Pallas kernels, exchange(): pl.pallas_call(kernel, out_shape=[jax.ShapeDtypeStruct(shape, BF16) for s...  586 us
    psum x1, waiting for transfers between devices, body(): sum_q, sum_kv = lax.psum((d_wq, d_wkv), 'sp')  162 us
    all_gather x3, waiting for transfers between devices, body(): lax.all_gather(block, 'sp', axis=0, tiled=True)  101 us
    dot_general x5, matrix products, contract_rows(): lax.dot_general(left_mat, right_mat, (((0,), (0,)), ((), ())), preferred_...  37.6 us
    dot_general x5, matrix products, contract_cols(): lax.dot_general(left_mat, right_mat, (((1,), (1,)), ((), ())), preferred_...  36.7 us
    dot_general x6, matrix products, matmul(): return jnp.dot(left_mat, right_mat, preferred_element_type=FLOAT)  34.8 us
  transfers between devices with their start and end apart: 7, of which 2 were waited for; matrix products, arithmetic and copies ran while one was open for 11% of the time, Pallas kernels for 15%

profile of v2, /device:TPU:0, one launch (start us, length us, event | category | flops | bytes accessed | tf_op | source)
XLA Modules:
  0.0 1217.5 jit_solution(11583822981877412555)
XLA Ops:
  14.9 4.6 copy.208
  27.3 66.5 %gather_inputs.1 = (bf16[8,144,2048]{2,1,0:T(8,128)(2,1)}, bf16[8,256,768]{2,1,0:T(8,128)(2,1)}, bf16[4,128,2176]{2,1,0:T(8,128)(2,1)}) custom-call(bf16[144,2048]{1,0:T(8,128)(2,1)} %pad_maximum_fusion.3.refs_0_, bf16[8,256,768]{2,1,0:T(8,128)(2,1)} %maximum_bitcast_fusion.refs_1_, bf16[128,2176]{1,0:T(8,128)(2,1)} %concatenate.61.refs_2_), custom_call_target="tpu_custom_call" | custom-call | bytes 195000000 | tf_op jit(solution)/shard_map/gather_inputs/pallas_call | solution.py:131
  109.5 3.9 convolution_convert_fusion.1
  121.3 3.6 dynamic-slice_convert_fusion.refs_3_
  124.9 4.9 dynamic-slice_convert_fusion.1
  130.8 58.3 %keys_and_experts.1 = (bf16[4,1024,256]{2,1,0:T(8,128)(2,1)}, bf16[8,256,768]{2,1,0:T(8,128)(2,1)}, bf16[8,256,768]{2,1,0:T(8,128)(2,1)}, bf16[8,96,2048]{2,1,0:T(8,128)(2,1)}) custom-call(bf16[1024,256]{1,0:T(8,128)(2,1)} %pad_maximum_fusion.5.refs_0_, bf16[4,256,768]{2,1,0:T(8,128)(2,1)} %get-tuple-element.204.refs_1_, ...), custom_call_target="tpu_custom_call" | custom-call | bytes 165000000 | tf_op jit(solution)/shard_map/keys_and_experts/pallas_call | solution.py:131
  192.4 4.0 fusion.100
  203.5 4.4 convolution_convert_fusion.2
  207.9 4.5 out_sum_pair.1
  212.5 4.4 fusion.11.refs_0_
  216.9 26.7 %out_sum_plane.1 = bf16[4,128,2048]{2,1,0:T(8,128)(2,1)} custom-call(bf16[4,128,2048]{2,1,0:T(8,128)(2,1)} %fusion.11.refs_0_), custom_call_target="tpu_custom_call" | custom-call | bytes 81000000 | tf_op jit(solution)/shard_map/out_sum_plane/pallas_call | solution.py:131
  249.2 60.1 %hidden_planes.1 = (bf16[4,128,2048]{2,1,0:T(8,128)(2,1)}, bf16[4,128,128]{2,1,0:T(8,128)(2,1)}, bf16[4,4,80,2048]{3,2,1,0:T(8,128)(2,1)}) custom-call(bf16[128,2048]{1,0:T(8,128)(2,1)} %multiply_convert_fusion.5.refs_0_, bf16[128,128]{1,0:T(8,128)(2,1)} %maximum_maximum_fusion.1.refs_1_, bf16[4,4,80,2048]{3,2,1,0:T(8,128)(2,1)} %bitcast.293), custom_call_target="tpu_custom_call" | custom-call | bytes 174000000 | tf_op jit(solution)/shard_map/hidden_planes/pallas_call | solution.py:131
  311.1 5.5 convolution_convert_fusion
  316.6 62.3 %rows_to_experts.1 = (bf16[4,4,80,2048]{3,2,1,0:T(8,128)(2,1)}, bf16[4,4,80,128]{3,2,1,0:T(8,128)(2,1)}) custom-call(bf16[4,4,80,2048]{3,2,1,0:T(8,128)(2,1)} %bitcast.294, bf16[4,4,80,128]{3,2,1,0:T(8,128)(2,1)} %bitcast.340), custom_call_target="tpu_custom_call" | custom-call | bytes 180000000 | tf_op jit(solution)/shard_map/rows_to_experts/pallas_call | solution.py:131
  380.4 9.8 fusion.104
  393.9 6.3 fusion.103
  400.1 8.8 multiply_convert_fusion.1
  409.0 5.9 convolution_convert_fusion.6
  414.9 6.9 fusion.105
  421.8 7.9 multiply_convert_fusion
  430.0 9.2 convolution_convert_fusion.7
  439.2 8.6 convolution_convert_fusion.5
  447.8 8.9 add_convert_fusion
  457.7 63.3 %rows_from_experts.1 = (bf16[4,4,80,2048]{3,2,1,0:T(8,128)(2,1)}, bf16[4,4,80,128]{3,2,1,0:T(8,128)(2,1)}, bf16[1,4,96,2048]{3,2,1,0:T(8,128)(2,1)}, bf16[1,4,25...) custom-call(bf16[4,4,80,2048]{3,2,1,0:T(8,128)(2,1)} %bitcast.319, bf16[4,4,80,128]{3,2,1,0:T(8,128)(2,1)} %maximum_maximum_fusion.refs_1_, ...), custom_call_target="tpu_custom_call" | custom-call | bytes 210000000 | tf_op jit(solution)/shard_map/rows_from_experts/pallas_call | solution.py:131
  521.0 3.6 fusion.16.refs_4_
  534.6 55.9 %hidden_grads_home.1 = (bf16[4,128,2048]{2,1,0:T(8,128)(2,1)}, bf16[4,128,128]{2,1,0:T(8,128)(2,1)}, bf16[4,96,2048]{2,1,0:T(8,128)(2,1)}, bf16[4,256,768]{2,1,0:T(8,128)(2,1)}, bf16[4,256,768]{2,1,0:T(8,128)(2,1)}) custom-call(bf16[4,128,2048]{2,1,0:T(8,128)(2,1)} %convolution_convert_fusion.10.refs_0_, ...), custom_call_target="tpu_custom_call" | custom-call | bytes 174000000 | tf_op jit(solution)/shard_map/hidden_grads_home/pallas_call | solution.py:131
  603.1 28.0 %gather_grads.1 = bf16[8,128,2048]{2,1,0:T(8,128)(2,1)} custom-call(bf16[128,2048]{1,0:T(8,128)(2,1)} %fusion.94.refs_0_), custom_call_target="tpu_custom_call" | custom-call | bytes 90000000 | tf_op jit(solution)/shard_map/gather_grads/pallas_call | solution.py:131
  631.1 6.9 convolution_convert_fusion.13
  640.2 3.9 fusion.7
  644.2 4.4 fusion.8
  655.9 73.0 %key_grads_planes.1 = (bf16[4,1024,256]{2,1,0:T(8,128)(2,1)}, bf16[4,4,80,2048]{3,2,1,0:T(8,128)(2,1)}) custom-call(bf16[4,1024,256]{2,1,0:T(8,128)(2,1)} %bitcast.308, bf16[4,4,80,2048]{3,2,1,0:T(8,128)(2,1)} %bitcast.320), custom_call_target="tpu_custom_call" | custom-call | bytes 180000000 | tf_op jit(solution)/shard_map/key_grads_planes/pallas_call | solution.py:131
  743.0 6.2 convolution_convert_fusion.8
  749.2 17.1 %key_grads_group.1 = bf16[2,1024,256]{2,1,0:T(8,128)(2,1)} custom-call(bf16[1024,256]{1,0:T(8,128)(2,1)} %reduce_sum.332.refs_0_), custom_call_target="tpu_custom_call" | custom-call | bytes 24000000 | tf_op jit(solution)/shard_map/key_grads_group/pallas_call | solution.py:131
  776.2 7.8 convolution_convert_fusion.3
  784.0 4.6 input_sum_pair.1
  788.6 4.5 fusion.10.refs_0_
  793.1 26.7 %input_sum_plane.1 = bf16[4,128,2048]{2,1,0:T(8,128)(2,1)} custom-call(bf16[4,128,2048]{2,1,0:T(8,128)(2,1)} %fusion.10.refs_0_), custom_call_target="tpu_custom_call" | custom-call | bytes 81000000 | tf_op jit(solution)/shard_map/input_sum_plane/pallas_call | solution.py:131
  823.8 7.8 convolution_convert_fusion.4
  831.6 39.2 %head_grads_to_shards.1 = (bf16[8,256,768]{2,1,0:T(8,128)(2,1)}, bf16[8,16,384]{2,1,0:T(8,128)(2,1)}) custom-call(bf16[8,256,768]{2,1,0:T(8,128)(2,1)} %bitcast.331, bf16[8,16,384]{2,1,0:T(8,128)(2,1)} %bitcast.352), custom_call_target="tpu_custom_call" | custom-call | bytes 108000000 | tf_op jit(solution)/shard_map/head_grads_to_shards/pallas_call | solution.py:131
  880.7 4.0 convolution_convert_fusion.9
  885.9 20.5 %collective-permute-start = (bf16[128,2048]{1,0:T(8,128)(2,1)}, bf16[128,2048]{1,0:T(8,128)(2,1)}, u32[]{:S(2)}, u32[]{:S(2)}) collective-permute-start(bf16[128,2048]{1,0:T(8,128)(2,1)} %get-tuple-element.170), channel_id=1, source_target_pairs={{0,8},{8,0},{16,24},{24,16},{1,9},{9,1},{17,25},{25,17},{2,10},{10... | collective-permute-start | bytes 1572872 | tf_op jit(solution)/shard_map/ppermute | solution.py:672
  907.8 6.3 convert_element_type.487
  914.1 9.0 convert_element_type.486
  923.1 101.0 %all-gather.6.cloned.1.call-done = bf16[16,256,768]{2,1,0:T(8,128)(2,1)} async-done(((bf16[4,256,768]{2,1,0:T(8,128)(2,1)}), bf16[16,256,768]{2,1,0:T(8,128)(2,1)}) %all-gather.6.cloned.1.call-update) | async-done | bytes 6291472 | tf_op jit(solution)/shard_map/all_gather | solution.py:597
  1024.2 9.3 convert_element_type.485
  1033.6 3.5 fusion.34
  1037.1 161.6 %all-reduce.9.cloned.1.call-done = (bf16[524,512]{1,0:T(8,128)(2,1)}, bf16[256,4096]{0,1:T(8,128)(2,1)}, bf16[512,2048]{1,0:T(8,128)(2,1)}) async-done(((bf16[524,512]{1,0:T(8,128)(2,1)}, bf16[256,4096]{0,1:T(8,128)(2,1)}, bf16[512,2048]{1,0:T(8,128)(2,1)}), (bf16[524,512]{1,0:T(8,128)(2,1)}, bf16[256,4096]{0,1:T(8,128)(2,1)}, bf16[512,2048]{1,0:T(8,128)(2,1)})) %all-reduce.9.cloned.1.call-update) | async-done | bytes 4730896 | tf_op jit(solution)/shard_map/psum | solution.py:744
  1203.5 4.4 copy.248
  (317 shorter events, 143.5 us)
Async XLA Ops:
  7.2 742.0 %all-gather.4.cloned.1.call-start = ((), (), s32[]{:S(2)}) async-start(), calls=%async_computation | async-start | bytes 7864320 | tf_op jit(solution)/shard_map/all_gather | solution.py:597
  19.5 3.8 copy-start.16
  93.8 4.8 copy-start.5
  99.8 4.1 copy-start.22
  105.8 7.5 copy-start.47
  108.1 10.5 copy-start.51
  108.1 9.1 copy-start.49
  113.4 3.9 copy-start.45
  121.3 69.8 %copy-start.23 = (bf16[8,128,4,64]{3,1,2,0:T(8,128)(2,1)}, bf16[8,128,4,64]{3,1,2,0:T(8,128)(2,1)S(1)}, u32[]{:S(2)}) copy-start(bf16[8,128,4,64]{3,1,2,0:T(8,128)(2,1)S(1)} %get-tuple-element.168) | copy-start | bytes 1572868
  199.8 3.7 copy-start.54
  202.6 5.3 copy-start.35
  390.3 9.8 slice-start.6
  393.8 6.3 slice-start.7
  393.8 6.3 copy-start.56
  400.1 21.7 %slice-start.4 = ((s8[5242880]{0:T(1024)(128)(4,1)}), s8[4194304]{0:T(1024)(128)(4,1)S(1)}, s32[]{:S(2)}) async-start(s8[5242880]{0:T(1024)(128)(4,1)} %bitcast.321), calls=%async_computation.8 | async-start | bytes 8388608
  409.0 12.8 %copy-start.60 = (bf16[1280,768]{1,0:T(8,128)(2,1)}, bf16[1280,768]{1,0:T(8,128)(2,1)S(1)}, u32[]{:S(2)}) copy-start(bf16[1280,768]{1,0:T(8,128)(2,1)S(1)} %get-tuple-element.160) | copy-start | bytes 5898244
  409.0 5.9 copy-start.59
  409.0 12.8 %slice-start.5 = ((s8[5242880]{0:T(1024)(128)(4,1)}), s8[1048576]{0:T(1024)(128)(4,1)S(1)}, s32[]{:S(2)}) async-start(s8[5242880]{0:T(1024)(128)(4,1)} %bitcast.321), calls=%async_computation.9 | async-start | bytes 2097152
  430.0 9.2 copy-start.61
  439.2 8.6 copy-start.57
  521.0 9.9 slice-start
  524.6 6.3 slice-start.1
  590.5 323.6 %all-gather.8.cloned.1.call-start = ((), (), s32[]{:S(2)}) async-start(), calls=%async_computation.2 | async-start | bytes 7864320 | tf_op jit(solution)/shard_map/all_gather | solution.py:597
  591.3 432.9 %all-gather.6.cloned.1.call-start = ((), (), s32[]{:S(2)}) async-start(), calls=%async_computation.1 | async-start | bytes 7864320 | tf_op jit(solution)/shard_map/all_gather | solution.py:597
  592.0 606.7 %all-reduce.9.cloned.1.call-start = ((), (), s32[]{:S(2)}) async-start(), calls=%async_computation.3 | async-start | bytes 9469952 | tf_op jit(solution)/shard_map/psum | solution.py:744
  592.1 3.8 copy-start.19
  644.1 4.4 copy-start.24
  644.1 4.4 copy-start.26
  648.6 3.7 copy-start.3
  648.6 4.0 copy-start.21
  766.3 6.3 copy-start.28
  766.3 6.3 copy-start.46
  766.3 6.3 copy-start.50
  767.9 6.4 copy-start.48
  793.1 29.0 %copy-start.9 = (bf16[1,128,2048]{2,1,0:T(8,128)(2,1)S(1)}, bf16[1,128,2048]{2,1,0:T(8,128)(2,1)}, u32[]{:S(2)}) copy-start(bf16[1,128,2048]{2,1,0:T(8,128)(2,1)} %param.15) | copy-start | bytes 1572868
  793.1 29.0 %copy-start.44 = (f32[1,2,8,128]{3,1,2,0:T(2,128)S(1)}, f32[1,2,8,128]{3,1,2,0:T(2,128)}, u32[]{:S(2)}) copy-start(f32[1,2,8,128]{3,1,2,0:T(2,128)} %copy-done.43) | copy-start | bytes 24580
  819.8 4.0 copy-start.36
  819.8 4.0 copy-start.40
  880.7 27.2 %slice-start.2 = ((s8[6291456]{0:T(1024)(128)(4,1)}), s8[4194304]{0:T(1024)(128)(4,1)S(1)}, s32[]{:S(2)}) async-start(s8[6291456]{0:T(1024)(128)(4,1)} %bitcast.317), calls=%async_computation.6 | async-start | bytes 8388608
  880.7 27.2 %slice-start.3 = ((s8[6291456]{0:T(1024)(128)(4,1)}), s8[2097152]{0:T(1024)(128)(4,1)S(1)}, s32[]{:S(2)}) async-start(s8[6291456]{0:T(1024)(128)(4,1)} %bitcast.317), calls=%async_computation.7 | async-start | bytes 4194304
  885.9 147.6 %collective-permute-start = (bf16[128,2048]{1,0:T(8,128)(2,1)}, bf16[128,2048]{1,0:T(8,128)(2,1)}, u32[]{:S(2)}, u32[]{:S(2)}) collective-permute-start(bf16[128,2048]{1,0:T(8,128)(2,1)} %get-tuple-element.170), channel_id=1, source_target_pairs={{0,8},{8,0},{16,24},{24,16},{1,9},{9,1},{17,25},{25,17},{2,10},{10... | collective-permute-start | bytes 1572872 | tf_op jit(solution)/shard_map/ppermute | solution.py:672
  906.4 127.1 %collective-permute-start.2 = (bf16[128,2048]{1,0:T(8,128)(2,1)}, bf16[128,2048]{1,0:T(8,128)(2,1)}, u32[]{:S(2)}, u32[]{:S(2)}) collective-permute-start(bf16[128,2048]{1,0:T(8,128)(2,1)} %get-tuple-element.171), channel_id=1, source_target_pairs={{0,24},{8,16},{16,8},{24,0},{1,25},{9,17},{17,9},{25,1},{2,26},{10... | collective-permute-start | bytes 1572872 | tf_op jit(solution)/shard_map/ppermute | solution.py:672
  906.9 126.6 %collective-permute-start.1 = (bf16[128,2048]{1,0:T(8,128)(2,1)}, bf16[128,2048]{1,0:T(8,128)(2,1)}, u32[]{:S(2)}, u32[]{:S(2)}) collective-permute-start(bf16[128,2048]{1,0:T(8,128)(2,1)} %get-tuple-element.172), channel_id=1, source_target_pairs={{0,16},{8,24},{16,0},{24,8},{1,17},{9,25},{17,1},{25,9},{2,18},{10... | collective-permute-start | bytes 1572872 | tf_op jit(solution)/shard_map/ppermute | solution.py:672
  1024.1 9.4 copy-start.10
  1024.1 9.4 copy-start.11
  1024.1 9.4 copy-start.13
  1024.1 9.4 copy-start.17
  1203.5 4.4 copy-start.27
  (29 other events, 72.9 us)
Sparse Core Ops, SparseCore 0:
  590.6 158.5 all-gather.3
  750.8 113.4 all-gather.7
  865.9 158.2 all-gather.5
  1027.2 171.5 all-reduce.8

commit v3 on v2

--- a/solution.py
+++ b/solution.py
@@ -65,6 +65,25 @@
     return index
 
 
+class _ShapeOnly:
+    def __init__(self, shape):
+        self.shape = tuple(shape)
+
+    @property
+    def at(self):
+        return self
+
+    def __getitem__(self, index):
+        index = index if isinstance(index, tuple) else (index,)
+        shape = []
+        for size, i in zip(self.shape, index):
+            if isinstance(i, slice):
+                shape.append(len(range(*i.indices(size))))
+            elif hasattr(i, "size") and hasattr(i, "start"):
+                shape.append(i.size)
+        return _ShapeOnly(tuple(shape) + self.shape[len(index) :])
+
+
 class Send(NamedTuple):
     src: Callable
     dst: Callable
@@ -76,10 +95,20 @@
 def exchange(name, cid, arrays, out_shapes, sends, micros):
     n_in, n_out = len(arrays), len(out_shapes)
     peers = sorted({(s.dz, s.df) for s in sends} - {(0, 0)})
+    stays = [k for k, s in enumerate(sends) if (s.dz, s.df) == (0, 0)]
+    stay_shapes = []
+
+    def probe(*refs):
+        for k in stays:
+            view = sends[k].src(refs, None, jnp.int32(0), jnp.int32(0))
+            stay_shapes.append(view.shape)
+
+    probe(*[_ShapeOnly(a.shape) for a in arrays])
 
     def kernel(*refs):
         ins, outs = refs[:n_in], refs[n_in : n_in + n_out]
-        send_sems, recv_sems = refs[n_in + n_out :]
+        send_sems, recv_sems = refs[n_in + n_out : n_in + n_out + 2]
+        bounce = dict(zip(stays, refs[n_in + n_out + 2 :]))
         z = lax.axis_index("sp")
         f = lax.axis_index("fsdp")
         barrier = pltpu.get_barrier_semaphore()
@@ -93,7 +122,12 @@
             src = s.src(ins, outs, z, f)
             dst = s.dst(ins, outs, z, f)
             if (s.dz, s.df) == (0, 0):
-                copies.append(pltpu.make_async_copy(src, dst, recv_sems.at[k]))
+                copies.append(
+                    (
+                        pltpu.make_async_copy(src, bounce[k], recv_sems.at[k]),
+                        pltpu.make_async_copy(bounce[k], dst, send_sems.at[k]),
+                    )
+                )
             else:
                 copies.append(
                     pltpu.make_async_remote_copy(
@@ -112,13 +146,18 @@
                 arrived.add(k)
                 s = sends[k]
                 if (s.dz, s.df) == (0, 0):
-                    copies[k].wait()
+                    copies[k][1].wait()
                 else:
                     copies[k].wait_recv()
 
         for k, s in enumerate(sends):
-            if s.after is None:
+            if k in stays:
+                copies[k][0].start()
+            elif s.after is None:
                 copies[k].start()
+        for k in stays:
+            copies[k][0].wait()
+            copies[k][1].start()
         for k, s in enumerate(sends):
             if s.after is not None:
                 arrive(s.after)
@@ -136,8 +175,11 @@
         scratch_shapes=[
             pltpu.SemaphoreType.DMA((len(sends),)),
             pltpu.SemaphoreType.DMA((len(sends),)),
-        ],
-        compiler_params=pltpu.CompilerParams(collective_id=cid, has_side_effects=True),
+        ]
+        + [pltpu.VMEM(shape, BF16) for shape in stay_shapes],
+        compiler_params=pltpu.CompilerParams(
+            collective_id=cid, has_side_effects=True, vmem_limit_bytes=32 * 1024 * 1024
+        ),
         cost_estimate=pl.CostEstimate(
             flops=0, bytes_accessed=int(micros * 3.0e6), transcendentals=0
         ),
@@ -187,6 +229,12 @@
     place = lax.div(f, parts)
     expert = z * plane_experts + place
 
+    def swap_f(block, mask):
+        return lax.ppermute(block, "fsdp", [(i, i ^ mask) for i in range(nf)])
+
+    def swap_z(block, mask):
+        return lax.ppermute(block, "sp", [(i, i ^ mask) for i in range(nsp)])
+
     small = jnp.concatenate(
         [
             attn_gain.astype(BF16),
@@ -502,11 +550,40 @@
     sigma = jax.nn.sigmoid(gate_pre)
     act_f = gate_pre * sigma
     hidden = (act_f * up_pre).astype(BF16)
+    dy_f = dy_in.astype(FLOAT)
+    d_result = (row_gate * dy_f).astype(BF16)
+
+    def by_shard(full, inner):
+        return full.astype(BF16).reshape((plane_experts, parts) + inner)
+
+    def pair_total(own, others):
+        total = lax.dynamic_index_in_dim(own, part, 1, keepdims=False).astype(FLOAT)
+        for other in others:
+            total = total + other.astype(FLOAT)
+        return total.astype(BF16)
+
+    d_down = by_shard(contract_rows(hidden, d_result), (hid_shard, width))
+    d_down = pair_total(
+        d_down,
+        [
+            swap_f(lax.dynamic_index_in_dim(d_down, flip(part, p), 1, keepdims=False), p)
+            for p in range(1, parts)
+        ],
+    )
+    d_down = jnp.stack(
+        [
+            swap_f(
+                lax.dynamic_index_in_dim(d_down, flip(place, s), 0, keepdims=False), s * parts
+            )
+            if s
+            else lax.dynamic_index_in_dim(d_down, place, 0, keepdims=False)
+            for s in range(plane_experts)
+        ]
+    )
+    all_down = lax.all_gather(d_down, "sp")
     result = matmul(hidden, wd_b)
-    dy_f = dy_in.astype(FLOAT)
     row_dgate = jnp.sum(result * dy_f, axis=1, keepdims=True)
     weighted = (row_gate * result).astype(BF16)
-    d_result = (row_gate * dy_f).astype(BF16)
     d_hidden = contract_cols(d_result, wd_b)
     d_gate_pre = (d_hidden * up_pre * sigma * (1.0 + gate_pre * (1.0 - sigma))).astype(BF16)
     d_up_pre = (d_hidden * act_f).astype(BF16)
@@ -516,11 +593,7 @@
         [dgate_high, dgate_low, jnp.zeros((n_rows, LANES - 2 * n_experts), BF16)], axis=1
     )
 
-    def by_shard(full, inner):
-        return full.astype(BF16).reshape((plane_experts, parts) + inner)
-
     d_weights = (
-        by_shard(contract_rows(hidden, d_result), (hid_shard, width)),
         by_shard(contract_rows(hn_in, d_gate_pre), (shard, hidden_size)),
         by_shard(contract_rows(hn_in, d_up_pre), (shard, hidden_size)),
     )
@@ -537,7 +610,7 @@
                     s * parts,
                 )
             )
-    for w in range(3):
+    for w in range(2):
         for p in range(1, parts):
             sends.append(
                 Send(
@@ -565,16 +638,16 @@
         flat = returned.reshape(nsp, plane_experts * cap, returned.shape[3])
         return jnp.einsum("drt,drc->dtc", pick, flat, preferred_element_type=FLOAT).astype(BF16)
 
-    summed = []
-    for own, others in zip(d_weights, d_others):
-        total = lax.dynamic_index_in_dim(own, part, 1, keepdims=False).astype(FLOAT)
-        summed.append((total + jnp.sum(others.astype(FLOAT), axis=0)).astype(BF16))
+    summed = [
+        pair_total(own, [others[p] for p in range(parts - 1)])
+        for own, others in zip(d_weights, d_others)
+    ]
     sends = [
         Send(lambda i, o, z, f, d=d, w=w: i[w].at[d], lambda i, o, z, f, d=d, w=w: o[w].at[d], d, 0)
         for w in range(2)
         for d in range(nsp)
     ]
-    for w in range(2, 5):
+    for w in range(2, 4):
         for s in range(plane_experts):
             sends.append(
                 Send(
@@ -593,9 +666,7 @@
         sends,
         58,
     )
-    all_down, all_gate, all_up = [
-        lax.all_gather(block, "sp", axis=0, tiled=True) for block in shards
-    ]
+    all_gate, all_up = [lax.all_gather(block, "sp", axis=0, tiled=True) for block in shards]
     d_home = jnp.sum(d_home.astype(FLOAT), axis=0)
     tail = jnp.sum(dgate_home.astype(FLOAT), axis=0)
     d_gates = tail[:, :n_experts] + tail[:, n_experts : 2 * n_experts]
@@ -608,6 +679,14 @@
     d_mid = grad_out + d_mid_norm
 
     d_attn_b = d_mid.astype(BF16)
+    d_attn_b, all_down = lax.optimization_barrier((d_attn_b, all_down))
+    grad_down = jnp.take(
+        all_down,
+        jnp.bitwise_xor(jnp.arange(plane_experts, dtype=jnp.int32), place),
+        axis=1,
+        mode="clip",
+    )
+    grad_down = grad_down.astype(FLOAT).reshape(n_experts, hid_shard, width)
     sends = [
         Send(lambda i, o, z, f: i[0], lambda i, o, z, f: o[0].at[f], 0, m)
         for m in range(0, nf, 2)
@@ -645,9 +724,28 @@
     d_kv = jnp.concatenate([d_key, d_val], axis=2).astype(BF16)
     d_kv = d_kv.reshape(seqs, nsp, rows, 2 * head_dim).transpose(1, 0, 2, 3)
     d_kv = d_kv.reshape(nsp, seqs * rows, 2 * head_dim)
+    d_kv = d_kv.reshape(nsp, rep, piece, 2 * head_dim)
+    (others,) = exchange(
+        "key_grads_group",
+        11,
+        (d_kv,),
+        ((rep - 1, nsp, piece, 2 * head_dim),),
+        [
+            Send(
+                lambda i, o, z, f, p=p: i[0].at[:, flip(lax.rem(f, rep), p)],
+                lambda i, o, z, f, p=p: o[0].at[p - 1],
+                0,
+                p,
+            )
+            for p in range(1, rep)
+        ],
+        6,
+    )
+    d_kv = lax.dynamic_index_in_dim(d_kv, lax.rem(f, rep), 1, keepdims=False)
+    d_kv = (d_kv.astype(FLOAT) + jnp.sum(others.astype(FLOAT), axis=0)).astype(BF16)
     sends = [
-        Send(lambda i, o, z, f, d=d: i[0].at[d], lambda i, o, z, f, d=d: o[0].at[d], d, 0)
-        for d in range(nsp)
+        Send(lambda i, o, z, f, d=d: i[0].at[d], lambda i, o, z, f, d=d: o[0].at[d - 1], d, 0)
+        for d in range(1, nsp)
     ]
     for s in range(plane_experts):
         sends.append(
@@ -658,35 +756,33 @@
                 s * parts,
             )
         )
-    d_kv, out_back = exchange(
+    others, out_back = exchange(
         "key_grads_planes",
         10,
         (d_kv, weighted.reshape(plane_experts, nsp, cap, width)),
-        ((nsp, seqs * rows, 2 * head_dim), (nsp, plane_experts, cap, width)),
+        ((nsp - 1, piece, 2 * head_dim), (nsp, plane_experts, cap, width)),
         sends,
         60,
     )
     out_blocks = combine(out_back)
     moe_sum = out_blocks[0].astype(FLOAT)
     for d in range(1, nsp):
-        moe_sum = moe_sum + lax.ppermute(
-            out_blocks[d], "sp", [(i, i ^ d) for i in range(nsp)]
-        ).astype(FLOAT)
+        moe_sum = moe_sum + swap_z(out_blocks[d], d).astype(FLOAT)
     mixed = (mid_rows + moe_sum).astype(BF16)[None]
-    d_kv = jnp.sum(d_kv.astype(FLOAT), axis=0).astype(BF16)
-    d_kv, all_down = lax.optimization_barrier((d_kv, all_down))
+    d_kv = (d_kv[0].astype(FLOAT) + jnp.sum(others.astype(FLOAT), axis=0)).astype(BF16)
+    d_kv, all_gate = lax.optimization_barrier((d_kv, all_gate))
     (d_kv,) = exchange(
-        "key_grads_group",
-        11,
+        "key_grads_share",
+        15,
         (d_kv,),
-        ((rep, seqs * rows, 2 * head_dim),),
+        ((rep, piece, 2 * head_dim),),
         [
-            Send(lambda i, o, z, f: i[0], lambda i, o, z, f, p=p: o[0].at[p], 0, p)
+            Send(lambda i, o, z, f: i[0], lambda i, o, z, f: o[0].at[lax.rem(f, rep)], 0, p)
             for p in range(rep)
         ],
-        8,
-    )
-    d_kv = jnp.sum(d_kv.astype(FLOAT), axis=0)
+        6,
+    )
+    d_kv = d_kv.reshape(seqs * rows, 2 * head_dim).astype(FLOAT)
     unused, q_pull = jax.vjp(prep_heads, q_lin, g_query)
     d_q_lin, d_q_gain = q_pull(dq.astype(FLOAT))
     unused, k_pull = jax.vjp(prep_heads, k_lin, g_key)
@@ -764,7 +860,7 @@
         pieces[4].reshape(shard, n_experts),
         all_gate.astype(FLOAT),
         all_up.astype(FLOAT),
-        all_down.astype(FLOAT),
+        grad_down,
     )
 
 

time: 1230 us -> 1100 us (0.89)
  waiting for transfers between devices: 264 us -> 187 us
  other arithmetic: 116 us -> 84.6 us
  local copies, waits for them, and re-layouts: 69.4 us -> 100 us
  matrix products: 144 us -> 123 us
  Pallas kernels: 586 us -> 570 us
  starting transfers between devices: 22.1 us -> 8.32 us
    all_gather x3 -> x2, waiting for transfers between devices: 101 us -> 4.45 us  [body(): lax.all_gather(block, 'sp', axis=0, tiled=True)]
    ppermute x3 -> x7, waiting for transfers between devices: 0.01 us -> 81.6 us  [the longest x3 61.6 us: swap_z(): return lax.ppermute(block, 'sp', [(i, i ^ mask) for i in range(nsp)])]
    psum x1, waiting for transfers between devices: 162 us -> 99.9 us  [body(): sum_q, sum_kv = lax.psum((d_wq, d_wkv), 'sp')]
    unnamed x150 -> x191, local copies, waits for them, and re-layouts: 22.1 us -> 39.1 us
    pallas_call x14 -> x15, Pallas kernels: 586 us -> 570 us  [exchange(): pl.pallas_call(kernel, out_shape=[jax.ShapeDtypeStruct(shape, BF16) for s...]
    ppermute x3 -> x7, starting transfers between devices: 22 us -> 7.94 us  [the longest x3 4.39 us: swap_z(): return lax.ppermute(block, 'sp', [(i, i ^ mask) for i in range(nsp)])]
  transfers between devices with their start and end apart: 7 -> 11, of which waited for: 2 -> 7; matrix products, arithmetic and copies ran while one was open for 11% -> 15% of each run, Pallas kernels for 15% -> 27%
where the time goes in v3:
time: 1100 us; the launch traced here: 1090 us
  Pallas kernels  570 us (52%)
  waiting for transfers between devices  187 us (17%)
  matrix products  123 us (11%)
  local copies, waits for them, and re-layouts  100 us (9%)
  other arithmetic  84.6 us (8%)
  between operations  15.8 us (1%)
    pallas_call x15, Pallas kernels, exchange(): pl.pallas_call(kernel, out_shape=[jax.ShapeDtypeStruct(shape, BF16) for s...  570 us
    psum x1, waiting for transfers between devices, body(): sum_q, sum_kv = lax.psum((d_wq, d_wkv), 'sp')  99.9 us
    ppermute x3, waiting for transfers between devices, swap_z(): return lax.ppermute(block, 'sp', [(i, i ^ mask) for i in range(nsp)])  61.6 us
    unnamed x191, local copies, waits for them, and re-layouts  39.1 us
    dot_general x5, matrix products, contract_cols(): lax.dot_general(left_mat, right_mat, (((1,), (1,)), ((), ())), preferred_...  35.7 us
    dot_general x6, matrix products, matmul(): return jnp.dot(left_mat, right_mat, preferred_element_type=FLOAT)  33.3 us
    dot_general x5, matrix products, contract_rows(): lax.dot_general(left_mat, right_mat, (((0,), (0,)), ((), ())), preferred_...  26.7 us
  transfers between devices with their start and end apart: 11, of which 7 were waited for; matrix products, arithmetic and copies ran while one was open for 15% of the time, Pallas kernels for 27%

profile of v3, /device:TPU:0, one launch (start us, length us, event | category | flops | bytes accessed | tf_op | source)
XLA Modules:
  0.0 1089.1 jit_solution(11800450476108636991)
XLA Ops:
  13.2 3.8 copy.240
  25.6 66.3 %gather_inputs.1 = (bf16[8,144,2048]{2,1,0:T(8,128)(2,1)S(1)}, bf16[8,256,768]{2,1,0:T(8,128)(2,1)S(1)}, bf16[4,128,2176]{2,1,0:T(8,128)(2,1)S(1)}) custom-call(bf16[144,2048]{1,0:T(8,128)(2,1)S(1)} %copy-done.3, bf16[8,256,768]{2,1,0:T(8,128)(2,1)S(1)} %maximum_bitcast_fusion.refs_1_, bf16[128,2176]{1,0:T(8,128)(2,1)S(1)} %copy-done.4), custom_call_target="tpu_custom_call" | custom-call | bytes 195000000 | tf_op jit(solution)/shard_map/gather_inputs/pallas_call | solution.py:170
  94.3 3.4 fusion.105
  112.8 57.9 %keys_and_experts.1 = (bf16[4,1024,256]{2,1,0:T(8,128)(2,1)S(1)}, bf16[8,256,768]{2,1,0:T(8,128)(2,1)S(1)}, bf16[8,256,768]{2,1,0:T(8,128)(2,1)S(1)}, bf16[8,96,2048]{2,1,0:T(8,128)(2,1)S(1)}) custom-call(bf16[1024,256]{1,0:T(8,128)(2,1)S(1)} %pad_maximum_fusion.6.refs_0_, bf16[4,256,768]{2,1,0:T(8,128)(2,1)S(1)} %get-tuple-element.222.refs_1_, ...), custom_call_target="tpu_custom_call" | custom-call | bytes 165000000 | tf_op jit(solution)/shard_map/keys_and_experts/pallas_call | solution.py:170
  180.5 4.0 fusion.103
  194.0 4.2 out_sum_pair.1
  202.6 26.5 %out_sum_plane.1 = bf16[4,128,2048]{2,1,0:T(8,128)(2,1)S(1)} custom-call(bf16[4,128,2048]{2,1,0:T(8,128)(2,1)S(1)} %fusion.11.refs_0_), custom_call_target="tpu_custom_call" | custom-call | bytes 81000000 | tf_op jit(solution)/shard_map/out_sum_plane/pallas_call | solution.py:170
  238.3 60.0 %hidden_planes.1 = (bf16[4,128,2048]{2,1,0:T(8,128)(2,1)S(1)}, bf16[4,128,128]{2,1,0:T(8,128)(2,1)S(1)}, bf16[4,4,80,2048]{3,2,1,0:T(8,128)(2,1)S(1)}) custom-call(bf16[128,2048]{1,0:T(8,128)(2,1)S(1)} %multiply_convert_fusion.5.refs_0_, bf16[128,128]{1,0:T(8,128)(2,1)S(1)} %maximum_maximum_fusion.1.refs_1_, bf16[4,4,80,2048]{3,2,1,0:T(8,128)(2,1)S(1)} %bitcast.321), custom_call_target="tpu_custom_call" | custom-call | bytes 174000000 | tf_op jit(solution)/shard_map/hidden_planes/pallas_call | solution.py:170
  300.9 62.1 %rows_to_experts.1 = (bf16[4,4,80,2048]{3,2,1,0:T(8,128)(2,1)S(1)}, bf16[4,4,80,128]{3,2,1,0:T(8,128)(2,1)S(1)}) custom-call(bf16[4,4,80,2048]{3,2,1,0:T(8,128)(2,1)S(1)} %bitcast.322, bf16[4,4,80,128]{3,2,1,0:T(8,128)(2,1)S(1)} %bitcast.344), custom_call_target="tpu_custom_call" | custom-call | bytes 180000000 | tf_op jit(solution)/shard_map/rows_to_experts/pallas_call | solution.py:170
  366.0 9.8 fusion.107
  377.7 6.3 fusion.106
  383.9 9.0 multiply_convert_fusion.1
  392.9 7.1 multiply_convert_fusion
  400.0 5.7 convolution_convert_fusion.5
  408.4 3.6 collective-permute-done
  417.7 9.4 collective-permute-done.3
  427.1 6.9 collective-permute-done.2
  436.0 11.0 %fusion.108 = f32[1280,2048]{1,0:T(8,128)} fusion(bf16[1280,768]{1,0:T(8,128)(2,1)} %get-tuple-element.173, bf16[2048,768]{1,0:T(8,128)(2,1)} %bitcast.361), kind=kOutput, calls=%fused_computation.267 | convolution fusion | flops 4026531840 | bytes 15597568 | tf_op jit(solution)/shard_map/dot_general | solution.py:50
  447.1 4.8 convolution_convert_fusion.7
  451.9 4.6 convolution_convert_fusion.6
  456.5 7.7 add_convert_fusion
  464.2 63.6 %rows_from_experts.1 = (bf16[4,4,80,2048]{3,2,1,0:T(8,128)(2,1)S(1)}, bf16[4,4,80,128]{3,2,1,0:T(8,128)(2,1)S(1)}, bf16[1,4,256,768]{3,2,1,0:T(8,128)(2,1)S(1)}, bf16[1,4,256,768]{3,2,1,0:T(8,128)(2,1)S(1)}) custom-call(bf16[4,4,80,2048]{3,2,1,0:T(8,128)(2,1)S(1)} %bitcast.338, bf16[4,4,80,128]{3,2,1,0:T(8,128)(2,1)S(1)} %maximum_maximum_fusion.refs_1_, ...), custom_call_target="tpu_custom_call" | custom-call | bytes 210000000 | tf_op jit(solution)/shard_map/rows_from_experts/pallas_call | solution.py:170
  530.3 66.5 %hidden_grads_home.1 = (bf16[4,128,2048]{2,1,0:T(8,128)(2,1)S(1)}, bf16[4,128,128]{2,1,0:T(8,128)(2,1)S(1)}, bf16[4,256,768]{2,1,0:T(8,128)(2,1)S(1)}, bf16[4,256,768]{2,1,0:T(8,128)(2,1)S(1)}) custom-call(bf16[4,128,2048]{2,1,0:T(8,128)(2,1)S(1)} %convolution_convert_fusion.10.refs_0_, bf16[4,128,128]{2,1,0:T(8,128)(2,1)S(1)} %convolution_convert_fusion.15.refs_1_, ...), custom_call_target="tpu_custom_call" | custom-call | bytes 174000000 | tf_op jit(solution)/shard_map/hidden_grads_home/pallas_call | solution.py:170
  606.5 28.4 %gather_grads.1 = bf16[8,128,2048]{2,1,0:T(8,128)(2,1)} custom-call(bf16[128,2048]{1,0:T(8,128)(2,1)S(1)} %fusion.96.refs_0_), custom_call_target="tpu_custom_call" | custom-call | bytes 90000000 | tf_op jit(solution)/shard_map/gather_grads/pallas_call | solution.py:170
  634.9 5.7 convolution_convert_fusion.13
  642.0 3.5 fusion.7
  645.5 4.3 fusion.8
  661.9 4.5 fusion.21
  671.5 60.6 %key_grads_planes.1 = (bf16[3,512,256]{2,1,0:T(8,128)(2,1)S(1)}, bf16[4,4,80,2048]{3,2,1,0:T(8,128)(2,1)S(1)}) custom-call(bf16[4,512,256]{2,1,0:T(8,128)(2,1)S(1)} %fusion.20.refs_0_, bf16[4,4,80,2048]{3,2,1,0:T(8,128)(2,1)S(1)} %bitcast.337), custom_call_target="tpu_custom_call" | custom-call | bytes 180000000 | tf_op jit(solution)/shard_map/key_grads_planes/pallas_call | solution.py:170
  746.5 5.0 convolution_convert_fusion.3
  751.5 4.2 input_sum_pair.1
  756.7 26.3 %input_sum_plane.1 = bf16[4,128,2048]{2,1,0:T(8,128)(2,1)S(1)} custom-call(bf16[4,128,2048]{2,1,0:T(8,128)(2,1)S(1)} %fusion.10.refs_0_), custom_call_target="tpu_custom_call" | custom-call | bytes 81000000 | tf_op jit(solution)/shard_map/input_sum_plane/pallas_call | solution.py:170
  784.8 5.8 convolution_convert_fusion.4
  790.6 39.1 %head_grads_to_shards.1 = (bf16[8,256,768]{2,1,0:T(8,128)(2,1)S(1)}, bf16[8,16,384]{2,1,0:T(8,128)(2,1)S(1)}) custom-call(bf16[8,256,768]{2,1,0:T(8,128)(2,1)S(1)} %bitcast.341, bf16[8,16,384]{2,1,0:T(8,128)(2,1)S(1)} %bitcast.345), custom_call_target="tpu_custom_call" | custom-call | bytes 108000000 | tf_op jit(solution)/shard_map/head_grads_to_shards/pallas_call | solution.py:170
  836.4 4.2 copy.278
  841.5 5.8 convolution_convert_fusion.8
  847.4 3.4 all-gather.7.cloned.1.call-done
  850.8 9.2 convert_element_type.535
  860.0 3.8 convolution_convert_fusion.9
  865.9 3.4 collective-permute-start.4
  869.3 6.5 gather_fusion
  875.8 8.9 convert_bitcast_fusion
  884.7 8.9 convert_element_type.534
  893.6 11.7 %copy.279 = f32[4,4,96,2048]{3,2,1,0:T(8,128)} copy(f32[4,4,96,2048]{3,2,0,1:T(8,128)} %convert_bitcast_fusion) | data formatting | bytes 25165824 | tf_op jit(solution)/shard_map/convert_element_type | solution.py:689
  905.4 61.6 %collective-permute-done.5 = bf16[128,2048]{1,0:T(8,128)(2,1)} collective-permute-done((bf16[128,2048]{1,0:T(8,128)(2,1)}, bf16[128,2048]{1,0:T(8,128)(2,1)}, u32[]{:S(2)}, u32[]{:S(2)}) %collective-permute-start.5) | collective-permute-done | bytes 524320 | tf_op jit(solution)/shard_map/ppermute | solution.py:236
  967.1 3.5 fusion.35
  970.6 99.9 %all-reduce.9.cloned.1.call-done = (bf16[524,512]{1,0:T(8,128)(2,1)}, bf16[256,4096]{0,1:T(8,128)(2,1)}, bf16[512,2048]{1,0:T(8,128)(2,1)}) async-done(((bf16[524,512]{1,0:T(8,128)(2,1)}, bf16[256,4096]{0,1:T(8,128)(2,1)}, bf16[512,2048]{1,0:T(8,128)(2,1)}), (bf16[524,512]{1,0:T(8,128)(2,1)}, bf16[256,4096]{0,1:T(8,128)(2,1)}, bf16[512,2048]{1,0:T(8,128)(2,1)})) %all-reduce.9.cloned.1.call-update) | async-done | bytes 4730896 | tf_op jit(solution)/shard_map/psum | solution.py:840
  1074.7 4.4 copy.280
  (373 shorter events, 146.4 us)
Async XLA Ops:
  7.2 599.3 %all-gather.9.cloned.1.call-start = ((), (), s32[]{:S(2)}) async-start(), calls=%async_computation.2 | async-start | bytes 7864320 | tf_op jit(solution)/shard_map/all_gather | solution.py:583
  91.9 5.9 copy-start.5
  103.2 73.2 %copy-start.17 = (f32[8,128,4,128]{3,2,1,0:T(4,128)}, f32[8,128,4,128]{3,2,1,0:T(4,128)S(1)}, u32[]{:S(2)}) copy-start(f32[8,128,4,128]{3,2,1,0:T(4,128)S(1)} %reshape.611) | copy-start | bytes 6291460
  105.2 71.2 %copy-start.57 = (f32[8,128,4]{1,2,0:T(4,128)}, f32[8,128,4]{1,2,0:T(4,128)S(1)}, u32[]{:S(2)}) copy-start(f32[8,128,4]{1,2,0:T(4,128)S(1)} %copy.247) | copy-start | bytes 49156
  106.9 70.1 %copy-start.48 = (f32[128,64]{1,0:T(8,128)}, f32[128,64]{1,0:T(8,128)S(1)}, u32[]{:S(2)}) copy-start(f32[128,64]{1,0:T(8,128)S(1)} %get-tuple-element.210) | copy-start | bytes 98308
  106.9 70.1 %copy-start.50 = (f32[128,64]{1,0:T(8,128)}, f32[128,64]{1,0:T(8,128)S(1)}, u32[]{:S(2)}) copy-start(f32[128,64]{1,0:T(8,128)S(1)} %get-tuple-element.211) | copy-start | bytes 98308
  202.6 27.8 %copy-start.30 = (bf16[1,128,2048]{2,1,0:T(8,128)(2,1)S(1)}, bf16[1,128,2048]{2,1,0:T(8,128)(2,1)}, u32[]{:S(2)}) copy-start(bf16[1,128,2048]{2,1,0:T(8,128)(2,1)} %param.15) | copy-start | bytes 1572868
  230.7 7.4 copy-start.22
  230.7 372.6 %copy-start.76 = (f32[128]{0:T(128)}, f32[128]{0:T(128)S(1)}, u32[]{:S(2)}) copy-start(f32[128]{0:T(128)S(1)} %get-tuple-element.197) | copy-start | bytes 1540
  232.7 5.5 copy-start.41
  365.5 10.3 slice-start.2
  366.0 9.8 slice-start.3
  375.8 8.2 slice-start.4
  377.7 6.3 slice-start.5
  377.7 6.3 copy-start.12
  408.4 3.6 collective-permute-start
  414.2 13.0 %collective-permute-start.3 = (bf16[96,2048]{1,0:T(8,128)(2,1)S(1)}, bf16[96,2048]{1,0:T(8,128)(2,1)S(1)}, u32[]{:S(2)}, u32[]{:S(2)}) collective-permute-start(bf16[96,2048]{1,0:T(8,128)(2,1)S(1)} %get-tuple-element.186), channel_id=1, source_target_pairs={{0,6},{1,7},{2,4},{3,5},{4,2},{5,3},{6,0},{7,1},{8,14},{9,15},{10,... | collective-permute-start | bytes 1179656 | tf_op jit(solution)/shard_map/ppermute | solution.py:233
  414.8 19.3 %collective-permute-start.2 = (bf16[96,2048]{1,0:T(8,128)(2,1)S(1)}, bf16[96,2048]{1,0:T(8,128)(2,1)S(1)}, u32[]{:S(2)}, u32[]{:S(2)}) collective-permute-start(bf16[96,2048]{1,0:T(8,128)(2,1)S(1)} %get-tuple-element.187), channel_id=1, source_target_pairs={{0,4},{1,5},{2,6},{3,7},{4,0},{5,1},{6,2},{7,3},{8,12},{9,13},{10,... | collective-permute-start | bytes 1179656 | tf_op jit(solution)/shard_map/ppermute | solution.py:233
  416.2 17.8 %collective-permute-start.1 = (bf16[96,2048]{1,0:T(8,128)(2,1)S(1)}, bf16[96,2048]{1,0:T(8,128)(2,1)S(1)}, u32[]{:S(2)}, u32[]{:S(2)}) collective-permute-start(bf16[96,2048]{1,0:T(8,128)(2,1)S(1)} %get-tuple-element.188), channel_id=1, source_target_pairs={{0,2},{1,3},{2,0},{3,1},{4,6},{5,7},{6,4},{7,5},{8,10},{9,11},{10,... | collective-permute-start | bytes 1179656 | tf_op jit(solution)/shard_map/ppermute | solution.py:233
  435.4 11.7 %slice-start.6 = ((s8[5242880]{0:T(1024)(128)(4,1)}), s8[1048576]{0:T(1024)(128)(4,1)S(1)}, s32[]{:S(2)}) async-start(s8[5242880]{0:T(1024)(128)(4,1)} %bitcast.352), calls=%async_computation.10 | async-start | bytes 2097152
  435.4 300.3 %all-gather.5.cloned.1.call-start = ((), (), s32[]{:S(2)}) async-start(), calls=%async_computation | async-start | bytes 7864320 | tf_op jit(solution)/shard_map/all_gather | solution.py:669
  436.0 11.1 %slice-start.7 = ((s8[5242880]{0:T(1024)(128)(4,1)}), s8[4194304]{0:T(1024)(128)(4,1)S(1)}, s32[]{:S(2)}) async-start(s8[5242880]{0:T(1024)(128)(4,1)} %bitcast.352), calls=%async_computation.11 | async-start | bytes 8388608
  436.0 11.1 %copy-start.80 = (bf16[1280,768]{1,0:T(8,128)(2,1)S(1)}, bf16[1280,768]{1,0:T(8,128)(2,1)}, u32[]{:S(2)}) copy-start(bf16[1280,768]{1,0:T(8,128)(2,1)} %get-tuple-element.173) | copy-start | bytes 5898244
  447.1 4.8 copy-start.81
  451.9 4.6 copy-start.13
  599.0 251.8 %all-gather.7.cloned.1.call-start = ((), (), s32[]{:S(2)}) async-start(), calls=%async_computation.1 | async-start | bytes 7864320 | tf_op jit(solution)/shard_map/all_gather | solution.py:669
  599.8 470.8 %all-reduce.9.cloned.1.call-start = ((), (), s32[]{:S(2)}) async-start(), calls=%async_computation.3 | async-start | bytes 9469952 | tf_op jit(solution)/shard_map/psum | solution.py:840
  600.4 4.5 copy-start.24
  603.3 31.6 %copy-start.33 = (f32[128,2048]{1,0:T(8,128)}, f32[128,2048]{1,0:T(8,128)S(1)}, u32[]{:S(2)}) copy-start(f32[128,2048]{1,0:T(8,128)S(1)} %get-tuple-element.216) | copy-start | bytes 3145732
  603.3 31.6 %copy-start.72 = (f32[128]{0:T(128)}, f32[128]{0:T(128)S(1)}, u32[]{:S(2)}) copy-start(f32[128]{0:T(128)S(1)} %multiply_multiply_fusion.3) | copy-start | bytes 1540
  606.4 28.5 %copy-start.79 = (f32[512,2048]{1,0:T(8,128)S(1)}, f32[512,2048]{1,0:T(8,128)}, u32[]{:S(2)}) copy-start(f32[512,2048]{1,0:T(8,128)} %param.23) | copy-start | bytes 12582916
  634.9 7.0 copy-start.27
  661.9 4.5 copy-start.20
  738.5 8.0 copy-start.10
  756.6 26.7 %copy-start.31 = (bf16[1,128,2048]{2,1,0:T(8,128)(2,1)S(1)}, bf16[1,128,2048]{2,1,0:T(8,128)(2,1)}, u32[]{:S(2)}) copy-start(bf16[1,128,2048]{2,1,0:T(8,128)(2,1)} %param.15) | copy-start | bytes 1572868
  756.6 26.7 %copy-start.62 = (f32[1,2,8,128]{3,1,2,0:T(2,128)S(1)}, f32[1,2,8,128]{3,1,2,0:T(2,128)}, u32[]{:S(2)}) copy-start(f32[1,2,8,128]{3,1,2,0:T(2,128)} %copy-done.61) | copy-start | bytes 24580
  756.6 26.7 %copy-start.74 = (f32[128]{0:T(128)S(1)}, f32[128]{0:T(128)}, u32[]{:S(2)}) copy-start(f32[128]{0:T(128)} %fusion.86) | copy-start | bytes 1540
  836.4 5.1 copy-start.53
  865.0 40.4 %collective-permute-start.6 = (bf16[128,2048]{1,0:T(8,128)(2,1)}, bf16[128,2048]{1,0:T(8,128)(2,1)}, u32[]{:S(2)}, u32[]{:S(2)}) collective-permute-start(bf16[128,2048]{1,0:T(8,128)(2,1)} %get-tuple-element.183), channel_id=1, source_target_pairs={{0,24},{8,16},{16,8},{24,0},{1,25},{9,17},{17,9},{25,1},{2,26},{10... | collective-permute-start | bytes 1572872 | tf_op jit(solution)/shard_map/ppermute | solution.py:236
  865.8 101.3 %collective-permute-start.5 = (bf16[128,2048]{1,0:T(8,128)(2,1)}, bf16[128,2048]{1,0:T(8,128)(2,1)}, u32[]{:S(2)}, u32[]{:S(2)}) collective-permute-start(bf16[128,2048]{1,0:T(8,128)(2,1)} %get-tuple-element.184), channel_id=1, source_target_pairs={{0,16},{8,24},{16,0},{24,8},{1,17},{9,25},{17,1},{25,9},{2,18},{10... | collective-permute-start | bytes 1572872 | tf_op jit(solution)/shard_map/ppermute | solution.py:236
  865.9 101.1 %collective-permute-start.4 = (bf16[128,2048]{1,0:T(8,128)(2,1)}, bf16[128,2048]{1,0:T(8,128)(2,1)}, u32[]{:S(2)}, u32[]{:S(2)}) collective-permute-start(bf16[128,2048]{1,0:T(8,128)(2,1)} %get-tuple-element.182), channel_id=1, source_target_pairs={{0,8},{8,0},{16,24},{24,16},{1,9},{9,1},{17,25},{25,17},{2,10},{10... | collective-permute-start | bytes 1572872 | tf_op jit(solution)/shard_map/ppermute | solution.py:236
  893.6 11.7 %copy-start.77 = (f32[128]{0:T(128)S(1)}, f32[128]{0:T(128)}, u32[]{:S(2)}) copy-start(f32[128]{0:T(128)} %copy-done.76) | copy-start | bytes 1540
  893.6 73.4 %copy-start.25 = (f32[128,2048]{1,0:T(8,128)S(1)}, f32[128,2048]{1,0:T(8,128)}, u32[]{:S(2)}) copy-start(f32[128,2048]{1,0:T(8,128)} %copy-done.22) | copy-start | bytes 3145732
  893.6 73.4 %copy-start.32 = (bf16[1,128,2048]{2,1,0:T(8,128)(2,1)S(1)}, bf16[1,128,2048]{2,1,0:T(8,128)(2,1)}, u32[]{:S(2)}) copy-start(bf16[1,128,2048]{2,1,0:T(8,128)(2,1)} %param.15) | copy-start | bytes 1572868
  893.6 73.4 %copy-start.34 = (f32[128,2048]{1,0:T(8,128)S(1)}, f32[128,2048]{1,0:T(8,128)}, u32[]{:S(2)}) copy-start(f32[128,2048]{1,0:T(8,128)} %copy-done.33) | copy-start | bytes 3145732
  893.6 73.4 %copy-start.36 = (f32[128,2048]{1,0:T(8,128)S(1)}, f32[128,2048]{1,0:T(8,128)}, u32[]{:S(2)}) copy-start(f32[128,2048]{1,0:T(8,128)} %copy-done.35) | copy-start | bytes 3145732
  893.6 73.4 %copy-start.40 = (bf16[1,128,2048]{2,1,0:T(8,128)(2,1)S(1)}, bf16[1,128,2048]{2,1,0:T(8,128)(2,1)}, u32[]{:S(2)}) copy-start(bf16[1,128,2048]{2,1,0:T(8,128)(2,1)} %param.29) | copy-start | bytes 1572868
  893.6 73.4 %copy-start.73 = (f32[128]{0:T(128)S(1)}, f32[128]{0:T(128)}, u32[]{:S(2)}) copy-start(f32[128]{0:T(128)} %copy-done.72) | copy-start | bytes 1540
  (53 other events, 116.1 us)
Sparse Core Ops, SparseCore 0:
  435.5 128.1 all-gather.8
  599.2 136.4 all-gather.4
  737.3 113.4 all-gather.6
  854.4 216.1 all-reduce.8

commit v4 on v3

--- a/solution.py
+++ b/solution.py
@@ -63,6 +63,10 @@
             index = index + bit * (1 - 2 * lax.rem(lax.div(index, bit), 2))
         bit *= 2
     return index
+
+
+def cols(block, size):
+    return pl.ds(pl.multiple_of(block * size, size), size)
 
 
 class _ShapeOnly:
@@ -186,6 +190,136 @@
         name=name,
     )(*arrays)
     return result
+
+
+def line_sum(cid, arrays, pieces, blocks):
+    n = len(arrays)
+    chunks = [
+        (k, c * (a.shape[0] // p), a.shape[0] // p)
+        for k, (a, p) in enumerate(zip(arrays, pieces))
+        for c in range(p)
+    ]
+    far = blocks.shape[0] - 1
+
+    def kernel(*refs):
+        ins, blocks_ref = refs[:n], refs[n]
+        outs, others_ref = refs[n + 1 : 2 * n + 1], refs[2 * n + 1]
+        own, got, swapped = (refs[2 * n + 2 + n * i : 2 * n + 2 + n * (i + 1)] for i in range(3))
+        load, store, in_s, in_r, swap_s, swap_r, back_s, back_r, far_s, far_r = refs[5 * n + 2 :]
+        z = lax.axis_index("sp")
+        f = lax.axis_index("fsdp")
+        inner = jnp.logical_or(z == 1, z == 2)
+        barrier = pltpu.get_barrier_semaphore()
+        for d in range(1, far + 1):
+            pl.semaphore_signal(barrier, inc=1, device_id=(flip(z, d), f), device_id_type=MESH)
+        pl.semaphore_wait(barrier, far)
+
+        def view(refs, c):
+            k, start, size = chunks[c]
+            return refs[k].at[pl.ds(start, size)]
+
+        def remote(src, dst, send, recv, c, dz):
+            return pltpu.make_async_remote_copy(
+                src_ref=view(src, c),
+                dst_ref=view(dst, c),
+                send_sem=send.at[c],
+                recv_sem=recv.at[c],
+                device_id=(flip(z, dz), f),
+                device_id_type=MESH,
+            )
+
+        loads = [
+            pltpu.make_async_copy(view(ins, c), view(own, c), load.at[c])
+            for c in range(len(chunks))
+        ]
+        stores = [
+            pltpu.make_async_copy(view(got, c), view(outs, c), store.at[c])
+            for c in range(len(chunks))
+        ]
+        far_copies = [
+            pltpu.make_async_remote_copy(
+                src_ref=blocks_ref.at[d],
+                dst_ref=others_ref.at[d - 1],
+                send_sem=far_s.at[d - 1],
+                recv_sem=far_r.at[d - 1],
+                device_id=(flip(z, d), f),
+                device_id_type=MESH,
+            )
+            for d in range(1, far + 1)
+        ]
+        inwards = [remote(own, got, in_s, in_r, c, 1) for c in range(len(chunks))]
+        swaps = [remote(own, swapped, swap_s, swap_r, c, 3) for c in range(len(chunks))]
+        backs = [remote(got, got, back_s, back_r, c, 1) for c in range(len(chunks))]
+        for copy in loads:
+            copy.start()
+
+        def add(left, right, to, c):
+            k, start, size = chunks[c]
+            step = 16
+
+            def rows(i, carry):
+                at = pl.ds(pl.multiple_of(start + i * step, step), step)
+                total = left[k][at, :].astype(FLOAT) + right[k][at, :].astype(FLOAT)
+                to[k][at, :] = total.astype(BF16)
+                return carry
+
+            lax.fori_loop(0, size // step, rows, 0)
+
+        @pl.when(jnp.logical_not(inner))
+        def _():
+            for c in range(len(chunks)):
+                loads[c].wait()
+                inwards[c].start()
+            for copy in far_copies:
+                copy.start()
+            for c in range(len(chunks)):
+                backs[c].wait_recv()
+                stores[c].start()
+            for c in range(len(chunks)):
+                inwards[c].wait_send()
+                stores[c].wait()
+
+        @pl.when(inner)
+        def _():
+            for copy in far_copies:
+                copy.start()
+            for c in range(len(chunks) + 1):
+                if c < len(chunks):
+                    loads[c].wait()
+                    inwards[c].wait_recv()
+                    add(own, got, own, c)
+                    swaps[c].start()
+                if c:
+                    swaps[c - 1].wait_recv()
+                    add(own, swapped, got, c - 1)
+                    backs[c - 1].start()
+                    stores[c - 1].start()
+            for c in range(len(chunks)):
+                swaps[c].wait_send()
+                backs[c].wait_send()
+                stores[c].wait()
+
+        for copy in far_copies:
+            copy.wait()
+
+    hbm = pl.BlockSpec(memory_space=pl.ANY)
+    buffers = [pltpu.VMEM(a.shape, BF16) for a in arrays]
+    count = len(chunks)
+    return pl.pallas_call(
+        kernel,
+        out_shape=[jax.ShapeDtypeStruct(a.shape, BF16) for a in arrays]
+        + [jax.ShapeDtypeStruct((far,) + blocks.shape[1:], BF16)],
+        in_specs=[hbm] * (n + 1),
+        out_specs=[hbm] * (n + 1),
+        scratch_shapes=buffers * 3
+        + [pltpu.SemaphoreType.DMA((count,))] * 8
+        + [pltpu.SemaphoreType.DMA((far,))] * 2,
+        compiler_params=pltpu.CompilerParams(
+            collective_id=cid, has_side_effects=True, vmem_limit_bytes=40 * 1024 * 1024
+        ),
+        cost_estimate=pl.CostEstimate(flops=0, bytes_accessed=int(4.0e8), transcendentals=0),
+        name="line_sum",
+    )(*arrays, blocks)
 
 
 def body(
@@ -248,10 +382,9 @@
     small = jnp.pad(small, (0, small_rows * width - small.shape[0])).reshape(small_rows, width)
     x_pay = jnp.concatenate([tokens[0], small], axis=0)
     pay_rows = rows + small_rows
-    by_head = query_weight.astype(BF16).reshape(shard, nf, q_cols)
-    key_b = jnp.repeat(key_weight.astype(BF16).reshape(shard, kv_heads, head_dim), rep, axis=1)
-    value_b = jnp.repeat(value_weight.astype(BF16).reshape(shard, kv_heads, head_dim), rep, axis=1)
-    qkv_pay = jnp.concatenate([by_head, key_b, value_b], axis=2).transpose(1, 0, 2)
+    query_b = query_weight.astype(BF16)
+    key_b = key_weight.astype(BF16)
+    value_b = value_weight.astype(BF16)
     routes = expert_ids[0]
     expert_iota = jnp.arange(n_experts, dtype=jnp.int32)
     routed = jnp.any(routes[:, :, None] == expert_iota[None, None, :], axis=1)
@@ -268,7 +401,8 @@
     def plane_cast(weight):
         return lax.dynamic_slice_in_dim(weight, z * plane_experts, plane_experts, 0).astype(BF16)
 
-    gate_pay, up_pay, down_pay = plane_cast(w_gate), plane_cast(w_up), plane_cast(w_down)
+    gate_up_pay = jnp.stack([plane_cast(w_gate), plane_cast(w_up)], axis=1)
+    down_pay = plane_cast(w_down)
 
     sends = []
     for m in range(0, nf, 2):
@@ -283,15 +417,44 @@
     for m in range(nf):
         sends.append(
             Send(
-                lambda i, o, z, f, m=m: i[1].at[flip(f, m)],
-                lambda i, o, z, f, m=m: o[1].at[f],
+                lambda i, o, z, f, m=m: i[1].at[:, cols(flip(f, m), q_cols)],
+                lambda i, o, z, f: o[1].at[cols(f, shard), pl.ds(0, q_cols)],
                 0,
                 m,
             )
         )
+    for m in range(0, nf, rep):
+        for w in range(2):
+            sends.append(
+                Send(
+                    lambda i, o, z, f, m=m, w=w: i[2 + w].at[
+                        :, cols(lax.div(flip(f, m), rep), head_dim)
+                    ],
+                    lambda i, o, z, f, w=w: o[1].at[
+                        cols(f, shard), pl.ds(q_cols + w * head_dim, head_dim)
+                    ],
+                    0,
+                    m,
+                )
+            )
+            for p in range(1, rep):
+                view = lambda i, o, z, f, m=m, w=w: o[1].at[
+                    cols(flip(f, m), shard), pl.ds(q_cols + w * head_dim, head_dim)
+                ]
+                if m == 0:
+                    sends.append(
+                        Send(
+                            lambda i, o, z, f, w=w: i[2 + w].at[:, cols(lax.div(f, rep), head_dim)],
+                            view,
+                            0,
+                            p,
+                        )
+                    )
+                else:
+                    sends.append(Send(view, view, 0, p, len(sends) - p))
     for m in range(nsp):
         sends.append(
-            Send(lambda i, o, z, f: i[2], lambda i, o, z, f, m=m: o[2].at[m], m, 0)
+            Send(lambda i, o, z, f: i[4], lambda i, o, z, f, m=m: o[2].at[m], m, 0)
         )
     for m in range(0, nf, 2):
         if m == 0:
@@ -311,11 +474,18 @@
     x_all, w_qkv, dy_z = exchange(
         "gather_inputs",
         0,
-        (x_pay, qkv_pay, dy_pay),
-        ((nf, pay_rows, width), (nf, shard, qkv_cols), (nsp, rows, wide)),
+        (x_pay, query_b, key_b, value_b, dy_pay),
+        ((nf, pay_rows, width), (width, qkv_cols), (nsp, rows, wide)),
         sends,
         65,
     )
+
+    x_all, gate_up_pay, down_pay = lax.optimization_barrier((x_all, gate_up_pay, down_pay))
+    weight_pieces = []
+    for pay in (gate_up_pay, down_pay):
+        for s in range(plane_experts):
+            block = lax.dynamic_index_in_dim(pay, flip(place, s), 0, keepdims=False)
+            weight_pieces.append(swap_f(block, s * parts) if s else block)
 
     small_all = x_all[:, rows:, :].reshape(nf, small_rows * width)
     at = 0
@@ -332,7 +502,6 @@
     xn_b = (
         rms_norm(x_all[:, :rows, :].astype(FLOAT), g_attn).astype(BF16).reshape(seqs * rows, width)
     )
-    w_qkv = w_qkv.reshape(width, qkv_cols)
     qkv_lin = matmul(xn_b, w_qkv)
     q_lin = qkv_lin[:, :q_cols].reshape(seqs, rows, my_heads, head_dim)
     k_lin = qkv_lin[:, q_cols : q_cols + head_dim].reshape(seqs, rows, 1, head_dim)
@@ -373,50 +542,9 @@
                     d,
                 )
             )
-    for which in range(3):
-        for s in range(plane_experts):
-            stage = len(sends)
-            sends.append(
-                Send(
-                    lambda i, o, z, f, s=s, w=which: i[1 + w].at[flip(lax.div(f, parts), s)],
-                    lambda i, o, z, f, w=which: o[1 + w].at[f],
-                    0,
-                    s * parts,
-                )
-            )
-            for p in range(1, parts):
-                if s == 0:
-                    forward = Send(
-                        lambda i, o, z, f, w=which: i[1 + w].at[lax.div(f, parts)],
-                        lambda i, o, z, f, w=which: o[1 + w].at[f],
-                        0,
-                        p,
-                    )
-                else:
-                    forward = Send(
-                        lambda i, o, z, f, s=s, w=which: o[1 + w].at[flip(f, s * parts)],
-                        lambda i, o, z, f, s=s, w=which: o[1 + w].at[flip(f, s * parts)],
-                        0,
-                        p,
-                        stage,
-                    )
-                sends.append(forward)
-    kv_z, gate_all, up_all, down_all = exchange(
-        "keys_and_experts",
-        1,
-        (kv_pay, gate_pay, up_pay, down_pay),
-        (
-            (nsp, seqs * rows, 2 * head_dim),
-            (nf, shard, hidden_size),
-            (nf, shard, hidden_size),
-            (nf, hid_shard, width),
-        ),
-        sends,
-        55,
-    )
-    wg_b = gate_all.reshape(width, hidden_size)
-    wu_b = up_all.reshape(width, hidden_size)
-    wd_b = down_all.reshape(hidden_size, width)
+    (kv_z,) = exchange(
+        "gather_keys", 1, (kv_pay,), ((nsp, seqs * rows, 2 * head_dim),), sends, 24
+    )
     kv_seq = kv_z.reshape(nsp, seqs, rows, 2 * head_dim).transpose(1, 0, 2, 3)
     kv_seq = kv_seq.reshape(seqs, nsp * rows, 2 * head_dim)
     keys = kv_seq[:, :, :head_dim]
@@ -438,7 +566,7 @@
     o_mat = o_rows.astype(BF16).reshape(seqs * rows, q_cols)
     wo_b = output_weight.astype(BF16)
 
-    def pair_then_plane(partial, name, cid):
+    def pair_then_plane(partial, name, cid, more=(), more_shapes=(), more_sends=()):
         split = partial.astype(BF16).reshape(nf // 2, 2, rows, width)
         (other,) = exchange(
             name + "_pair",
@@ -459,13 +587,44 @@
             )
             for j in range(nf // 2)
         ]
-        (blocks,) = exchange(
-            name + "_plane", cid + 1, (summed,), ((nf // 2, rows, width),), sends, 27
-        )
-        return jnp.sum(blocks.astype(FLOAT), axis=0)
-
+        blocks, *rest = exchange(
+            name + "_plane",
+            cid + 1,
+            (summed, *more),
+            ((nf // 2, rows, width), *more_shapes),
+            sends + list(more_sends),
+            27,
+        )
+        return jnp.sum(blocks.astype(FLOAT), axis=0), rest
+
+    sends = []
+    for w in range(2):
+        for s in range(plane_experts):
+            for p in range(parts):
+                at = (lambda s=s: lambda f: (slice(None), flip(f, s * parts)))()
+                if w:
+                    at = (lambda s=s: lambda f: (flip(f, s * parts),))()
+                sends.append(
+                    Send(
+                        lambda i, o, z, f, k=1 + w * plane_experts + s: i[k],
+                        lambda i, o, z, f, w=w, at=at: o[1 + w].at[at(f)],
+                        0,
+                        p,
+                    )
+                )
+    branch, (gate_up_all, down_all) = pair_then_plane(
+        matmul(o_mat, wo_b),
+        "out_sum",
+        3,
+        weight_pieces,
+        ((2, nf, shard, hidden_size), (nf, hid_shard, width)),
+        sends,
+    )
+    wg_b = gate_up_all[0].reshape(width, hidden_size)
+    wu_b = gate_up_all[1].reshape(width, hidden_size)
+    wd_b = down_all.reshape(hidden_size, width)
     x_rows = tokens[0].astype(FLOAT)
-    mid_rows = x_rows + pair_then_plane(matmul(o_mat, wo_b), "out_sum", 3)
+    mid_rows = x_rows + branch
     hn_b = rms_norm(mid_rows, g_ffn).astype(BF16)
     logits = matmul(hn_b, wr_b)
     logits = jnp.where(routed, logits, -1e30)
@@ -580,7 +739,8 @@
             for s in range(plane_experts)
         ]
     )
-    all_down = lax.all_gather(d_down, "sp")
+    in_order = jnp.bitwise_xor(jnp.arange(plane_experts, dtype=jnp.int32), place)
+    all_down = lax.all_gather(jnp.take(d_down, in_order, axis=0, mode="clip"), "sp")
     result = matmul(hidden, wd_b)
     row_dgate = jnp.sum(result * dy_f, axis=1, keepdims=True)
     weighted = (row_gate * result).astype(BF16)
@@ -652,21 +812,20 @@
             sends.append(
                 Send(
                     lambda i, o, z, f, s=s, w=w: i[w].at[flip(lax.div(f, parts), s)],
-                    lambda i, o, z, f, s=s, w=w: o[w].at[lax.div(f, parts)],
+                    lambda i, o, z, f, s=s, w=w: o[2].at[w - 2, lax.div(f, parts)],
                     0,
                     s * parts,
                 )
             )
-    d_home, dgate_home, *shards = exchange(
+    d_home, dgate_home, shards = exchange(
         "hidden_grads_home",
         8,
         (combine(d_back), combine(dgate_back), *summed),
-        [(nsp, rows, width), (nsp, rows, LANES)]
-        + [(plane_experts,) + tuple(shape) for shape in shard_shapes],
+        ((nsp, rows, width), (nsp, rows, LANES), (2, plane_experts, shard, hidden_size)),
         sends,
         58,
     )
-    all_gate, all_up = [lax.all_gather(block, "sp", axis=0, tiled=True) for block in shards]
+    all_gate_up = lax.all_gather(shards, "sp")
     d_home = jnp.sum(d_home.astype(FLOAT), axis=0)
     tail = jnp.sum(dgate_home.astype(FLOAT), axis=0)
     d_gates = tail[:, :n_experts] + tail[:, n_experts : 2 * n_experts]
@@ -680,13 +839,7 @@
 
     d_attn_b = d_mid.astype(BF16)
     d_attn_b, all_down = lax.optimization_barrier((d_attn_b, all_down))
-    grad_down = jnp.take(
-        all_down,
-        jnp.bitwise_xor(jnp.arange(plane_experts, dtype=jnp.int32), place),
-        axis=1,
-        mode="clip",
-    )
-    grad_down = grad_down.astype(FLOAT).reshape(n_experts, hid_shard, width)
+    grad_down = all_down.astype(FLOAT).reshape(n_experts, hid_shard, width)
     sends = [
         Send(lambda i, o, z, f: i[0], lambda i, o, z, f: o[0].at[f], 0, m)
         for m in range(0, nf, 2)
@@ -765,12 +918,7 @@
         60,
     )
     out_blocks = combine(out_back)
-    moe_sum = out_blocks[0].astype(FLOAT)
-    for d in range(1, nsp):
-        moe_sum = moe_sum + swap_z(out_blocks[d], d).astype(FLOAT)
-    mixed = (mid_rows + moe_sum).astype(BF16)[None]
     d_kv = (d_kv[0].astype(FLOAT) + jnp.sum(others.astype(FLOAT), axis=0)).astype(BF16)
-    d_kv, all_gate = lax.optimization_barrier((d_kv, all_gate))
     (d_kv,) = exchange(
         "key_grads_share",
         15,
@@ -793,8 +941,8 @@
     d_qkv = jnp.concatenate([dq_b, dk_b, dv_b], axis=1)
     share = 1.0 / rep
     d_qkv_shared = jnp.concatenate([dq_b, dk_b * BF16(share), dv_b * BF16(share)], axis=1)
-    d_w_qkv = contract_rows(xn_b, d_qkv).astype(BF16).reshape(nf, shard, qkv_cols)
-    d_xn = pair_then_plane(contract_cols(d_qkv_shared, w_qkv), "input_sum", 13)
+    d_w_qkv = contract_rows(xn_b, d_qkv).astype(BF16)
+    d_xn, unused = pair_then_plane(contract_cols(d_qkv_shared, w_qkv), "input_sum", 13)
     unused, attn_pull = jax.vjp(rms_norm, x_rows, g_attn)
     d_x_norm, d_attn_gain = attn_pull(d_xn)
     grad_tokens = (d_mid + d_x_norm)[None]
@@ -813,34 +961,65 @@
     small_cols = pl.cdiv(small_size, kv_heads * head_dim) * kv_heads * head_dim // small_rows
     small_cols = pl.cdiv(small_cols, LANES) * LANES
     smalls = jnp.pad(smalls, ((0, 0), (0, small_rows * small_cols - small_size)))
-    d_w_shard, small_shard = exchange(
+    kv_cols = kv_heads * head_dim
+    sends = []
+    for m in range(nf):
+        sends.append(
+            Send(
+                lambda i, o, z, f, m=m: i[0].at[cols(flip(f, m), shard), pl.ds(0, q_cols)],
+                lambda i, o, z, f: o[0].at[:, cols(f, q_cols)],
+                0,
+                m,
+            )
+        )
+        sends.append(
+            Send(lambda i, o, z, f, m=m: i[1].at[flip(f, m)], lambda i, o, z, f: o[2].at[f], 0, m)
+        )
+    for m in range(0, nf, rep):
+        for w in range(2):
+            sends.append(
+                Send(
+                    lambda i, o, z, f, m=m, w=w: i[0].at[
+                        cols(flip(f, m), shard), pl.ds(q_cols + w * head_dim, head_dim)
+                    ],
+                    lambda i, o, z, f, w=w: o[1].at[
+                        pl.ds(w * shard, shard), cols(lax.div(f, rep), head_dim)
+                    ],
+                    0,
+                    m,
+                )
+            )
+    d_wq, d_wkv, small_shard = exchange(
         "head_grads_to_shards",
         12,
         (d_w_qkv, smalls.reshape(nf, small_rows, small_cols)),
-        ((nf, shard, qkv_cols), (nf, small_rows, small_cols)),
-        [
-            Send(
-                lambda i, o, z, f, m=m, w=w: i[w].at[flip(f, m)],
-                lambda i, o, z, f, m=m, w=w: o[w].at[f],
-                0,
-                m,
-            )
-            for w in range(2)
-            for m in range(nf)
-        ],
+        (
+            (shard, n_heads * head_dim),
+            (2 * shard, kv_cols),
+            (nf, small_rows, small_cols),
+        ),
+        sends,
         36,
     )
-    d_wq = d_w_shard[:, :, :q_cols].transpose(1, 0, 2).reshape(shard, n_heads * head_dim)
-    d_wkv = d_w_shard[::rep, :, q_cols:].reshape(kv_heads, shard, 2, head_dim)
-    d_wkv = d_wkv.transpose(2, 1, 0, 3).reshape(2 * shard, kv_heads * head_dim)
     small_sum = jnp.sum(small_shard.astype(FLOAT), axis=0).astype(BF16)
-    sum_out = lax.psum(d_wo.astype(BF16), "sp").astype(FLOAT)
-    kv_cols = kv_heads * head_dim
-    d_wkv = jnp.concatenate([d_wkv, small_sum.reshape(-1, kv_cols)], axis=0)
-    sum_q, sum_kv = lax.psum((d_wq, d_wkv), "sp")
+    if nsp == 4:
+        sum_q, sum_out, sum_kv, small_sum, out_others = line_sum(
+            16, (d_wq, d_wo.astype(BF16), d_wkv, small_sum), (4, 4, 1, 1), out_blocks
+        )
+        out_others = [out_others[d] for d in range(nsp - 1)]
+    else:
+        sum_q, sum_out, sum_kv, small_sum = lax.psum(
+            (d_wq, d_wo.astype(BF16), d_wkv, small_sum), "sp"
+        )
+        out_others = [swap_z(out_blocks[d], d) for d in range(1, nsp)]
+    moe_sum = out_blocks[0].astype(FLOAT)
+    for block in out_others:
+        moe_sum = moe_sum + block.astype(FLOAT)
+    mixed = (mid_rows + moe_sum).astype(BF16)[None]
+    sum_out = sum_out.astype(FLOAT)
     sum_q = sum_q.astype(FLOAT)
     sum_kv = sum_kv.astype(FLOAT)
-    small_sum = sum_kv[2 * shard :].reshape(-1)
+    small_sum = small_sum.astype(FLOAT).reshape(-1)
     at = 0
     pieces = []
     for size in (shard, shard, head_dim // nf, head_dim // nf, shard * n_experts):
@@ -858,8 +1037,8 @@
         sum_out,
         pieces[1],
         pieces[4].reshape(shard, n_experts),
-        all_gate.astype(FLOAT),
-        all_up.astype(FLOAT),
+        all_gate_up[:, 0].astype(FLOAT).reshape(n_experts, shard, hidden_size),
+        all_gate_up[:, 1].astype(FLOAT).reshape(n_experts, shard, hidden_size),
         grad_down,
     )
 

time: 1100 us -> 1040 us (0.945)
  waiting for transfers between devices: 187 us -> 29.4 us
  Pallas kernels: 570 us -> 696 us
  local copies, waits for them, and re-layouts: 100 us -> 81.2 us
  matrix products: 123 us -> 108 us
    pallas_call x0 -> x1, Pallas kernels: none -> 169 us  [line_sum(): pl.pallas_call(kernel, out_shape=[jax.ShapeDtypeStruct(a.shape, BF16) for...]
    psum x1 -> x0, waiting for transfers between devices: 99.9 us -> none  [body(): sum_q, sum_kv = lax.psum((d_wq, d_wkv), 'sp')]
    ppermute x3 -> x0, waiting for transfers between devices: 61.6 us -> none  [swap_z(): return lax.ppermute(block, 'sp', [(i, i ^ mask) for i in range(nsp)])]
    pallas_call x15, Pallas kernels: 570 us -> 527 us  [exchange(): pl.pallas_call(kernel, out_shape=[jax.ShapeDtypeStruct(shape, BF16) for s...]
    convert_element_type x1 -> x0, local copies, waits for them, and re-layouts: 11.7 us -> none  [body(): grad_down = grad_down.astype(FLOAT).reshape(n_experts, hid_shard, width)]
    ppermute x4 -> x10, waiting for transfers between devices: 20 us -> 29.4 us  [swap_f(): return lax.ppermute(block, 'fsdp', [(i, i ^ mask) for i in range(nf)])]
    convert_element_type x4 -> x8, other arithmetic: 29.5 us -> 26.1 us  [the longest x1 6.55 us: body(): all_gate_up[:, 0].astype(FLOAT).reshape(n_experts, shard, hidden_size)]
    unnamed x191 -> x216, local copies, waits for them, and re-layouts: 39.1 us -> 40 us
  transfers between devices with their start and end apart: 11 -> 12, of which waited for: 7 -> 4; matrix products, arithmetic and copies ran while one was open for 15% -> 15% of each run, Pallas kernels for 27% -> 47%
where the time goes in v4:
time: 1040 us; the launch traced here: 1030 us
  Pallas kernels  696 us (67%)
  matrix products  108 us (10%)
  other arithmetic  88.1 us (8%)
  local copies, waits for them, and re-layouts  81.2 us (8%)
  waiting for transfers between devices  29.4 us (3%)
  between operations  16.4 us (2%)
    pallas_call x15, Pallas kernels, exchange(): pl.pallas_call(kernel, out_shape=[jax.ShapeDtypeStruct(shape, BF16) for s...  527 us
    pallas_call x1, Pallas kernels, line_sum(): pl.pallas_call(kernel, out_shape=[jax.ShapeDtypeStruct(a.shape, BF16) for...  169 us
    unnamed x216, local copies, waits for them, and re-layouts  40 us
    dot_general x5, matrix products, contract_cols(): lax.dot_general(left_mat, right_mat, (((1,), (1,)), ((), ())), preferred_...  34.7 us
    ppermute x10, waiting for transfers between devices, swap_f(): return lax.ppermute(block, 'fsdp', [(i, i ^ mask) for i in range(nf)])  29.4 us
    dot_general x6, matrix products, matmul(): return jnp.dot(left_mat, right_mat, preferred_element_type=FLOAT)  25.6 us
    dot_general x5, matrix products, contract_rows(): lax.dot_general(left_mat, right_mat, (((0,), (0,)), ((), ())), preferred_...  24.9 us
  transfers between devices with their start and end apart: 12, of which 4 were waited for; matrix products, arithmetic and copies ran while one was open for 15% of the time, Pallas kernels for 47%

profile of v4, /device:TPU:0, one launch (start us, length us, event | category | flops | bytes accessed | tf_op | source)
XLA Modules:
  0.0 1029.4 jit_solution(12202986727385775170)
XLA Ops:
  11.7 2.6 convert_element_type.431.refs_1_
  16.1 3.3 dynamic-slice_convert_fusion
  19.4 3.2 fusion.27
  27.3 65.5 %gather_inputs.1 = (bf16[8,144,2048]{2,1,0:T(8,128)(2,1)S(1)}, bf16[2048,768]{1,0:T(8,128)(2,1)S(1)}, bf16[4,128,2176]{2,1,0:T(8,128)(2,1)S(1)}) custom-call(bf16[144,2048]{1,0:T(8,128)(2,1)S(1)} %pad_maximum_fusion.5.refs_0_, bf16[256,4096]{1,0:T(8,128)(2,1)S(1)} %convert_element_type.431.refs_1_, bf16[256,512]{1,0:T(8,128)(2,1)S(1)} %convert_element_type.432.refs_2_, ...), custom_call_target="tpu_custom_call" | custom-call | bytes 195000000 | tf_op jit(solution)/shard_map/gather_inputs/pallas_call | solution.py:174
  98.0 3.5 dynamic-slice_bitcast_fusion.1
  110.3 3.4 fusion.101
  119.7 23.8 %gather_keys.1 = bf16[4,1024,256]{2,1,0:T(8,128)(2,1)S(1)} custom-call(bf16[1024,256]{1,0:T(8,128)(2,1)S(1)} %pad_maximum_fusion.6.refs_0_), custom_call_target="tpu_custom_call" | custom-call | bytes 72000000 | tf_op jit(solution)/shard_map/gather_keys/pallas_call | solution.py:174
  155.2 4.0 fusion.99
  168.7 4.2 out_sum_pair.1
  183.7 9.0 collective-permute-done.5.refs_8_
  192.6 26.1 %out_sum_plane.1 = (bf16[4,128,2048]{2,1,0:T(8,128)(2,1)S(1)}, bf16[2,8,256,768]{3,2,1,0:T(8,128)(2,1)S(1)}, bf16[8,96,2048]{2,1,0:T(8,128)(2,1)S(1)}) custom-call(bf16[4,128,2048]{2,1,0:T(8,128)(2,1)S(1)} %fusion.11.refs_0_, bf16[2,256,768]{2,1,0:T(8,128)(2,1)S(1)} %get-tuple-element.177.refs_1_, bf16[2,256,768]{2,1,0:T(8,128)(2,1)} %collective-permute-done.refs_2_, ...), custom_call_target="tpu_custom_call" | custom-call | bytes 81000000 | tf_op jit(solution)/shard_map/out_sum_plane/pallas_call | solution.py:174
  222.1 61.7 %hidden_planes.1 = (bf16[4,128,2048]{2,1,0:T(8,128)(2,1)S(1)}, bf16[4,128,128]{2,1,0:T(8,128)(2,1)S(1)}, bf16[4,4,80,2048]{3,2,1,0:T(8,128)(2,1)S(1)}) custom-call(bf16[128,2048]{1,0:T(8,128)(2,1)S(1)} %multiply_convert_fusion.6.refs_0_, bf16[128,128]{1,0:T(8,128)(2,1)S(1)} %maximum_maximum_fusion.1.refs_1_, bf16[4,4,80,2048]{3,2,1,0:T(8,128)(2,1)S(1)} %bitcast.318), custom_call_target="tpu_custom_call" | custom-call | bytes 174000000 | tf_op jit(solution)/shard_map/hidden_planes/pallas_call | solution.py:174
  288.5 61.2 %rows_to_experts.1 = (bf16[4,4,80,2048]{3,2,1,0:T(8,128)(2,1)S(1)}, bf16[4,4,80,128]{3,2,1,0:T(8,128)(2,1)S(1)}) custom-call(bf16[4,4,80,2048]{3,2,1,0:T(8,128)(2,1)S(1)} %bitcast.319, bf16[4,4,80,128]{3,2,1,0:T(8,128)(2,1)S(1)} %bitcast.342), custom_call_target="tpu_custom_call" | custom-call | bytes 180000000 | tf_op jit(solution)/shard_map/rows_to_experts/pallas_call | solution.py:174
  349.7 6.2 fusion.102
  355.9 6.2 fusion.103
  362.6 3.5 fusion.1
  366.2 9.3 multiply_convert_fusion.1
  375.5 7.0 multiply_convert_fusion
  382.5 4.5 convolution_convert_fusion.5
  387.2 3.4 collective-permute-done.6
  394.9 9.4 collective-permute-done.9
  404.3 7.6 collective-permute-done.8
  415.4 8.9 fusion.104
  424.3 7.5 convolution_convert_fusion.6
  431.9 4.7 convolution_convert_fusion.7
  436.6 8.0 add_convert_fusion
  444.7 63.7 %rows_from_experts.1 = (bf16[4,4,80,2048]{3,2,1,0:T(8,128)(2,1)S(1)}, bf16[4,4,80,128]{3,2,1,0:T(8,128)(2,1)S(1)}, bf16[1,4,256,768]{3,2,1,0:T(8,128)(2,1)S(1)}, bf16[1,4,256,768]{3,2,1,0:T(8,128)(2,1)S(1)}) custom-call(bf16[4,4,80,2048]{3,2,1,0:T(8,128)(2,1)S(1)} %bitcast.336, bf16[4,4,80,128]{3,2,1,0:T(8,128)(2,1)S(1)} %maximum_maximum_fusion.refs_1_, ...), custom_call_target="tpu_custom_call" | custom-call | bytes 210000000 | tf_op jit(solution)/shard_map/rows_from_experts/pallas_call | solution.py:174
  510.9 64.3 %hidden_grads_home.1 = (bf16[4,128,2048]{2,1,0:T(8,128)(2,1)S(1)}, bf16[4,128,128]{2,1,0:T(8,128)(2,1)S(1)}, bf16[2,4,256,768]{3,2,1,0:T(8,128)(2,1)S(1)}) custom-call(bf16[4,128,2048]{2,1,0:T(8,128)(2,1)S(1)} %convolution_convert_fusion.10.refs_0_, bf16[4,128,128]{2,1,0:T(8,128)(2,1)S(1)} %convolution_convert_fusion.15.refs_1_, ...), custom_call_target="tpu_custom_call" | custom-call | bytes 174000000 | tf_op jit(solution)/shard_map/hidden_grads_home/pallas_call | solution.py:174
  582.9 27.7 %gather_grads.1 = bf16[8,128,2048]{2,1,0:T(8,128)(2,1)S(1)} custom-call(bf16[128,2048]{1,0:T(8,128)(2,1)S(1)} %fusion.90.refs_0_), custom_call_target="tpu_custom_call" | custom-call | bytes 90000000 | tf_op jit(solution)/shard_map/gather_grads/pallas_call | solution.py:174
  612.7 3.3 convolution_convert_fusion.13
  617.5 3.6 fusion.7
  621.1 4.5 fusion.8
  629.8 2.7 key_grads_group.1
  637.3 2.6 fusion.19
  647.6 60.7 %key_grads_planes.1 = (bf16[3,512,256]{2,1,0:T(8,128)(2,1)S(1)}, bf16[4,4,80,2048]{3,2,1,0:T(8,128)(2,1)S(1)}) custom-call(bf16[4,512,256]{2,1,0:T(8,128)(2,1)S(1)} %fusion.20.refs_0_, bf16[4,4,80,2048]{3,2,1,0:T(8,128)(2,1)S(1)} %bitcast.335), custom_call_target="tpu_custom_call" | custom-call | bytes 180000000 | tf_op jit(solution)/shard_map/key_grads_planes/pallas_call | solution.py:174
  721.6 5.1 convolution_convert_fusion.3
  726.8 4.2 input_sum_pair.1
  731.8 26.2 %input_sum_plane.1 = bf16[4,128,2048]{2,1,0:T(8,128)(2,1)S(1)} custom-call(bf16[4,128,2048]{2,1,0:T(8,128)(2,1)S(1)} %fusion.10.refs_0_), custom_call_target="tpu_custom_call" | custom-call | bytes 81000000 | tf_op jit(solution)/shard_map/input_sum_plane/pallas_call | solution.py:174
  759.8 5.8 convolution_convert_fusion.4.refs_0_
  765.7 33.7 %head_grads_to_shards.1 = (bf16[256,4096]{1,0:T(8,128)(2,1)S(1)}, bf16[512,512]{1,0:T(8,128)(2,1)S(1)}, bf16[8,16,384]{2,1,0:T(8,128)(2,1)S(1)}) custom-call(bf16[2048,768]{1,0:T(8,128)(2,1)S(1)} %convolution_convert_fusion.4.refs_0_, bf16[8,16,384]{2,1,0:T(8,128)(2,1)S(1)} %bitcast.343), custom_call_target="tpu_custom_call" | custom-call | bytes 108000000 | tf_op jit(solution)/shard_map/head_grads_to_shards/pallas_call | solution.py:174
  800.7 3.9 convolution_convert_fusion.9.refs_4_
  807.1 168.9 %line_sum.1 = (bf16[256,4096]{1,0:T(8,128)(2,1)S(1)}, bf16[512,2048]{1,0:T(8,128)(2,1)S(1)}, bf16[512,512]{1,0:T(8,128)(2,1)S(1)}, bf16[16,384]{1,0:T(8,128)(2,1)S(1)}, bf16[3,128,2048]{2,1,0:T(8,128)(2,1)S(1)}) custom-call(bf16[256,4096]{1,0:T(8,128)(2,1)S(1)} %copy-done.12, bf16[512,2048]{1,0:T(8,128)(2,1)S(1)} %convolution_convert_fusion.8.refs_1_, ...), custom_call_target="tpu_custom_call" | custom-call | bytes 400000000 | tf_op jit(solution)/shard_map/line_sum/pallas_call | solution.py:308
  979.9 4.2 convert_element_type.539
  989.7 2.8 add_convert_fusion.2
  994.3 9.1 bitcast_convert_fusion
  1003.4 5.6 fusion.92
  1009.0 6.5 bitcast_convert_fusion.2
  1015.5 6.5 bitcast_convert_fusion.1
  (392 shorter events, 139.5 us)
Async XLA Ops:
  7.2 575.7 %all-gather.5.cloned.1.call-start = ((), (), s32[]{:S(2)}) async-start(), calls=%async_computation | async-start | bytes 7864320 | tf_op jit(solution)/shard_map/all_gather | solution.py:743
  98.0 9.1 slice-start
  98.0 7.0 copy-start.45
  98.0 9.1 slice-start.1
  101.5 91.1 %collective-permute-start = (bf16[2,256,768]{2,1,0:T(8,128)(2,1)}, bf16[2,256,768]{2,1,0:T(8,128)(2,1)}, u32[]{:S(2)}, u32[]{:S(2)}) collective-permute-start(bf16[2,256,768]{2,1,0:T(8,128)(2,1)} %get-tuple-element.176), channel_id=1, source_target_pairs={{0,2},{1,3},{2,0},{3,1},{4,6},{5,7},{6,4},{7,5},{8,10},{9,11},{10,... | collective-permute-start | bytes 2359304 | tf_op jit(solution)/shard_map/ppermute | solution.py:367
  102.1 90.6 %collective-permute-start.1 = (bf16[2,256,768]{2,1,0:T(8,128)(2,1)}, bf16[2,256,768]{2,1,0:T(8,128)(2,1)}, u32[]{:S(2)}, u32[]{:S(2)}) collective-permute-start(bf16[2,256,768]{2,1,0:T(8,128)(2,1)} %get-tuple-element.175), channel_id=1, source_target_pairs={{0,4},{1,5},{2,6},{3,7},{4,0},{5,1},{6,2},{7,3},{8,12},{9,13},{10,... | collective-permute-start | bytes 2359304 | tf_op jit(solution)/shard_map/ppermute | solution.py:367
  102.6 90.1 %collective-permute-start.2 = (bf16[2,256,768]{2,1,0:T(8,128)(2,1)}, bf16[2,256,768]{2,1,0:T(8,128)(2,1)}, u32[]{:S(2)}, u32[]{:S(2)}) collective-permute-start(bf16[2,256,768]{2,1,0:T(8,128)(2,1)} %get-tuple-element.174), channel_id=1, source_target_pairs={{0,6},{1,7},{2,4},{3,5},{4,2},{5,3},{6,0},{7,1},{8,14},{9,15},{10,... | collective-permute-start | bytes 2359304 | tf_op jit(solution)/shard_map/ppermute | solution.py:367
  106.1 74.2 %collective-permute-start.3 = (bf16[96,2048]{1,0:T(8,128)(2,1)}, bf16[96,2048]{1,0:T(8,128)(2,1)}, u32[]{:S(2)}, u32[]{:S(2)}) collective-permute-start(bf16[96,2048]{1,0:T(8,128)(2,1)} %get-tuple-element.188), channel_id=1, source_target_pairs={{0,2},{1,3},{2,0},{3,1},{4,6},{5,7},{6,4},{7,5},{8,10},{9,11},{10,... | collective-permute-start | bytes 1179656 | tf_op jit(solution)/shard_map/ppermute | solution.py:367
  106.6 77.1 %collective-permute-start.4 = (bf16[96,2048]{1,0:T(8,128)(2,1)}, bf16[96,2048]{1,0:T(8,128)(2,1)}, u32[]{:S(2)}, u32[]{:S(2)}) collective-permute-start(bf16[96,2048]{1,0:T(8,128)(2,1)} %get-tuple-element.187), channel_id=1, source_target_pairs={{0,4},{1,5},{2,6},{3,7},{4,0},{5,1},{6,2},{7,3},{8,12},{9,13},{10,... | collective-permute-start | bytes 1179656 | tf_op jit(solution)/shard_map/ppermute | solution.py:367
  109.6 4.2 copy-start.49
  114.9 4.5 copy-start.79
  117.5 25.9 %copy-start.81 = (f32[128]{0:T(128)}, f32[128]{0:T(128)S(1)}, u32[]{:S(2)}) copy-start(f32[128]{0:T(128)S(1)} %reshape.609) | copy-start | bytes 1540
  117.5 25.9 %copy-start.77 = (f32[8,128]{1,0:T(8,128)}, f32[8,128]{1,0:T(8,128)S(1)}, u32[]{:S(2)}) copy-start(f32[8,128]{1,0:T(8,128)S(1)} %bitcast_rsqrt_fusion) | copy-start | bytes 12292
  119.1 32.6 %copy-start.56 = (f32[128,64]{1,0:T(8,128)}, f32[128,64]{1,0:T(8,128)S(1)}, u32[]{:S(2)}) copy-start(f32[128,64]{1,0:T(8,128)S(1)} %get-tuple-element.208) | copy-start | bytes 98308
  119.1 32.6 %copy-start.58 = (f32[128,64]{1,0:T(8,128)}, f32[128,64]{1,0:T(8,128)S(1)}, u32[]{:S(2)}) copy-start(f32[128,64]{1,0:T(8,128)S(1)} %get-tuple-element.209) | copy-start | bytes 98308
  147.2 4.5 copy-start.28
  147.3 4.5 copy-start.83
  177.7 4.4 copy-start.14
  180.3 12.4 %collective-permute-start.5 = (bf16[96,2048]{1,0:T(8,128)(2,1)S(1)}, bf16[96,2048]{1,0:T(8,128)(2,1)S(1)}, u32[]{:S(2)}, u32[]{:S(2)}) collective-permute-start(bf16[96,2048]{1,0:T(8,128)(2,1)S(1)} %copy-done.67), channel_id=1, source_target_pairs={{0,6},{1,7},{2,4},{3,5},{4,2},{5,3},{6,0},{7,1},{8,14},{9,15},{10,... | collective-permute-start | bytes 1179656 | tf_op jit(solution)/shard_map/ppermute | solution.py:367
  288.4 67.4 %copy-start.55 = (bf16[1,8,256,768]{3,2,1,0:T(8,128)(2,1)}, bf16[1,8,256,768]{3,2,1,0:T(8,128)(2,1)S(1)}, u32[]{:S(2)}) copy-start(bf16[1,8,256,768]{3,2,1,0:T(8,128)(2,1)S(1)} %get-tuple-element.169) | copy-start | bytes 9437188
  288.5 67.4 %copy-start.54 = (bf16[1,8,256,768]{3,2,1,0:T(8,128)(2,1)}, bf16[1,8,256,768]{3,2,1,0:T(8,128)(2,1)S(1)}, u32[]{:S(2)}) copy-start(bf16[1,8,256,768]{3,2,1,0:T(8,128)(2,1)S(1)} %get-tuple-element.170) | copy-start | bytes 9437188
  349.7 6.2 copy-start.18
  362.6 12.9 %slice-start.2 = ((s8[5242880]{0:T(1024)(128)(4,1)}), s8[4194304]{0:T(1024)(128)(4,1)S(1)}, s32[]{:S(2)}) async-start(s8[5242880]{0:T(1024)(128)(4,1)} %bitcast.337), calls=%async_computation.4 | async-start | bytes 8388608
  366.2 9.3 slice-start.3
  387.1 3.5 collective-permute-start.6
  391.3 13.0 %collective-permute-start.9 = (bf16[96,2048]{1,0:T(8,128)(2,1)S(1)}, bf16[96,2048]{1,0:T(8,128)(2,1)S(1)}, u32[]{:S(2)}, u32[]{:S(2)}) collective-permute-start(bf16[96,2048]{1,0:T(8,128)(2,1)S(1)} %get-tuple-element.183), channel_id=1, source_target_pairs={{0,6},{1,7},{2,4},{3,5},{4,2},{5,3},{6,0},{7,1},{8,14},{9,15},{10,... | collective-permute-start | bytes 1179656 | tf_op jit(solution)/shard_map/ppermute | solution.py:367
  393.1 18.8 %collective-permute-start.8 = (bf16[96,2048]{1,0:T(8,128)(2,1)S(1)}, bf16[96,2048]{1,0:T(8,128)(2,1)S(1)}, u32[]{:S(2)}, u32[]{:S(2)}) collective-permute-start(bf16[96,2048]{1,0:T(8,128)(2,1)S(1)} %get-tuple-element.184), channel_id=1, source_target_pairs={{0,4},{1,5},{2,6},{3,7},{4,0},{5,1},{6,2},{7,3},{8,12},{9,13},{10,... | collective-permute-start | bytes 1179656 | tf_op jit(solution)/shard_map/ppermute | solution.py:367
  393.7 18.2 %collective-permute-start.7 = (bf16[96,2048]{1,0:T(8,128)(2,1)S(1)}, bf16[96,2048]{1,0:T(8,128)(2,1)S(1)}, u32[]{:S(2)}, u32[]{:S(2)}) collective-permute-start(bf16[96,2048]{1,0:T(8,128)(2,1)S(1)} %get-tuple-element.185), channel_id=1, source_target_pairs={{0,2},{1,3},{2,0},{3,1},{4,6},{5,7},{6,4},{7,5},{8,10},{9,11},{10,... | collective-permute-start | bytes 1179656 | tf_op jit(solution)/shard_map/ppermute | solution.py:367
  413.9 589.5 %all-gather.7.cloned.1.call-start = ((), (), s32[]{:S(2)}) async-start(), calls=%async_computation.1 | async-start | bytes 15728640 | tf_op jit(solution)/shard_map/all_gather | solution.py:828
  415.4 16.4 %slice-start.4 = ((s8[5242880]{0:T(1024)(128)(4,1)}), s8[4194304]{0:T(1024)(128)(4,1)S(1)}, s32[]{:S(2)}) async-start(s8[5242880]{0:T(1024)(128)(4,1)} %bitcast.349), calls=%async_computation.6 | async-start | bytes 8388608
  424.3 7.6 slice-start.5
  424.3 7.6 copy-start.96
  431.9 4.7 copy-start.97
  579.2 31.4 %copy-start.42 = (f32[128,2048]{1,0:T(8,128)}, f32[128,2048]{1,0:T(8,128)S(1)}, u32[]{:S(2)}) copy-start(f32[128,2048]{1,0:T(8,128)S(1)} %get-tuple-element.214) | copy-start | bytes 3145732
  579.3 31.5 %copy-start.90 = (f32[128]{0:T(128)}, f32[128]{0:T(128)S(1)}, u32[]{:S(2)}) copy-start(f32[128]{0:T(128)S(1)} %get-tuple-element.158) | copy-start | bytes 1540
  581.3 29.4 %copy-start.86 = (f32[128]{0:T(128)}, f32[128]{0:T(128)S(1)}, u32[]{:S(2)}) copy-start(f32[128]{0:T(128)S(1)} %multiply_multiply_fusion.3) | copy-start | bytes 1540
  582.9 29.8 %copy-start.94 = (f32[512,2048]{1,0:T(8,128)S(1)}, f32[512,2048]{1,0:T(8,128)}, u32[]{:S(2)}) copy-start(f32[512,2048]{1,0:T(8,128)} %param.23) | copy-start | bytes 12582916
  612.7 4.7 copy-start.38
  621.0 4.6 copy-start.51
  621.0 4.6 copy-start.53
  713.7 7.9 copy-start.21
  731.8 26.7 %copy-start.32 = (bf16[1,128,2048]{2,1,0:T(8,128)(2,1)S(1)}, bf16[1,128,2048]{2,1,0:T(8,128)(2,1)}, u32[]{:S(2)}) copy-start(bf16[1,128,2048]{2,1,0:T(8,128)(2,1)} %param.15) | copy-start | bytes 1572868
  731.8 26.7 %copy-start.74 = (f32[1,2,8,128]{3,1,2,0:T(2,128)S(1)}, f32[1,2,8,128]{3,1,2,0:T(2,128)}, u32[]{:S(2)}) copy-start(f32[1,2,8,128]{3,1,2,0:T(2,128)} %copy-done.73) | copy-start | bytes 24580
  800.7 4.0 copy-start.61
  979.9 4.3 copy-start.9
  984.2 5.5 copy-start.33
  988.6 4.0 copy-start.46
  988.6 4.0 copy-start.87
  (68 other events, 153.0 us)
Sparse Core Ops, SparseCore 0:
  414.0 125.4 all-gather.4
  577.0 244.0 all-gather.6

commit v5 on v4

--- a/solution.py
+++ b/solution.py
@@ -190,6 +190,270 @@
         name=name,
     )(*arrays)
     return result
+
+
+def rows_to_experts(cid, tokens, lanes, pick, plane_experts, parts):
+    planes, picked, count = pick.shape
+    cap = picked // plane_experts
+    arrays = (tokens, lanes)
+    widths = [a.shape[1] for a in arrays]
+    order = [0, 1, 3, 2] if planes == 4 else list(range(planes))
+    early = 2 if planes == 4 else planes - 1
+    step = 512
+
+    def kernel(tokens_ref, lanes_ref, pick_ref, rows_ref, lane_rows_ref, *scratch):
+        here, chosen = scratch[:2], scratch[2:4]
+        z_send, z_recv, row_send, row_recv = scratch[4:]
+        ins, outs = (tokens_ref, lanes_ref), (rows_ref, lane_rows_ref)
+        z = lax.axis_index("sp")
+        f = lax.axis_index("fsdp")
+        barrier = pltpu.get_barrier_semaphore()
+        for d in range(1, planes):
+            pl.semaphore_signal(barrier, inc=1, device_id=(flip(z, d), f), device_id_type=MESH)
+        for s in range(1, plane_experts):
+            pl.semaphore_signal(
+                barrier, inc=1, device_id=(z, flip(f, s * parts)), device_id_type=MESH
+            )
+        pl.semaphore_wait(barrier, planes + plane_experts - 2)
+
+        def across(d, w):
+            if d == 0:
+                return pltpu.make_async_copy(ins[w], here[w].at[0], z_recv.at[w])
+            return pltpu.make_async_remote_copy(
+                src_ref=ins[w],
+                dst_ref=here[w].at[d],
+                send_sem=z_send.at[2 * d + w],
+                recv_sem=z_recv.at[2 * d + w],
+                device_id=(flip(z, d), f),
+                device_id_type=MESH,
+            )
+
+        def onward(d, s, w):
+            src = chosen[w].at[d, pl.ds(s * cap, cap)]
+            dst = outs[w].at[s, d]
+            k = (d * plane_experts + s) * 2 + w
+            if s == 0:
+                return pltpu.make_async_copy(src, dst, row_recv.at[k])
+            return pltpu.make_async_remote_copy(
+                src_ref=src,
+                dst_ref=dst,
+                send_sem=row_send.at[k],
+                recv_sem=row_recv.at[k],
+                device_id=(z, flip(f, s * parts)),
+                device_id_type=MESH,
+            )
+
+        for d in order[: early + 1]:
+            for w in range(2):
+                across(d, w).start()
+        for turn, d in enumerate(order):
+            for w in range(2):
+                if d == 0:
+                    across(d, w).wait()
+                else:
+                    across(d, w).wait_recv()
+            if turn == 1:
+                for later in order[early + 1 :]:
+                    for w in range(2):
+                        across(later, w).start()
+
+            def columns(i, carry):
+                at = pl.ds(pl.multiple_of(i * step, step), step)
+                chosen[0][d, :, at] = jnp.dot(
+                    pick_ref[d], here[0][d, :, at], preferred_element_type=FLOAT
+                ).astype(BF16)
+                return carry
+
+            lax.fori_loop(0, widths[0] // step, columns, 0)
+            chosen[1][d] = jnp.dot(
+                pick_ref[d], here[1][d], preferred_element_type=FLOAT
+            ).astype(BF16)
+            for s in range(plane_experts):
+                for w in range(2):
+                    onward(d, s, w).start()
+        for d in range(planes):
+            for w in range(2):
+                if d:
+                    across(d, w).wait_send()
+                for s in range(plane_experts):
+                    onward(d, s, w).wait()
+
+    hbm = pl.BlockSpec(memory_space=pl.ANY)
+    sems = planes * plane_experts * 2
+    return pl.pallas_call(
+        kernel,
+        out_shape=[
+            jax.ShapeDtypeStruct((plane_experts, planes, cap, width), BF16) for width in widths
+        ],
+        in_specs=[hbm, hbm, pl.BlockSpec(memory_space=pltpu.VMEM)],
+        out_specs=[hbm, hbm],
+        scratch_shapes=[pltpu.VMEM((planes, count, width), BF16) for width in widths]
+        + [pltpu.VMEM((planes, picked, width), BF16) for width in widths]
+        + [pltpu.SemaphoreType.DMA((2 * planes,))] * 2
+        + [pltpu.SemaphoreType.DMA((sems,))] * 2,
+        compiler_params=pltpu.CompilerParams(
+            collective_id=cid, has_side_effects=True, vmem_limit_bytes=40 * 1024 * 1024
+        ),
+        cost_estimate=pl.CostEstimate(flops=0, bytes_accessed=int(2.1e8), transcendentals=0),
+        name="rows_to_experts",
+    )(tokens, lanes, pick)
+
+
+def rows_from_experts(cid, rows_in, lanes_in, pick, weights):
+    planes, picked, count = pick.shape
+    plane_experts, _, cap, _ = rows_in.shape
+    parts = weights[0].shape[1]
+    inner_shape = weights[0].shape[2:]
+    widths = (rows_in.shape[3], lanes_in.shape[3])
+    order = [2, 3, 1, 0] if planes == 4 else list(range(planes - 1, -1, -1))
+    step = 512
+
+    def kernel(rows_ref, lanes_ref, pick_ref, first_ref, second_ref, *rest):
+        outs, shards_ref = rest[:2], rest[2]
+        back, partial, own, others = rest[3:5], rest[5:7], rest[7], rest[8]
+        row_send, row_recv, z_send, z_recv, pair_send, pair_recv, load, w_send, w_recv = rest[9:]
+        ins, weight_refs = (rows_ref, lanes_ref), (first_ref, second_ref)
+        z = lax.axis_index("sp")
+        f = lax.axis_index("fsdp")
+        part = lax.rem(f, parts)
+        place = lax.div(f, parts)
+        barrier = pltpu.get_barrier_semaphore()
+        for d in range(1, planes):
+            pl.semaphore_signal(barrier, inc=1, device_id=(flip(z, d), f), device_id_type=MESH)
+        near = list(range(1, parts)) + [s * parts for s in range(1, plane_experts)]
+        for m in near:
+            pl.semaphore_signal(barrier, inc=1, device_id=(z, flip(f, m)), device_id_type=MESH)
+        pl.semaphore_wait(barrier, planes - 1 + len(near))
+
+        def pair(w, p):
+            k = w * (parts - 1) + p - 1
+            return pltpu.make_async_remote_copy(
+                src_ref=weight_refs[w].at[:, flip(part, p)],
+                dst_ref=others.at[p - 1, w],
+                send_sem=pair_send.at[k],
+                recv_sem=pair_recv.at[k],
+                device_id=(z, flip(f, p)),
+                device_id_type=MESH,
+            )
+
+        def load_own(w):
+            return pltpu.make_async_copy(weight_refs[w].at[:, part], own.at[w], load.at[w])
+
+        def home(d, s, w):
+            src = ins[w].at[s, d]
+            dst = back[w].at[d, pl.ds(s * cap, cap)]
+            k = (d * plane_experts + s) * 2 + w
+            if s == 0:
+                return pltpu.make_async_copy(src, dst, row_recv.at[k])
+            return pltpu.make_async_remote_copy(
+                src_ref=src,
+                dst_ref=dst,
+                send_sem=row_send.at[k],
+                recv_sem=row_recv.at[k],
+                device_id=(z, flip(f, s * parts)),
+                device_id_type=MESH,
+            )
+
+        def across(d, w):
+            src, dst = partial[w].at[d], outs[w].at[d]
+            if d == 0:
+                return pltpu.make_async_copy(src, dst, z_recv.at[w])
+            return pltpu.make_async_remote_copy(
+                src_ref=src,
+                dst_ref=dst,
+                send_sem=z_send.at[2 * d + w],
+                recv_sem=z_recv.at[2 * d + w],
+                device_id=(flip(z, d), f),
+                device_id_type=MESH,
+            )
+
+        def to_shard(s, w):
+            src, dst = own.at[w, flip(place, s)], shards_ref.at[w, place]
+            if s == 0:
+                return pltpu.make_async_copy(src, dst, w_recv.at[w])
+            return pltpu.make_async_remote_copy(
+                src_ref=src,
+                dst_ref=dst,
+                send_sem=w_send.at[2 * s + w],
+                recv_sem=w_recv.at[2 * s + w],
+                device_id=(z, flip(f, s * parts)),
+                device_id_type=MESH,
+            )
+
+        for w in range(2):
+            load_own(w).start()
+            for p in range(1, parts):
+                pair(w, p).start()
+        for d in order:
+            for s in range(plane_experts):
+                for w in range(2):
+                    home(d, s, w).start()
+        for w in range(2):
+            load_own(w).wait()
+            for p in range(1, parts):
+                pair(w, p).wait()
+
+            def add(i, carry):
+                e = lax.div(i, inner_shape[0] // 16)
+                at = pl.ds(pl.multiple_of(lax.rem(i, inner_shape[0] // 16) * 16, 16), 16)
+                total = own[w, e, at, :].astype(FLOAT)
+                for p in range(parts - 1):
+                    total = total + others[p, w, e, at, :].astype(FLOAT)
+                own[w, e, at, :] = total.astype(BF16)
+                return carry
+
+            lax.fori_loop(0, plane_experts * (inner_shape[0] // 16), add, 0)
+        for turn, d in enumerate(order):
+            for s in range(plane_experts):
+                for w in range(2):
+                    home(d, s, w).wait()
+            if turn == planes - 2:
+                for s in range(plane_experts):
+                    for w in range(2):
+                        to_shard(s, w).start()
+
+            def columns(i, carry):
+                at = pl.ds(pl.multiple_of(i * step, step), step)
+                partial[0][d, :, at] = contract_rows(pick_ref[d], back[0][d, :, at]).astype(BF16)
+                return carry
+
+            lax.fori_loop(0, widths[0] // step, columns, 0)
+            partial[1][d] = contract_rows(pick_ref[d], back[1][d]).astype(BF16)
+            for w in range(2):
+                across(d, w).start()
+        for d in range(planes):
+            for w in range(2):
+                across(d, w).wait()
+        for s in range(plane_experts):
+            for w in range(2):
+                to_shard(s, w).wait()
+
+    hbm = pl.BlockSpec(memory_space=pl.ANY)
+    dma = pltpu.SemaphoreType.DMA
+    row_count = planes * plane_experts * 2
+    return pl.pallas_call(
+        kernel,
+        out_shape=[jax.ShapeDtypeStruct((planes, count, width), BF16) for width in widths]
+        + [jax.ShapeDtypeStruct((2, plane_experts) + inner_shape, BF16)],
+        in_specs=[hbm, hbm, pl.BlockSpec(memory_space=pltpu.VMEM), hbm, hbm],
+        out_specs=[hbm] * 3,
+        scratch_shapes=[pltpu.VMEM((planes, picked, width), BF16) for width in widths]
+        + [pltpu.VMEM((planes, count, width), BF16) for width in widths]
+        + [
+            pltpu.VMEM((2, plane_experts) + inner_shape, BF16),
+            pltpu.VMEM((parts - 1, 2, plane_experts) + inner_shape, BF16),
+        ]
+        + [dma((row_count,))] * 2
+        + [dma((2 * planes,))] * 2
+        + [dma((2 * (parts - 1),))] * 2
+        + [dma((2,))]
+        + [dma((2 * plane_experts,))] * 2,
+        compiler_params=pltpu.CompilerParams(
+            collective_id=cid, has_side_effects=True, vmem_limit_bytes=48 * 1024 * 1024
+        ),
+        cost_estimate=pl.CostEstimate(flops=0, bytes_accessed=int(2.7e8), transcendentals=0),
+        name="rows_from_experts",
+    )(rows_in, lanes_in, pick, *weights)
 
 
 def line_sum(cid, arrays, pieces, blocks):
@@ -480,12 +744,52 @@
         65,
     )
 
+    own_experts = z * plane_experts + jnp.bitwise_xor(
+        place, jnp.arange(plane_experts, dtype=jnp.int32)
+    )
+    own_hot = (expert_iota[:, None] == own_experts[None, :]).astype(FLOAT)
+    routed_z = lax.dot_general(
+        own_hot,
+        dy_z[:, :, width : width + n_experts].astype(FLOAT),
+        (((0,), (2,)), ((), ())),
+        preferred_element_type=FLOAT,
+    ).transpose(1, 0, 2)
+    earlier = jnp.triu(jnp.ones((rows, rows), FLOAT), 1)
+    rank = jnp.dot(
+        routed_z.reshape(nsp * plane_experts, rows), earlier, preferred_element_type=FLOAT
+    ).reshape(nsp, plane_experts, rows)
+    rank = rank * routed_z + (routed_z - 1.0)
+    pick = (
+        rank[:, :, None, :] == jnp.arange(cap, dtype=FLOAT)[None, None, :, None]
+    ).astype(BF16)
+    pick = pick.reshape(nsp, plane_experts * cap, rows)
+
+    def select(source):
+        picked = jnp.einsum("drt,dtc->drc", pick, source, preferred_element_type=FLOAT)
+        return picked.astype(BF16).reshape(nsp, plane_experts, cap, source.shape[2])
+
     x_all, gate_up_pay, down_pay = lax.optimization_barrier((x_all, gate_up_pay, down_pay))
-    weight_pieces = []
-    for pay in (gate_up_pay, down_pay):
-        for s in range(plane_experts):
-            block = lax.dynamic_index_in_dim(pay, flip(place, s), 0, keepdims=False)
-            weight_pieces.append(swap_f(block, s * parts) if s else block)
+    dy_pick = select(dy_z[:, :, :width])
+    gate_up_pieces, down_pieces = [], []
+    for s in range(plane_experts):
+        gate_up_pieces.append(
+            lax.dynamic_index_in_dim(gate_up_pay, flip(place, s), 0, keepdims=False)
+        )
+        down_pieces.append(lax.dynamic_index_in_dim(down_pay, flip(place, s), 0, keepdims=False))
+    dy_pieces = [dy_pick[:, 0].reshape(nsp * cap, width)]
+    for s in range(1, plane_experts):
+        parts_of = [down_pieces[s], dy_pick[:, s].reshape(nsp * cap, width)]
+        if s == plane_experts - 1:
+            parts_of.append(gate_up_pieces[s].reshape(-1, width))
+        else:
+            gate_up_pieces[s] = swap_f(gate_up_pieces[s], s * parts)
+        down_pieces[s] = swap_f(jnp.concatenate(parts_of, axis=0), s * parts)
+        dy_pieces.append(down_pieces[s][hid_shard : hid_shard + nsp * cap])
+        if s == plane_experts - 1:
+            gate_up_pieces[s] = down_pieces[s][hid_shard + nsp * cap :].reshape(
+                2, shard, hidden_size
+            )
+    dy_in = jnp.concatenate(dy_pieces, axis=0)
 
     small_all = x_all[:, rows:, :].reshape(nf, small_rows * width)
     at = 0
@@ -606,7 +910,9 @@
                     at = (lambda s=s: lambda f: (flip(f, s * parts),))()
                 sends.append(
                     Send(
-                        lambda i, o, z, f, k=1 + w * plane_experts + s: i[k],
+                        lambda i, o, z, f, w=w, k=1 + w * plane_experts + s: (
+                            i[k].at[pl.ds(0, hid_shard)] if w else i[k]
+                        ),
                         lambda i, o, z, f, w=w, at=at: o[1 + w].at[at(f)],
                         0,
                         p,
@@ -616,7 +922,7 @@
         matmul(o_mat, wo_b),
         "out_sum",
         3,
-        weight_pieces,
+        gate_up_pieces + down_pieces,
         ((2, nf, shard, hidden_size), (nf, hid_shard, width)),
         sends,
     )
@@ -635,70 +941,14 @@
         high = exact.astype(BF16)
         return high, (exact - high.astype(FLOAT)).astype(BF16)
 
-    own_experts = z * plane_experts + jnp.bitwise_xor(
-        place, jnp.arange(plane_experts, dtype=jnp.int32)
-    )
-    own_hot = (expert_iota[:, None] == own_experts[None, :]).astype(FLOAT)
-    routed_z = lax.dot_general(
-        own_hot,
-        dy_z[:, :, width : width + n_experts].astype(FLOAT),
-        (((0,), (2,)), ((), ())),
-        preferred_element_type=FLOAT,
-    ).transpose(1, 0, 2)
-    earlier = jnp.triu(jnp.ones((rows, rows), FLOAT), 1)
-    rank = jnp.dot(
-        routed_z.reshape(nsp * plane_experts, rows), earlier, preferred_element_type=FLOAT
-    ).reshape(nsp, plane_experts, rows)
-    rank = rank * routed_z + (routed_z - 1.0)
-    pick = (
-        rank[:, :, None, :] == jnp.arange(cap, dtype=FLOAT)[None, None, :, None]
-    ).astype(BF16)
-    pick = pick.reshape(nsp, plane_experts * cap, rows)
-
-    def select(source):
-        picked = jnp.einsum("drt,dtc->drc", pick, source, preferred_element_type=FLOAT)
-        return picked.astype(BF16).reshape(nsp, plane_experts, cap, source.shape[2])
-
-    def to_experts(which):
-        return [
-            Send(
-                lambda i, o, z, f, s=s: i[which].at[:, s],
-                lambda i, o, z, f, s=s: o[which].at[s],
-                0,
-                s * parts,
-            )
-            for s in range(plane_experts)
-        ]
-
     gate_high, gate_low = two_parts(gates)
     gate_lanes = jnp.concatenate(
         [gate_high, gate_low, jnp.zeros((rows, LANES - 2 * n_experts), BF16)], axis=1
     )
-    hn_z, gate_z, dy_rows = exchange(
-        "hidden_planes",
-        5,
-        (hn_b, gate_lanes, select(dy_z[:, :, :width])),
-        ((nsp, rows, width), (nsp, rows, LANES), (plane_experts, nsp, cap, width)),
-        [
-            Send(lambda i, o, z, f, w=w: i[w], lambda i, o, z, f, d=d, w=w: o[w].at[d], d, 0)
-            for w in range(2)
-            for d in range(nsp)
-        ]
-        + to_experts(2),
-        58,
-    )
-    hn_rows, gate_rows = exchange(
-        "rows_to_experts",
-        6,
-        (select(hn_z), select(gate_z)),
-        ((plane_experts, nsp, cap, width), (plane_experts, nsp, cap, LANES)),
-        to_experts(0) + to_experts(1),
-        60,
-    )
+    hn_rows, gate_rows = rows_to_experts(5, hn_b, gate_lanes, pick, plane_experts, parts)
 
     n_rows = plane_experts * nsp * cap
     hn_in = hn_rows.reshape(n_rows, width)
-    dy_in = dy_rows.reshape(n_rows, width)
     hot = (jnp.arange(n_experts, dtype=jnp.int32) == expert).astype(FLOAT)
     tail = gate_rows.reshape(n_rows, LANES)[:, : 2 * n_experts].astype(FLOAT)
     row_gate = jnp.sum(
@@ -729,24 +979,22 @@
             for p in range(1, parts)
         ],
     )
-    d_down = jnp.stack(
-        [
-            swap_f(
-                lax.dynamic_index_in_dim(d_down, flip(place, s), 0, keepdims=False), s * parts
-            )
-            if s
-            else lax.dynamic_index_in_dim(d_down, place, 0, keepdims=False)
-            for s in range(plane_experts)
-        ]
-    )
-    in_order = jnp.bitwise_xor(jnp.arange(plane_experts, dtype=jnp.int32), place)
-    all_down = lax.all_gather(jnp.take(d_down, in_order, axis=0, mode="clip"), "sp")
+    d_down = [
+        swap_f(lax.dynamic_index_in_dim(d_down, flip(place, s), 0, keepdims=False), s * parts)
+        if s
+        else lax.dynamic_index_in_dim(d_down, place, 0, keepdims=False)
+        for s in range(plane_experts)
+    ]
     result = matmul(hidden, wd_b)
     row_dgate = jnp.sum(result * dy_f, axis=1, keepdims=True)
     weighted = (row_gate * result).astype(BF16)
     d_hidden = contract_cols(d_result, wd_b)
     d_gate_pre = (d_hidden * up_pre * sigma * (1.0 + gate_pre * (1.0 - sigma))).astype(BF16)
     d_up_pre = (d_hidden * act_f).astype(BF16)
+    d_down, d_gate_pre, d_up_pre = lax.optimization_barrier((d_down, d_gate_pre, d_up_pre))
+    in_order = jnp.bitwise_xor(jnp.arange(plane_experts, dtype=jnp.int32), place)
+    d_down = jnp.take(jnp.stack(d_down), in_order, axis=0, mode="clip")
+    all_down = lax.all_gather(d_down, "sp")
     d_in = (contract_cols(d_gate_pre, wg_b) + contract_cols(d_up_pre, wu_b)).astype(BF16)
     dgate_high, dgate_low = two_parts(row_dgate * hot[None, :])
     dgate_lanes = jnp.concatenate(
@@ -757,74 +1005,19 @@
         by_shard(contract_rows(hn_in, d_gate_pre), (shard, hidden_size)),
         by_shard(contract_rows(hn_in, d_up_pre), (shard, hidden_size)),
     )
-    shard_shapes = [w.shape[2:] for w in d_weights]
-
-    sends = []
-    for w in range(2):
-        for s in range(plane_experts):
-            sends.append(
-                Send(
-                    lambda i, o, z, f, s=s, w=w: i[w].at[s],
-                    lambda i, o, z, f, s=s, w=w: o[w].at[:, s],
-                    0,
-                    s * parts,
-                )
-            )
-    for w in range(2):
-        for p in range(1, parts):
-            sends.append(
-                Send(
-                    lambda i, o, z, f, p=p, w=w: i[2 + w].at[:, flip(lax.rem(f, parts), p)],
-                    lambda i, o, z, f, p=p, w=w: o[2 + w].at[p - 1],
-                    0,
-                    p,
-                )
-            )
-    d_back, dgate_back, *d_others = exchange(
-        "rows_from_experts",
+
+    d_home, dgate_home, shards = rows_from_experts(
         7,
-        (
-            d_in.reshape(plane_experts, nsp, cap, width),
-            dgate_lanes.reshape(plane_experts, nsp, cap, LANES),
-        )
-        + d_weights,
-        [(nsp, plane_experts, cap, width), (nsp, plane_experts, cap, LANES)]
-        + [(parts - 1, plane_experts) + tuple(shape) for shape in shard_shapes],
-        sends,
-        70,
+        d_in.reshape(plane_experts, nsp, cap, width),
+        dgate_lanes.reshape(plane_experts, nsp, cap, LANES),
+        pick,
+        d_weights,
     )
 
     def combine(returned):
         flat = returned.reshape(nsp, plane_experts * cap, returned.shape[3])
         return jnp.einsum("drt,drc->dtc", pick, flat, preferred_element_type=FLOAT).astype(BF16)
 
-    summed = [
-        pair_total(own, [others[p] for p in range(parts - 1)])
-        for own, others in zip(d_weights, d_others)
-    ]
-    sends = [
-        Send(lambda i, o, z, f, d=d, w=w: i[w].at[d], lambda i, o, z, f, d=d, w=w: o[w].at[d], d, 0)
-        for w in range(2)
-        for d in range(nsp)
-    ]
-    for w in range(2, 4):
-        for s in range(plane_experts):
-            sends.append(
-                Send(
-                    lambda i, o, z, f, s=s, w=w: i[w].at[flip(lax.div(f, parts), s)],
-                    lambda i, o, z, f, s=s, w=w: o[2].at[w - 2, lax.div(f, parts)],
-                    0,
-                    s * parts,
-                )
-            )
-    d_home, dgate_home, shards = exchange(
-        "hidden_grads_home",
-        8,
-        (combine(d_back), combine(dgate_back), *summed),
-        ((nsp, rows, width), (nsp, rows, LANES), (2, plane_experts, shard, hidden_size)),
-        sends,
-        58,
-    )
     all_gate_up = lax.all_gather(shards, "sp")
     d_home = jnp.sum(d_home.astype(FLOAT), axis=0)
     tail = jnp.sum(dgate_home.astype(FLOAT), axis=0)
@@ -838,8 +1031,6 @@
     d_mid = grad_out + d_mid_norm
 
     d_attn_b = d_mid.astype(BF16)
-    d_attn_b, all_down = lax.optimization_barrier((d_attn_b, all_down))
-    grad_down = all_down.astype(FLOAT).reshape(n_experts, hid_shard, width)
     sends = [
         Send(lambda i, o, z, f: i[0], lambda i, o, z, f: o[0].at[f], 0, m)
         for m in range(0, nf, 2)
@@ -877,6 +1068,8 @@
     d_kv = jnp.concatenate([d_key, d_val], axis=2).astype(BF16)
     d_kv = d_kv.reshape(seqs, nsp, rows, 2 * head_dim).transpose(1, 0, 2, 3)
     d_kv = d_kv.reshape(nsp, seqs * rows, 2 * head_dim)
+    d_kv, all_down = lax.optimization_barrier((d_kv, all_down))
+    grad_down = all_down.astype(FLOAT).reshape(n_experts, hid_shard, width)
     d_kv = d_kv.reshape(nsp, rep, piece, 2 * head_dim)
     (others,) = exchange(
         "key_grads_group",
@@ -931,6 +1124,7 @@
         6,
     )
     d_kv = d_kv.reshape(seqs * rows, 2 * head_dim).astype(FLOAT)
+    dq, grad_down = lax.optimization_barrier((dq, grad_down))
     unused, q_pull = jax.vjp(prep_heads, q_lin, g_query)
     d_q_lin, d_q_gain = q_pull(dq.astype(FLOAT))
     unused, k_pull = jax.vjp(prep_heads, k_lin, g_key)

time: 1040 us -> 1000 us (0.962)
  Pallas kernels: 696 us -> 627 us
  local copies, waits for them, and re-layouts: 81.2 us -> 96.8 us
    pallas_call x15 -> x11, Pallas kernels: 527 us -> 297 us  [exchange(): pl.pallas_call(kernel, out_shape=[jax.ShapeDtypeStruct(shape, BF16) for s...]
    pallas_call x0 -> x2, Pallas kernels: none -> 167 us  [the longest x1 98.4 us: rows_from_experts(): pl.pallas_call(kernel, out_shape=[jax.ShapeDtypeStruct((planes, count, wi...]
    unnamed x216 -> x256, local copies, waits for them, and re-layouts: 40 us -> 43 us
    ppermute x10 -> x9, waiting for transfers between devices: 29.4 us -> 29.8 us  [swap_f(): return lax.ppermute(block, 'fsdp', [(i, i ^ mask) for i in range(nf)])]
  transfers between devices with their start and end apart: 12 -> 11, of which waited for: 4 -> 6; matrix products, arithmetic and copies ran while one was open for 15% -> 19% of each run, Pallas kernels for 47% -> 47%
where the time goes in v5:
time: 1000 us; the launch traced here: 990 us
  Pallas kernels  627 us (63%)
  matrix products  117 us (12%)
  local copies, waits for them, and re-layouts  96.8 us (10%)
  other arithmetic  94.6 us (9%)
  waiting for transfers between devices  29.8 us (3%)
  between operations  16.6 us (2%)
    pallas_call x11, Pallas kernels, exchange(): pl.pallas_call(kernel, out_shape=[jax.ShapeDtypeStruct(shape, BF16) for s...  297 us
    pallas_call x1, Pallas kernels, line_sum(): pl.pallas_call(kernel, out_shape=[jax.ShapeDtypeStruct(a.shape, BF16) for...  163 us
    pallas_call x1, Pallas kernels, rows_from_experts(): pl.pallas_call(kernel, out_shape=[jax.ShapeDtypeStruct((planes, count, wi...  98.4 us
    pallas_call x1, Pallas kernels, rows_to_experts(): pl.pallas_call(kernel, out_shape=[jax.ShapeDtypeStruct((plane_experts, pl...  68.8 us
    unnamed x256, local copies, waits for them, and re-layouts  43 us
    dot_general x5, matrix products, contract_cols(): lax.dot_general(left_mat, right_mat, (((1,), (1,)), ((), ())), preferred_...  33.7 us
    dot_general x6, matrix products, matmul(): return jnp.dot(left_mat, right_mat, preferred_element_type=FLOAT)  30.2 us
    ppermute x9, waiting for transfers between devices, swap_f(): return lax.ppermute(block, 'fsdp', [(i, i ^ mask) for i in range(nf)])  29.8 us
  transfers between devices with their start and end apart: 11, of which 6 were waited for; matrix products, arithmetic and copies ran while one was open for 19% of the time, Pallas kernels for 47%

profile of v5, /device:TPU:0, one launch (start us, length us, event | category | flops | bytes accessed | tf_op | source)
XLA Modules:
  0.0 990.1 jit_solution(768698171138719461)
XLA Ops:
  12.7 3.3 dynamic-slice_convert_fusion
  15.9 3.2 fusion.27
  23.9 65.5 %gather_inputs.1 = (bf16[8,144,2048]{2,1,0:T(8,128)(2,1)S(1)}, bf16[2048,768]{1,0:T(8,128)(2,1)S(1)}, bf16[4,128,2176]{2,1,0:T(8,128)(2,1)S(1)}) custom-call(bf16[144,2048]{1,0:T(8,128)(2,1)S(1)} %pad_maximum_fusion.9.refs_0_, bf16[256,4096]{1,0:T(8,128)(2,1)S(1)} %convert_element_type.380.refs_1_, bf16[256,512]{1,0:T(8,128)(2,1)S(1)} %convert_element_type.381.refs_2_, ...), custom_call_target="tpu_custom_call" | custom-call | bytes 195000000 | tf_op jit(solution)/shard_map/gather_inputs/pallas_call | solution.py:174
  94.8 3.6 constant_dynamic-slice_fusion
  119.8 3.4 fusion.104
  125.9 2.9 reshape.561
  137.3 23.8 %gather_keys.1 = bf16[4,1024,256]{2,1,0:T(8,128)(2,1)S(1)} custom-call(bf16[1024,256]{1,0:T(8,128)(2,1)S(1)} %pad_maximum_fusion.10.refs_0_), custom_call_target="tpu_custom_call" | custom-call | bytes 72000000 | tf_op jit(solution)/shard_map/gather_keys/pallas_call | solution.py:174
  161.4 4.7 fusion.54
  166.1 9.8 fusion.102
  183.2 4.4 convolution_convert_fusion.1
  190.9 4.2 out_sum_pair.1
  197.7 4.4 fusion.10.refs_0_
  211.1 8.2 collective-permute-done.refs_2_
  223.9 26.4 %out_sum_plane.1 = (bf16[4,128,2048]{2,1,0:T(8,128)(2,1)S(1)}, bf16[2,8,256,768]{3,2,1,0:T(8,128)(2,1)}, bf16[8,96,2048]{2,1,0:T(8,128)(2,1)S(1)}) custom-call(bf16[4,128,2048]{2,1,0:T(8,128)(2,1)S(1)} %copy-done.4, bf16[2,256,768]{2,1,0:T(8,128)(2,1)S(1)} %copy-done.9, bf16[2,256,768]{2,1,0:T(8,128)(2,1)} %collective-permute-done.refs_2_, ...), custom_call_target="tpu_custom_call" | custom-call | bytes 81000000 | tf_op jit(solution)/shard_map/out_sum_plane/pallas_call | solution.py:174
  255.9 68.8 %rows_to_experts.1 = (bf16[4,4,80,2048]{3,2,1,0:T(8,128)(2,1)S(1)}, bf16[4,4,80,128]{3,2,1,0:T(8,128)(2,1)S(1)}) custom-call(bf16[128,2048]{1,0:T(8,128)(2,1)S(1)} %multiply_convert_fusion.6.tokens_ref, bf16[128,128]{1,0:T(8,128)(2,1)S(1)} %maximum_maximum_fusion.1.lanes_ref, bf16[4,320,128]{2,1,0:T(8,128)(2,1)S(1)} %copy-done.10), custom_call_target="tpu_custom_call" | custom-call | bytes 210000000 | tf_op jit(solution)/shard_map/rows_to_experts/pallas_call | solution.py:283
  324.7 6.2 fusion.106
  330.9 6.2 fusion.105
  339.7 14.1 %multiply_convert_fusion.1 = (bf16[1280,768]{1,0:T(8,128)(2,1)}, bf16[1280,768]{1,0:T(8,128)(2,1)}, bf16[1280,768]{1,0:T(8,128)(2,1)S(1)}) fusion(f32[1280,768]{1,0:T(8,128)} %fusion.105, f32[1280,768]{1,0:T(8,128)} %fusion.106, bf16[768,2048]{1,0:T(8,128)(2,1)S(1)} %bitcast.322, f32[1280]{0:T(1024)S(1)} %fusion.57, bf16[320,2048]{1,0:T(8,128)(2,1)S(1)} %slice.229, ...), kind=kOutput, calls=%fused_computation.36 | convolution fusion | flops 4067491840 | bytes 22156288 | tf_op jit(solution)/shard_map/dot_general | solution.py:50
  353.8 4.7 convolution_convert_fusion.6
  358.7 3.4 collective-permute-done.5
  366.4 8.5 collective-permute-done.6
  374.9 8.0 collective-permute-done.7
  384.9 9.5 multiply_convert_fusion
  395.1 6.4 fusion.107
  401.5 8.6 convolution_convert_fusion.4
  410.2 5.9 convolution_convert_fusion.5
  416.1 6.1 add_convert_fusion
  422.2 98.4 %rows_from_experts.1 = (bf16[4,128,2048]{2,1,0:T(8,128)(2,1)S(1)}, bf16[4,128,128]{2,1,0:T(8,128)(2,1)S(1)}, bf16[2,4,256,768]{3,2,1,0:T(8,128)(2,1)S(1)}) custom-call(bf16[4,4,80,2048]{3,2,1,0:T(8,128)(2,1)} %bitcast.334, bf16[4,4,80,128]{3,2,1,0:T(8,128)(2,1)S(1)} %maximum_maximum_fusion.lanes_ref, bf16[4,320,128]{2,1,0:T(8,128)(2,1)S(1)} %copy-done.10, ...), custom_call_target="tpu_custom_call" | custom-call | bytes 270000000 | tf_op jit(solution)/shard_map/rows_from_experts/pallas_call | solution.py:434
  529.4 27.8 %gather_grads.1 = bf16[8,128,2048]{2,1,0:T(8,128)(2,1)S(1)} custom-call(bf16[128,2048]{1,0:T(8,128)(2,1)S(1)} %fusion.92.refs_0_), custom_call_target="tpu_custom_call" | custom-call | bytes 90000000 | tf_op jit(solution)/shard_map/gather_grads/pallas_call | solution.py:174
  559.3 3.3 convolution_convert_fusion.11
  564.0 3.5 fusion.6
  567.6 4.6 fusion.7
  578.5 3.9 fusion.34
  582.6 3.7 convolution_convert_fusion.7.refs_1_
  591.8 81.2 %key_grads_planes.1 = (bf16[3,512,256]{2,1,0:T(8,128)(2,1)S(1)}, bf16[4,4,80,2048]{3,2,1,0:T(8,128)(2,1)S(1)}) custom-call(bf16[4,512,256]{2,1,0:T(8,128)(2,1)S(1)} %fusion.20.refs_0_, bf16[4,4,80,2048]{3,2,1,0:T(8,128)(2,1)S(1)} %bitcast.310), custom_call_target="tpu_custom_call" | custom-call | bytes 180000000 | tf_op jit(solution)/shard_map/key_grads_planes/pallas_call | solution.py:174
  680.0 9.2 bitcast_convert_fusion.2
  701.5 3.7 convolution_convert_fusion.2
  705.2 4.2 input_sum_pair.1
  710.2 26.2 %input_sum_plane.1 = bf16[4,128,2048]{2,1,0:T(8,128)(2,1)S(1)} custom-call(bf16[4,128,2048]{2,1,0:T(8,128)(2,1)S(1)} %fusion.9.refs_0_), custom_call_target="tpu_custom_call" | custom-call | bytes 81000000 | tf_op jit(solution)/shard_map/input_sum_plane/pallas_call | solution.py:174
  738.3 5.8 convolution_convert_fusion.3.refs_0_
  744.1 33.7 %head_grads_to_shards.1 = (bf16[256,4096]{1,0:T(8,128)(2,1)S(1)}, bf16[512,512]{1,0:T(8,128)(2,1)S(1)}, bf16[8,16,384]{2,1,0:T(8,128)(2,1)S(1)}) custom-call(bf16[2048,768]{1,0:T(8,128)(2,1)S(1)} %convolution_convert_fusion.3.refs_0_, bf16[8,16,384]{2,1,0:T(8,128)(2,1)S(1)} %bitcast.314), custom_call_target="tpu_custom_call" | custom-call | bytes 108000000 | tf_op jit(solution)/shard_map/head_grads_to_shards/pallas_call | solution.py:174
  779.2 3.9 convolution_convert_fusion.8.refs_4_
  783.1 162.6 %line_sum.1 = (bf16[256,4096]{1,0:T(8,128)(2,1)S(1)}, bf16[512,2048]{1,0:T(8,128)(2,1)S(1)}, bf16[512,512]{1,0:T(8,128)(2,1)S(1)}, bf16[16,384]{1,0:T(8,128)(2,1)S(1)}, bf16[3,128,2048]{2,1,0:T(8,128)(2,1)S(1)}) custom-call(bf16[256,4096]{1,0:T(8,128)(2,1)S(1)} %copy-done.16, bf16[512,2048]{1,0:T(8,128)(2,1)S(1)} %copy-done.14, ...), custom_call_target="tpu_custom_call" | custom-call | bytes 400000000 | tf_op jit(solution)/shard_map/line_sum/pallas_call | solution.py:572
  949.7 4.2 convert_element_type.471
  959.5 2.8 add_convert_fusion.2
  964.1 5.6 fusion.94
  969.7 6.5 bitcast_convert_fusion
  976.2 6.5 bitcast_convert_fusion.1
  (430 shorter events, 147.6 us)
Async XLA Ops:
  7.2 579.1 %all-gather.5.cloned.1.call-start = ((), (), s32[]{:S(2)}) async-start(), calls=%async_computation | async-start | bytes 7864320 | tf_op jit(solution)/shard_map/all_gather | solution.py:997
  98.3 4.6 copy-start.18
  105.8 10.7 %slice-start = ((s8[4718592]{0:T(1024)(128)(4,1)}), s8[524288]{0:T(1024)(128)(4,1)S(1)}, s32[]{:S(2)}) async-start(s8[4718592]{0:T(1024)(128)(4,1)} %bitcast.300), calls=%async_computation.2 | async-start | bytes 1048576
  107.6 4.9 copy-start.66
  107.6 8.8 slice-start.1
  109.3 98.8 %collective-permute-start.2 = (bf16[608,2048]{1,0:T(8,128)(2,1)}, bf16[608,2048]{1,0:T(8,128)(2,1)S(1)}, u32[]{:S(2)}, u32[]{:S(2)}) collective-permute-start(bf16[608,2048]{1,0:T(8,128)(2,1)} %pad_maximum_fusion.2), channel_id=1, source_target_pairs={{0,6},{1,7},{2,4},{3,5},{4,2},{5,3},{6,0},{7,1},{8,14},{9,15},{10,... | collective-permute-start | bytes 7471112 | tf_op jit(solution)/shard_map/ppermute | solution.py:631
  111.1 91.9 %collective-permute-start.3 = (bf16[416,2048]{1,0:T(8,128)(2,1)}, bf16[416,2048]{1,0:T(8,128)(2,1)}, u32[]{:S(2)}, u32[]{:S(2)}) collective-permute-start(bf16[416,2048]{1,0:T(8,128)(2,1)} %pad_maximum_fusion.4), channel_id=1, source_target_pairs={{0,2},{1,3},{2,0},{3,1},{4,6},{5,7},{6,4},{7,5},{8,10},{9,11},{10,... | collective-permute-start | bytes 5111816 | tf_op jit(solution)/shard_map/ppermute | solution.py:631
  113.9 91.7 %collective-permute-start.4 = (bf16[416,2048]{1,0:T(8,128)(2,1)}, bf16[416,2048]{1,0:T(8,128)(2,1)}, u32[]{:S(2)}, u32[]{:S(2)}) collective-permute-start(bf16[416,2048]{1,0:T(8,128)(2,1)} %pad_maximum_fusion.5), channel_id=1, source_target_pairs={{0,4},{1,5},{2,6},{3,7},{4,0},{5,1},{6,2},{7,3},{8,12},{9,13},{10,... | collective-permute-start | bytes 5111816 | tf_op jit(solution)/shard_map/ppermute | solution.py:631
  115.4 103.9 %collective-permute-start = (bf16[2,256,768]{2,1,0:T(8,128)(2,1)}, bf16[2,256,768]{2,1,0:T(8,128)(2,1)}, u32[]{:S(2)}, u32[]{:S(2)}) collective-permute-start(bf16[2,256,768]{2,1,0:T(8,128)(2,1)} %get-tuple-element.181), channel_id=1, source_target_pairs={{0,2},{1,3},{2,0},{3,1},{4,6},{5,7},{6,4},{7,5},{8,10},{9,11},{10,... | collective-permute-start | bytes 2359304 | tf_op jit(solution)/shard_map/ppermute | solution.py:631
  115.9 104.2 %collective-permute-start.1 = (bf16[2,256,768]{2,1,0:T(8,128)(2,1)}, bf16[2,256,768]{2,1,0:T(8,128)(2,1)}, u32[]{:S(2)}, u32[]{:S(2)}) collective-permute-start(bf16[2,256,768]{2,1,0:T(8,128)(2,1)} %get-tuple-element.180), channel_id=1, source_target_pairs={{0,4},{1,5},{2,6},{3,7},{4,0},{5,1},{6,2},{7,3},{8,12},{9,13},{10,... | collective-permute-start | bytes 2359304 | tf_op jit(solution)/shard_map/ppermute | solution.py:631
  125.9 6.0 copy-start.93
  131.8 4.9 copy-start.85
  131.9 4.8 copy-start.98
  132.0 4.7 copy-start.96
  136.7 24.7 %copy-start.54 = (bf16[8,128,4,64]{3,1,2,0:T(8,128)(2,1)}, bf16[8,128,4,64]{3,1,2,0:T(8,128)(2,1)S(1)}, u32[]{:S(2)}) copy-start(bf16[8,128,4,64]{3,1,2,0:T(8,128)(2,1)S(1)} %get-tuple-element.185) | copy-start | bytes 1572868
  136.7 24.7 %copy-start.56 = (bf16[8,128,4,64]{3,1,2,0:T(8,128)(2,1)}, bf16[8,128,4,64]{3,1,2,0:T(8,128)(2,1)S(1)}, u32[]{:S(2)}) copy-start(bf16[8,128,4,64]{3,1,2,0:T(8,128)(2,1)S(1)} %get-tuple-element.186) | copy-start | bytes 1572868
  161.2 16.5 %copy-start.40 = (bf16[8,4,128,256]{3,2,1,0:T(8,128)(2,1)}, bf16[8,4,128,256]{3,2,1,0:T(8,128)(2,1)S(1)}, u32[]{:S(2)}) copy-start(bf16[8,4,128,256]{3,2,1,0:T(8,128)(2,1)S(1)} %copy.180) | copy-start | bytes 6291460
  250.3 87.3 %copy-start.27 = (bf16[8,96,2048]{2,1,0:T(8,128)(2,1)}, bf16[8,96,2048]{2,1,0:T(8,128)(2,1)S(1)}, u32[]{:S(2)}) copy-start(bf16[8,96,2048]{2,1,0:T(8,128)(2,1)S(1)} %get-tuple-element.58) | copy-start | bytes 9437188
  250.4 4.6 copy-start.48
  255.5 75.4 %copy-start.60 = (bf16[1,8,256,768]{3,2,1,0:T(8,128)(2,1)}, bf16[1,8,256,768]{3,2,1,0:T(8,128)(2,1)S(1)}, u32[]{:S(2)}) copy-start(bf16[1,8,256,768]{3,2,1,0:T(8,128)(2,1)S(1)} %get-tuple-element.172) | copy-start | bytes 9437188
  255.5 75.4 %copy-start.58 = (bf16[1,8,256,768]{3,2,1,0:T(8,128)(2,1)}, bf16[1,8,256,768]{3,2,1,0:T(8,128)(2,1)S(1)}, u32[]{:S(2)}) copy-start(bf16[1,8,256,768]{3,2,1,0:T(8,128)(2,1)S(1)} %get-tuple-element.171) | copy-start | bytes 9437188
  324.7 6.2 copy-start.23
  337.7 16.1 %copy-start.73 = (bf16[320,2048]{1,0:T(8,128)(2,1)}, bf16[320,2048]{1,0:T(8,128)(2,1)S(1)}, u32[]{:S(2)}) copy-start(bf16[320,2048]{1,0:T(8,128)(2,1)S(1)} %slice.229) | copy-start | bytes 3932164
  353.8 4.7 copy-start.119
  358.7 3.5 collective-permute-start.5
  362.9 12.0 %collective-permute-start.6 = (bf16[96,2048]{1,0:T(8,128)(2,1)S(1)}, bf16[96,2048]{1,0:T(8,128)(2,1)S(1)}, u32[]{:S(2)}, u32[]{:S(2)}) collective-permute-start(bf16[96,2048]{1,0:T(8,128)(2,1)S(1)} %get-tuple-element.189), channel_id=1, source_target_pairs={{0,2},{1,3},{2,0},{3,1},{4,6},{5,7},{6,4},{7,5},{8,10},{9,11},{10,... | collective-permute-start | bytes 1179656 | tf_op jit(solution)/shard_map/ppermute | solution.py:631
  363.5 19.3 %collective-permute-start.7 = (bf16[96,2048]{1,0:T(8,128)(2,1)S(1)}, bf16[96,2048]{1,0:T(8,128)(2,1)S(1)}, u32[]{:S(2)}, u32[]{:S(2)}) collective-permute-start(bf16[96,2048]{1,0:T(8,128)(2,1)S(1)} %get-tuple-element.188), channel_id=1, source_target_pairs={{0,4},{1,5},{2,6},{3,7},{4,0},{5,1},{6,2},{7,3},{8,12},{9,13},{10,... | collective-permute-start | bytes 1179656 | tf_op jit(solution)/shard_map/ppermute | solution.py:631
  365.1 17.8 %collective-permute-start.8 = (bf16[96,2048]{1,0:T(8,128)(2,1)S(1)}, bf16[96,2048]{1,0:T(8,128)(2,1)S(1)}, u32[]{:S(2)}, u32[]{:S(2)}) collective-permute-start(bf16[96,2048]{1,0:T(8,128)(2,1)S(1)} %get-tuple-element.187), channel_id=1, source_target_pairs={{0,6},{1,7},{2,4},{3,5},{4,2},{5,3},{6,0},{7,1},{8,14},{9,15},{10,... | collective-permute-start | bytes 1179656 | tf_op jit(solution)/shard_map/ppermute | solution.py:631
  384.9 10.1 %copy-start.116 = (bf16[1280,768]{1,0:T(8,128)(2,1)S(1)}, bf16[1280,768]{1,0:T(8,128)(2,1)}, u32[]{:S(2)}) copy-start(bf16[1280,768]{1,0:T(8,128)(2,1)} %get-tuple-element.60) | copy-start | bytes 5898244
  384.9 579.2 %all-gather.7.cloned.1.call-start = ((), (), s32[]{:S(2)}) async-start(), calls=%async_computation.1 | async-start | bytes 15728640 | tf_op jit(solution)/shard_map/all_gather | solution.py:1021
  395.0 15.1 %slice-start.2 = ((s8[5242880]{0:T(1024)(128)(4,1)}), s8[1048576]{0:T(1024)(128)(4,1)S(1)}, s32[]{:S(2)}) async-start(s8[5242880]{0:T(1024)(128)(4,1)} %bitcast.319), calls=%async_computation.4 | async-start | bytes 2097152
  401.5 8.7 slice-start.3
  401.5 8.7 copy-start.117
  410.2 5.9 copy-start.59
  410.2 5.9 copy-start.118
  528.0 50.0 %copy-start.104 = (f32[128]{0:T(128)}, f32[128]{0:T(128)S(1)}, u32[]{:S(2)}) copy-start(f32[128]{0:T(128)S(1)} %get-tuple-element.160) | copy-start | bytes 1540
  528.0 29.2 %copy-start.100 = (f32[128]{0:T(128)}, f32[128]{0:T(128)S(1)}, u32[]{:S(2)}) copy-start(f32[128]{0:T(128)S(1)} %multiply_multiply_fusion.3) | copy-start | bytes 1540
  529.4 29.8 %copy-start.111 = (f32[512,2048]{1,0:T(8,128)S(1)}, f32[512,2048]{1,0:T(8,128)}, u32[]{:S(2)}) copy-start(f32[512,2048]{1,0:T(8,128)} %param.23) | copy-start | bytes 12582916
  559.3 4.8 copy-start.41
  567.6 4.6 copy-start.55
  567.6 4.6 copy-start.57
  696.2 5.3 copy-start.26
  700.2 5.0 copy-start.76
  710.2 26.7 %copy-start.35 = (bf16[1,128,2048]{2,1,0:T(8,128)(2,1)S(1)}, bf16[1,128,2048]{2,1,0:T(8,128)(2,1)}, u32[]{:S(2)}) copy-start(bf16[1,128,2048]{2,1,0:T(8,128)(2,1)} %param.15) | copy-start | bytes 1572868
  710.2 26.7 %copy-start.88 = (f32[1,2,8,128]{3,1,2,0:T(2,128)S(1)}, f32[1,2,8,128]{3,1,2,0:T(2,128)}, u32[]{:S(2)}) copy-start(f32[1,2,8,128]{3,1,2,0:T(2,128)} %copy-done.87) | copy-start | bytes 24580
  710.2 26.7 %copy-start.102 = (f32[128]{0:T(128)S(1)}, f32[128]{0:T(128)}, u32[]{:S(2)}) copy-start(f32[128]{0:T(128)} %fusion.81) | copy-start | bytes 1540
  744.1 35.0 %copy-start.69 = (pred[4,320,128]{2,1,0:T(32,128)(4,1)S(1)}, pred[4,320,128]{2,1,0:T(32,128)(4,1)}, u32[]{:S(2)}) copy-start(pred[4,320,128]{2,1,0:T(32,128)(4,1)} %copy-done.68) | copy-start | bytes 491524
  954.0 5.5 copy-start.36
  (87 other events, 204.3 us)
Sparse Core Ops, SparseCore 0:
  385.0 161.6 all-gather.4
  548.2 238.7 all-gather.6

commit v6 on v5

--- a/solution.py
+++ b/solution.py
@@ -678,15 +678,21 @@
                 m,
             )
         )
-    for m in range(nf):
-        sends.append(
-            Send(
-                lambda i, o, z, f, m=m: i[1].at[:, cols(flip(f, m), q_cols)],
-                lambda i, o, z, f: o[1].at[cols(f, shard), pl.ds(0, q_cols)],
-                0,
-                m,
-            )
-        )
+    for m in range(0, nf, 2):
+        if m == 0:
+            sends.append(
+                Send(lambda i, o, z, f: i[0], lambda i, o, z, f: o[0].at[f], 0, 1)
+            )
+        else:
+            sends.append(
+                Send(
+                    lambda i, o, z, f, m=m: o[0].at[flip(f, m)],
+                    lambda i, o, z, f, m=m: o[0].at[flip(f, m)],
+                    0,
+                    1,
+                    m // 2,
+                )
+            )
     for m in range(0, nf, rep):
         for w in range(2):
             sends.append(
@@ -716,25 +722,19 @@
                     )
                 else:
                     sends.append(Send(view, view, 0, p, len(sends) - p))
+    for m in range(nf):
+        sends.append(
+            Send(
+                lambda i, o, z, f, m=m: i[1].at[:, cols(flip(f, m), q_cols)],
+                lambda i, o, z, f: o[1].at[cols(f, shard), pl.ds(0, q_cols)],
+                0,
+                m,
+            )
+        )
     for m in range(nsp):
         sends.append(
             Send(lambda i, o, z, f: i[4], lambda i, o, z, f, m=m: o[2].at[m], m, 0)
         )
-    for m in range(0, nf, 2):
-        if m == 0:
-            sends.append(
-                Send(lambda i, o, z, f: i[0], lambda i, o, z, f: o[0].at[f], 0, 1)
-            )
-        else:
-            sends.append(
-                Send(
-                    lambda i, o, z, f, m=m: o[0].at[flip(f, m)],
-                    lambda i, o, z, f, m=m: o[0].at[flip(f, m)],
-                    0,
-                    1,
-                    m // 2,
-                )
-            )
     x_all, w_qkv, dy_z = exchange(
         "gather_inputs",
         0,
@@ -764,31 +764,25 @@
     ).astype(BF16)
     pick = pick.reshape(nsp, plane_experts * cap, rows)
 
-    def select(source):
-        picked = jnp.einsum("drt,dtc->drc", pick, source, preferred_element_type=FLOAT)
-        return picked.astype(BF16).reshape(nsp, plane_experts, cap, source.shape[2])
-
-    x_all, gate_up_pay, down_pay = lax.optimization_barrier((x_all, gate_up_pay, down_pay))
-    dy_pick = select(dy_z[:, :, :width])
-    gate_up_pieces, down_pieces = [], []
+    x_all, gate_up_pay = lax.optimization_barrier((x_all, gate_up_pay))
+    by_expert = pick.reshape(nsp, plane_experts, cap, rows)
+    gate_up_pieces, dy_pieces = [], []
     for s in range(plane_experts):
-        gate_up_pieces.append(
-            lax.dynamic_index_in_dim(gate_up_pay, flip(place, s), 0, keepdims=False)
+        weights = lax.dynamic_index_in_dim(gate_up_pay, flip(place, s), 0, keepdims=False)
+        dy_rows = jnp.einsum(
+            "drt,dtc->drc", by_expert[:, s], dy_z[:, :, :width], preferred_element_type=FLOAT
         )
-        down_pieces.append(lax.dynamic_index_in_dim(down_pay, flip(place, s), 0, keepdims=False))
-    dy_pieces = [dy_pick[:, 0].reshape(nsp * cap, width)]
-    for s in range(1, plane_experts):
-        parts_of = [down_pieces[s], dy_pick[:, s].reshape(nsp * cap, width)]
-        if s == plane_experts - 1:
-            parts_of.append(gate_up_pieces[s].reshape(-1, width))
-        else:
-            gate_up_pieces[s] = swap_f(gate_up_pieces[s], s * parts)
-        down_pieces[s] = swap_f(jnp.concatenate(parts_of, axis=0), s * parts)
-        dy_pieces.append(down_pieces[s][hid_shard : hid_shard + nsp * cap])
-        if s == plane_experts - 1:
-            gate_up_pieces[s] = down_pieces[s][hid_shard + nsp * cap :].reshape(
-                2, shard, hidden_size
-            )
+        dy_rows = dy_rows.astype(BF16).reshape(nsp * cap, width)
+        if s and s == plane_experts - 1:
+            both = jnp.concatenate([dy_rows, weights.reshape(-1, width)], axis=0)
+            both = swap_f(both, s * parts)
+            dy_rows = both[: nsp * cap]
+            weights = both[nsp * cap :].reshape(2, shard, hidden_size)
+        elif s:
+            weights = swap_f(weights, s * parts)
+            dy_rows = swap_f(dy_rows, s * parts)
+        gate_up_pieces.append(weights)
+        dy_pieces.append(dy_rows)
     dy_in = jnp.concatenate(dy_pieces, axis=0)
 
     small_all = x_all[:, rows:, :].reshape(nf, small_rows * width)
@@ -902,33 +896,21 @@
         return jnp.sum(blocks.astype(FLOAT), axis=0), rest
 
     sends = []
-    for w in range(2):
-        for s in range(plane_experts):
-            for p in range(parts):
-                at = (lambda s=s: lambda f: (slice(None), flip(f, s * parts)))()
-                if w:
-                    at = (lambda s=s: lambda f: (flip(f, s * parts),))()
-                sends.append(
-                    Send(
-                        lambda i, o, z, f, w=w, k=1 + w * plane_experts + s: (
-                            i[k].at[pl.ds(0, hid_shard)] if w else i[k]
-                        ),
-                        lambda i, o, z, f, w=w, at=at: o[1 + w].at[at(f)],
-                        0,
-                        p,
-                    )
+    for s in range(plane_experts):
+        for p in range(parts):
+            sends.append(
+                Send(
+                    lambda i, o, z, f, s=s: i[1 + s],
+                    lambda i, o, z, f, s=s: o[1].at[:, flip(f, s * parts)],
+                    0,
+                    p,
                 )
-    branch, (gate_up_all, down_all) = pair_then_plane(
-        matmul(o_mat, wo_b),
-        "out_sum",
-        3,
-        gate_up_pieces + down_pieces,
-        ((2, nf, shard, hidden_size), (nf, hid_shard, width)),
-        sends,
+            )
+    branch, (gate_up_all,) = pair_then_plane(
+        matmul(o_mat, wo_b), "out_sum", 3, gate_up_pieces, ((2, nf, shard, hidden_size),), sends
     )
     wg_b = gate_up_all[0].reshape(width, hidden_size)
     wu_b = gate_up_all[1].reshape(width, hidden_size)
-    wd_b = down_all.reshape(hidden_size, width)
     x_rows = tokens[0].astype(FLOAT)
     mid_rows = x_rows + branch
     hn_b = rms_norm(mid_rows, g_ffn).astype(BF16)
@@ -946,6 +928,11 @@
         [gate_high, gate_low, jnp.zeros((rows, LANES - 2 * n_experts), BF16)], axis=1
     )
     hn_rows, gate_rows = rows_to_experts(5, hn_b, gate_lanes, pick, plane_experts, parts)
+    hn_rows, down_pay = lax.optimization_barrier((hn_rows, down_pay))
+    down_pieces = []
+    for s in range(plane_experts):
+        block = lax.dynamic_index_in_dim(down_pay, flip(place, s), 0, keepdims=False)
+        down_pieces.append(swap_f(block, s * parts) if s else block)
 
     n_rows = plane_experts * nsp * cap
     hn_in = hn_rows.reshape(n_rows, width)
@@ -972,6 +959,7 @@
         return total.astype(BF16)
 
     d_down = by_shard(contract_rows(hidden, d_result), (hid_shard, width))
+    d_down, down_pieces = lax.optimization_barrier((d_down, down_pieces))
     d_down = pair_total(
         d_down,
         [
@@ -985,6 +973,13 @@
         else lax.dynamic_index_in_dim(d_down, place, 0, keepdims=False)
         for s in range(plane_experts)
     ]
+    down_pieces = jnp.stack(down_pieces)
+    down_pieces = jnp.stack(
+        [swap_f(down_pieces, p) if p else down_pieces for p in range(parts)], axis=1
+    ).reshape(nf, hid_shard, width)
+    wd_b = jnp.take(
+        down_pieces, jnp.bitwise_xor(jnp.arange(nf, dtype=jnp.int32), f), axis=0, mode="clip"
+    ).reshape(hidden_size, width)
     result = matmul(hidden, wd_b)
     row_dgate = jnp.sum(result * dy_f, axis=1, keepdims=True)
     weighted = (row_gate * result).astype(BF16)

time: 1000 us -> 974 us (0.974)
  waiting for transfers between devices: 29.8 us -> 2.61 us
  matrix products: 117 us -> 127 us
    ppermute x9 -> x13, waiting for transfers between devices: 29.8 us -> 2.58 us  [swap_f(): return lax.ppermute(block, 'fsdp', [(i, i ^ mask) for i in range(nf)])]
    unnamed x256 -> x250, local copies, waits for them, and re-layouts: 43 us -> 38.7 us
  transfers between devices with their start and end apart: 11 -> 15, of which waited for: 6 -> 1; matrix products, arithmetic and copies ran while one was open for 19% -> 24% of each run, Pallas kernels for 47% -> 59%
where the time goes in v6:
time: 974 us; the launch traced here: 963 us
  Pallas kernels  626 us (64%)
  matrix products  127 us (13%)
  other arithmetic  89.5 us (9%)
  local copies, waits for them, and re-layouts  89.4 us (9%)
  between operations  16.7 us (2%)
  starting transfers between devices  12.5 us (1%)
    pallas_call x11, Pallas kernels, exchange(): pl.pallas_call(kernel, out_shape=[jax.ShapeDtypeStruct(shape, BF16) for s...  292 us
    pallas_call x1, Pallas kernels, line_sum(): pl.pallas_call(kernel, out_shape=[jax.ShapeDtypeStruct(a.shape, BF16) for...  163 us
    pallas_call x1, Pallas kernels, rows_from_experts(): pl.pallas_call(kernel, out_shape=[jax.ShapeDtypeStruct((planes, count, wi...  97.8 us
    pallas_call x1, Pallas kernels, rows_to_experts(): pl.pallas_call(kernel, out_shape=[jax.ShapeDtypeStruct((plane_experts, pl...  73.1 us
    unnamed x250, local copies, waits for them, and re-layouts  38.7 us
    dot_general x5, matrix products, contract_cols(): lax.dot_general(left_mat, right_mat, (((1,), (1,)), ((), ())), preferred_...  37.5 us
    dot_general x5, matrix products, contract_rows(): lax.dot_general(left_mat, right_mat, (((0,), (0,)), ((), ())), preferred_...  30.7 us
    dot_general x6, matrix products, matmul(): return jnp.dot(left_mat, right_mat, preferred_element_type=FLOAT)  26.9 us
  transfers between devices with their start and end apart: 15, of which 1 were waited for; matrix products, arithmetic and copies ran while one was open for 24% of the time, Pallas kernels for 59%

profile of v6, /device:TPU:0, one launch (start us, length us, event | category | flops | bytes accessed | tf_op | source)
XLA Modules:
  0.0 963.1 jit_solution(12546655042075999013)
XLA Ops:
  8.2 3.9 convert_element_type.389.refs_1_
  12.7 3.2 fusion.26
  21.5 60.9 %gather_inputs.1 = (bf16[8,144,2048]{2,1,0:T(8,128)(2,1)S(1)}, bf16[2048,768]{1,0:T(8,128)(2,1)S(1)}, bf16[4,128,2176]{2,1,0:T(8,128)(2,1)S(1)}) custom-call(bf16[144,2048]{1,0:T(8,128)(2,1)S(1)} %pad_maximum_fusion.9.refs_0_, bf16[256,4096]{1,0:T(8,128)(2,1)S(1)} %copy-done.4, bf16[256,512]{1,0:T(8,128)(2,1)S(1)} %convert_element_type.390.refs_2_, ...), custom_call_target="tpu_custom_call" | custom-call | bytes 195000000 | tf_op jit(solution)/shard_map/gather_inputs/pallas_call | solution.py:174
  86.3 3.6 constant_dynamic-slice_fusion
  106.2 3.4 fusion.107
  116.4 24.3 %gather_keys.1 = bf16[4,1024,256]{2,1,0:T(8,128)(2,1)S(1)} custom-call(bf16[1024,256]{1,0:T(8,128)(2,1)S(1)} %pad_maximum_fusion.10.refs_0_), custom_call_target="tpu_custom_call" | custom-call | bytes 72000000 | tf_op jit(solution)/shard_map/gather_keys/pallas_call | solution.py:174
  142.2 2.9 reshape.580
  145.1 2.8 multiply_reduce_fusion.2
  152.0 4.7 fusion.57
  156.7 9.6 fusion.105
  175.8 4.2 out_sum_pair.1
  188.2 3.3 dynamic-slice_convert_fusion
  197.6 26.6 %out_sum_plane.1 = (bf16[4,128,2048]{2,1,0:T(8,128)(2,1)S(1)}, bf16[2,8,256,768]{3,2,1,0:T(8,128)(2,1)S(1)}) custom-call(bf16[4,128,2048]{2,1,0:T(8,128)(2,1)S(1)} %fusion.10.refs_0_, bf16[2,256,768]{2,1,0:T(8,128)(2,1)S(1)} %copy-done.11, bf16[2,256,768]{2,1,0:T(8,128)(2,1)} %collective-permute-done.refs_2_, ...), custom_call_target="tpu_custom_call" | custom-call | bytes 81000000 | tf_op jit(solution)/shard_map/out_sum_plane/pallas_call | solution.py:174
  226.1 73.1 %rows_to_experts.1 = (bf16[4,4,80,2048]{3,2,1,0:T(8,128)(2,1)S(1)}, bf16[4,4,80,128]{3,2,1,0:T(8,128)(2,1)S(1)}) custom-call(bf16[128,2048]{1,0:T(8,128)(2,1)S(1)} %multiply_convert_fusion.6.tokens_ref, bf16[128,128]{1,0:T(8,128)(2,1)S(1)} %maximum_maximum_fusion.1.lanes_ref, bf16[4,320,128]{2,1,0:T(8,128)(2,1)S(1)} %copy-done.12), custom_call_target="tpu_custom_call" | custom-call | bytes 210000000 | tf_op jit(solution)/shard_map/rows_to_experts/pallas_call | solution.py:283
  305.5 4.3 fusion.108
  312.7 6.6 multiply_convert_fusion.3
  319.4 6.9 convolution_convert_fusion.5
  327.4 2.5 collective-permute-done.8
  337.1 4.4 gather_fusion
  341.5 13.0 %multiply_convert_fusion.1 = (bf16[1280,768]{1,0:T(8,128)(2,1)}, bf16[1280,768]{1,0:T(8,128)(2,1)}) fusion(f32[1280,768]{1,0:T(8,128)} %copy-done.113, f32[1280,768]{1,0:T(8,128)} %get-tuple-element.229, bf16[768,2048]{1,0:T(8,128)(2,1)} %bitcast.350, f32[1280]{0:T(1024)S(1)} %fusion.60, bf16[320,2048]{1,0:T(8,128)(2,1)} %copy-done.66, ...), kind=kOutput, calls=%fused_computation.36 | convolution fusion | flops 4065525760 | bytes 20190208 | tf_op jit(solution)/shard_map/dot_general | solution.py:50
  357.8 9.7 %multiply_convert_fusion = (bf16[1280,2048]{1,0:T(8,128)(2,1)}, f32[1280]{0:T(1024)S(1)}) fusion(f32[1280]{0:T(1024)S(1)} %fusion.60, bf16[320,2048]{1,0:T(8,128)(2,1)} %copy-done.66, bf16[320,2048]{1,0:T(8,128)(2,1)} %collective-permute-done.4, bf16[320,2048]{1,0:T(8,128)(2,1)} %collective-permute-done.3, bf16[320,2048]{1,0:T(8,128)(2,1)} %bitcast.364, ...), kind=kOutput, calls=%fused_computation.11 | convolution fusion | flops 4057987840 | bytes 15607808 | tf_op jit(solution)/shard_map/dot_general | solution.py:56
  368.1 8.9 fusion.109
  377.0 8.6 convolution_convert_fusion.3
  385.6 5.7 convolution_convert_fusion.4
  391.3 8.5 add_convert_fusion
  399.8 97.8 %rows_from_experts.1 = (bf16[4,128,2048]{2,1,0:T(8,128)(2,1)S(1)}, bf16[4,128,128]{2,1,0:T(8,128)(2,1)S(1)}, bf16[2,4,256,768]{3,2,1,0:T(8,128)(2,1)S(1)}) custom-call(bf16[4,4,80,2048]{3,2,1,0:T(8,128)(2,1)} %bitcast.344, bf16[4,4,80,128]{3,2,1,0:T(8,128)(2,1)S(1)} %maximum_maximum_fusion.lanes_ref, bf16[4,320,128]{2,1,0:T(8,128)(2,1)S(1)} %copy-done.12, ...), custom_call_target="tpu_custom_call" | custom-call | bytes 270000000 | tf_op jit(solution)/shard_map/rows_from_experts/pallas_call | solution.py:434
  505.9 27.0 %gather_grads.1 = bf16[8,128,2048]{2,1,0:T(8,128)(2,1)S(1)} custom-call(bf16[128,2048]{1,0:T(8,128)(2,1)S(1)} %fusion.95.refs_0_), custom_call_target="tpu_custom_call" | custom-call | bytes 90000000 | tf_op jit(solution)/shard_map/gather_grads/pallas_call | solution.py:174
  535.0 3.3 convolution_convert_fusion.14
  540.6 3.9 fusion.6
  544.5 4.6 fusion.7
  556.2 4.9 fusion.33
  561.2 3.7 convolution_convert_fusion.6.refs_1_
  564.9 2.7 key_grads_group.1
  570.3 80.3 %key_grads_planes.1 = (bf16[3,512,256]{2,1,0:T(8,128)(2,1)S(1)}, bf16[4,4,80,2048]{3,2,1,0:T(8,128)(2,1)S(1)}) custom-call(bf16[4,512,256]{2,1,0:T(8,128)(2,1)S(1)} %fusion.20.refs_0_, bf16[4,4,80,2048]{3,2,1,0:T(8,128)(2,1)S(1)} %bitcast.324), custom_call_target="tpu_custom_call" | custom-call | bytes 180000000 | tf_op jit(solution)/shard_map/key_grads_planes/pallas_call | solution.py:174
  656.4 9.2 bitcast_convert_fusion.2
  674.1 3.7 convolution_convert_fusion.1
  677.8 4.2 input_sum_pair.1
  682.9 26.2 %input_sum_plane.1 = bf16[4,128,2048]{2,1,0:T(8,128)(2,1)S(1)} custom-call(bf16[4,128,2048]{2,1,0:T(8,128)(2,1)S(1)} %fusion.9.refs_0_), custom_call_target="tpu_custom_call" | custom-call | bytes 81000000 | tf_op jit(solution)/shard_map/input_sum_plane/pallas_call | solution.py:174
  710.9 5.8 convolution_convert_fusion.2.refs_0_
  716.7 33.7 %head_grads_to_shards.1 = (bf16[256,4096]{1,0:T(8,128)(2,1)S(1)}, bf16[512,512]{1,0:T(8,128)(2,1)S(1)}, bf16[8,16,384]{2,1,0:T(8,128)(2,1)S(1)}) custom-call(bf16[2048,768]{1,0:T(8,128)(2,1)S(1)} %convolution_convert_fusion.2.refs_0_, bf16[8,16,384]{2,1,0:T(8,128)(2,1)S(1)} %bitcast.328), custom_call_target="tpu_custom_call" | custom-call | bytes 108000000 | tf_op jit(solution)/shard_map/head_grads_to_shards/pallas_call | solution.py:174
  751.7 3.9 convolution_convert_fusion.7.refs_4_
  755.7 163.1 %line_sum.1 = (bf16[256,4096]{1,0:T(8,128)(2,1)S(1)}, bf16[512,2048]{1,0:T(8,128)(2,1)S(1)}, bf16[512,512]{1,0:T(8,128)(2,1)S(1)}, bf16[16,384]{1,0:T(8,128)(2,1)S(1)}, bf16[3,128,2048]{2,1,0:T(8,128)(2,1)S(1)}) custom-call(bf16[256,4096]{1,0:T(8,128)(2,1)S(1)} %copy-done.19, bf16[512,2048]{1,0:T(8,128)(2,1)S(1)} %copy-done.17, ...), custom_call_target="tpu_custom_call" | custom-call | bytes 400000000 | tf_op jit(solution)/shard_map/line_sum/pallas_call | solution.py:572
  922.7 4.2 convert_element_type.483
  927.0 2.5 convert_element_type.485
  932.6 2.8 add_convert_fusion.2
  937.2 5.6 fusion.98
  942.8 6.5 bitcast_convert_fusion
  949.3 6.5 bitcast_convert_fusion.1
  (437 shorter events, 134.5 us)
Async XLA Ops:
  7.2 557.7 %all-gather.5.cloned.1.call-start = ((), (), s32[]{:S(2)}) async-start(), calls=%async_computation | async-start | bytes 7864320 | tf_op jit(solution)/shard_map/all_gather | solution.py:992
  92.3 7.7 copy-start.71
  92.3 10.0 %slice-start = ((s8[4718592]{0:T(1024)(128)(4,1)}), s8[4194304]{0:T(1024)(128)(4,1)S(1)}, s32[]{:S(2)}) async-start(s8[4718592]{0:T(1024)(128)(4,1)} %bitcast.314), calls=%async_computation.2 | async-start | bytes 8388608
  92.9 9.4 slice-start.1
  94.4 97.9 %collective-permute-start.2 = (bf16[512,2048]{1,0:T(8,128)(2,1)}, bf16[512,2048]{1,0:T(8,128)(2,1)}, u32[]{:S(2)}, u32[]{:S(2)}) collective-permute-start(bf16[512,2048]{1,0:T(8,128)(2,1)} %pad_maximum_fusion.3), channel_id=1, source_target_pairs={{0,6},{1,7},{2,4},{3,5},{4,2},{5,3},{6,0},{7,1},{8,14},{9,15},{10,... | collective-permute-start | bytes 6291464 | tf_op jit(solution)/shard_map/ppermute | solution.py:631
  95.1 101.4 %collective-permute-start = (bf16[2,256,768]{2,1,0:T(8,128)(2,1)}, bf16[2,256,768]{2,1,0:T(8,128)(2,1)}, u32[]{:S(2)}, u32[]{:S(2)}) collective-permute-start(bf16[2,256,768]{2,1,0:T(8,128)(2,1)} %get-tuple-element.186), channel_id=1, source_target_pairs={{0,2},{1,3},{2,0},{3,1},{4,6},{5,7},{6,4},{7,5},{8,10},{9,11},{10,... | collective-permute-start | bytes 2359304 | tf_op jit(solution)/shard_map/ppermute | solution.py:631
  96.4 100.1 %collective-permute-start.1 = (bf16[2,256,768]{2,1,0:T(8,128)(2,1)}, bf16[2,256,768]{2,1,0:T(8,128)(2,1)}, u32[]{:S(2)}, u32[]{:S(2)}) collective-permute-start(bf16[2,256,768]{2,1,0:T(8,128)(2,1)} %get-tuple-element.185), channel_id=1, source_target_pairs={{0,4},{1,5},{2,6},{3,7},{4,0},{5,1},{6,2},{7,3},{8,12},{9,13},{10,... | collective-permute-start | bytes 2359304 | tf_op jit(solution)/shard_map/ppermute | solution.py:631
  99.5 219.9 %collective-permute-start.3 = (bf16[320,2048]{1,0:T(8,128)(2,1)}, bf16[320,2048]{1,0:T(8,128)(2,1)}, u32[]{:S(2)}, u32[]{:S(2)}) collective-permute-start(bf16[320,2048]{1,0:T(8,128)(2,1)} %bitcast.39), channel_id=1, source_target_pairs={{0,2},{1,3},{2,0},{3,1},{4,6},{5,7},{6,4},{7,5},{8,10},{9,11},{10,... | collective-permute-start | bytes 3932168 | tf_op jit(solution)/shard_map/ppermute | solution.py:631
  101.6 217.8 %collective-permute-start.4 = (bf16[320,2048]{1,0:T(8,128)(2,1)}, bf16[320,2048]{1,0:T(8,128)(2,1)}, u32[]{:S(2)}, u32[]{:S(2)}) collective-permute-start(bf16[320,2048]{1,0:T(8,128)(2,1)} %bitcast.41), channel_id=1, source_target_pairs={{0,4},{1,5},{2,6},{3,7},{4,0},{5,1},{6,2},{7,3},{8,12},{9,13},{10,... | collective-permute-start | bytes 3932168 | tf_op jit(solution)/shard_map/ppermute | solution.py:631
  114.2 26.4 %copy-start.92 = (f32[128]{0:T(128)}, f32[128]{0:T(128)S(1)}, u32[]{:S(2)}) copy-start(f32[128]{0:T(128)S(1)} %reshape.618) | copy-start | bytes 1540
  115.8 34.5 %copy-start.61 = (f32[128,64]{1,0:T(8,128)}, f32[128,64]{1,0:T(8,128)S(1)}, u32[]{:S(2)}) copy-start(f32[128,64]{1,0:T(8,128)S(1)} %get-tuple-element.222) | copy-start | bytes 98308
  115.8 34.5 %copy-start.63 = (f32[128,64]{1,0:T(8,128)}, f32[128,64]{1,0:T(8,128)S(1)}, u32[]{:S(2)}) copy-start(f32[128,64]{1,0:T(8,128)S(1)} %get-tuple-element.223) | copy-start | bytes 98308
  185.7 124.1 %copy-start.96 = (f32[16]{0:T(128)}, f32[16]{0:T(128)S(1)}, u32[]{:S(2)}) copy-start(f32[16]{0:T(128)S(1)} %compare_convert_fusion) | copy-start | bytes 196
  185.7 5.7 copy-start.3
  185.7 5.7 copy-start.6
  197.6 27.0 %copy-start.31 = (bf16[1,128,2048]{2,1,0:T(8,128)(2,1)S(1)}, bf16[1,128,2048]{2,1,0:T(8,128)(2,1)}, u32[]{:S(2)}) copy-start(bf16[1,128,2048]{2,1,0:T(8,128)(2,1)} %param.15) | copy-start | bytes 1572868
  224.9 279.7 %copy-start.90 = (f32[128]{0:T(128)}, f32[128]{0:T(128)S(1)}, u32[]{:S(2)}) copy-start(f32[128]{0:T(128)S(1)} %fusion.83) | copy-start | bytes 1540
  299.3 13.4 %copy-start.22 = (bf16[4,4,80,2048]{3,2,1,0:T(8,128)(2,1)}, bf16[4,4,80,2048]{3,2,1,0:T(8,128)(2,1)S(1)}, u32[]{:S(2)}) copy-start(bf16[4,4,80,2048]{3,2,1,0:T(8,128)(2,1)S(1)} %get-tuple-element.60) | copy-start | bytes 15728644
  299.9 9.9 %copy-start.57 = (bf16[1,8,256,768]{3,2,1,0:T(8,128)(2,1)}, bf16[1,8,256,768]{3,2,1,0:T(8,128)(2,1)S(1)}, u32[]{:S(2)}) copy-start(bf16[1,8,256,768]{3,2,1,0:T(8,128)(2,1)S(1)} %get-tuple-element.180) | copy-start | bytes 9437188
  299.9 12.8 %copy-start.59 = (bf16[1,8,256,768]{3,2,1,0:T(8,128)(2,1)}, bf16[1,8,256,768]{3,2,1,0:T(8,128)(2,1)S(1)}, u32[]{:S(2)}) copy-start(bf16[1,8,256,768]{3,2,1,0:T(8,128)(2,1)S(1)} %get-tuple-element.181) | copy-start | bytes 9437188
  301.9 24.4 %collective-permute-start.5 = (bf16[96,2048]{1,0:T(8,128)(2,1)S(1)}, bf16[96,2048]{1,0:T(8,128)(2,1)S(1)}, u32[]{:S(2)}, u32[]{:S(2)}) collective-permute-start(bf16[96,2048]{1,0:T(8,128)(2,1)S(1)} %get-tuple-element.200), channel_id=1, source_target_pairs={{0,2},{1,3},{2,0},{3,1},{4,6},{5,7},{6,4},{7,5},{8,10},{9,11},{10,... | collective-permute-start | bytes 1179656 | tf_op jit(solution)/shard_map/ppermute | solution.py:631
  302.5 23.8 %collective-permute-start.6 = (bf16[96,2048]{1,0:T(8,128)(2,1)S(1)}, bf16[96,2048]{1,0:T(8,128)(2,1)S(1)}, u32[]{:S(2)}, u32[]{:S(2)}) collective-permute-start(bf16[96,2048]{1,0:T(8,128)(2,1)S(1)} %get-tuple-element.199), channel_id=1, source_target_pairs={{0,4},{1,5},{2,6},{3,7},{4,0},{5,1},{6,2},{7,3},{8,12},{9,13},{10,... | collective-permute-start | bytes 1179656 | tf_op jit(solution)/shard_map/ppermute | solution.py:631
  303.1 23.2 %collective-permute-start.7 = (bf16[96,2048]{1,0:T(8,128)(2,1)S(1)}, bf16[96,2048]{1,0:T(8,128)(2,1)S(1)}, u32[]{:S(2)}, u32[]{:S(2)}) collective-permute-start(bf16[96,2048]{1,0:T(8,128)(2,1)S(1)} %get-tuple-element.198), channel_id=1, source_target_pairs={{0,6},{1,7},{2,4},{3,5},{4,2},{5,3},{6,0},{7,1},{8,14},{9,15},{10,... | collective-permute-start | bytes 1179656 | tf_op jit(solution)/shard_map/ppermute | solution.py:631
  309.8 9.5 copy-start.113
  312.7 6.7 copy-start.66
  312.7 6.7 copy-start.65
  319.3 7.0 copy-start.116
  326.5 3.5 collective-permute-start.8
  326.8 8.3 collective-permute-start.12
  331.6 23.0 %collective-permute-start.10 = (bf16[96,2048]{1,0:T(8,128)(2,1)}, bf16[96,2048]{1,0:T(8,128)(2,1)S(1)}, u32[]{:S(2)}, u32[]{:S(2)}) collective-permute-start(bf16[96,2048]{1,0:T(8,128)(2,1)} %get-tuple-element.195), channel_id=1, source_target_pairs={{0,4},{1,5},{2,6},{3,7},{4,0},{5,1},{6,2},{7,3},{8,12},{9,13},{10,... | collective-permute-start | bytes 1179656 | tf_op jit(solution)/shard_map/ppermute | solution.py:631
  332.2 22.4 %collective-permute-start.11 = (bf16[96,2048]{1,0:T(8,128)(2,1)}, bf16[96,2048]{1,0:T(8,128)(2,1)}, u32[]{:S(2)}, u32[]{:S(2)}) collective-permute-start(bf16[96,2048]{1,0:T(8,128)(2,1)} %get-tuple-element.194), channel_id=1, source_target_pairs={{0,6},{1,7},{2,4},{3,5},{4,2},{5,3},{6,0},{7,1},{8,14},{9,15},{10,... | collective-permute-start | bytes 1179656 | tf_op jit(solution)/shard_map/ppermute | solution.py:631
  333.6 21.0 %collective-permute-start.9 = (bf16[96,2048]{1,0:T(8,128)(2,1)}, bf16[96,2048]{1,0:T(8,128)(2,1)}, u32[]{:S(2)}, u32[]{:S(2)}) collective-permute-start(bf16[96,2048]{1,0:T(8,128)(2,1)} %get-tuple-element.196), channel_id=1, source_target_pairs={{0,2},{1,3},{2,0},{3,1},{4,6},{5,7},{6,4},{7,5},{8,10},{9,11},{10,... | collective-permute-start | bytes 1179656 | tf_op jit(solution)/shard_map/ppermute | solution.py:631
  357.7 9.8 %copy-start.97 = (f32[16]{0:T(128)S(1)}, f32[16]{0:T(128)}, u32[]{:S(2)}) copy-start(f32[16]{0:T(128)} %copy-done.96) | copy-start | bytes 196
  357.8 10.3 %copy-start.114 = (bf16[1280,768]{1,0:T(8,128)(2,1)S(1)}, bf16[1280,768]{1,0:T(8,128)(2,1)}, u32[]{:S(2)}) copy-start(bf16[1280,768]{1,0:T(8,128)(2,1)} %get-tuple-element.70) | copy-start | bytes 5898244
  357.8 579.4 %all-gather.7.cloned.1.call-start = ((), (), s32[]{:S(2)}) async-start(), calls=%async_computation.1 | async-start | bytes 15728640 | tf_op jit(solution)/shard_map/all_gather | solution.py:1016
  368.0 17.5 %slice-start.2 = ((s8[5242880]{0:T(1024)(128)(4,1)}), s8[4194304]{0:T(1024)(128)(4,1)S(1)}, s32[]{:S(2)}) async-start(s8[5242880]{0:T(1024)(128)(4,1)} %bitcast.333), calls=%async_computation.4 | async-start | bytes 8388608
  377.0 8.6 slice-start.3
  377.0 8.6 copy-start.115
  385.6 5.7 copy-start.58
  504.5 51.2 %copy-start.104 = (f32[128]{0:T(128)}, f32[128]{0:T(128)S(1)}, u32[]{:S(2)}) copy-start(f32[128]{0:T(128)S(1)} %get-tuple-element.170) | copy-start | bytes 1540
  504.6 28.4 %copy-start.98 = (f32[128]{0:T(128)}, f32[128]{0:T(128)S(1)}, u32[]{:S(2)}) copy-start(f32[128]{0:T(128)S(1)} %multiply_multiply_fusion.3) | copy-start | bytes 1540
  505.9 29.1 %copy-start.108 = (f32[512,2048]{1,0:T(8,128)S(1)}, f32[512,2048]{1,0:T(8,128)}, u32[]{:S(2)}) copy-start(f32[512,2048]{1,0:T(8,128)} %param.23) | copy-start | bytes 12582916
  535.0 5.5 copy-start.38
  656.4 9.2 copy-start.52
  682.8 26.7 %copy-start.79 = (f32[1,2,8,128]{3,1,2,0:T(2,128)S(1)}, f32[1,2,8,128]{3,1,2,0:T(2,128)}, u32[]{:S(2)}) copy-start(f32[1,2,8,128]{3,1,2,0:T(2,128)} %copy-done.78) | copy-start | bytes 24580
  682.9 26.7 %copy-start.100 = (f32[128]{0:T(128)S(1)}, f32[128]{0:T(128)}, u32[]{:S(2)}) copy-start(f32[128]{0:T(128)} %fusion.84) | copy-start | bytes 1540
  716.6 35.0 %copy-start.70 = (pred[4,320,128]{2,1,0:T(32,128)(4,1)S(1)}, pred[4,320,128]{2,1,0:T(32,128)(4,1)}, u32[]{:S(2)}) copy-start(pred[4,320,128]{2,1,0:T(32,128)(4,1)} %get-tuple-element.219) | copy-start | bytes 491524
  927.0 5.6 copy-start.33
  (88 other events, 247.8 us)
Sparse Core Ops, SparseCore 0:
  357.9 160.9 all-gather.4
  521.0 238.8 all-gather.6

commit v7 on v6

--- a/solution.py
+++ b/solution.py
@@ -94,6 +94,17 @@
     dz: int
     df: int
     after: int | None = None
+    planes: tuple | None = None
+
+
+def only_on(planes, z, do):
+    if planes is None:
+        do()
+        return
+    here = z == planes[0]
+    for plane in planes[1:]:
+        here = jnp.logical_or(here, z == plane)
+    pl.when(here)(do)
 
 
 def exchange(name, cid, arrays, out_shapes, sends, micros):
@@ -152,13 +163,13 @@
                 if (s.dz, s.df) == (0, 0):
                     copies[k][1].wait()
                 else:
-                    copies[k].wait_recv()
+                    only_on(s.planes, flip(z, s.dz), copies[k].wait_recv)
 
         for k, s in enumerate(sends):
             if k in stays:
                 copies[k][0].start()
             elif s.after is None:
-                copies[k].start()
+                only_on(s.planes, z, copies[k].start)
         for k in stays:
             copies[k][0].wait()
             copies[k][1].start()
@@ -168,7 +179,7 @@
                 copies[k].start()
         for k, s in enumerate(sends):
             if (s.dz, s.df) != (0, 0):
-                copies[k].wait_send()
+                only_on(s.planes, z, copies[k].wait_send)
             arrive(k)
 
     result = pl.pallas_call(
@@ -456,7 +467,7 @@
     )(rows_in, lanes_in, pick, *weights)
 
 
-def line_sum(cid, arrays, pieces, blocks):
+def line_sum(cid, arrays, pieces, blocks, handed):
     n = len(arrays)
     chunks = [
         (k, c * (a.shape[0] // p), a.shape[0] // p)
@@ -464,12 +475,14 @@
         for c in range(p)
     ]
     far = blocks.shape[0] - 1
+    assert far == 3
 
     def kernel(*refs):
-        ins, blocks_ref = refs[:n], refs[n]
-        outs, others_ref = refs[n + 1 : 2 * n + 1], refs[2 * n + 1]
-        own, got, swapped = (refs[2 * n + 2 + n * i : 2 * n + 2 + n * (i + 1)] for i in range(3))
-        load, store, in_s, in_r, swap_s, swap_r, back_s, back_r, far_s, far_r = refs[5 * n + 2 :]
+        ins, blocks_ref, handed_ref = refs[:n], refs[n], refs[n + 1]
+        outs, others_ref = refs[n + 2 : 2 * n + 2], refs[2 * n + 2]
+        own, got, swapped = (refs[2 * n + 3 + n * i : 2 * n + 3 + n * (i + 1)] for i in range(3))
+        mine, theirs = refs[5 * n + 3 : 5 * n + 5]
+        load, store, in_s, in_r, swap_s, swap_r, back_s, back_r, far_s, far_r = refs[5 * n + 5 :]
         z = lax.axis_index("sp")
         f = lax.axis_index("fsdp")
         inner = jnp.logical_or(z == 1, z == 2)
@@ -500,17 +513,26 @@
             pltpu.make_async_copy(view(got, c), view(outs, c), store.at[c])
             for c in range(len(chunks))
         ]
-        far_copies = [
-            pltpu.make_async_remote_copy(
-                src_ref=blocks_ref.at[d],
-                dst_ref=others_ref.at[d - 1],
-                send_sem=far_s.at[d - 1],
-                recv_sem=far_r.at[d - 1],
+
+        def block_copy(src, dst, send, recv, d):
+            return pltpu.make_async_remote_copy(
+                src_ref=src,
+                dst_ref=dst,
+                send_sem=far_s.at[send],
+                recv_sem=far_r.at[recv],
                 device_id=(flip(z, d), f),
                 device_id_type=MESH,
             )
-            for d in range(1, far + 1)
+
+        near = block_copy(blocks_ref.at[1], others_ref.at[0], 0, 0, 1)
+        block_loads = [
+            pltpu.make_async_copy(blocks_ref.at[2 + k], mine.at[k], far_r.at[2 + k])
+            for k in range(2)
+        ] + [
+            pltpu.make_async_copy(handed_ref.at[k], theirs.at[k], far_r.at[4 + k])
+            for k in range(2)
         ]
+        beyond = [block_copy(mine.at[k], others_ref.at[1], 1 + k, 1, 2 + k) for k in range(2)]
         inwards = [remote(own, got, in_s, in_r, c, 1) for c in range(len(chunks))]
         swaps = [remote(own, swapped, swap_s, swap_r, c, 3) for c in range(len(chunks))]
         backs = [remote(got, got, back_s, back_r, c, 1) for c in range(len(chunks))]
@@ -529,13 +551,23 @@
 
             lax.fori_loop(0, size // step, rows, 0)
 
+        def pass_on(k):
+            def rows(i, carry):
+                at = pl.ds(pl.multiple_of(i * 16, 16), 16)
+                total = mine[k, at, :].astype(FLOAT) + theirs[1 - k, at, :].astype(FLOAT)
+                mine[k, at, :] = total.astype(BF16)
+                return carry
+
+            lax.fori_loop(0, blocks.shape[1] // 16, rows, 0)
+            beyond[k].start()
+
+        near.start()
+
         @pl.when(jnp.logical_not(inner))
         def _():
             for c in range(len(chunks)):
                 loads[c].wait()
                 inwards[c].start()
-            for copy in far_copies:
-                copy.start()
             for c in range(len(chunks)):
                 backs[c].wait_recv()
                 stores[c].start()
@@ -545,8 +577,12 @@
 
         @pl.when(inner)
         def _():
-            for copy in far_copies:
+            for copy in block_loads:
                 copy.start()
+            for copy in block_loads:
+                copy.wait()
+            for k in range(2):
+                pass_on(k)
             for c in range(len(chunks) + 1):
                 if c < len(chunks):
                     loads[c].wait()
@@ -563,8 +599,11 @@
                 backs[c].wait_send()
                 stores[c].wait()
 
-        for copy in far_copies:
-            copy.wait()
+            for copy in beyond:
+                copy.wait_send()
+
+        near.wait()
+        beyond[0].wait_recv()
 
     hbm = pl.BlockSpec(memory_space=pl.ANY)
     buffers = [pltpu.VMEM(a.shape, BF16) for a in arrays]
@@ -572,18 +611,19 @@
     return pl.pallas_call(
         kernel,
         out_shape=[jax.ShapeDtypeStruct(a.shape, BF16) for a in arrays]
-        + [jax.ShapeDtypeStruct((far,) + blocks.shape[1:], BF16)],
-        in_specs=[hbm] * (n + 1),
+        + [jax.ShapeDtypeStruct((2,) + blocks.shape[1:], BF16)],
+        in_specs=[hbm] * (n + 2),
         out_specs=[hbm] * (n + 1),
         scratch_shapes=buffers * 3
+        + [pltpu.VMEM((2,) + blocks.shape[1:], BF16)] * 2
         + [pltpu.SemaphoreType.DMA((count,))] * 8
-        + [pltpu.SemaphoreType.DMA((far,))] * 2,
+        + [pltpu.SemaphoreType.DMA((6,))] * 2,
         compiler_params=pltpu.CompilerParams(
             collective_id=cid, has_side_effects=True, vmem_limit_bytes=40 * 1024 * 1024
         ),
         cost_estimate=pl.CostEstimate(flops=0, bytes_accessed=int(4.0e8), transcendentals=0),
         name="line_sum",
-    )(*arrays, blocks)
+    )(*arrays, blocks, handed)
 
 
 def body(
@@ -801,21 +841,36 @@
         rms_norm(x_all[:, :rows, :].astype(FLOAT), g_attn).astype(BF16).reshape(seqs * rows, width)
     )
     qkv_lin = matmul(xn_b, w_qkv)
-    q_lin = qkv_lin[:, :q_cols].reshape(seqs, rows, my_heads, head_dim)
-    k_lin = qkv_lin[:, q_cols : q_cols + head_dim].reshape(seqs, rows, 1, head_dim)
+
+    def split_heads(flat):
+        flat = flat.reshape(seqs, rows, -1)
+        return jnp.stack(
+            [
+                flat[:, :, h * head_dim : (h + 1) * head_dim]
+                for h in range(flat.shape[2] // head_dim)
+            ],
+            axis=1,
+        )
+
+    def join_heads(split):
+        joined = jnp.concatenate([split[:, h] for h in range(split.shape[1])], axis=2)
+        return joined.reshape(seqs * rows, -1)
+
+    q_lin = split_heads(qkv_lin[:, :q_cols])
+    k_lin = split_heads(qkv_lin[:, q_cols : q_cols + head_dim])
     v_b = qkv_lin[:, q_cols + head_dim :].astype(BF16)
     half_dim = head_dim // 2
     inverse_freq = THETA ** (-(jnp.arange(half_dim, dtype=FLOAT) * 2.0 / head_dim))
     positions = (z * rows + jnp.arange(rows, dtype=jnp.int32)).astype(FLOAT)
     angles = positions[:, None] * inverse_freq[None, :]
-    cosine = jnp.cos(angles)[None, :, None, :]
-    sine_part = jnp.sin(angles)[None, :, None, :]
+    cosine = jnp.cos(angles)[None, None]
+    sine_part = jnp.sin(angles)[None, None]
 
     def prep_heads(linear, gain_vec):
         return rotate(rms_norm(linear, gain_vec), cosine, sine_part)
 
-    q_b = prep_heads(q_lin, g_query).astype(BF16)
-    k_b = prep_heads(k_lin, g_key).astype(BF16).reshape(seqs * rows, head_dim)
+    q_rows = prep_heads(q_lin, g_query).astype(BF16)
+    k_b = join_heads(prep_heads(k_lin, g_key).astype(BF16))
 
     kv_pay = jnp.concatenate([k_b, v_b], axis=1)
     piece = seqs * rows // rep
@@ -848,7 +903,6 @@
     keys = kv_seq[:, :, :head_dim]
     values = kv_seq[:, :, head_dim:]
 
-    q_rows = q_b.transpose(0, 2, 1, 3)
     plane_of = jnp.bitwise_xor(jnp.arange(nsp, dtype=jnp.int32), z)
     key_pos = (plane_of[:, None] * rows + jnp.arange(rows, dtype=jnp.int32)[None, :]).reshape(-1)
     query_pos = z * rows + jnp.arange(rows, dtype=jnp.int32)
@@ -856,12 +910,10 @@
     scores = (
         jnp.einsum("nhqd,nkd->nhqk", q_rows, keys, preferred_element_type=FLOAT) * score_scale
     )
-    scores = jnp.where(causal[None, None], scores, -1e30)
-    row_top = jnp.max(scores, axis=3, keepdims=True)
-    expo = jnp.exp(scores - row_top)
+    expo = jnp.where(causal[None, None], jnp.exp(scores), 0.0)
     probs = (expo / jnp.sum(expo, axis=3, keepdims=True)).astype(BF16)
-    o_rows = jnp.einsum("nhqk,nkd->nqhd", probs, values, preferred_element_type=FLOAT)
-    o_mat = o_rows.astype(BF16).reshape(seqs * rows, q_cols)
+    o_rows = jnp.einsum("nhqk,nkd->nhqd", probs, values, preferred_element_type=FLOAT)
+    o_mat = join_heads(o_rows.astype(BF16))
     wo_b = output_weight.astype(BF16)
 
     def pair_then_plane(partial, name, cid, more=(), more_shapes=(), more_sends=()):
@@ -1046,8 +1098,7 @@
     (da_all,) = exchange("gather_grads", 9, (d_attn_b,), ((nf, rows, width),), sends, 30)
     da_all = da_all.reshape(seqs * rows, width)
     d_wo = contract_rows(o_mat, da_all)
-    d_o = contract_cols(da_all, wo_b).astype(BF16).reshape(seqs, rows, my_heads, head_dim)
-    d_o = d_o.transpose(0, 2, 1, 3)
+    d_o = split_heads(contract_cols(da_all, wo_b).astype(BF16))
     d_val = jnp.einsum("nhqk,nhqd->nkd", probs, d_o, preferred_element_type=FLOAT)
     d_probs = jnp.einsum("nhqd,nkd->nhqk", d_o, values, preferred_element_type=FLOAT)
     probs_f = probs.astype(FLOAT)
@@ -1055,7 +1106,7 @@
         probs_f * (d_probs - jnp.sum(probs_f * d_probs, axis=3, keepdims=True))
     ).astype(BF16)
     dq = (
-        jnp.einsum("nhqk,nkd->nqhd", d_scores, keys, preferred_element_type=FLOAT) * score_scale
+        jnp.einsum("nhqk,nkd->nhqd", d_scores, keys, preferred_element_type=FLOAT) * score_scale
     ).astype(BF16)
     d_key = (
         jnp.einsum("nhqk,nhqd->nkd", d_scores, q_rows, preferred_element_type=FLOAT) * score_scale
@@ -1123,9 +1174,9 @@
     unused, q_pull = jax.vjp(prep_heads, q_lin, g_query)
     d_q_lin, d_q_gain = q_pull(dq.astype(FLOAT))
     unused, k_pull = jax.vjp(prep_heads, k_lin, g_key)
-    d_k_lin, d_k_gain = k_pull(d_kv[:, :head_dim].reshape(seqs, rows, 1, head_dim))
-    dq_b = d_q_lin.astype(BF16).reshape(seqs * rows, q_cols)
-    dk_b = d_k_lin.astype(BF16).reshape(seqs * rows, head_dim)
+    d_k_lin, d_k_gain = k_pull(d_kv[:, :head_dim].reshape(seqs, 1, rows, head_dim))
+    dq_b = join_heads(d_q_lin.astype(BF16))
+    dk_b = join_heads(d_k_lin.astype(BF16))
     dv_b = d_kv[:, head_dim:].astype(BF16)
     d_qkv = jnp.concatenate([dq_b, dk_b, dv_b], axis=1)
     share = 1.0 / rep
@@ -1178,14 +1229,26 @@
                     m,
                 )
             )
-    d_wq, d_wkv, small_shard = exchange(
+    if nsp == 4:
+        sends.append(
+            Send(
+                lambda i, o, z, f: i[2].at[pl.ds(2, 2)],
+                lambda i, o, z, f: o[3],
+                1,
+                0,
+                None,
+                (0, 3),
+            )
+        )
+    d_wq, d_wkv, small_shard, handed = exchange(
         "head_grads_to_shards",
         12,
-        (d_w_qkv, smalls.reshape(nf, small_rows, small_cols)),
+        (d_w_qkv, smalls.reshape(nf, small_rows, small_cols), out_blocks),
         (
             (shard, n_heads * head_dim),
             (2 * shard, kv_cols),
             (nf, small_rows, small_cols),
+            (2, rows, width),
         ),
         sends,
         36,
@@ -1193,9 +1256,9 @@
     small_sum = jnp.sum(small_shard.astype(FLOAT), axis=0).astype(BF16)
     if nsp == 4:
         sum_q, sum_out, sum_kv, small_sum, out_others = line_sum(
-            16, (d_wq, d_wo.astype(BF16), d_wkv, small_sum), (4, 4, 1, 1), out_blocks
+            16, (d_wq, d_wo.astype(BF16), d_wkv, small_sum), (4, 4, 1, 1), out_blocks, handed
         )
-        out_others = [out_others[d] for d in range(nsp - 1)]
+        out_others = [out_others[d] for d in range(2)]
     else:
         sum_q, sum_out, sum_kv, small_sum = lax.psum(
             (d_wq, d_wo.astype(BF16), d_wkv, small_sum), "sp"
@@ -1214,6 +1277,9 @@
     for size in (shard, shard, head_dim // nf, head_dim // nf, shard * n_experts):
         pieces.append(small_sum[at : at + size])
         at += size
+    grad_gate = all_gate_up[:, 0].astype(FLOAT).reshape(n_experts, shard, hidden_size)
+    all_gate_up, grad_gate = lax.optimization_barrier((all_gate_up, grad_gate))
+    grad_up = all_gate_up[:, 1].astype(FLOAT).reshape(n_experts, shard, hidden_size)
     return (
         mixed,
         grad_tokens,
@@ -1226,8 +1292,8 @@
         sum_out,
         pieces[1],
         pieces[4].reshape(shard, n_experts),
-        all_gate_up[:, 0].astype(FLOAT).reshape(n_experts, shard, hidden_size),
-        all_gate_up[:, 1].astype(FLOAT).reshape(n_experts, shard, hidden_size),
+        grad_gate,
+        grad_up,
         grad_down,
     )
 

time: 974 us -> 963 us (0.989)
  Pallas kernels: 626 us -> 616 us
    pallas_call x1, Pallas kernels: 163 us -> 142 us  [line_sum(): pl.pallas_call(kernel, out_shape=[jax.ShapeDtypeStruct(a.shape, BF16) for...]
    pallas_call x11, Pallas kernels: 292 us -> 304 us  [exchange(): pl.pallas_call(kernel, out_shape=[jax.ShapeDtypeStruct(shape, BF16) for s...]
    unnamed x250 -> x278, local copies, waits for them, and re-layouts: 38.7 us -> 48.7 us
  transfers between devices with their start and end apart: 15 -> 15, of which waited for: 1 -> 2; matrix products, arithmetic and copies ran while one was open for 24% -> 22% of each run, Pallas kernels for 59% -> 58%
where the time goes in v7:
time: 963 us; the launch traced here: 953 us
  Pallas kernels  616 us (64%)
  matrix products  123 us (13%)
  local copies, waits for them, and re-layouts  92.7 us (10%)
  other arithmetic  88.3 us (9%)
  between operations  16.6 us (2%)
  starting transfers between devices  12.5 us (1%)
    pallas_call x11, Pallas kernels, exchange(): pl.pallas_call(kernel, out_shape=[jax.ShapeDtypeStruct(shape, BF16) for s...  304 us
    pallas_call x1, Pallas kernels, line_sum(): pl.pallas_call(kernel, out_shape=[jax.ShapeDtypeStruct(a.shape, BF16) for...  142 us
    pallas_call x1, Pallas kernels, rows_from_experts(): pl.pallas_call(kernel, out_shape=[jax.ShapeDtypeStruct((planes, count, wi...  97.9 us
    pallas_call x1, Pallas kernels, rows_to_experts(): pl.pallas_call(kernel, out_shape=[jax.ShapeDtypeStruct((plane_experts, pl...  72.4 us
    unnamed x278, local copies, waits for them, and re-layouts  48.7 us
    dot_general x5, matrix products, contract_cols(): lax.dot_general(left_mat, right_mat, (((1,), (1,)), ((), ())), preferred_...  38.5 us
    dot_general x6, matrix products, matmul(): return jnp.dot(left_mat, right_mat, preferred_element_type=FLOAT)  28.8 us
    dot_general x5, matrix products, contract_rows(): lax.dot_general(left_mat, right_mat, (((0,), (0,)), ((), ())), preferred_...  28.6 us
  transfers between devices with their start and end apart: 15, of which 2 were waited for; matrix products, arithmetic and copies ran while one was open for 22% of the time, Pallas kernels for 58%

profile of v7, /device:TPU:0, one launch (start us, length us, event | category | flops | bytes accessed | tf_op | source)
XLA Modules:
  0.0 952.9 jit_solution(13997610291955126071)
XLA Ops:
  15.5 3.9 convert_element_type.379.refs_1_
  19.4 3.2 fusion.18
  28.3 60.9 %gather_inputs.1 = (bf16[8,144,2048]{2,1,0:T(8,128)(2,1)S(1)}, bf16[2048,768]{1,0:T(8,128)(2,1)S(1)}, bf16[4,128,2176]{2,1,0:T(8,128)(2,1)S(1)}) custom-call(bf16[144,2048]{1,0:T(8,128)(2,1)S(1)} %pad_maximum_fusion.10.refs_0_, bf16[256,4096]{1,0:T(8,128)(2,1)S(1)} %copy-done.4, bf16[256,512]{1,0:T(8,128)(2,1)S(1)} %copy-done.16, ...), custom_call_target="tpu_custom_call" | custom-call | bytes 195000000 | tf_op jit(solution)/shard_map/gather_inputs/pallas_call | solution.py:185
  93.1 3.6 constant_dynamic-slice_fusion
  104.9 2.7 reshape.586
  107.5 2.6 pad_maximum_fusion.4
  110.9 3.1 fusion.2
  115.5 3.0 fusion.4
  118.6 3.4 fusion.96
  126.2 24.3 %gather_keys.1 = bf16[4,1024,256]{2,1,0:T(8,128)(2,1)S(1)} custom-call(bf16[1024,256]{1,0:T(8,128)(2,1)S(1)} %pad_maximum_fusion.11.refs_0_), custom_call_target="tpu_custom_call" | custom-call | bytes 72000000 | tf_op jit(solution)/shard_map/gather_keys/pallas_call | solution.py:185
  168.9 2.6 slice_bitcast_fusion.27
  171.4 4.5 convolution_convert_fusion
  176.0 4.2 out_sum_pair.1
  183.6 2.6 convolution_convert_fusion.9
  186.2 3.4 dynamic-slice_convert_fusion
  196.9 26.1 %out_sum_plane.1 = (bf16[4,128,2048]{2,1,0:T(8,128)(2,1)S(1)}, bf16[2,8,256,768]{3,2,1,0:T(8,128)(2,1)S(1)}) custom-call(bf16[4,128,2048]{2,1,0:T(8,128)(2,1)S(1)} %fusion.9.refs_0_, bf16[2,256,768]{2,1,0:T(8,128)(2,1)S(1)} %copy-done.9, bf16[2,256,768]{2,1,0:T(8,128)(2,1)} %collective-permute-done.refs_2_, ...), custom_call_target="tpu_custom_call" | custom-call | bytes 81000000 | tf_op jit(solution)/shard_map/out_sum_plane/pallas_call | solution.py:185
  226.2 72.4 %rows_to_experts.1 = (bf16[4,4,80,2048]{3,2,1,0:T(8,128)(2,1)S(1)}, bf16[4,4,80,128]{3,2,1,0:T(8,128)(2,1)S(1)}) custom-call(bf16[128,2048]{1,0:T(8,128)(2,1)S(1)} %multiply_convert_fusion.6.tokens_ref, bf16[128,128]{1,0:T(8,128)(2,1)S(1)} %maximum_maximum_fusion.1.lanes_ref, bf16[4,320,128]{2,1,0:T(8,128)(2,1)S(1)} %get-tuple-element.228.pick_ref), custom_call_target="tpu_custom_call" | custom-call | bytes 210000000 | tf_op jit(solution)/shard_map/rows_to_experts/pallas_call | solution.py:294
  303.5 4.3 fusion.97
  310.3 6.6 multiply_convert_fusion.3
  317.0 6.7 convolution_convert_fusion.5
  324.8 2.5 collective-permute-done.8
  334.4 4.4 gather_fusion
  338.8 13.0 %multiply_convert_fusion.1 = (bf16[1280,768]{1,0:T(8,128)(2,1)}, bf16[1280,768]{1,0:T(8,128)(2,1)}) fusion(f32[1280,768]{1,0:T(8,128)} %copy-done.122, f32[1280,768]{1,0:T(8,128)} %get-tuple-element.239, bf16[768,2048]{1,0:T(8,128)(2,1)} %bitcast.377, f32[1280]{0:T(1024)S(1)} %fusion.52, bf16[320,2048]{1,0:T(8,128)(2,1)} %copy-done.85, ...), kind=kOutput, calls=%fused_computation.32 | convolution fusion | flops 4065525760 | bytes 20190208 | tf_op jit(solution)/shard_map/dot_general | solution.py:50
  355.0 9.5 multiply_convert_fusion
  365.0 11.0 %fusion.98 = f32[1280,2048]{1,0:T(8,128)} fusion(bf16[1280,768]{1,0:T(8,128)(2,1)} %get-tuple-element.73, bf16[2048,768]{1,0:T(8,128)(2,1)} %bitcast.384), kind=kOutput, calls=%fused_computation.284 | convolution fusion | flops 4026531840 | bytes 15597568 | tf_op jit(solution)/shard_map/dot_general | solution.py:50
  376.0 8.6 convolution_convert_fusion.3
  384.7 5.7 convolution_convert_fusion.4
  390.4 8.5 add_convert_fusion
  398.9 97.9 %rows_from_experts.1 = (bf16[4,128,2048]{2,1,0:T(8,128)(2,1)S(1)}, bf16[4,128,128]{2,1,0:T(8,128)(2,1)S(1)}, bf16[2,4,256,768]{3,2,1,0:T(8,128)(2,1)S(1)}) custom-call(bf16[4,4,80,2048]{3,2,1,0:T(8,128)(2,1)} %bitcast.368, bf16[4,4,80,128]{3,2,1,0:T(8,128)(2,1)S(1)} %maximum_maximum_fusion.lanes_ref, bf16[4,320,128]{2,1,0:T(8,128)(2,1)S(1)} %get-tuple-element.228.pick_ref, ...), custom_call_target="tpu_custom_call" | custom-call | bytes 270000000 | tf_op jit(solution)/shard_map/rows_from_experts/pallas_call | solution.py:445
  505.0 27.0 %gather_grads.1 = bf16[8,128,2048]{2,1,0:T(8,128)(2,1)S(1)} custom-call(bf16[128,2048]{1,0:T(8,128)(2,1)S(1)} %fusion.86.refs_0_), custom_call_target="tpu_custom_call" | custom-call | bytes 90000000 | tf_op jit(solution)/shard_map/gather_grads/pallas_call | solution.py:185
  538.5 4.9 fusion.6
  543.5 4.1 fusion.17
  554.3 3.8 bitcast_convert_fusion.3.refs_1_
  558.1 2.7 key_grads_group.1
  563.5 79.5 %key_grads_planes.1 = (bf16[3,512,256]{2,1,0:T(8,128)(2,1)S(1)}, bf16[4,4,80,2048]{3,2,1,0:T(8,128)(2,1)S(1)}) custom-call(bf16[4,512,256]{2,1,0:T(8,128)(2,1)S(1)} %fusion.16.refs_0_, bf16[4,4,80,2048]{3,2,1,0:T(8,128)(2,1)S(1)} %bitcast.346), custom_call_target="tpu_custom_call" | custom-call | bytes 180000000 | tf_op jit(solution)/shard_map/key_grads_planes/pallas_call | solution.py:185
  648.6 9.3 bitcast_convert_fusion.2
  662.0 4.2 fusion.15
  670.6 3.7 convolution_convert_fusion.1
  674.3 4.2 input_sum_pair.1
  679.4 26.3 %input_sum_plane.1 = bf16[4,128,2048]{2,1,0:T(8,128)(2,1)S(1)} custom-call(bf16[4,128,2048]{2,1,0:T(8,128)(2,1)S(1)} %fusion.8.refs_0_), custom_call_target="tpu_custom_call" | custom-call | bytes 81000000 | tf_op jit(solution)/shard_map/input_sum_plane/pallas_call | solution.py:185
  707.6 3.9 convolution_convert_fusion.6.refs_2_.refs_4_
  711.8 3.8 convolution_convert_fusion.2.refs_0_
  715.5 47.1 %head_grads_to_shards.1 = (bf16[256,4096]{1,0:T(8,128)(2,1)S(1)}, bf16[512,512]{1,0:T(8,128)(2,1)S(1)}, bf16[8,16,384]{2,1,0:T(8,128)(2,1)S(1)}, bf16[2,128,2048]{2,1,0:T(8,128)(2,1)S(1)}) custom-call(bf16[2048,768]{1,0:T(8,128)(2,1)S(1)} %convolution_convert_fusion.2.refs_0_, bf16[8,16,384]{2,1,0:T(8,128)(2,1)S(1)} %bitcast.350, ...), custom_call_target="tpu_custom_call" | custom-call | bytes 108000000 | tf_op jit(solution)/shard_map/head_grads_to_shards/pallas_call | solution.py:185
  769.3 142.1 %line_sum.1 = (bf16[256,4096]{1,0:T(8,128)(2,1)S(1)}, bf16[512,2048]{1,0:T(8,128)(2,1)S(1)}, bf16[512,512]{1,0:T(8,128)(2,1)S(1)}, bf16[16,384]{1,0:T(8,128)(2,1)S(1)}, bf16[2,128,2048]{2,1,0:T(8,128)(2,1)S(1)}) custom-call(bf16[256,4096]{1,0:T(8,128)(2,1)S(1)} %copy-done.15, bf16[512,2048]{1,0:T(8,128)(2,1)S(1)} %copy-done.13, ...), custom_call_target="tpu_custom_call" | custom-call | bytes 400000000 | tf_op jit(solution)/shard_map/line_sum/pallas_call | solution.py:611
  915.9 4.2 convert_element_type.470
  928.6 3.3 slice.314
  931.9 6.5 bitcast_convert_fusion.1
  939.1 6.5 bitcast_convert_fusion
  (463 shorter events, 144.1 us)
Async XLA Ops:
  7.2 550.9 %all-gather.5.cloned.1.call-start = ((), (), s32[]{:S(2)}) async-start(), calls=%async_computation | async-start | bytes 7864320 | tf_op jit(solution)/shard_map/all_gather | solution.py:1044
  96.7 99.1 %collective-permute-start.1 = (bf16[2,256,768]{2,1,0:T(8,128)(2,1)}, bf16[2,256,768]{2,1,0:T(8,128)(2,1)}, u32[]{:S(2)}, u32[]{:S(2)}) collective-permute-start(bf16[2,256,768]{2,1,0:T(8,128)(2,1)} %get-tuple-element.175), channel_id=1, source_target_pairs={{0,4},{1,5},{2,6},{3,7},{4,0},{5,1},{6,2},{7,3},{8,12},{9,13},{10,... | collective-permute-start | bytes 2359304 | tf_op jit(solution)/shard_map/ppermute | solution.py:671
  97.2 98.6 %collective-permute-start = (bf16[2,256,768]{2,1,0:T(8,128)(2,1)}, bf16[2,256,768]{2,1,0:T(8,128)(2,1)}, u32[]{:S(2)}, u32[]{:S(2)}) collective-permute-start(bf16[2,256,768]{2,1,0:T(8,128)(2,1)} %get-tuple-element.176), channel_id=1, source_target_pairs={{0,2},{1,3},{2,0},{3,1},{4,6},{5,7},{6,4},{7,5},{8,10},{9,11},{10,... | collective-permute-start | bytes 2359304 | tf_op jit(solution)/shard_map/ppermute | solution.py:671
  98.4 6.0 copy-start.92
  100.0 216.9 %collective-permute-start.3 = (bf16[320,2048]{1,0:T(8,128)(2,1)}, bf16[320,2048]{1,0:T(8,128)(2,1)}, u32[]{:S(2)}, u32[]{:S(2)}) collective-permute-start(bf16[320,2048]{1,0:T(8,128)(2,1)} %bitcast.50), channel_id=1, source_target_pairs={{0,2},{1,3},{2,0},{3,1},{4,6},{5,7},{6,4},{7,5},{8,10},{9,11},{10,... | collective-permute-start | bytes 3932168 | tf_op jit(solution)/shard_map/ppermute | solution.py:671
  102.8 214.1 %collective-permute-start.4 = (bf16[320,2048]{1,0:T(8,128)(2,1)}, bf16[320,2048]{1,0:T(8,128)(2,1)}, u32[]{:S(2)}, u32[]{:S(2)}) collective-permute-start(bf16[320,2048]{1,0:T(8,128)(2,1)} %bitcast.52), channel_id=1, source_target_pairs={{0,4},{1,5},{2,6},{3,7},{4,0},{5,1},{6,2},{7,3},{8,12},{9,13},{10,... | collective-permute-start | bytes 3932168 | tf_op jit(solution)/shard_map/ppermute | solution.py:671
  110.2 81.4 %collective-permute-start.2 = (bf16[512,2048]{1,0:T(8,128)(2,1)}, bf16[512,2048]{1,0:T(8,128)(2,1)}, u32[]{:S(2)}, u32[]{:S(2)}) collective-permute-start(bf16[512,2048]{1,0:T(8,128)(2,1)} %pad_maximum_fusion.4), channel_id=1, source_target_pairs={{0,6},{1,7},{2,4},{3,5},{4,2},{5,3},{6,0},{7,1},{8,14},{9,15},{10,... | collective-permute-start | bytes 6291464 | tf_op jit(solution)/shard_map/ppermute | solution.py:671
  124.0 29.9 %copy-start.114 = (f32[128]{0:T(128)}, f32[128]{0:T(128)S(1)}, u32[]{:S(2)}) copy-start(f32[128]{0:T(128)S(1)} %reshape.618) | copy-start | bytes 1540
  124.1 26.5 %copy-start.112 = (f32[128]{0:T(128)}, f32[128]{0:T(128)S(1)}, u32[]{:S(2)}) copy-start(f32[128]{0:T(128)S(1)} %reshape.619) | copy-start | bytes 1540
  124.4 31.0 %copy-start.77 = (f32[128,64]{1,0:T(8,128)}, f32[128,64]{1,0:T(8,128)S(1)}, u32[]{:S(2)}) copy-start(f32[128,64]{1,0:T(8,128)S(1)} %get-tuple-element.232) | copy-start | bytes 98308
  124.4 31.0 %copy-start.79 = (f32[128,64]{1,0:T(8,128)}, f32[128,64]{1,0:T(8,128)S(1)}, u32[]{:S(2)}) copy-start(f32[128,64]{1,0:T(8,128)S(1)} %get-tuple-element.233) | copy-start | bytes 98308
  150.7 10.0 %copy-start.59 = (bf16[8,4,128,256]{3,2,1,0:T(8,128)(2,1)}, bf16[8,4,128,256]{3,2,1,0:T(8,128)(2,1)S(1)}, u32[]{:S(2)}) copy-start(bf16[8,4,128,256]{3,2,1,0:T(8,128)(2,1)S(1)} %copy.139) | copy-start | bytes 6291460
  183.6 6.0 copy-start.3
  225.4 73.3 %copy-start.58 = (bf16[4,96,2048]{2,1,0:T(8,128)(2,1)S(1)}, bf16[4,96,2048]{2,1,0:T(8,128)(2,1)}, u32[]{:S(2)}) copy-start(bf16[4,96,2048]{2,1,0:T(8,128)(2,1)} %dynamic-slice_convert_fusion) | copy-start | bytes 4718596
  298.7 11.6 %copy-start.22 = (bf16[4,4,80,2048]{3,2,1,0:T(8,128)(2,1)}, bf16[4,4,80,2048]{3,2,1,0:T(8,128)(2,1)S(1)}, u32[]{:S(2)}) copy-start(bf16[4,4,80,2048]{3,2,1,0:T(8,128)(2,1)S(1)} %get-tuple-element.63) | copy-start | bytes 15728644
  298.9 24.8 %collective-permute-start.7 = (bf16[96,2048]{1,0:T(8,128)(2,1)S(1)}, bf16[96,2048]{1,0:T(8,128)(2,1)S(1)}, u32[]{:S(2)}, u32[]{:S(2)}) collective-permute-start(bf16[96,2048]{1,0:T(8,128)(2,1)S(1)} %get-tuple-element.192), channel_id=1, source_target_pairs={{0,6},{1,7},{2,4},{3,5},{4,2},{5,3},{6,0},{7,1},{8,14},{9,15},{10,... | collective-permute-start | bytes 1179656 | tf_op jit(solution)/shard_map/ppermute | solution.py:671
  299.6 24.1 %collective-permute-start.6 = (bf16[96,2048]{1,0:T(8,128)(2,1)S(1)}, bf16[96,2048]{1,0:T(8,128)(2,1)S(1)}, u32[]{:S(2)}, u32[]{:S(2)}) collective-permute-start(bf16[96,2048]{1,0:T(8,128)(2,1)S(1)} %get-tuple-element.193), channel_id=1, source_target_pairs={{0,4},{1,5},{2,6},{3,7},{4,0},{5,1},{6,2},{7,3},{8,12},{9,13},{10,... | collective-permute-start | bytes 1179656 | tf_op jit(solution)/shard_map/ppermute | solution.py:671
  301.0 22.7 %collective-permute-start.5 = (bf16[96,2048]{1,0:T(8,128)(2,1)S(1)}, bf16[96,2048]{1,0:T(8,128)(2,1)S(1)}, u32[]{:S(2)}, u32[]{:S(2)}) collective-permute-start(bf16[96,2048]{1,0:T(8,128)(2,1)S(1)} %get-tuple-element.194), channel_id=1, source_target_pairs={{0,2},{1,3},{2,0},{3,1},{4,6},{5,7},{6,4},{7,5},{8,10},{9,11},{10,... | collective-permute-start | bytes 1179656 | tf_op jit(solution)/shard_map/ppermute | solution.py:671
  303.0 4.8 copy-start.73
  303.1 7.2 copy-start.75
  307.8 9.1 copy-start.122
  310.3 6.7 copy-start.85
  310.3 6.7 copy-start.83
  316.9 6.7 copy-start.125
  323.8 3.5 collective-permute-start.8
  324.2 8.3 collective-permute-start.12
  329.0 22.8 %collective-permute-start.11 = (bf16[96,2048]{1,0:T(8,128)(2,1)}, bf16[96,2048]{1,0:T(8,128)(2,1)S(1)}, u32[]{:S(2)}, u32[]{:S(2)}) collective-permute-start(bf16[96,2048]{1,0:T(8,128)(2,1)} %get-tuple-element.188), channel_id=1, source_target_pairs={{0,6},{1,7},{2,4},{3,5},{4,2},{5,3},{6,0},{7,1},{8,14},{9,15},{10,... | collective-permute-start | bytes 1179656 | tf_op jit(solution)/shard_map/ppermute | solution.py:671
  329.6 22.2 %collective-permute-start.10 = (bf16[96,2048]{1,0:T(8,128)(2,1)}, bf16[96,2048]{1,0:T(8,128)(2,1)}, u32[]{:S(2)}, u32[]{:S(2)}) collective-permute-start(bf16[96,2048]{1,0:T(8,128)(2,1)} %get-tuple-element.189), channel_id=1, source_target_pairs={{0,4},{1,5},{2,6},{3,7},{4,0},{5,1},{6,2},{7,3},{8,12},{9,13},{10,... | collective-permute-start | bytes 1179656 | tf_op jit(solution)/shard_map/ppermute | solution.py:671
  331.0 20.8 %collective-permute-start.9 = (bf16[96,2048]{1,0:T(8,128)(2,1)}, bf16[96,2048]{1,0:T(8,128)(2,1)}, u32[]{:S(2)}, u32[]{:S(2)}) collective-permute-start(bf16[96,2048]{1,0:T(8,128)(2,1)} %get-tuple-element.190), channel_id=1, source_target_pairs={{0,2},{1,3},{2,0},{3,1},{4,6},{5,7},{6,4},{7,5},{8,10},{9,11},{10,... | collective-permute-start | bytes 1179656 | tf_op jit(solution)/shard_map/ppermute | solution.py:671
  334.4 4.5 copy-start.84
  355.0 573.6 %all-gather.7.cloned.1.call-start = ((), (), s32[]{:S(2)}) async-start(), calls=%async_computation.1 | async-start | bytes 15728640 | tf_op jit(solution)/shard_map/all_gather | solution.py:1068
  365.0 11.0 %copy-start.123 = (bf16[1280,768]{1,0:T(8,128)(2,1)S(1)}, bf16[1280,768]{1,0:T(8,128)(2,1)}, u32[]{:S(2)}) copy-start(bf16[1280,768]{1,0:T(8,128)(2,1)} %get-tuple-element.73) | copy-start | bytes 5898244
  365.0 19.6 %slice-start = ((s8[5242880]{0:T(1024)(128)(4,1)}), s8[4194304]{0:T(1024)(128)(4,1)S(1)}, s32[]{:S(2)}) async-start(s8[5242880]{0:T(1024)(128)(4,1)} %bitcast.355), calls=%async_computation.2 | async-start | bytes 8388608
  376.0 8.6 slice-start.1
  376.0 8.6 copy-start.124
  384.6 5.7 copy-start.74
  503.5 28.5 %copy-start.116 = (f32[128]{0:T(128)}, f32[128]{0:T(128)S(1)}, u32[]{:S(2)}) copy-start(f32[128]{0:T(128)S(1)} %multiply_multiply_fusion.4) | copy-start | bytes 1540
  505.0 27.0 %copy-start.121 = (f32[512,2048]{1,0:T(8,128)S(1)}, f32[512,2048]{1,0:T(8,128)}, u32[]{:S(2)}) copy-start(f32[512,2048]{1,0:T(8,128)} %param.23) | copy-start | bytes 12582916
  532.1 6.4 slice-start.2
  538.5 4.9 copy-start.87
  538.5 4.9 copy-start.89
  648.6 9.3 copy-start.90
  707.6 4.2 copy-start.82
  915.9 4.3 copy-start.11
  920.2 4.8 copy-start.33
  928.6 9.9 %slice-start.4 = ((s8[12582912]{0:T(1024)(128)(4,1)}), s8[4194304]{0:T(1024)(128)(4,1)S(1)}, s32[]{:S(2)}) async-start(s8[12582912]{0:T(1024)(128)(4,1)} %bitcast.362), calls=%async_computation.6 | async-start | bytes 8388608
  928.6 9.9 %slice-start.5 = ((s8[12582912]{0:T(1024)(128)(4,1)}), s8[4194304]{0:T(1024)(128)(4,1)S(1)}, s32[]{:S(2)}) async-start(s8[12582912]{0:T(1024)(128)(4,1)} %bitcast.362), calls=%async_computation.7 | async-start | bytes 8388608
  931.9 6.6 slice-start.6
  (101 other events, 196.3 us)
Sparse Core Ops, SparseCore 0:
  355.1 160.9 all-gather.4
  518.2 251.3 all-gather.6

commit v8 on v7

--- a/solution.py
+++ b/solution.py
@@ -478,11 +478,11 @@
     assert far == 3
 
     def kernel(*refs):
-        ins, blocks_ref, handed_ref = refs[:n], refs[n], refs[n + 1]
-        outs, others_ref = refs[n + 2 : 2 * n + 2], refs[2 * n + 2]
-        own, got, swapped = (refs[2 * n + 3 + n * i : 2 * n + 3 + n * (i + 1)] for i in range(3))
-        mine, theirs = refs[5 * n + 3 : 5 * n + 5]
-        load, store, in_s, in_r, swap_s, swap_r, back_s, back_r, far_s, far_r = refs[5 * n + 5 :]
+        ins, blocks_ref, handed_refs = refs[:n], refs[n], refs[n + 1 : n + 3]
+        outs, others_ref = refs[n + 3 : 2 * n + 3], refs[2 * n + 3]
+        own, got, swapped = (refs[2 * n + 4 + n * i : 2 * n + 4 + n * (i + 1)] for i in range(3))
+        mine, theirs = refs[5 * n + 4 : 5 * n + 6]
+        load, store, in_s, in_r, swap_s, swap_r, back_s, back_r, far_s, far_r = refs[5 * n + 6 :]
         z = lax.axis_index("sp")
         f = lax.axis_index("fsdp")
         inner = jnp.logical_or(z == 1, z == 2)
@@ -529,7 +529,7 @@
             pltpu.make_async_copy(blocks_ref.at[2 + k], mine.at[k], far_r.at[2 + k])
             for k in range(2)
         ] + [
-            pltpu.make_async_copy(handed_ref.at[k], theirs.at[k], far_r.at[4 + k])
+            pltpu.make_async_copy(handed_refs[k], theirs.at[k], far_r.at[4 + k])
             for k in range(2)
         ]
         beyond = [block_copy(mine.at[k], others_ref.at[1], 1 + k, 1, 2 + k) for k in range(2)]
@@ -561,13 +561,12 @@
             lax.fori_loop(0, blocks.shape[1] // 16, rows, 0)
             beyond[k].start()
 
-        near.start()
-
         @pl.when(jnp.logical_not(inner))
         def _():
             for c in range(len(chunks)):
                 loads[c].wait()
                 inwards[c].start()
+            near.start()
             for c in range(len(chunks)):
                 backs[c].wait_recv()
                 stores[c].start()
@@ -577,6 +576,7 @@
 
         @pl.when(inner)
         def _():
+            near.start()
             for copy in block_loads:
                 copy.start()
             for copy in block_loads:
@@ -612,7 +612,7 @@
         kernel,
         out_shape=[jax.ShapeDtypeStruct(a.shape, BF16) for a in arrays]
         + [jax.ShapeDtypeStruct((2,) + blocks.shape[1:], BF16)],
-        in_specs=[hbm] * (n + 2),
+        in_specs=[hbm] * (n + 3),
         out_specs=[hbm] * (n + 1),
         scratch_shapes=buffers * 3
         + [pltpu.VMEM((2,) + blocks.shape[1:], BF16)] * 2
@@ -623,7 +623,7 @@
         ),
         cost_estimate=pl.CostEstimate(flops=0, bytes_accessed=int(4.0e8), transcendentals=0),
         name="line_sum",
-    )(*arrays, blocks, handed)
+    )(*arrays, blocks, *handed)
 
 
 def body(
@@ -1182,7 +1182,16 @@
     share = 1.0 / rep
     d_qkv_shared = jnp.concatenate([dq_b, dk_b * BF16(share), dv_b * BF16(share)], axis=1)
     d_w_qkv = contract_rows(xn_b, d_qkv).astype(BF16)
-    d_xn, unused = pair_then_plane(contract_cols(d_qkv_shared, w_qkv), "input_sum", 13)
+
+    def hand_over(which, i_at, o_at):
+        return Send(
+            lambda i, o, z, f: i[i_at].at[which], lambda i, o, z, f: o[o_at], 1, 0, None, (0, 3)
+        )
+
+    more = ((), (), ())
+    if nsp == 4:
+        more = ((out_blocks,), ((rows, width),), (hand_over(2, 1, 1),))
+    d_xn, handed = pair_then_plane(contract_cols(d_qkv_shared, w_qkv), "input_sum", 13, *more)
     unused, attn_pull = jax.vjp(rms_norm, x_rows, g_attn)
     d_x_norm, d_attn_gain = attn_pull(d_xn)
     grad_tokens = (d_mid + d_x_norm)[None]
@@ -1230,17 +1239,8 @@
                 )
             )
     if nsp == 4:
-        sends.append(
-            Send(
-                lambda i, o, z, f: i[2].at[pl.ds(2, 2)],
-                lambda i, o, z, f: o[3],
-                1,
-                0,
-                None,
-                (0, 3),
-            )
-        )
-    d_wq, d_wkv, small_shard, handed = exchange(
+        sends.append(hand_over(3, 2, 3))
+    d_wq, d_wkv, small_shard, handed_last = exchange(
         "head_grads_to_shards",
         12,
         (d_w_qkv, smalls.reshape(nf, small_rows, small_cols), out_blocks),
@@ -1248,7 +1248,7 @@
             (shard, n_heads * head_dim),
             (2 * shard, kv_cols),
             (nf, small_rows, small_cols),
-            (2, rows, width),
+            (rows, width),
         ),
         sends,
         36,
@@ -1256,7 +1256,7 @@
     small_sum = jnp.sum(small_shard.astype(FLOAT), axis=0).astype(BF16)
     if nsp == 4:
         sum_q, sum_out, sum_kv, small_sum, out_others = line_sum(
-            16, (d_wq, d_wo.astype(BF16), d_wkv, small_sum), (4, 4, 1, 1), out_blocks, handed
+            16, (d_wq, d_wo.astype(BF16), d_wkv, small_sum), (8, 8, 2, 1), out_blocks, (handed[0], handed_last)
         )
         out_others = [out_others[d] for d in range(2)]
     else:

time: 963 us -> 949 us (0.985)
  Pallas kernels: 616 us -> 605 us
    pallas_call x11, Pallas kernels: 304 us -> 290 us  [exchange(): pl.pallas_call(kernel, out_shape=[jax.ShapeDtypeStruct(shape, BF16) for s...]
    unnamed x278 -> x260, local copies, waits for them, and re-layouts: 48.7 us -> 49.7 us
where the time goes in v8:
time: 949 us; the launch traced here: 938 us
  Pallas kernels  605 us (64%)
  matrix products  121 us (13%)
  local copies, waits for them, and re-layouts  93.1 us (10%)
  other arithmetic  86.4 us (9%)
  between operations  16.6 us (2%)
  starting transfers between devices  12.5 us (1%)
    pallas_call x11, Pallas kernels, exchange(): pl.pallas_call(kernel, out_shape=[jax.ShapeDtypeStruct(shape, BF16) for s...  290 us
    pallas_call x1, Pallas kernels, line_sum(): pl.pallas_call(kernel, out_shape=[jax.ShapeDtypeStruct(a.shape, BF16) for...  144 us
    pallas_call x1, Pallas kernels, rows_from_experts(): pl.pallas_call(kernel, out_shape=[jax.ShapeDtypeStruct((planes, count, wi...  97.9 us
    pallas_call x1, Pallas kernels, rows_to_experts(): pl.pallas_call(kernel, out_shape=[jax.ShapeDtypeStruct((plane_experts, pl...  72.4 us
    unnamed x260, local copies, waits for them, and re-layouts  49.7 us
    dot_general x5, matrix products, contract_cols(): lax.dot_general(left_mat, right_mat, (((1,), (1,)), ((), ())), preferred_...  38.5 us
    dot_general x5, matrix products, contract_rows(): lax.dot_general(left_mat, right_mat, (((0,), (0,)), ((), ())), preferred_...  31 us
    dot_general x6, matrix products, matmul(): return jnp.dot(left_mat, right_mat, preferred_element_type=FLOAT)  28.8 us
  transfers between devices with their start and end apart: 15, of which 2 were waited for; matrix products, arithmetic and copies ran while one was open for 22% of the time, Pallas kernels for 58%

profile of v8, /device:TPU:0, one launch (start us, length us, event | category | flops | bytes accessed | tf_op | source)
XLA Modules:
  0.0 938.1 jit_solution(2973988527951343638)
XLA Ops:
  15.5 3.9 convert_element_type.379.refs_1_
  19.4 3.2 fusion.18
  28.3 60.9 %gather_inputs.1 = (bf16[8,144,2048]{2,1,0:T(8,128)(2,1)S(1)}, bf16[2048,768]{1,0:T(8,128)(2,1)S(1)}, bf16[4,128,2176]{2,1,0:T(8,128)(2,1)S(1)}) custom-call(bf16[144,2048]{1,0:T(8,128)(2,1)S(1)} %pad_maximum_fusion.10.refs_0_, bf16[256,4096]{1,0:T(8,128)(2,1)S(1)} %copy-done.4, bf16[256,512]{1,0:T(8,128)(2,1)S(1)} %copy-done.16, ...), custom_call_target="tpu_custom_call" | custom-call | bytes 195000000 | tf_op jit(solution)/shard_map/gather_inputs/pallas_call | solution.py:185
  93.1 3.6 constant_dynamic-slice_fusion
  104.9 2.7 reshape.586
  107.6 2.6 pad_maximum_fusion.4
  110.9 3.1 fusion.2
  115.5 3.0 fusion.4
  118.6 3.4 fusion.96
  126.2 24.3 %gather_keys.1 = bf16[4,1024,256]{2,1,0:T(8,128)(2,1)S(1)} custom-call(bf16[1024,256]{1,0:T(8,128)(2,1)S(1)} %pad_maximum_fusion.11.refs_0_), custom_call_target="tpu_custom_call" | custom-call | bytes 72000000 | tf_op jit(solution)/shard_map/gather_keys/pallas_call | solution.py:185
  171.4 4.5 convolution_convert_fusion
  176.0 4.2 out_sum_pair.1
  183.6 2.6 convolution_convert_fusion.9
  186.2 3.4 dynamic-slice_convert_fusion
  196.9 26.1 %out_sum_plane.1 = (bf16[4,128,2048]{2,1,0:T(8,128)(2,1)S(1)}, bf16[2,8,256,768]{3,2,1,0:T(8,128)(2,1)S(1)}) custom-call(bf16[4,128,2048]{2,1,0:T(8,128)(2,1)S(1)} %fusion.9.refs_0_, bf16[2,256,768]{2,1,0:T(8,128)(2,1)S(1)} %copy-done.9, bf16[2,256,768]{2,1,0:T(8,128)(2,1)} %collective-permute-done.refs_2_, ...), custom_call_target="tpu_custom_call" | custom-call | bytes 81000000 | tf_op jit(solution)/shard_map/out_sum_plane/pallas_call | solution.py:185
  226.2 72.4 %rows_to_experts.1 = (bf16[4,4,80,2048]{3,2,1,0:T(8,128)(2,1)S(1)}, bf16[4,4,80,128]{3,2,1,0:T(8,128)(2,1)S(1)}) custom-call(bf16[128,2048]{1,0:T(8,128)(2,1)S(1)} %multiply_convert_fusion.6.tokens_ref, bf16[128,128]{1,0:T(8,128)(2,1)S(1)} %maximum_maximum_fusion.1.lanes_ref, bf16[4,320,128]{2,1,0:T(8,128)(2,1)S(1)} %get-tuple-element.232.pick_ref), custom_call_target="tpu_custom_call" | custom-call | bytes 210000000 | tf_op jit(solution)/shard_map/rows_to_experts/pallas_call | solution.py:294
  303.5 4.3 fusion.97
  310.3 6.6 multiply_convert_fusion.3
  317.0 6.7 convolution_convert_fusion.5
  324.8 2.5 collective-permute-done.8
  334.4 4.4 gather_fusion
  338.9 13.0 %multiply_convert_fusion.1 = (bf16[1280,768]{1,0:T(8,128)(2,1)}, bf16[1280,768]{1,0:T(8,128)(2,1)}) fusion(f32[1280,768]{1,0:T(8,128)} %copy-done.111, f32[1280,768]{1,0:T(8,128)} %get-tuple-element.243, bf16[768,2048]{1,0:T(8,128)(2,1)} %bitcast.379, f32[1280]{0:T(1024)S(1)} %fusion.52, bf16[320,2048]{1,0:T(8,128)(2,1)} %copy-done.81, ...), kind=kOutput, calls=%fused_computation.32 | convolution fusion | flops 4065525760 | bytes 20190208 | tf_op jit(solution)/shard_map/dot_general | solution.py:50
  355.0 9.4 %multiply_convert_fusion = (bf16[1280,2048]{1,0:T(8,128)(2,1)}, f32[1280]{0:T(1024)S(1)}) fusion(f32[1280]{0:T(1024)S(1)} %fusion.52, bf16[320,2048]{1,0:T(8,128)(2,1)} %copy-done.81, bf16[320,2048]{1,0:T(8,128)(2,1)} %collective-permute-done.4, bf16[320,2048]{1,0:T(8,128)(2,1)} %collective-permute-done.3, bf16[320,2048]{1,0:T(8,128)(2,1)} %bitcast.395, ...), kind=kOutput, calls=%fused_computation.10 | convolution fusion | flops 4057987840 | bytes 15607808 | tf_op jit(solution)/shard_map/dot_general | solution.py:56
  365.0 11.0 %fusion.98 = f32[1280,2048]{1,0:T(8,128)} fusion(bf16[1280,768]{1,0:T(8,128)(2,1)} %get-tuple-element.75, bf16[2048,768]{1,0:T(8,128)(2,1)} %bitcast.386), kind=kOutput, calls=%fused_computation.284 | convolution fusion | flops 4026531840 | bytes 15597568 | tf_op jit(solution)/shard_map/dot_general | solution.py:50
  376.1 8.7 convolution_convert_fusion.3
  384.7 5.7 convolution_convert_fusion.4
  390.5 8.5 add_convert_fusion
  399.0 97.9 %rows_from_experts.1 = (bf16[4,128,2048]{2,1,0:T(8,128)(2,1)S(1)}, bf16[4,128,128]{2,1,0:T(8,128)(2,1)S(1)}, bf16[2,4,256,768]{3,2,1,0:T(8,128)(2,1)S(1)}) custom-call(bf16[4,4,80,2048]{3,2,1,0:T(8,128)(2,1)} %bitcast.370, bf16[4,4,80,128]{3,2,1,0:T(8,128)(2,1)S(1)} %maximum_maximum_fusion.lanes_ref, bf16[4,320,128]{2,1,0:T(8,128)(2,1)S(1)} %get-tuple-element.232.pick_ref, ...), custom_call_target="tpu_custom_call" | custom-call | bytes 270000000 | tf_op jit(solution)/shard_map/rows_from_experts/pallas_call | solution.py:445
  504.1 27.0 %gather_grads.1 = bf16[8,128,2048]{2,1,0:T(8,128)(2,1)S(1)} custom-call(bf16[128,2048]{1,0:T(8,128)(2,1)S(1)} %fusion.86.refs_0_), custom_call_target="tpu_custom_call" | custom-call | bytes 90000000 | tf_op jit(solution)/shard_map/gather_grads/pallas_call | solution.py:185
  537.2 3.9 fusion.6
  541.1 4.1 fusion.17
  551.0 3.8 bitcast_convert_fusion.3.refs_1_
  554.7 2.7 key_grads_group.1
  557.7 2.5 copy-done.7
  560.2 79.3 %key_grads_planes.1 = (bf16[3,512,256]{2,1,0:T(8,128)(2,1)S(1)}, bf16[4,4,80,2048]{3,2,1,0:T(8,128)(2,1)S(1)}) custom-call(bf16[4,512,256]{2,1,0:T(8,128)(2,1)S(1)} %fusion.16.refs_0_, bf16[4,4,80,2048]{3,2,1,0:T(8,128)(2,1)S(1)} %bitcast.348), custom_call_target="tpu_custom_call" | custom-call | bytes 180000000 | tf_op jit(solution)/shard_map/key_grads_planes/pallas_call | solution.py:185
  645.1 9.1 bitcast_convert_fusion.2
  657.9 4.1 fusion.15
  665.4 3.7 convolution_convert_fusion.1
  669.1 4.2 input_sum_pair.1
  675.5 26.3 %input_sum_plane.1 = (bf16[4,128,2048]{2,1,0:T(8,128)(2,1)S(1)}, bf16[128,2048]{1,0:T(8,128)(2,1)S(1)}) custom-call(bf16[4,128,2048]{2,1,0:T(8,128)(2,1)S(1)} %fusion.8.refs_0_, bf16[4,128,2048]{2,1,0:T(8,128)(2,1)S(1)} %convolution_convert_fusion.6.refs_1_.refs_2_.refs_4_), custom_call_target="tpu_custom_call" | custom-call | bytes 81000000 | tf_op jit(solution)/shard_map/input_sum_plane/pallas_call | solution.py:185
  704.0 6.2 convolution_convert_fusion.2.refs_0_
  710.3 33.7 %head_grads_to_shards.1 = (bf16[256,4096]{1,0:T(8,128)(2,1)S(1)}, bf16[512,512]{1,0:T(8,128)(2,1)S(1)}, bf16[8,16,384]{2,1,0:T(8,128)(2,1)S(1)}, bf16[128,2048]{1,0:T(8,128)(2,1)S(1)}) custom-call(bf16[2048,768]{1,0:T(8,128)(2,1)S(1)} %convolution_convert_fusion.2.refs_0_, bf16[8,16,384]{2,1,0:T(8,128)(2,1)S(1)} %bitcast.352, ...), custom_call_target="tpu_custom_call" | custom-call | bytes 108000000 | tf_op jit(solution)/shard_map/head_grads_to_shards/pallas_call | solution.py:185
  752.1 144.5 %line_sum.1 = (bf16[256,4096]{1,0:T(8,128)(2,1)S(1)}, bf16[512,2048]{1,0:T(8,128)(2,1)S(1)}, bf16[512,512]{1,0:T(8,128)(2,1)S(1)}, bf16[16,384]{1,0:T(8,128)(2,1)S(1)}, bf16[2,128,2048]{2,1,0:T(8,128)(2,1)S(1)}) custom-call(bf16[256,4096]{1,0:T(8,128)(2,1)S(1)} %copy-done.15, bf16[512,2048]{1,0:T(8,128)(2,1)S(1)} %copy-done.13, ...), custom_call_target="tpu_custom_call" | custom-call | bytes 400000000 | tf_op jit(solution)/shard_map/line_sum/pallas_call | solution.py:611
  901.1 4.2 convert_element_type.470
  905.3 2.5 convert_element_type.472
  913.7 3.3 slice.314
  917.1 6.5 bitcast_convert_fusion.1
  924.2 6.5 bitcast_convert_fusion
  (446 shorter events, 140.8 us)
Async XLA Ops:
  7.2 547.6 %all-gather.5.cloned.1.call-start = ((), (), s32[]{:S(2)}) async-start(), calls=%async_computation | async-start | bytes 7864320 | tf_op jit(solution)/shard_map/all_gather | solution.py:1044
  96.7 99.1 %collective-permute-start.1 = (bf16[2,256,768]{2,1,0:T(8,128)(2,1)}, bf16[2,256,768]{2,1,0:T(8,128)(2,1)}, u32[]{:S(2)}, u32[]{:S(2)}) collective-permute-start(bf16[2,256,768]{2,1,0:T(8,128)(2,1)} %get-tuple-element.179), channel_id=1, source_target_pairs={{0,4},{1,5},{2,6},{3,7},{4,0},{5,1},{6,2},{7,3},{8,12},{9,13},{10,... | collective-permute-start | bytes 2359304 | tf_op jit(solution)/shard_map/ppermute | solution.py:671
  97.2 98.6 %collective-permute-start = (bf16[2,256,768]{2,1,0:T(8,128)(2,1)}, bf16[2,256,768]{2,1,0:T(8,128)(2,1)}, u32[]{:S(2)}, u32[]{:S(2)}) collective-permute-start(bf16[2,256,768]{2,1,0:T(8,128)(2,1)} %get-tuple-element.180), channel_id=1, source_target_pairs={{0,2},{1,3},{2,0},{3,1},{4,6},{5,7},{6,4},{7,5},{8,10},{9,11},{10,... | collective-permute-start | bytes 2359304 | tf_op jit(solution)/shard_map/ppermute | solution.py:671
  98.4 6.0 copy-start.87
  100.0 216.9 %collective-permute-start.3 = (bf16[320,2048]{1,0:T(8,128)(2,1)}, bf16[320,2048]{1,0:T(8,128)(2,1)}, u32[]{:S(2)}, u32[]{:S(2)}) collective-permute-start(bf16[320,2048]{1,0:T(8,128)(2,1)} %bitcast.50), channel_id=1, source_target_pairs={{0,2},{1,3},{2,0},{3,1},{4,6},{5,7},{6,4},{7,5},{8,10},{9,11},{10,... | collective-permute-start | bytes 3932168 | tf_op jit(solution)/shard_map/ppermute | solution.py:671
  102.8 214.1 %collective-permute-start.4 = (bf16[320,2048]{1,0:T(8,128)(2,1)}, bf16[320,2048]{1,0:T(8,128)(2,1)}, u32[]{:S(2)}, u32[]{:S(2)}) collective-permute-start(bf16[320,2048]{1,0:T(8,128)(2,1)} %bitcast.52), channel_id=1, source_target_pairs={{0,4},{1,5},{2,6},{3,7},{4,0},{5,1},{6,2},{7,3},{8,12},{9,13},{10,... | collective-permute-start | bytes 3932168 | tf_op jit(solution)/shard_map/ppermute | solution.py:671
  110.2 81.4 %collective-permute-start.2 = (bf16[512,2048]{1,0:T(8,128)(2,1)}, bf16[512,2048]{1,0:T(8,128)(2,1)}, u32[]{:S(2)}, u32[]{:S(2)}) collective-permute-start(bf16[512,2048]{1,0:T(8,128)(2,1)} %pad_maximum_fusion.4), channel_id=1, source_target_pairs={{0,6},{1,7},{2,4},{3,5},{4,2},{5,3},{6,0},{7,1},{8,14},{9,15},{10,... | collective-permute-start | bytes 6291464 | tf_op jit(solution)/shard_map/ppermute | solution.py:671
  124.0 29.9 %copy-start.108 = (f32[128]{0:T(128)}, f32[128]{0:T(128)S(1)}, u32[]{:S(2)}) copy-start(f32[128]{0:T(128)S(1)} %reshape.618) | copy-start | bytes 1540
  124.1 26.5 %copy-start.106 = (f32[128]{0:T(128)}, f32[128]{0:T(128)S(1)}, u32[]{:S(2)}) copy-start(f32[128]{0:T(128)S(1)} %reshape.619) | copy-start | bytes 1540
  124.4 31.0 %copy-start.74 = (f32[128,64]{1,0:T(8,128)}, f32[128,64]{1,0:T(8,128)S(1)}, u32[]{:S(2)}) copy-start(f32[128,64]{1,0:T(8,128)S(1)} %get-tuple-element.236) | copy-start | bytes 98308
  124.4 31.0 %copy-start.76 = (f32[128,64]{1,0:T(8,128)}, f32[128,64]{1,0:T(8,128)S(1)}, u32[]{:S(2)}) copy-start(f32[128,64]{1,0:T(8,128)S(1)} %get-tuple-element.237) | copy-start | bytes 98308
  150.7 10.0 %copy-start.57 = (bf16[8,4,128,256]{3,2,1,0:T(8,128)(2,1)}, bf16[8,4,128,256]{3,2,1,0:T(8,128)(2,1)S(1)}, u32[]{:S(2)}) copy-start(bf16[8,4,128,256]{3,2,1,0:T(8,128)(2,1)S(1)} %copy.139) | copy-start | bytes 6291460
  183.6 6.0 copy-start.3
  225.4 73.3 %copy-start.56 = (bf16[4,96,2048]{2,1,0:T(8,128)(2,1)S(1)}, bf16[4,96,2048]{2,1,0:T(8,128)(2,1)}, u32[]{:S(2)}) copy-start(bf16[4,96,2048]{2,1,0:T(8,128)(2,1)} %dynamic-slice_convert_fusion) | copy-start | bytes 4718596
  298.7 11.6 %copy-start.24 = (bf16[4,4,80,2048]{3,2,1,0:T(8,128)(2,1)}, bf16[4,4,80,2048]{3,2,1,0:T(8,128)(2,1)S(1)}, u32[]{:S(2)}) copy-start(bf16[4,4,80,2048]{3,2,1,0:T(8,128)(2,1)S(1)} %get-tuple-element.65) | copy-start | bytes 15728644
  298.9 24.8 %collective-permute-start.7 = (bf16[96,2048]{1,0:T(8,128)(2,1)S(1)}, bf16[96,2048]{1,0:T(8,128)(2,1)S(1)}, u32[]{:S(2)}, u32[]{:S(2)}) collective-permute-start(bf16[96,2048]{1,0:T(8,128)(2,1)S(1)} %get-tuple-element.196), channel_id=1, source_target_pairs={{0,6},{1,7},{2,4},{3,5},{4,2},{5,3},{6,0},{7,1},{8,14},{9,15},{10,... | collective-permute-start | bytes 1179656 | tf_op jit(solution)/shard_map/ppermute | solution.py:671
  299.5 24.2 %collective-permute-start.6 = (bf16[96,2048]{1,0:T(8,128)(2,1)S(1)}, bf16[96,2048]{1,0:T(8,128)(2,1)S(1)}, u32[]{:S(2)}, u32[]{:S(2)}) collective-permute-start(bf16[96,2048]{1,0:T(8,128)(2,1)S(1)} %get-tuple-element.197), channel_id=1, source_target_pairs={{0,4},{1,5},{2,6},{3,7},{4,0},{5,1},{6,2},{7,3},{8,12},{9,13},{10,... | collective-permute-start | bytes 1179656 | tf_op jit(solution)/shard_map/ppermute | solution.py:671
  301.0 22.7 %collective-permute-start.5 = (bf16[96,2048]{1,0:T(8,128)(2,1)S(1)}, bf16[96,2048]{1,0:T(8,128)(2,1)S(1)}, u32[]{:S(2)}, u32[]{:S(2)}) collective-permute-start(bf16[96,2048]{1,0:T(8,128)(2,1)S(1)} %get-tuple-element.198), channel_id=1, source_target_pairs={{0,2},{1,3},{2,0},{3,1},{4,6},{5,7},{6,4},{7,5},{8,10},{9,11},{10,... | collective-permute-start | bytes 1179656 | tf_op jit(solution)/shard_map/ppermute | solution.py:671
  303.0 4.8 copy-start.70
  303.0 7.2 copy-start.72
  307.8 9.1 copy-start.111
  310.3 6.7 copy-start.81
  310.3 6.7 copy-start.79
  316.9 6.7 copy-start.114
  323.8 3.5 collective-permute-start.8
  324.2 8.3 collective-permute-start.12
  329.0 22.8 %collective-permute-start.11 = (bf16[96,2048]{1,0:T(8,128)(2,1)}, bf16[96,2048]{1,0:T(8,128)(2,1)S(1)}, u32[]{:S(2)}, u32[]{:S(2)}) collective-permute-start(bf16[96,2048]{1,0:T(8,128)(2,1)} %get-tuple-element.192), channel_id=1, source_target_pairs={{0,6},{1,7},{2,4},{3,5},{4,2},{5,3},{6,0},{7,1},{8,14},{9,15},{10,... | collective-permute-start | bytes 1179656 | tf_op jit(solution)/shard_map/ppermute | solution.py:671
  329.6 22.3 %collective-permute-start.10 = (bf16[96,2048]{1,0:T(8,128)(2,1)}, bf16[96,2048]{1,0:T(8,128)(2,1)}, u32[]{:S(2)}, u32[]{:S(2)}) collective-permute-start(bf16[96,2048]{1,0:T(8,128)(2,1)} %get-tuple-element.193), channel_id=1, source_target_pairs={{0,4},{1,5},{2,6},{3,7},{4,0},{5,1},{6,2},{7,3},{8,12},{9,13},{10,... | collective-permute-start | bytes 1179656 | tf_op jit(solution)/shard_map/ppermute | solution.py:671
  331.0 20.8 %collective-permute-start.9 = (bf16[96,2048]{1,0:T(8,128)(2,1)}, bf16[96,2048]{1,0:T(8,128)(2,1)}, u32[]{:S(2)}, u32[]{:S(2)}) collective-permute-start(bf16[96,2048]{1,0:T(8,128)(2,1)} %get-tuple-element.194), channel_id=1, source_target_pairs={{0,2},{1,3},{2,0},{3,1},{4,6},{5,7},{6,4},{7,5},{8,10},{9,11},{10,... | collective-permute-start | bytes 1179656 | tf_op jit(solution)/shard_map/ppermute | solution.py:671
  334.4 4.4 copy-start.80
  355.0 558.7 %all-gather.7.cloned.1.call-start = ((), (), s32[]{:S(2)}) async-start(), calls=%async_computation.1 | async-start | bytes 15728640 | tf_op jit(solution)/shard_map/all_gather | solution.py:1068
  365.0 11.0 %copy-start.112 = (bf16[1280,768]{1,0:T(8,128)(2,1)S(1)}, bf16[1280,768]{1,0:T(8,128)(2,1)}, u32[]{:S(2)}) copy-start(bf16[1280,768]{1,0:T(8,128)(2,1)} %get-tuple-element.75) | copy-start | bytes 5898244
  365.0 19.7 %slice-start.2 = ((s8[5242880]{0:T(1024)(128)(4,1)}), s8[4194304]{0:T(1024)(128)(4,1)S(1)}, s32[]{:S(2)}) async-start(s8[5242880]{0:T(1024)(128)(4,1)} %bitcast.357), calls=%async_computation.4 | async-start | bytes 8388608
  376.0 8.7 slice-start.3
  376.0 8.7 copy-start.113
  384.7 5.7 copy-start.71
  504.1 27.0 %copy-start.110 = (f32[512,2048]{1,0:T(8,128)S(1)}, f32[512,2048]{1,0:T(8,128)}, u32[]{:S(2)}) copy-start(f32[512,2048]{1,0:T(8,128)} %param.23) | copy-start | bytes 12582916
  531.1 6.1 slice-start.4
  537.2 3.9 copy-start.83
  665.2 3.9 copy-start.78
  665.2 8.2 slice-start
  665.4 7.9 slice-start.1
  669.1 4.2 copy-start.86
  901.1 4.3 copy-start.11
  905.3 4.8 copy-start.36
  913.7 9.9 %slice-start.6 = ((s8[12582912]{0:T(1024)(128)(4,1)}), s8[4194304]{0:T(1024)(128)(4,1)S(1)}, s32[]{:S(2)}) async-start(s8[12582912]{0:T(1024)(128)(4,1)} %bitcast.364), calls=%async_computation.8 | async-start | bytes 8388608
  913.7 9.9 %slice-start.7 = ((s8[12582912]{0:T(1024)(128)(4,1)}), s8[4194304]{0:T(1024)(128)(4,1)S(1)}, s32[]{:S(2)}) async-start(s8[12582912]{0:T(1024)(128)(4,1)} %bitcast.364), calls=%async_computation.9 | async-start | bytes 8388608
  917.1 6.6 slice-start.8
  (92 other events, 169.4 us)
Sparse Core Ops, SparseCore 0:
  355.1 160.9 all-gather.4
  518.3 265.6 all-gather.6

commit v9 on v8

--- a/solution.py
+++ b/solution.py
@@ -1256,7 +1256,7 @@
     small_sum = jnp.sum(small_shard.astype(FLOAT), axis=0).astype(BF16)
     if nsp == 4:
         sum_q, sum_out, sum_kv, small_sum, out_others = line_sum(
-            16, (d_wq, d_wo.astype(BF16), d_wkv, small_sum), (8, 8, 2, 1), out_blocks, (handed[0], handed_last)
+            16, (d_wq, d_wo.astype(BF16), d_wkv, small_sum), (16, 16, 4, 1), out_blocks, (handed[0], handed_last)
         )
         out_others = [out_others[d] for d in range(2)]
     else:

time: 949 us -> 948 us (level)
  no operation moved by 1% of the time
where the time goes in v9:
time: 948 us; the launch traced here: 937 us
  Pallas kernels  604 us (64%)
  matrix products  121 us (13%)
  local copies, waits for them, and re-layouts  93.1 us (10%)
  other arithmetic  86.4 us (9%)
  between operations  16.6 us (2%)
  starting transfers between devices  12.5 us (1%)
    pallas_call x11, Pallas kernels, exchange(): pl.pallas_call(kernel, out_shape=[jax.ShapeDtypeStruct(shape, BF16) for s...  290 us
    pallas_call x1, Pallas kernels, line_sum(): pl.pallas_call(kernel, out_shape=[jax.ShapeDtypeStruct(a.shape, BF16) for...  144 us
    pallas_call x1, Pallas kernels, rows_from_experts(): pl.pallas_call(kernel, out_shape=[jax.ShapeDtypeStruct((planes, count, wi...  97.9 us
    pallas_call x1, Pallas kernels, rows_to_experts(): pl.pallas_call(kernel, out_shape=[jax.ShapeDtypeStruct((plane_experts, pl...  72.4 us
    unnamed x260, local copies, waits for them, and re-layouts  49.7 us
    dot_general x5, matrix products, contract_cols(): lax.dot_general(left_mat, right_mat, (((1,), (1,)), ((), ())), preferred_...  38.5 us
    dot_general x5, matrix products, contract_rows(): lax.dot_general(left_mat, right_mat, (((0,), (0,)), ((), ())), preferred_...  31 us
    dot_general x6, matrix products, matmul(): return jnp.dot(left_mat, right_mat, preferred_element_type=FLOAT)  28.8 us
  transfers between devices with their start and end apart: 15, of which 2 were waited for; matrix products, arithmetic and copies ran while one was open for 22% of the time, Pallas kernels for 58%

profile of v9, /device:TPU:0, one launch (start us, length us, event | category | flops | bytes accessed | tf_op | source)
XLA Modules:
  0.0 937.4 jit_solution(2422557541838086107)
XLA Ops:
  15.5 3.9 convert_element_type.379.refs_1_
  19.4 3.2 fusion.18
  28.3 60.9 %gather_inputs.1 = (bf16[8,144,2048]{2,1,0:T(8,128)(2,1)S(1)}, bf16[2048,768]{1,0:T(8,128)(2,1)S(1)}, bf16[4,128,2176]{2,1,0:T(8,128)(2,1)S(1)}) custom-call(bf16[144,2048]{1,0:T(8,128)(2,1)S(1)} %pad_maximum_fusion.10.refs_0_, bf16[256,4096]{1,0:T(8,128)(2,1)S(1)} %copy-done.4, bf16[256,512]{1,0:T(8,128)(2,1)S(1)} %copy-done.16, ...), custom_call_target="tpu_custom_call" | custom-call | bytes 195000000 | tf_op jit(solution)/shard_map/gather_inputs/pallas_call | solution.py:185
  93.1 3.6 constant_dynamic-slice_fusion
  104.9 2.7 reshape.586
  107.6 2.6 pad_maximum_fusion.4
  110.9 3.1 fusion.2
  115.5 3.0 fusion.4
  118.6 3.4 fusion.96
  126.2 24.3 %gather_keys.1 = bf16[4,1024,256]{2,1,0:T(8,128)(2,1)S(1)} custom-call(bf16[1024,256]{1,0:T(8,128)(2,1)S(1)} %pad_maximum_fusion.11.refs_0_), custom_call_target="tpu_custom_call" | custom-call | bytes 72000000 | tf_op jit(solution)/shard_map/gather_keys/pallas_call | solution.py:185
  171.4 4.5 convolution_convert_fusion
  176.0 4.2 out_sum_pair.1
  183.6 2.6 convolution_convert_fusion.9
  186.2 3.4 dynamic-slice_convert_fusion
  196.9 26.1 %out_sum_plane.1 = (bf16[4,128,2048]{2,1,0:T(8,128)(2,1)S(1)}, bf16[2,8,256,768]{3,2,1,0:T(8,128)(2,1)S(1)}) custom-call(bf16[4,128,2048]{2,1,0:T(8,128)(2,1)S(1)} %fusion.9.refs_0_, bf16[2,256,768]{2,1,0:T(8,128)(2,1)S(1)} %copy-done.9, bf16[2,256,768]{2,1,0:T(8,128)(2,1)} %collective-permute-done.refs_2_, ...), custom_call_target="tpu_custom_call" | custom-call | bytes 81000000 | tf_op jit(solution)/shard_map/out_sum_plane/pallas_call | solution.py:185
  226.2 72.4 %rows_to_experts.1 = (bf16[4,4,80,2048]{3,2,1,0:T(8,128)(2,1)S(1)}, bf16[4,4,80,128]{3,2,1,0:T(8,128)(2,1)S(1)}) custom-call(bf16[128,2048]{1,0:T(8,128)(2,1)S(1)} %multiply_convert_fusion.6.tokens_ref, bf16[128,128]{1,0:T(8,128)(2,1)S(1)} %maximum_maximum_fusion.1.lanes_ref, bf16[4,320,128]{2,1,0:T(8,128)(2,1)S(1)} %get-tuple-element.232.pick_ref), custom_call_target="tpu_custom_call" | custom-call | bytes 210000000 | tf_op jit(solution)/shard_map/rows_to_experts/pallas_call | solution.py:294
  303.5 4.3 fusion.97
  310.3 6.6 multiply_convert_fusion.3
  317.0 6.7 convolution_convert_fusion.5
  324.8 2.5 collective-permute-done.8
  334.4 4.4 gather_fusion
  338.9 13.0 %multiply_convert_fusion.1 = (bf16[1280,768]{1,0:T(8,128)(2,1)}, bf16[1280,768]{1,0:T(8,128)(2,1)}) fusion(f32[1280,768]{1,0:T(8,128)} %copy-done.111, f32[1280,768]{1,0:T(8,128)} %get-tuple-element.243, bf16[768,2048]{1,0:T(8,128)(2,1)} %bitcast.379, f32[1280]{0:T(1024)S(1)} %fusion.52, bf16[320,2048]{1,0:T(8,128)(2,1)} %copy-done.81, ...), kind=kOutput, calls=%fused_computation.32 | convolution fusion | flops 4065525760 | bytes 20190208 | tf_op jit(solution)/shard_map/dot_general | solution.py:50
  355.0 9.4 %multiply_convert_fusion = (bf16[1280,2048]{1,0:T(8,128)(2,1)}, f32[1280]{0:T(1024)S(1)}) fusion(f32[1280]{0:T(1024)S(1)} %fusion.52, bf16[320,2048]{1,0:T(8,128)(2,1)} %copy-done.81, bf16[320,2048]{1,0:T(8,128)(2,1)} %collective-permute-done.4, bf16[320,2048]{1,0:T(8,128)(2,1)} %collective-permute-done.3, bf16[320,2048]{1,0:T(8,128)(2,1)} %bitcast.395, ...), kind=kOutput, calls=%fused_computation.10 | convolution fusion | flops 4057987840 | bytes 15607808 | tf_op jit(solution)/shard_map/dot_general | solution.py:56
  365.0 11.0 %fusion.98 = f32[1280,2048]{1,0:T(8,128)} fusion(bf16[1280,768]{1,0:T(8,128)(2,1)} %get-tuple-element.75, bf16[2048,768]{1,0:T(8,128)(2,1)} %bitcast.386), kind=kOutput, calls=%fused_computation.284 | convolution fusion | flops 4026531840 | bytes 15597568 | tf_op jit(solution)/shard_map/dot_general | solution.py:50
  376.1 8.7 convolution_convert_fusion.3
  384.7 5.7 convolution_convert_fusion.4
  390.5 8.5 add_convert_fusion
  399.0 97.9 %rows_from_experts.1 = (bf16[4,128,2048]{2,1,0:T(8,128)(2,1)S(1)}, bf16[4,128,128]{2,1,0:T(8,128)(2,1)S(1)}, bf16[2,4,256,768]{3,2,1,0:T(8,128)(2,1)S(1)}) custom-call(bf16[4,4,80,2048]{3,2,1,0:T(8,128)(2,1)} %bitcast.370, bf16[4,4,80,128]{3,2,1,0:T(8,128)(2,1)S(1)} %maximum_maximum_fusion.lanes_ref, bf16[4,320,128]{2,1,0:T(8,128)(2,1)S(1)} %get-tuple-element.232.pick_ref, ...), custom_call_target="tpu_custom_call" | custom-call | bytes 270000000 | tf_op jit(solution)/shard_map/rows_from_experts/pallas_call | solution.py:445
  504.1 27.0 %gather_grads.1 = bf16[8,128,2048]{2,1,0:T(8,128)(2,1)S(1)} custom-call(bf16[128,2048]{1,0:T(8,128)(2,1)S(1)} %fusion.86.refs_0_), custom_call_target="tpu_custom_call" | custom-call | bytes 90000000 | tf_op jit(solution)/shard_map/gather_grads/pallas_call | solution.py:185
  537.2 3.9 fusion.6
  541.1 4.1 fusion.17
  551.0 3.8 bitcast_convert_fusion.3.refs_1_
  554.7 2.7 key_grads_group.1
  557.7 2.5 copy-done.7
  560.2 79.3 %key_grads_planes.1 = (bf16[3,512,256]{2,1,0:T(8,128)(2,1)S(1)}, bf16[4,4,80,2048]{3,2,1,0:T(8,128)(2,1)S(1)}) custom-call(bf16[4,512,256]{2,1,0:T(8,128)(2,1)S(1)} %fusion.16.refs_0_, bf16[4,4,80,2048]{3,2,1,0:T(8,128)(2,1)S(1)} %bitcast.348), custom_call_target="tpu_custom_call" | custom-call | bytes 180000000 | tf_op jit(solution)/shard_map/key_grads_planes/pallas_call | solution.py:185
  645.1 9.1 bitcast_convert_fusion.2
  657.9 4.1 fusion.15
  665.4 3.7 convolution_convert_fusion.1
  669.1 4.2 input_sum_pair.1
  675.5 26.3 %input_sum_plane.1 = (bf16[4,128,2048]{2,1,0:T(8,128)(2,1)S(1)}, bf16[128,2048]{1,0:T(8,128)(2,1)S(1)}) custom-call(bf16[4,128,2048]{2,1,0:T(8,128)(2,1)S(1)} %fusion.8.refs_0_, bf16[4,128,2048]{2,1,0:T(8,128)(2,1)S(1)} %convolution_convert_fusion.6.refs_1_.refs_2_.refs_4_), custom_call_target="tpu_custom_call" | custom-call | bytes 81000000 | tf_op jit(solution)/shard_map/input_sum_plane/pallas_call | solution.py:185
  704.0 6.2 convolution_convert_fusion.2.refs_0_
  710.3 33.7 %head_grads_to_shards.1 = (bf16[256,4096]{1,0:T(8,128)(2,1)S(1)}, bf16[512,512]{1,0:T(8,128)(2,1)S(1)}, bf16[8,16,384]{2,1,0:T(8,128)(2,1)S(1)}, bf16[128,2048]{1,0:T(8,128)(2,1)S(1)}) custom-call(bf16[2048,768]{1,0:T(8,128)(2,1)S(1)} %convolution_convert_fusion.2.refs_0_, bf16[8,16,384]{2,1,0:T(8,128)(2,1)S(1)} %bitcast.352, ...), custom_call_target="tpu_custom_call" | custom-call | bytes 108000000 | tf_op jit(solution)/shard_map/head_grads_to_shards/pallas_call | solution.py:185
  752.1 143.8 %line_sum.1 = (bf16[256,4096]{1,0:T(8,128)(2,1)S(1)}, bf16[512,2048]{1,0:T(8,128)(2,1)S(1)}, bf16[512,512]{1,0:T(8,128)(2,1)S(1)}, bf16[16,384]{1,0:T(8,128)(2,1)S(1)}, bf16[2,128,2048]{2,1,0:T(8,128)(2,1)S(1)}) custom-call(bf16[256,4096]{1,0:T(8,128)(2,1)S(1)} %copy-done.15, bf16[512,2048]{1,0:T(8,128)(2,1)S(1)} %copy-done.13, ...), custom_call_target="tpu_custom_call" | custom-call | bytes 400000000 | tf_op jit(solution)/shard_map/line_sum/pallas_call | solution.py:611
  900.4 4.2 convert_element_type.470
  904.7 2.5 convert_element_type.472
  913.1 3.3 slice.314
  916.4 6.5 bitcast_convert_fusion.1
  923.6 6.5 bitcast_convert_fusion
  (446 shorter events, 140.8 us)
Async XLA Ops:
  7.2 547.6 %all-gather.5.cloned.1.call-start = ((), (), s32[]{:S(2)}) async-start(), calls=%async_computation | async-start | bytes 7864320 | tf_op jit(solution)/shard_map/all_gather | solution.py:1044
  96.7 99.1 %collective-permute-start.1 = (bf16[2,256,768]{2,1,0:T(8,128)(2,1)}, bf16[2,256,768]{2,1,0:T(8,128)(2,1)}, u32[]{:S(2)}, u32[]{:S(2)}) collective-permute-start(bf16[2,256,768]{2,1,0:T(8,128)(2,1)} %get-tuple-element.179), channel_id=1, source_target_pairs={{0,4},{1,5},{2,6},{3,7},{4,0},{5,1},{6,2},{7,3},{8,12},{9,13},{10,... | collective-permute-start | bytes 2359304 | tf_op jit(solution)/shard_map/ppermute | solution.py:671
  97.2 98.6 %collective-permute-start = (bf16[2,256,768]{2,1,0:T(8,128)(2,1)}, bf16[2,256,768]{2,1,0:T(8,128)(2,1)}, u32[]{:S(2)}, u32[]{:S(2)}) collective-permute-start(bf16[2,256,768]{2,1,0:T(8,128)(2,1)} %get-tuple-element.180), channel_id=1, source_target_pairs={{0,2},{1,3},{2,0},{3,1},{4,6},{5,7},{6,4},{7,5},{8,10},{9,11},{10,... | collective-permute-start | bytes 2359304 | tf_op jit(solution)/shard_map/ppermute | solution.py:671
  98.4 6.0 copy-start.87
  100.0 216.9 %collective-permute-start.3 = (bf16[320,2048]{1,0:T(8,128)(2,1)}, bf16[320,2048]{1,0:T(8,128)(2,1)}, u32[]{:S(2)}, u32[]{:S(2)}) collective-permute-start(bf16[320,2048]{1,0:T(8,128)(2,1)} %bitcast.50), channel_id=1, source_target_pairs={{0,2},{1,3},{2,0},{3,1},{4,6},{5,7},{6,4},{7,5},{8,10},{9,11},{10,... | collective-permute-start | bytes 3932168 | tf_op jit(solution)/shard_map/ppermute | solution.py:671
  102.8 214.1 %collective-permute-start.4 = (bf16[320,2048]{1,0:T(8,128)(2,1)}, bf16[320,2048]{1,0:T(8,128)(2,1)}, u32[]{:S(2)}, u32[]{:S(2)}) collective-permute-start(bf16[320,2048]{1,0:T(8,128)(2,1)} %bitcast.52), channel_id=1, source_target_pairs={{0,4},{1,5},{2,6},{3,7},{4,0},{5,1},{6,2},{7,3},{8,12},{9,13},{10,... | collective-permute-start | bytes 3932168 | tf_op jit(solution)/shard_map/ppermute | solution.py:671
  110.2 81.4 %collective-permute-start.2 = (bf16[512,2048]{1,0:T(8,128)(2,1)}, bf16[512,2048]{1,0:T(8,128)(2,1)}, u32[]{:S(2)}, u32[]{:S(2)}) collective-permute-start(bf16[512,2048]{1,0:T(8,128)(2,1)} %pad_maximum_fusion.4), channel_id=1, source_target_pairs={{0,6},{1,7},{2,4},{3,5},{4,2},{5,3},{6,0},{7,1},{8,14},{9,15},{10,... | collective-permute-start | bytes 6291464 | tf_op jit(solution)/shard_map/ppermute | solution.py:671
  124.0 29.9 %copy-start.108 = (f32[128]{0:T(128)}, f32[128]{0:T(128)S(1)}, u32[]{:S(2)}) copy-start(f32[128]{0:T(128)S(1)} %reshape.618) | copy-start | bytes 1540
  124.1 26.5 %copy-start.106 = (f32[128]{0:T(128)}, f32[128]{0:T(128)S(1)}, u32[]{:S(2)}) copy-start(f32[128]{0:T(128)S(1)} %reshape.619) | copy-start | bytes 1540
  124.4 31.0 %copy-start.74 = (f32[128,64]{1,0:T(8,128)}, f32[128,64]{1,0:T(8,128)S(1)}, u32[]{:S(2)}) copy-start(f32[128,64]{1,0:T(8,128)S(1)} %get-tuple-element.236) | copy-start | bytes 98308
  124.4 31.0 %copy-start.76 = (f32[128,64]{1,0:T(8,128)}, f32[128,64]{1,0:T(8,128)S(1)}, u32[]{:S(2)}) copy-start(f32[128,64]{1,0:T(8,128)S(1)} %get-tuple-element.237) | copy-start | bytes 98308
  150.7 10.0 %copy-start.57 = (bf16[8,4,128,256]{3,2,1,0:T(8,128)(2,1)}, bf16[8,4,128,256]{3,2,1,0:T(8,128)(2,1)S(1)}, u32[]{:S(2)}) copy-start(bf16[8,4,128,256]{3,2,1,0:T(8,128)(2,1)S(1)} %copy.139) | copy-start | bytes 6291460
  183.6 6.0 copy-start.3
  225.4 73.3 %copy-start.56 = (bf16[4,96,2048]{2,1,0:T(8,128)(2,1)S(1)}, bf16[4,96,2048]{2,1,0:T(8,128)(2,1)}, u32[]{:S(2)}) copy-start(bf16[4,96,2048]{2,1,0:T(8,128)(2,1)} %dynamic-slice_convert_fusion) | copy-start | bytes 4718596
  298.7 11.6 %copy-start.24 = (bf16[4,4,80,2048]{3,2,1,0:T(8,128)(2,1)}, bf16[4,4,80,2048]{3,2,1,0:T(8,128)(2,1)S(1)}, u32[]{:S(2)}) copy-start(bf16[4,4,80,2048]{3,2,1,0:T(8,128)(2,1)S(1)} %get-tuple-element.65) | copy-start | bytes 15728644
  298.9 24.8 %collective-permute-start.7 = (bf16[96,2048]{1,0:T(8,128)(2,1)S(1)}, bf16[96,2048]{1,0:T(8,128)(2,1)S(1)}, u32[]{:S(2)}, u32[]{:S(2)}) collective-permute-start(bf16[96,2048]{1,0:T(8,128)(2,1)S(1)} %get-tuple-element.196), channel_id=1, source_target_pairs={{0,6},{1,7},{2,4},{3,5},{4,2},{5,3},{6,0},{7,1},{8,14},{9,15},{10,... | collective-permute-start | bytes 1179656 | tf_op jit(solution)/shard_map/ppermute | solution.py:671
  299.5 24.2 %collective-permute-start.6 = (bf16[96,2048]{1,0:T(8,128)(2,1)S(1)}, bf16[96,2048]{1,0:T(8,128)(2,1)S(1)}, u32[]{:S(2)}, u32[]{:S(2)}) collective-permute-start(bf16[96,2048]{1,0:T(8,128)(2,1)S(1)} %get-tuple-element.197), channel_id=1, source_target_pairs={{0,4},{1,5},{2,6},{3,7},{4,0},{5,1},{6,2},{7,3},{8,12},{9,13},{10,... | collective-permute-start | bytes 1179656 | tf_op jit(solution)/shard_map/ppermute | solution.py:671
  301.0 22.7 %collective-permute-start.5 = (bf16[96,2048]{1,0:T(8,128)(2,1)S(1)}, bf16[96,2048]{1,0:T(8,128)(2,1)S(1)}, u32[]{:S(2)}, u32[]{:S(2)}) collective-permute-start(bf16[96,2048]{1,0:T(8,128)(2,1)S(1)} %get-tuple-element.198), channel_id=1, source_target_pairs={{0,2},{1,3},{2,0},{3,1},{4,6},{5,7},{6,4},{7,5},{8,10},{9,11},{10,... | collective-permute-start | bytes 1179656 | tf_op jit(solution)/shard_map/ppermute | solution.py:671
  303.0 4.8 copy-start.70
  303.0 7.2 copy-start.72
  307.8 9.1 copy-start.111
  310.3 6.7 copy-start.81
  310.3 6.7 copy-start.79
  316.9 6.7 copy-start.114
  323.8 3.5 collective-permute-start.8
  324.2 8.3 collective-permute-start.12
  329.0 22.8 %collective-permute-start.11 = (bf16[96,2048]{1,0:T(8,128)(2,1)}, bf16[96,2048]{1,0:T(8,128)(2,1)S(1)}, u32[]{:S(2)}, u32[]{:S(2)}) collective-permute-start(bf16[96,2048]{1,0:T(8,128)(2,1)} %get-tuple-element.192), channel_id=1, source_target_pairs={{0,6},{1,7},{2,4},{3,5},{4,2},{5,3},{6,0},{7,1},{8,14},{9,15},{10,... | collective-permute-start | bytes 1179656 | tf_op jit(solution)/shard_map/ppermute | solution.py:671
  329.6 22.3 %collective-permute-start.10 = (bf16[96,2048]{1,0:T(8,128)(2,1)}, bf16[96,2048]{1,0:T(8,128)(2,1)}, u32[]{:S(2)}, u32[]{:S(2)}) collective-permute-start(bf16[96,2048]{1,0:T(8,128)(2,1)} %get-tuple-element.193), channel_id=1, source_target_pairs={{0,4},{1,5},{2,6},{3,7},{4,0},{5,1},{6,2},{7,3},{8,12},{9,13},{10,... | collective-permute-start | bytes 1179656 | tf_op jit(solution)/shard_map/ppermute | solution.py:671
  331.0 20.8 %collective-permute-start.9 = (bf16[96,2048]{1,0:T(8,128)(2,1)}, bf16[96,2048]{1,0:T(8,128)(2,1)}, u32[]{:S(2)}, u32[]{:S(2)}) collective-permute-start(bf16[96,2048]{1,0:T(8,128)(2,1)} %get-tuple-element.194), channel_id=1, source_target_pairs={{0,2},{1,3},{2,0},{3,1},{4,6},{5,7},{6,4},{7,5},{8,10},{9,11},{10,... | collective-permute-start | bytes 1179656 | tf_op jit(solution)/shard_map/ppermute | solution.py:671
  334.4 4.4 copy-start.80
  355.0 558.1 %all-gather.7.cloned.1.call-start = ((), (), s32[]{:S(2)}) async-start(), calls=%async_computation.1 | async-start | bytes 15728640 | tf_op jit(solution)/shard_map/all_gather | solution.py:1068
  365.0 11.0 %copy-start.112 = (bf16[1280,768]{1,0:T(8,128)(2,1)S(1)}, bf16[1280,768]{1,0:T(8,128)(2,1)}, u32[]{:S(2)}) copy-start(bf16[1280,768]{1,0:T(8,128)(2,1)} %get-tuple-element.75) | copy-start | bytes 5898244
  365.0 19.7 %slice-start.2 = ((s8[5242880]{0:T(1024)(128)(4,1)}), s8[4194304]{0:T(1024)(128)(4,1)S(1)}, s32[]{:S(2)}) async-start(s8[5242880]{0:T(1024)(128)(4,1)} %bitcast.357), calls=%async_computation.4 | async-start | bytes 8388608
  376.0 8.7 slice-start.3
  376.0 8.7 copy-start.113
  384.7 5.7 copy-start.71
  504.1 27.0 %copy-start.110 = (f32[512,2048]{1,0:T(8,128)S(1)}, f32[512,2048]{1,0:T(8,128)}, u32[]{:S(2)}) copy-start(f32[512,2048]{1,0:T(8,128)} %param.23) | copy-start | bytes 12582916
  531.1 6.1 slice-start.4
  537.2 3.9 copy-start.83
  665.2 3.9 copy-start.78
  665.2 8.2 slice-start
  665.4 7.9 slice-start.1
  669.1 4.2 copy-start.86
  900.4 4.3 copy-start.11
  904.7 4.8 copy-start.36
  913.1 9.9 %slice-start.6 = ((s8[12582912]{0:T(1024)(128)(4,1)}), s8[4194304]{0:T(1024)(128)(4,1)S(1)}, s32[]{:S(2)}) async-start(s8[12582912]{0:T(1024)(128)(4,1)} %bitcast.364), calls=%async_computation.8 | async-start | bytes 8388608
  913.1 9.9 %slice-start.7 = ((s8[12582912]{0:T(1024)(128)(4,1)}), s8[4194304]{0:T(1024)(128)(4,1)S(1)}, s32[]{:S(2)}) async-start(s8[12582912]{0:T(1024)(128)(4,1)} %bitcast.364), calls=%async_computation.9 | async-start | bytes 8388608
  916.4 6.6 slice-start.8
  (92 other events, 169.4 us)
Sparse Core Ops, SparseCore 0:
  355.1 160.9 all-gather.4
  518.3 259.6 all-gather.6
